TPU v7x, 32 devices: a whole 2x2x4 slice. The times are simulated.
32 devices in a mesh: expert: 8 (over y, x, core), wshard: 4 (over z).
Axes of the slice: x: 2, y: 2, z: 4, core: 2. Of those that a mesh axis runs over, the one named last changes fastest.
Arguments:
- tokens: bfloat16 [32768, 1024], P(('expert', 'wshard')), may hold values from -6 to 6
- gain_attn: bfloat16 [1024], P('wshard'), may hold values from 0.099609375 to 1.8984375
- w_query: bfloat16 [1024, 1024], P('wshard'), may hold values from -0.1875 to 0.1875
- key_weight: bfloat16 [1024, 512], P('wshard'), may hold values from -0.1875 to 0.1875
- value_weight: bfloat16 [1024, 512], P('wshard'), may hold values from -0.1875 to 0.1875
- w_out: bfloat16 [1024, 1024], P('wshard'), may hold values from -1.5 to 1.5
- gain_ffn: bfloat16 [1024], P('wshard'), may hold values from 0.099609375 to 1.8984375
- w_router: bfloat16 [1024, 8], P('wshard'), may hold values from -0.09375 to 0.09375
- w_gate: bfloat16 [8, 1024, 512], P('expert'), may hold values from -0.1875 to 0.1875
- w_up: bfloat16 [8, 1024, 512], P('expert'), may hold values from -0.1875 to 0.1875
- w_down: bfloat16 [8, 512, 1024], P('expert'), may hold values from -0.75 to 0.75
- routes: int32 [32768, 4], P(('expert', 'wshard')), may hold values from 0 to 7, all different within a row; in each aligned block of 512 rows (0 to 511, 512 to 1023, ...) at most 512 rows name the same one
- cotangent: bfloat16 [32768, 1024], P(('expert', 'wshard')), may hold values from -6 to 6
Outputs:
- mixed: bfloat16 [32768, 1024], P(('expert', 'wshard'))
- d_tokens: float32 [32768, 1024], P(('expert', 'wshard'))
- d_gain_attn: float32 [1024], P('wshard')
- d_w_query: float32 [1024, 1024], P('wshard')
- d_w_key: float32 [1024, 512], P('wshard')
- d_w_value: float32 [1024, 512], P('wshard')
- d_w_out: float32 [1024, 1024], P('wshard')
- d_gain_ffn: float32 [1024], P('wshard')
- d_w_router: float32 [1024, 8], P('wshard')
- d_w_gate: float32 [8, 1024, 512], P('expert')
- d_w_up: float32 [8, 1024, 512], P('expert')
- d_w_down: float32 [8, 512, 1024], P('expert')
Inputs may be any that keep to these rules, and one draw needn't show every extreme that they name: `routes`: each row names 4 different experts; in each aligned block of 512 rows (one micro-batch of one device) no expert is named more than 512 times, and one is named exactly 512 times in some block.
All inputs are finite; a program needn't handle non-finite values.
Results may differ from a plain program's by a relative error of at most 0.018.
Values may be sent and summed in bfloat16 or wider, within the bound.
A program may use at most 512 MiB of HBM per device.

v0:
```python
import jax
import jax.numpy as jnp
from jax import lax
from jax.sharding import PartitionSpec as P

QUERY_HEADS = 16
KEY_VALUE_HEADS = 8
HEAD_WIDTH = 64
SEQUENCE_LENGTH = 1024
BLOCK = 256
MICRO = 2


def rotary_embed(values, token_positions, orient):
    head_size = values.shape[-1]
    half_size = head_size // 2
    frequency = jnp.exp(
        -jnp.log(10000.0) * jnp.arange(half_size).astype(jnp.float32) * 2.0 / head_size
    )
    angles = token_positions.astype(jnp.float32)[:, None] * frequency[None, :]
    cosine = jnp.cos(angles)[:, None, :]
    sines = orient * jnp.sin(angles)[:, None, :]
    leading = values[..., :half_size]
    trailing = values[..., half_size:]
    return jnp.concatenate(
        [leading * cosine - trailing * sines, trailing * cosine + leading * sines], axis=-1
    )


def norm_back(grad_norm, inputs, inverse, gain):
    gain_grad = jnp.sum(grad_norm * inputs * inverse, axis=0)
    scaled = grad_norm * gain
    inner = jnp.mean(scaled * inputs, axis=-1, keepdims=True)
    return (inverse * scaled - inputs * inverse * inverse * inverse * inner, gain_grad)


def masked_scores(query_rows, keys_part, allowed, scale_factor):
    scores = (
        jnp.einsum("bsgd,btd->bgst", query_rows, keys_part, preferred_element_type=jnp.float32)
        * scale_factor
    )
    return jnp.where(allowed, scores, -1e30)


def head_forward(query_rows, keys_part, vals_part, allowed, scale_factor):
    scores = masked_scores(query_rows, keys_part, allowed, scale_factor)
    largest = jnp.max(scores, axis=-1, keepdims=True)
    totals = jnp.sum(jnp.exp(scores - largest), axis=-1, keepdims=True)
    logsum = largest + jnp.log(totals)
    weights = jnp.exp(scores - logsum).astype(jnp.bfloat16)
    result = jnp.einsum("bgst,btd->bsgd", weights, vals_part, preferred_element_type=jnp.float32)
    return (result, logsum)


def head_backward(query_rows, keys_part, vals_part, logsum, grad_out, allowed, scale_factor):
    scores = masked_scores(query_rows, keys_part, allowed, scale_factor)
    probs = jnp.exp(scores - logsum)
    weights = probs.astype(jnp.bfloat16)
    value_gradient_rows = jnp.einsum(
        "bgst,bsgd->btd", weights, grad_out, preferred_element_type=jnp.float32
    )
    grad_probs = jnp.einsum(
        "bsgd,btd->bgst", grad_out, vals_part, preferred_element_type=jnp.float32
    )
    inner = jnp.sum(grad_probs * probs, axis=-1, keepdims=True)
    grad_scores = (probs * (grad_probs - inner)).astype(jnp.bfloat16)
    grad_query = (
        jnp.einsum("bgst,btd->bsgd", grad_scores, keys_part, preferred_element_type=jnp.float32)
        * scale_factor
    )
    key_gradient_rows = (
        jnp.einsum("bgst,bsgd->btd", grad_scores, query_rows, preferred_element_type=jnp.float32)
        * scale_factor
    )
    return (grad_query, key_gradient_rows, value_gradient_rows)


def expert_rows(received, w_gate, w_up, w_down):
    gate = jnp.einsum("...jcd,jdf->...jcf", received, w_gate, preferred_element_type=jnp.float32)
    upval = jnp.einsum("...jcd,jdf->...jcf", received, w_up, preferred_element_type=jnp.float32)
    hidden = (jax.nn.silu(gate) * upval).astype(jnp.bfloat16)
    produced = jnp.einsum(
        "...jcf,jfd->...jcd", hidden, w_down, preferred_element_type=jnp.float32
    ).astype(jnp.bfloat16)
    return (produced, gate, upval)


def on_device(
    tokens,
    gain_attn,
    w_query,
    key_weight,
    value_weight,
    w_out,
    gain_ffn,
    w_router,
    w_gate,
    w_up,
    w_down,
    routes,
    cotangent,
):
    gain_one, query_w, key_matrix, value_matrix, out_w, router_w, gain_two = (
        lax.all_gather(gain_attn, "wshard", axis=0, tiled=True),
        lax.all_gather(w_query, "wshard", axis=0, tiled=True),
        lax.all_gather(key_weight, "wshard", axis=0, tiled=True),
        lax.all_gather(value_weight, "wshard", axis=0, tiled=True),
        lax.all_gather(w_out, "wshard", axis=0, tiled=True),
        lax.all_gather(w_router, "wshard", axis=0, tiled=True),
        lax.all_gather(gain_ffn, "wshard", axis=0, tiled=True),
    )
    gain_one = gain_one.astype(jnp.float32)
    gain_two = gain_two.astype(jnp.float32)
    total_row_count, width = tokens.shape
    top_count = routes.shape[1]
    expert_count = router_w.shape[1]
    owners = lax.axis_size("expert")
    local_count = w_gate.shape[0]
    head_groups = QUERY_HEADS // KEY_VALUE_HEADS
    sequence_count = total_row_count // SEQUENCE_LENGTH
    scale_factor = HEAD_WIDTH ** (-0.5)
    token_positions = jnp.arange(total_row_count) % SEQUENCE_LENGTH
    blocks = jnp.arange(SEQUENCE_LENGTH) // BLOCK
    allowed = blocks[None, :] <= blocks[:, None]
    inputs = tokens.astype(jnp.float32)
    inverse_one = lax.rsqrt(jnp.mean(inputs * inputs, axis=-1, keepdims=True) + 1e-06)
    normalized_input = (inputs * inverse_one * gain_one).astype(jnp.bfloat16)
    qpre = jnp.dot(normalized_input, query_w, preferred_element_type=jnp.float32).reshape(
        total_row_count, QUERY_HEADS, HEAD_WIDTH
    )
    prerotation_keys = jnp.dot(
        normalized_input, key_matrix, preferred_element_type=jnp.float32
    ).reshape(total_row_count, KEY_VALUE_HEADS, HEAD_WIDTH)
    value_rows = jnp.dot(normalized_input, value_matrix, preferred_element_type=jnp.float32).astype(
        jnp.bfloat16
    )
    query_rows = rotary_embed(qpre, token_positions, 1.0).astype(jnp.bfloat16)
    complete_keys = rotary_embed(prerotation_keys, token_positions, 1.0).astype(jnp.bfloat16)
    query_head_rows = jnp.moveaxis(
        query_rows.reshape(
            sequence_count, SEQUENCE_LENGTH, KEY_VALUE_HEADS, head_groups, HEAD_WIDTH
        ),
        2,
        0,
    )
    key_head_rows = jnp.moveaxis(
        complete_keys.reshape(sequence_count, SEQUENCE_LENGTH, KEY_VALUE_HEADS, HEAD_WIDTH), 2, 0
    )
    value_head_rows = jnp.moveaxis(
        value_rows.reshape(sequence_count, SEQUENCE_LENGTH, KEY_VALUE_HEADS, HEAD_WIDTH), 2, 0
    )
    head_out, logsums = lax.map(
        lambda single_entry: head_forward(
            single_entry[0], single_entry[1], single_entry[2], allowed, scale_factor
        ),
        (query_head_rows, key_head_rows, value_head_rows),
    )
    attended_rows = (
        jnp.moveaxis(head_out, 0, 2)
        .reshape(total_row_count, QUERY_HEADS * HEAD_WIDTH)
        .astype(jnp.bfloat16)
    )
    resid = inputs + jnp.dot(attended_rows, out_w, preferred_element_type=jnp.float32)
    inverse_two = lax.rsqrt(jnp.mean(resid * resid, axis=-1, keepdims=True) + 1e-06)
    moe_in = (resid * inverse_two * gain_two).astype(jnp.bfloat16)
    logits = jnp.dot(moe_in, router_w, preferred_element_type=jnp.float32)
    picked = (routes[:, :, None] == jnp.arange(expert_count)[None, None, :]).astype(jnp.float32)
    top = jnp.einsum("tke,te->tk", picked, logits)
    gates = jax.nn.softmax(top, axis=-1)
    mb_rows = total_row_count // MICRO
    capacity = 2 * mb_rows * top_count // expert_count
    kept_parts = []
    combined_parts = []
    for micro_index in range(MICRO):
        lower = micro_index * mb_rows
        route_part = routes[lower : lower + mb_rows].reshape(-1)
        hits = (route_part[:, None] == jnp.arange(expert_count)[None, :]).astype(jnp.int32)
        before = jnp.cumsum(hits, axis=0) - hits
        slot_index = jnp.sum(before * hits, axis=1)
        target = route_part * capacity + slot_index
        copies = jnp.repeat(moe_in[lower : lower + mb_rows], top_count, axis=0)
        sending = jnp.zeros((expert_count * capacity, width), jnp.bfloat16).at[target].set(copies)
        sending = sending.reshape(owners, local_count, capacity, width)
        arrived = lax.all_to_all(sending, "expert", split_axis=0, concat_axis=0, tiled=True)
        made, expert_gate_part, up_part = expert_rows(arrived, w_gate, w_up, w_down)
        back = lax.all_to_all(made, "expert", split_axis=0, concat_axis=0, tiled=True)
        received = arrived
        gate = expert_gate_part
        upval = up_part
        gathered = back.reshape(expert_count * capacity, width)[target].reshape(
            mb_rows, top_count, width
        )
        gate_part = gates[lower : lower + mb_rows]
        combined_parts.append(jnp.sum(gathered.astype(jnp.float32) * gate_part[:, :, None], axis=1))
        kept_parts.append((target, sending, gathered, received, gate, upval))
    combined = jnp.concatenate(combined_parts, axis=0)
    mixed = (resid + combined).astype(jnp.bfloat16)
    grad_in = cotangent.astype(jnp.float32)
    router_grad = jnp.zeros((width, expert_count), jnp.float32)
    gate_grad = jnp.zeros(w_gate.shape, jnp.float32)
    up_grad = jnp.zeros(w_up.shape, jnp.float32)
    down_grad = jnp.zeros(w_down.shape, jnp.float32)
    grad_moe_parts = []
    for micro_index in range(MICRO):
        lower = micro_index * mb_rows
        target, sending, gathered, received, gate, upval = kept_parts[micro_index]
        grad_part = grad_in[lower : lower + mb_rows]
        gate_part = gates[lower : lower + mb_rows]
        moe_part = moe_in[lower : lower + mb_rows]
        grad_gates = jnp.sum(gathered.astype(jnp.float32) * grad_part[:, None, :], axis=-1)
        grad_top = gate_part * (grad_gates - jnp.sum(gate_part * grad_gates, axis=1, keepdims=True))
        grad_logits = jnp.einsum("tk,tke->te", grad_top, picked[lower : lower + mb_rows]).astype(
            jnp.bfloat16
        )
        router_grad = router_grad + jnp.einsum(
            "td,te->de", moe_part, grad_logits, preferred_element_type=jnp.float32
        )
        grad_moe = jnp.einsum(
            "te,de->td", grad_logits, router_w, preferred_element_type=jnp.float32
        )
        routed = (
            (gate_part[:, :, None] * grad_part[:, None, :])
            .astype(jnp.bfloat16)
            .reshape(mb_rows * top_count, width)
        )
        grad_send = jnp.zeros((expert_count * capacity, width), jnp.bfloat16).at[target].set(routed)
        grad_recv = lax.all_to_all(
            grad_send.reshape(owners, local_count, capacity, width),
            "expert",
            split_axis=0,
            concat_axis=0,
            tiled=True,
        )
        expert_in = lax.all_to_all(sending, "expert", split_axis=0, concat_axis=0, tiled=True)
        gate = jnp.einsum("njcd,jdf->njcf", expert_in, w_gate, preferred_element_type=jnp.float32)
        upval = jnp.einsum("njcd,jdf->njcf", expert_in, w_up, preferred_element_type=jnp.float32)
        sigma = jax.nn.sigmoid(gate)
        silu_gate = gate * sigma
        hidden = (silu_gate * upval).astype(jnp.bfloat16)
        grad_hidden = jnp.einsum(
            "njcd,jfd->njcf", grad_recv, w_down, preferred_element_type=jnp.float32
        ).astype(jnp.bfloat16)
        down_grad = down_grad + jnp.einsum(
            "njcf,njcd->jfd", hidden, grad_recv, preferred_element_type=jnp.float32
        )
        grad_hidden = grad_hidden.astype(jnp.float32)
        grad_gate = (grad_hidden * upval * sigma * (1.0 + gate * (1.0 - sigma))).astype(
            jnp.bfloat16
        )
        grad_up = (grad_hidden * silu_gate).astype(jnp.bfloat16)
        gate_grad = gate_grad + jnp.einsum(
            "njcd,njcf->jdf", expert_in, grad_gate, preferred_element_type=jnp.float32
        )
        up_grad = up_grad + jnp.einsum(
            "njcd,njcf->jdf", expert_in, grad_up, preferred_element_type=jnp.float32
        )
        grad_inputs = (
            jnp.einsum("njcf,jdf->njcd", grad_gate, w_gate, preferred_element_type=jnp.float32)
            + jnp.einsum("njcf,jdf->njcd", grad_up, w_up, preferred_element_type=jnp.float32)
        ).astype(jnp.bfloat16)
        grad_back = lax.all_to_all(grad_inputs, "expert", split_axis=0, concat_axis=0, tiled=True)
        grad_rows = grad_back.reshape(expert_count * capacity, width)[target].reshape(
            mb_rows, top_count, width
        )
        grad_moe_parts.append(grad_moe + jnp.sum(grad_rows.astype(jnp.float32), axis=1))
    grad_moe = jnp.concatenate(grad_moe_parts, axis=0)
    grad_norm_two, gain_two_grad = norm_back(grad_moe, resid, inverse_two, gain_two)
    grad_resid = grad_in + grad_norm_two
    grad_z = grad_resid.astype(jnp.bfloat16)
    out_grad = jnp.einsum("ti,td->id", attended_rows, grad_z, preferred_element_type=jnp.float32)
    attention_gradient = jnp.einsum(
        "td,id->ti", grad_z, out_w, preferred_element_type=jnp.float32
    ).astype(jnp.bfloat16)
    heads_gradient = jnp.moveaxis(
        attention_gradient.reshape(
            sequence_count, SEQUENCE_LENGTH, KEY_VALUE_HEADS, head_groups, HEAD_WIDTH
        ),
        2,
        0,
    )
    grad_query, key_gradient_rows, value_gradient_rows = lax.map(
        lambda single_entry: head_backward(
            single_entry[0],
            single_entry[1],
            single_entry[2],
            single_entry[3],
            single_entry[4],
            allowed,
            scale_factor,
        ),
        (query_head_rows, key_head_rows, value_head_rows, logsums, heads_gradient),
    )
    grad_query = jnp.moveaxis(grad_query, 0, 2).reshape(total_row_count, QUERY_HEADS, HEAD_WIDTH)
    key_gradient_rows = jnp.moveaxis(key_gradient_rows, 0, 2).reshape(
        total_row_count, KEY_VALUE_HEADS, HEAD_WIDTH
    )
    value_gradient_rows = (
        jnp.moveaxis(value_gradient_rows, 0, 2)
        .reshape(total_row_count, KEY_VALUE_HEADS * HEAD_WIDTH)
        .astype(jnp.bfloat16)
    )
    grad_qpre = (
        rotary_embed(grad_query, token_positions, -1.0)
        .reshape(total_row_count, QUERY_HEADS * HEAD_WIDTH)
        .astype(jnp.bfloat16)
    )
    prerotation_key_gradient = (
        rotary_embed(key_gradient_rows, token_positions, -1.0)
        .reshape(total_row_count, KEY_VALUE_HEADS * HEAD_WIDTH)
        .astype(jnp.bfloat16)
    )
    query_grad = jnp.einsum(
        "td,ti->di", normalized_input, grad_qpre, preferred_element_type=jnp.float32
    )
    key_grad = jnp.einsum(
        "td,ti->di", normalized_input, prerotation_key_gradient, preferred_element_type=jnp.float32
    )
    value_grad = jnp.einsum(
        "td,ti->di", normalized_input, value_gradient_rows, preferred_element_type=jnp.float32
    )
    grad_normed = (
        jnp.einsum("ti,di->td", grad_qpre, query_w, preferred_element_type=jnp.float32)
        + jnp.einsum(
            "ti,di->td", prerotation_key_gradient, key_matrix, preferred_element_type=jnp.float32
        )
        + jnp.einsum(
            "ti,di->td", value_gradient_rows, value_matrix, preferred_element_type=jnp.float32
        )
    )
    grad_norm_one, gain_one_grad = norm_back(grad_normed, inputs, inverse_one, gain_one)
    d_tokens = grad_resid + grad_norm_one
    summed = lax.psum(
        (gain_one_grad, query_grad, key_grad, value_grad, out_grad, router_grad, gain_two_grad),
        ("expert", "wshard"),
    )
    shard_index = lax.axis_index("wshard")
    shards = (gain_attn, w_query, key_weight, value_weight, w_out, w_router, gain_ffn)
    reduced = tuple(
        (
            lax.dynamic_slice_in_dim(whole, shard_index * piece.shape[0], piece.shape[0], 0)
            for whole, piece in zip(summed, shards)
        )
    )
    expert_sums = (
        lax.psum(gate_grad.astype(jnp.bfloat16), "wshard").astype(jnp.float32),
        lax.psum(up_grad.astype(jnp.bfloat16), "wshard").astype(jnp.float32),
        lax.psum(down_grad.astype(jnp.bfloat16), "wshard").astype(jnp.float32),
    )
    return (
        mixed,
        d_tokens,
        reduced[0],
        reduced[1],
        reduced[2],
        reduced[3],
        reduced[4],
        reduced[6],
        reduced[5],
        expert_sums[0],
        expert_sums[1],
        expert_sums[2],
    )


def solution(mesh):
    placed = (
        P(("expert", "wshard"), None),
        P("wshard"),
        P("wshard", None),
        P("wshard", None),
        P("wshard", None),
        P("wshard", None),
        P("wshard"),
        P("wshard", None),
        P("expert", None, None),
        P("expert", None, None),
        P("expert", None, None),
        P(("expert", "wshard"), None),
        P(("expert", "wshard"), None),
    )
    return jax.shard_map(
        on_device,
        mesh=mesh,
        in_specs=placed,
        out_specs=(
            P(("expert", "wshard"), None),
            P(("expert", "wshard"), None),
            P("wshard"),
            P("wshard", None),
            P("wshard", None),
            P("wshard", None),
            P("wshard", None),
            P("wshard"),
            P("wshard", None),
            P("expert", None, None),
            P("expert", None, None),
            P("expert", None, None),
        ),
        check_vma=False,
    )
```

profile of v0, /device:TPU:0, one launch (start us, length us, event | category | flops | bytes accessed | tf_op | source)
XLA Modules:
  0.0 1576.5 jit_solution(3095306981776786165)
XLA Ops:
  18.5 12.8 all-gather
  39.0 13.6 all_gather.27
  76.1 10.2 mul.674
  95.2 21.3 %all-gather.11.cloned.1.call-done = bf16[1024,1024]{1,0:T(8,128)(2,1)} async-done(((bf16[256,1024]{1,0:T(8,128)(2,1)}), bf16[1024,1024]{1,0:T(8,128)(2,1)}) %all-gather.11.cloned.1.call-update) | async-done | bytes 2097168 | tf_op jit(solution)/shard_map/all_gather | solution.py:105
  123.0 81.7 %while.30 = (s32[]{:T(128)}, bf16[8,1,1024,2,64]{2,4,3,1,0:T(8,128)(2,1)}, f32[8,1,2,1024,1]{3,2,4,1,0:T(2,128)}, bf16[8,1,1024,64]{2,3,1,0:T(8,128)(2,1)}, bf16...) while((s32[]{:T(128)}, ...), condition=%wide.region_4.5_spmd.clone.clone, body=%wide.region_1.4_spmd.clone.sunk.clone | while | flops 560986112 | bytes 30480972 | solution.py:152
  217.2 26.4 %scatter_custom_fusion.2 = bf16[4096,1024]{1,0:T(8,128)(2,1)} fusion(s32[2048]{0:T(1024)S(1)} %bitcast.684, f32[2048,1024]{1,0:T(8,128)} %mul.674, f32[2048]{0:T(1024)S(1)} %mul.672, bf16[]{:T(256)} %constant.121.clone.1), kind=kCustom, calls=%fused_computation.162 | custom fusion | flops 4194304 | bytes 16785410 | tf_op jit(solution)/shard_map/scatter | solution.py:226
  261.6 15.5 scatter_custom_fusion
  277.2 65.4 %all-to-all-done.4 = bf16[8,1,512,1024]{3,2,1,0:T(8,128)(2,1)} async-done(((bf16[8,1,512,1024]{3,2,1,0:T(8,128)(2,1)}), bf16[8,1,512,1024]{3,2,1,0:T(8,128)(2,1)}, u32[]{:S(2)}, u32[]{:S(2)}) %all-to-all-start.4) | async-done | bytes 8388640 | tf_op jit(solution)/shard_map/all_to_all | solution.py:227
  369.3 16.3 %scatter_custom_fusion.3 = bf16[4096,1024]{1,0:T(8,128)(2,1)} fusion(s32[2048]{0:T(1024)S(1)} %bitcast.687, f32[2048,1024]{1,0:T(8,128)} %mul.687, f32[2048]{0:T(1024)S(1)} %mul.685, bf16[]{:T(256)} %constant.121.clone.1), kind=kCustom, calls=%fused_computation.163 | custom fusion | flops 4194304 | bytes 16785410 | tf_op jit(solution)/shard_map/scatter | solution.py:226
  385.6 56.2 %all-to-all-done = bf16[8,1,512,1024]{3,2,1,0:T(8,128)(2,1)} async-done(((bf16[8,1,512,1024]{3,2,1,0:T(8,128)(2,1)}), bf16[8,1,512,1024]{3,2,1,0:T(8,128)(2,1)}, u32[]{:S(2)}, u32[]{:S(2)}) %all-to-all-start) | async-done | bytes 8388640 | tf_op jit(solution)/shard_map/all_to_all | solution.py:184
  458.0 15.3 scatter_custom_fusion.1
  473.3 68.1 %all-to-all-done.6 = bf16[8,1,512,1024]{3,2,1,0:T(8,128)(2,1)} async-done(((bf16[8,1,512,1024]{3,2,1,0:T(8,128)(2,1)}), bf16[8,1,512,1024]{3,2,1,0:T(8,128)(2,1)}, u32[]{:S(2)}, u32[]{:S(2)}) %all-to-all-start.6) | async-done | bytes 8388640 | tf_op jit(solution)/shard_map/all_to_all | solution.py:227
  563.4 15.3 fusion.73
  588.9 15.5 fusion.113
  604.4 36.3 %all-to-all-done.2 = bf16[8,1,512,1024]{3,2,1,0:T(8,128)(2,1)} async-done(((bf16[8,1,512,1024]{3,2,1,0:T(8,128)(2,1)}), bf16[8,1,512,1024]{3,2,1,0:T(8,128)(2,1)}, u32[]{:S(2)}, u32[]{:S(2)}) %all-to-all-start.2) | async-done | bytes 8388640 | tf_op jit(solution)/shard_map/all_to_all | solution.py:184
  654.6 85.1 %all-to-all-done.5 = bf16[8,1,512,1024]{3,2,1,0:T(8,128)(2,1)} async-done(((bf16[8,1,512,1024]{3,2,1,0:T(8,128)(2,1)}), bf16[8,1,512,1024]{3,2,1,0:T(8,128)(2,1)}, u32[]{:S(2)}, u32[]{:S(2)}) %all-to-all-start.5) | async-done | bytes 8388640 | tf_op jit(solution)/shard_map/all_to_all | solution.py:261
  761.4 15.3 fusion.77
  785.3 53.4 %all-to-all-done.1 = bf16[8,1,512,1024]{3,2,1,0:T(8,128)(2,1)} async-done(((bf16[8,1,512,1024]{3,2,1,0:T(8,128)(2,1)}), bf16[8,1,512,1024]{3,2,1,0:T(8,128)(2,1)}, u32[]{:S(2)}, u32[]{:S(2)}) %all-to-all-start.1) | async-done | bytes 8388640 | tf_op jit(solution)/shard_map/all_to_all | solution.py:186
  846.5 10.5 fusion.134
  864.0 15.3 fusion.114
  879.3 58.9 %all-to-all-done.3 = bf16[8,1,512,1024]{3,2,1,0:T(8,128)(2,1)} async-done(((bf16[8,1,512,1024]{3,2,1,0:T(8,128)(2,1)}), bf16[8,1,512,1024]{3,2,1,0:T(8,128)(2,1)}, u32[]{:S(2)}, u32[]{:S(2)}) %all-to-all-start.3) | async-done | bytes 8388640 | tf_op jit(solution)/shard_map/all_to_all | solution.py:186
  943.3 10.3 fusion.169
  969.5 10.9 fusion.93
  980.3 10.1 fusion.172
  990.5 15.6 gather_fusion.2
  1024.8 15.5 gather_fusion
  1048.6 15.5 gather_fusion.1
  1072.4 15.9 %gather_fusion.3 = bf16[2048,1024]{1,0:T(8,128)(2,1)} fusion(bf16[4096,1024]{1,0:T(8,128)(2,1)} %bitcast.100, s32[2048]{0:T(1024)S(1)} %broadcast_clamp_fusion), kind=kCustom, calls=%fused_computation.3 | custom fusion | bytes 8396800 | tf_op jit(solution)/shard_map/gather | solution.py:262
  1109.7 20.1 %multiply_reduce_fusion = (f32[512,4]{1,0:T(8,128)S(1)}, f32[512,1024]{1,0:T(8,128)}, f32[512,1024]{1,0:T(8,128)}, f32[512,4]{1,0:T(8,128)S(1)}) fusion(f32[512,4,1024]{2,1,0:T(4,128)} %reshape.658, f32[512,1024]{1,0:T(8,128)} %copy-done.10, f32[512,4]{1,0:T(8,128)S(1)} %copy-done.27, f32[512,4,1024]{2,1,0:T(4,128)} %reshape.657, ...), kind=kLoop, calls=%fused_computation.137 | loop fusion | flops 15724544 | bytes 25198592 | tf_op jit(solution)/shard_map/reduce_sum | solution.py:210
  1153.8 155.5 %while.31 = (s32[]{:T(128)}, f32[8,1,1024,2,64]{2,4,3,1,0:T(8,128)}, f32[8,1,1024,64]{2,3,1,0:T(8,128)S(1)}, bf16[8,1,1024,64]{2,3,1,0:T(8,128)(2,1)}, bf16[8,1,...) while((s32[]{:T(128)}, ...), condition=%wide.region_29.30_spmd.clone.clone, body=%wide.region_27.29_spmd.clone.sunk.clone | while | flops 1374877696 | bytes 69665896 | solution.py:281
  1347.1 40.8 %all-reduce = (f32[1024]{0:T(1024)S(1)}, f32[1024]{0:T(1024)S(1)}, f32[1024,8]{0,1:T(8,128)S(1)}) all-reduce(f32[1024]{0:T(1024)S(1)} %get-tuple-element.271, f32[1024]{0:T(1024)S(1)} %copy-done.66, f32[1024,8]{0,1:T(8,128)S(1)} %convolution_add_fusion.2), channel_id=1, replica_groups=mesh['expert'=8,'wshard'=4] {'expert','wshard'}, use_global_device_ids=true, to_apply=%region_32.33 | all-reduce | flops 10240 | bytes 81920 | tf_op jit(solution)/shard_map/psum | solution.py:332
  1404.7 156.1 %all-reduce.6.cloned.1.call-done = (f32[1024,1024]{1,0:T(8,128)}, f32[1024,512]{1,0:T(8,128)}, f32[1024,512]{1,0:T(8,128)}, f32[1024,1024]{1,0:T(8,128)}) async-done(((f32[1024,1024]{1,0:T(8,128)}, f32[1024,512]{1,0:T(8,128)}, f32[1024,512]{1,0:T(8,128)}, f32[1024,1024]{1,0:T(8,128)}), (f32[1024,1024]{1,0:T(8,128)}, f32[1024,512]{1,0:T(8,128)}, f32[1024,512]{1,0:T(8,128)}, ...) | async-done | bytes 12582928 | tf_op jit(solution)/shard_map/psum | solution.py:332
  (451 shorter events, 622.5 us)
Async XLA Ops:
  7.2 556.2 %copy-start = (bf16[1,1024,512]{2,1,0:T(8,128)(2,1)S(1)}, bf16[1,1024,512]{2,1,0:T(8,128)(2,1)}, u32[]{:S(2)}) copy-start(bf16[1,1024,512]{2,1,0:T(8,128)(2,1)} %param.26) | copy-start | bytes 3145732
  7.2 80.4 %all-gather.9.cloned.1.call-start = ((), (), s32[]{:S(2)}) async-start(), calls=%async_computation.9 | async-start | bytes 1310720 | tf_op jit(solution)/shard_map/all_gather | solution.py:106
  7.9 83.7 %all-gather.7.cloned.1.call-start = ((), (), s32[]{:S(2)}) async-start(), calls=%async_computation.8 | async-start | bytes 1310720 | tf_op jit(solution)/shard_map/all_gather | solution.py:107
  8.7 107.8 %all-gather.11.cloned.1.call-start = ((), (), s32[]{:S(2)}) async-start(), calls=%async_computation.10 | async-start | bytes 2621440 | tf_op jit(solution)/shard_map/all_gather | solution.py:105
  9.4 195.3 %all-gather.13.cloned.1.call-start = ((), (), s32[]{:S(2)}) async-start(), calls=%async_computation.11 | async-start | bytes 2621440 | tf_op jit(solution)/shard_map/all_gather | solution.py:108
  11.1 27.9 %copy-start.68 = (bf16[256,8]{0,1:T(8,128)(2,1)S(1)}, bf16[256,8]{0,1:T(8,128)(2,1)}, u32[]{:S(2)}) copy-start(bf16[256,8]{0,1:T(8,128)(2,1)} %param.24) | copy-start | bytes 12292
  18.0 186.7 %copy-start.6 = (bf16[1024,1024]{0,1:T(8,128)(2,1)}, bf16[1024,1024]{0,1:T(8,128)(2,1)S(1)}, u32[]{:S(2)}) copy-start(bf16[1024,1024]{0,1:T(8,128)(2,1)S(1)} %copy.133) | copy-start | bytes 6291460
  18.5 98.0 %copy-start.54 = (f32[1024]{0:T(1024)}, f32[1024]{0:T(1024)S(1)}, u32[]{:S(2)}) copy-start(f32[1024]{0:T(1024)S(1)} %add_rsqrt_fusion.1) | copy-start | bytes 12292
  31.3 85.2 %copy-start.56 = (f32[4,1,256]{2,1,0:T(1,128)}, f32[4,1,256]{2,1,0:T(1,128)S(1)}, u32[]{:S(2)}) copy-start(f32[4,1,256]{2,1,0:T(1,128)S(1)} %convert_element_type.442) | copy-start | bytes 12292
  39.0 170.6 %copy-start.50 = (f32[4,1,256]{2,1,0:T(1,128)}, f32[4,1,256]{2,1,0:T(1,128)S(1)}, u32[]{:S(2)}) copy-start(f32[4,1,256]{2,1,0:T(1,128)S(1)} %convert_element_type.443) | copy-start | bytes 12292
  87.5 33.2 %copy-start.22 = (f32[1024,32]{0,1:T(8,128)}, f32[1024,32]{0,1:T(8,128)S(1)}, u32[]{:S(2)}) copy-start(f32[1024,32]{0,1:T(8,128)S(1)} %get-tuple-element.355) | copy-start | bytes 393220
  87.6 174.0 %copy-start.60 = (s32[2048,1]{0,1:T(1,128)}, s32[2048,1]{0,1:T(1,128)S(1)}, u32[]{:S(2)}) copy-start(s32[2048,1]{0,1:T(1,128)S(1)} %compare_select_fusion.1) | copy-start | bytes 24580
  210.3 38.2 %copy-start.4 = (bf16[1024,1024]{0,1:T(8,128)(2,1)}, bf16[1024,1024]{0,1:T(8,128)(2,1)S(1)}, u32[]{:S(2)}) copy-start(bf16[1024,1024]{0,1:T(8,128)(2,1)S(1)} %multiply_convert_fusion.4) | copy-start | bytes 6291460
  217.0 26.6 %copy-start.24 = (f32[512,4]{1,0:T(8,128)}, f32[512,4]{1,0:T(8,128)S(1)}, u32[]{:S(2)}) copy-start(f32[512,4]{1,0:T(8,128)S(1)} %get-tuple-element.345) | copy-start | bytes 24580
  243.6 99.0 %all-to-all-start.4 = ((bf16[8,1,512,1024]{3,2,1,0:T(8,128)(2,1)}), bf16[8,1,512,1024]{3,2,1,0:T(8,128)(2,1)}, u32[]{:S(2)}, u32[]{:S(2)}) async-start(bf16[8,1,512,1024]{3,2,1,0:T(8,128)(2,1)} %bitcast.650), calls=%async_computation.4 | async-start | bytes 16777216 | tf_op jit(solution)/shard_map/all_to_all | solution.py:227
  342.6 99.2 %all-to-all-start = ((bf16[8,1,512,1024]{3,2,1,0:T(8,128)(2,1)}), bf16[8,1,512,1024]{3,2,1,0:T(8,128)(2,1)}, u32[]{:S(2)}, u32[]{:S(2)}) async-start(bf16[8,1,512,1024]{3,2,1,0:T(8,128)(2,1)} %bitcast.647), calls=%async_computation | async-start | bytes 16777216 | tf_op jit(solution)/shard_map/all_to_all | solution.py:184
  369.1 88.8 %copy-start.62 = (s32[2048,1]{0,1:T(1,128)}, s32[2048,1]{0,1:T(1,128)S(1)}, u32[]{:S(2)}) copy-start(s32[2048,1]{0,1:T(1,128)S(1)} %compare_select_fusion) | copy-start | bytes 24580
  441.8 99.6 %all-to-all-start.6 = ((bf16[8,1,512,1024]{3,2,1,0:T(8,128)(2,1)}), bf16[8,1,512,1024]{3,2,1,0:T(8,128)(2,1)}, u32[]{:S(2)}, u32[]{:S(2)}) async-start(bf16[8,1,512,1024]{3,2,1,0:T(8,128)(2,1)} %bitcast.648), calls=%async_computation.6 | async-start | bytes 16777216 | tf_op jit(solution)/shard_map/all_to_all | solution.py:227
  541.3 99.4 %all-to-all-start.2 = ((bf16[8,1,512,1024]{3,2,1,0:T(8,128)(2,1)}), bf16[8,1,512,1024]{3,2,1,0:T(8,128)(2,1)}, u32[]{:S(2)}, u32[]{:S(2)}) async-start(bf16[8,1,512,1024]{3,2,1,0:T(8,128)(2,1)} %bitcast.649), calls=%async_computation.2 | async-start | bytes 16777216 | tf_op jit(solution)/shard_map/all_to_all | solution.py:184
  640.7 99.0 %all-to-all-start.5 = ((bf16[8,1,512,1024]{3,2,1,0:T(8,128)(2,1)}), bf16[8,1,512,1024]{3,2,1,0:T(8,128)(2,1)}, u32[]{:S(2)}, u32[]{:S(2)}) async-start(bf16[8,1,512,1024]{3,2,1,0:T(8,128)(2,1)} %fusion.113), calls=%async_computation.5 | async-start | bytes 16777216 | tf_op jit(solution)/shard_map/all_to_all | solution.py:261
  739.7 99.0 %all-to-all-start.1 = ((bf16[8,1,512,1024]{3,2,1,0:T(8,128)(2,1)}), bf16[8,1,512,1024]{3,2,1,0:T(8,128)(2,1)}, u32[]{:S(2)}, u32[]{:S(2)}) async-start(bf16[8,1,512,1024]{3,2,1,0:T(8,128)(2,1)} %convert_bitcast_fusion.1), calls=%async_computation.1 | async-start | bytes 16777216 | tf_op jit(solution)/shard_map/all_to_all | solution.py:186
  785.3 58.9 %copy-start.49 = (s32[1024,4]{0,1:T(4,128)S(1)}, s32[1024,4]{0,1:T(4,128)}, u32[]{:S(2)}) copy-start(s32[1024,4]{0,1:T(4,128)} %param.28) | copy-start | bytes 49156
  785.3 61.2 %copy-start.61 = (s32[2048,1]{0,1:T(1,128)S(1)}, s32[2048,1]{0,1:T(1,128)}, u32[]{:S(2)}) copy-start(s32[2048,1]{0,1:T(1,128)} %copy-done.60) | copy-start | bytes 24580
  785.3 61.2 %copy-start.63 = (s32[2048,1]{0,1:T(1,128)S(1)}, s32[2048,1]{0,1:T(1,128)}, u32[]{:S(2)}) copy-start(s32[2048,1]{0,1:T(1,128)} %copy-done.62) | copy-start | bytes 24580
  838.7 99.5 %all-to-all-start.3 = ((bf16[8,1,512,1024]{3,2,1,0:T(8,128)(2,1)}), bf16[8,1,512,1024]{3,2,1,0:T(8,128)(2,1)}, u32[]{:S(2)}, u32[]{:S(2)}) async-start(bf16[8,1,512,1024]{3,2,1,0:T(8,128)(2,1)} %convert_bitcast_fusion), calls=%async_computation.3 | async-start | bytes 16777216 | tf_op jit(solution)/shard_map/all_to_all | solution.py:186
  938.3 134.1 %all-to-all-start.7 = ((bf16[8,1,512,1024]{3,2,1,0:T(8,128)(2,1)}), bf16[8,1,512,1024]{3,2,1,0:T(8,128)(2,1)}, u32[]{:S(2)}, u32[]{:S(2)}) async-start(bf16[8,1,512,1024]{3,2,1,0:T(8,128)(2,1)} %fusion.114), calls=%async_computation.7 | async-start | bytes 16777216 | tf_op jit(solution)/shard_map/all_to_all | solution.py:261
  943.3 385.6 %all-reduce.8.cloned.1.call-start = ((), (), s32[]{:S(2)}) async-start(), calls=%async_computation.13 | async-start | bytes 6291456 | tf_op jit(solution)/shard_map/psum | solution.py:345
  943.3 26.1 %slice-start.2 = ((s8[8388608]{0:T(1024)(128)(4,1)}), s8[4194304]{0:T(1024)(128)(4,1)S(1)}, s32[]{:S(2)}) async-start(s8[8388608]{0:T(1024)(128)(4,1)} %bitcast.694), calls=%async_computation.16 | async-start | bytes 8388608
  990.4 570.4 %all-reduce.6.cloned.1.call-start = ((), (), s32[]{:S(2)}) async-start(), calls=%async_computation.12 | async-start | bytes 25165824 | tf_op jit(solution)/shard_map/psum | solution.py:332
  1153.8 155.6 %copy-start.23 = (f32[1024,32]{0,1:T(8,128)S(1)}, f32[1024,32]{0,1:T(8,128)}, u32[]{:S(2)}) copy-start(f32[1024,32]{0,1:T(8,128)} %copy-done.22) | copy-start | bytes 393220
  1153.8 155.6 %copy-start.34 = (f32[1024,32]{0,1:T(8,128)S(1)}, f32[1024,32]{0,1:T(8,128)}, u32[]{:S(2)}) copy-start(f32[1024,32]{0,1:T(8,128)} %get-tuple-element.353) | copy-start | bytes 393220
  1401.6 167.6 %copy-start.1 = (bf16[1,1024,512]{2,1,0:T(8,128)(2,1)S(1)}, bf16[1,1024,512]{2,1,0:T(8,128)(2,1)}, u32[]{:S(2)}) copy-start(bf16[1,1024,512]{2,1,0:T(8,128)(2,1)} %param.26) | copy-start | bytes 3145732
  (73 other events, 465.5 us)
Sparse Core Ops, SparseCore 0:
  9.6 30.7 all-gather.8
  42.0 27.3 all-gather.6
  71.0 45.4 all-gather.10
  117.9 44.6 all-gather.12
  990.6 120.8 all-reduce.7
  1329.0 231.8 all-reduce.5
where the time goes:
time: 1590 us; the launch traced here: 1580 us
  waiting for transfers between devices  603 us (38%)
  matrix products  407 us (26%)
  local copies, waits for them, and re-layouts  255 us (16%)
  other arithmetic  178 us (11%)
  blocking collectives  74.9 us (5%)
  starting transfers between devices  41.4 us (3%)
    psum x1, waiting for transfers between devices, on_device(): lax.psum((gain_one_grad, query_grad, key_grad, value_grad, out_grad, rout...  156 us
    all_to_all x2, waiting for transfers between devices, on_device(): lax.all_to_all(grad_send.reshape(owners, local_count, capacity, width), '...  133 us
    all_to_all x2, waiting for transfers between devices, on_device(): lax.all_to_all(made, 'expert', split_axis=0, concat_axis=0, tiled=True)  112 us
    all_to_all x2, waiting for transfers between devices, on_device(): lax.all_to_all(sending, 'expert', split_axis=0, concat_axis=0, tiled=True)  92.4 us
    all_to_all x2, waiting for transfers between devices, on_device(): lax.all_to_all(grad_inputs, 'expert', split_axis=0, concat_axis=0, tiled=...  85.1 us
    scatter x2, other arithmetic, on_device(): jnp.zeros((expert_count * capacity, width), jnp.bfloat16).at[target]  42.7 us
    dot_general x16, matrix products, masked_scores(): jnp.einsum('bsgd,btd->bgst', query_rows, keys_part, preferred_element_typ...  41.5 us
    psum x1, blocking collectives, on_device(): lax.psum((gain_one_grad, query_grad, key_grad, value_grad, out_grad, rout...  40.8 us
  transfers between devices with their start and end apart: 14, of which 9 were waited for; matrix products, arithmetic and copies ran while one was open for 50% of the time, Pallas kernels for 0%

commit v1 on v0

v1 whole, which is shorter than its diff:
```python
import functools
import jax
import jax.numpy as jnp
import numpy as np
from jax import lax
from jax.experimental import pallas as pl
from jax.experimental.pallas import tpu as pltpu
from jax.sharding import PartitionSpec as P

QUERY_HEADS = 16
KEY_VALUE_HEADS = 8
HEAD_WIDTH = 64
SEQUENCE_LENGTH = 1024
BLOCK = 256
TILE = 256
LANES = 128
F32 = jnp.float32
BF16 = jnp.bfloat16
ANY = pl.BlockSpec(memory_space=pl.ANY)
VMEM = pl.BlockSpec(memory_space=pltpu.VMEM)
VMEM_BYTES = 60 * 1024 * 1024


def dot(a, b):
    return jnp.dot(a, b, preferred_element_type=F32)


def dot_nt(a, b):
    return lax.dot_general(a, b, (((1,), (1,)), ((), ())), preferred_element_type=F32)


def dot_tn(a, b):
    return lax.dot_general(a, b, (((0,), (0,)), ((), ())), preferred_element_type=F32)


def params(**kw):
    return pltpu.CompilerParams(vmem_limit_bytes=VMEM_BYTES, **kw)


def cost(flops, nbytes, transcendentals=0):
    return pl.CostEstimate(flops=int(flops), bytes_accessed=int(nbytes), transcendentals=int(transcendentals))


def rope_tables(rows):
    half = HEAD_WIDTH // 2
    freq = np.exp(-np.log(10000.0) * np.arange(half, dtype=np.float32) * 2.0 / HEAD_WIDTH).astype(np.float32)
    pos = (np.arange(rows) % SEQUENCE_LENGTH).astype(np.float32)
    angles = (pos[:, None] * freq[None, :]).astype(np.float32)
    cos, sin = np.cos(angles), np.sin(angles)
    return (
        np.concatenate([cos, cos, cos, cos], 1).astype(np.float32),
        np.concatenate([-sin, sin, -sin, sin], 1).astype(np.float32),
    )


def rope(u, cos, sin):
    half = HEAD_WIDTH // 2
    lane = lax.broadcasted_iota(jnp.int32, u.shape, 1)
    swapped = jnp.where(
        lane % HEAD_WIDTH < half, pltpu.roll(u, LANES - half, 1), pltpu.roll(u, half, 1)
    )
    return u * cos + swapped * sin


def row_block(width):
    return pl.BlockSpec((TILE, width), lambda i: (i, 0))


def whole_block(shape):
    return pl.BlockSpec(shape, lambda i: (0,) * len(shape))


def project_kernel(x_ref, gain_ref, w_ref, cos_ref, sin_ref, n_ref, q_ref, k_ref, v_ref):
    x = x_ref[...].astype(F32)
    inverse = lax.rsqrt(jnp.mean(x * x, axis=-1, keepdims=True) + 1e-06)
    normed = (x * inverse * gain_ref[...].astype(F32)).astype(BF16)
    n_ref[...] = normed
    cos, sin = cos_ref[...], sin_ref[...]
    step = 512
    for at in range(0, w_ref.shape[1], step):
        made = dot(normed, w_ref[:, at : at + step])
        for lo in range(0, step, LANES):
            u = made[:, lo : lo + LANES]
            c = at + lo
            if c < q_ref.shape[1]:
                q_ref[:, c : c + LANES] = (rope(u, cos, sin).astype(BF16) * jnp.asarray(HEAD_WIDTH**-0.5, BF16))
            elif c < q_ref.shape[1] + k_ref.shape[1]:
                c -= q_ref.shape[1]
                k_ref[:, c : c + LANES] = rope(u, cos, sin).astype(BF16)
            else:
                c -= q_ref.shape[1] + k_ref.shape[1]
                v_ref[:, c : c + LANES] = u.astype(BF16)


def project(tokens, gain, weights, cos, sin):
    rows, width = tokens.shape
    qw, kw = QUERY_HEADS * HEAD_WIDTH, KEY_VALUE_HEADS * HEAD_WIDTH
    return pl.pallas_call(
        project_kernel,
        grid=(rows // TILE,),
        in_specs=[row_block(width), whole_block((1, width)), whole_block(weights.shape), row_block(LANES), row_block(LANES)],
        out_specs=[row_block(width), row_block(qw), row_block(kw), row_block(kw)],
        out_shape=[jax.ShapeDtypeStruct((rows, w), BF16) for w in (width, qw, kw, kw)],
        compiler_params=params(),
        cost_estimate=cost(2 * rows * width * (qw + 2 * kw), 12 * rows * width),
        name="project",
    )(tokens, gain, weights, cos, sin)


def attend_kernel(q_ref, k_ref, v_ref, o_ref):
    for c in range(2):
        k = k_ref[:, c * HEAD_WIDTH : (c + 1) * HEAD_WIDTH]
        v = v_ref[:, c * HEAD_WIDTH : (c + 1) * HEAD_WIDTH]
        for h in range(2):
            at = (2 * c + h) * HEAD_WIDTH
            for b in range(SEQUENCE_LENGTH // BLOCK):
                n = (b + 1) * BLOCK
                rows = slice(b * BLOCK, (b + 1) * BLOCK)
                s = dot_nt(q_ref[rows, at : at + HEAD_WIDTH], k[:n])
                p = jnp.exp(s - jnp.max(s, axis=-1, keepdims=True))
                total = jnp.sum(p, axis=-1, keepdims=True)
                o = dot((p * (1.0 / total)).astype(BF16), v[:n])
                o_ref[rows, at : at + HEAD_WIDTH] = o.astype(BF16)


def head_block(width, sequence=SEQUENCE_LENGTH):
    return pl.BlockSpec((sequence, width), lambda s, i: (s, i))


def attend(queries, keys, vals):
    rows = queries.shape[0]
    steps = KEY_VALUE_HEADS // 2
    flops = 2 * QUERY_HEADS * rows * SEQUENCE_LENGTH * HEAD_WIDTH * 2
    return pl.pallas_call(
        attend_kernel,
        grid=(rows // SEQUENCE_LENGTH, steps),
        in_specs=[head_block(4 * HEAD_WIDTH), head_block(2 * HEAD_WIDTH), head_block(2 * HEAD_WIDTH)],
        out_specs=head_block(4 * HEAD_WIDTH),
        out_shape=jax.ShapeDtypeStruct(queries.shape, BF16),
        compiler_params=params(),
        cost_estimate=cost(flops * 8, 6 * rows * 1024, QUERY_HEADS * rows * 640),
        name="attend",
    )(queries, keys, vals)


def attend_back_kernel(q_ref, k_ref, v_ref, g_ref, cos_ref, sin_ref, dq_ref, dk_ref, dv_ref, dk_acc, dv_acc, dq_acc):
    dk_acc[...] = jnp.zeros_like(dk_acc)
    dv_acc[...] = jnp.zeros_like(dv_acc)
    for c in range(2):
        lanes = slice(c * HEAD_WIDTH, (c + 1) * HEAD_WIDTH)
        k, v = k_ref[:, lanes], v_ref[:, lanes]
        for h in range(2):
            at = slice((2 * c + h) * HEAD_WIDTH, (2 * c + h + 1) * HEAD_WIDTH)
            for b in range(SEQUENCE_LENGTH // BLOCK):
                n = (b + 1) * BLOCK
                rows = slice(b * BLOCK, (b + 1) * BLOCK)
                q, g = q_ref[rows, at], g_ref[rows, at]
                s = dot_nt(k[:n], q)
                dp = dot_nt(v[:n], g)
                p = jnp.exp(s - jnp.max(s, axis=0, keepdims=True))
                p = p * (1.0 / jnp.sum(p, axis=0, keepdims=True))
                ds = (p * (dp - jnp.sum(p * dp, axis=0, keepdims=True))).astype(BF16)
                dv_acc[:n, lanes] += dot(p.astype(BF16), g)
                dk_acc[:n, lanes] += dot(ds, q)
                dq_acc[rows, at] = dot_tn(ds, k[:n])
    cos, sin = cos_ref[...], -sin_ref[...]
    scale = HEAD_WIDTH**-0.5
    dq_ref[:, :LANES] = rope(dq_acc[:, :LANES] * scale, cos, sin).astype(BF16)
    dq_ref[:, LANES:] = rope(dq_acc[:, LANES:] * scale, cos, sin).astype(BF16)
    dk_ref[...] = rope(dk_acc[...], cos, sin).astype(BF16)
    dv_ref[...] = dv_acc[...].astype(BF16)


def attend_back(queries, keys, vals, grad, cos, sin):
    rows = queries.shape[0]
    steps = KEY_VALUE_HEADS // 2
    flops = 5 * QUERY_HEADS * rows * SEQUENCE_LENGTH * HEAD_WIDTH * 2
    table = pl.BlockSpec((SEQUENCE_LENGTH, LANES), lambda s, i: (s, 0))
    two, four = head_block(2 * HEAD_WIDTH), head_block(4 * HEAD_WIDTH)
    return pl.pallas_call(
        attend_back_kernel,
        grid=(rows // SEQUENCE_LENGTH, steps),
        in_specs=[four, two, two, four, table, table],
        out_specs=[four, two, two],
        out_shape=[jax.ShapeDtypeStruct(a.shape, BF16) for a in (queries, keys, vals)],
        scratch_shapes=[
            pltpu.VMEM((SEQUENCE_LENGTH, LANES), F32),
            pltpu.VMEM((SEQUENCE_LENGTH, LANES), F32),
            pltpu.VMEM((SEQUENCE_LENGTH, 2 * LANES), F32),
        ],
        compiler_params=params(),
        cost_estimate=cost(flops * 8, 12 * rows * 1024, QUERY_HEADS * rows * 640),
        name="attend_back",
    )(queries, keys, vals, grad, cos, sin)


def middle_kernel(a_ref, w_ref, x_ref, gain_ref, router_ref, routes_ref, r_ref, m_ref, mt_ref, gates_ref):
    resid = x_ref[...].astype(F32) + dot(a_ref[...], w_ref[...])
    r_ref[...] = resid
    inverse = lax.rsqrt(jnp.mean(resid * resid, axis=-1, keepdims=True) + 1e-06)
    moe_in = (resid * inverse * gain_ref[...].astype(F32)).astype(BF16)
    m_ref[...] = moe_in
    mt_ref[...] = moe_in.T
    logits = dot(moe_in, router_ref[...])
    lane = lax.broadcasted_iota(jnp.int32, logits.shape, 1)
    routes = routes_ref[...]
    picked = lane == routes[:, 0:1]
    for k in range(1, routes.shape[1]):
        picked = jnp.logical_or(picked, lane == routes[:, k : k + 1])
    logits = jnp.where(picked, logits, -1e30)
    weights = jnp.where(picked, jnp.exp(logits - jnp.max(logits, axis=-1, keepdims=True)), 0.0)
    gates_ref[...] = weights / jnp.sum(weights, axis=-1, keepdims=True)


def middle(attended, out_w, tokens, gain, router_w, routes):
    rows, width = tokens.shape
    return pl.pallas_call(
        middle_kernel,
        grid=(rows // TILE,),
        in_specs=[
            row_block(width),
            whole_block(out_w.shape),
            row_block(width),
            whole_block((1, width)),
            whole_block(router_w.shape),
            row_block(routes.shape[1]),
        ],
        out_specs=[row_block(width), row_block(width), pl.BlockSpec((width, TILE), lambda i: (0, i)), row_block(LANES)],
        out_shape=[
            jax.ShapeDtypeStruct((rows, width), F32),
            jax.ShapeDtypeStruct((rows, width), BF16),
            jax.ShapeDtypeStruct((width, rows), BF16),
            jax.ShapeDtypeStruct((rows, LANES), F32),
        ],
        compiler_params=params(),
        cost_estimate=cost(2 * rows * width * (width + LANES), 14 * rows * width),
        name="middle",
    )(attended, out_w, tokens, gain, router_w, routes)


def moe_kernel(slots, chunks, first, last, me_ref, *refs):
    refs = list(refs)
    take = lambda count: [refs.pop(0) for _ in range(count)]
    x_hbm, xt_hbm, dy_hbm, dyt_hbm, gates_ref = take(5)
    if not first:
        made_in, dmoe_in, gg_in = take(3)
    weights = [[take(count) for count in per_slot] for per_slot in chunks]
    made_out, dmoe_out, gg_ref = take(3)
    grads = [take(3) for _ in slots]
    x, xt, dy, dyt, made, dmoe, wg, wu, wd, hg, dg, du, stage, sem_in, sem_w, sem_out, sem_acc = take(17)
    rows = x.shape[0]
    tiles = rows // TILE

    def load(source, target, sem):
        copy = pltpu.make_async_copy(source, target, sem)
        copy.start()
        return copy

    def load_weights(index):
        buffer = index % 2
        out = []
        for which, target in enumerate((wg, wu, wd)):
            at, copies = 0, []
            for piece, ref in enumerate(weights[index][which]):
                count = ref.shape[0]
                copies.append(load(ref, target.at[buffer, at : at + count], sem_w.at[buffer, which, piece]))
                at += count
            out.append(copies)
        return out

    pending = {0: load_weights(0)}
    inputs = [load(a, b, sem_in.at[i]) for i, (a, b) in enumerate(((x_hbm, x), (dy_hbm, dy)))]
    if not first:
        acc = [load(made_in, made, sem_acc.at[0]), load(dmoe_in, dmoe, sem_acc.at[1])]
        gg_ref[...] = gg_in[...]
    else:
        acc = []
        made[...] = jnp.zeros_like(made)
        dmoe[...] = jnp.zeros_like(dmoe)
        gg_ref[...] = jnp.zeros_like(gg_ref)
    late = [load(a, b, sem_in.at[i]) for i, (a, b) in enumerate(((xt_hbm, xt), (dyt_hbm, dyt)), 2)]
    for copy in inputs:
        copy.wait()
    stores = []
    lane = lax.broadcasted_iota(jnp.int32, (TILE, LANES), 1)
    for index, slot in enumerate(slots):
        buffer = index % 2
        for copies in pending.pop(index):
            for copy in copies:
                copy.wait()
        if index + 1 < len(slots):
            pending[index + 1] = load_weights(index + 1)
        for copy in acc:
            copy.wait()
        acc = []
        me = me_ref[0] ^ slot
        g_w, u_w, d_w = wg.at[buffer], wu.at[buffer], wd.at[buffer]

        def rows_step(i, carry):
            at = pl.ds(pl.multiple_of(i * TILE, TILE), TILE)
            xi, yi = x[at], dy[at]
            gate, upval, pre = dot(xi, g_w[...]), dot(xi, u_w[...]), dot_nt(yi, d_w[...])
            column = jnp.sum(jnp.where(lane == me, gates_ref[at], 0.0), axis=1, keepdims=True)
            sigma = 1.0 / (1.0 + jnp.exp(-gate))
            silu = gate * sigma
            hidden = silu * upval
            gained = jnp.sum(hidden * pre, axis=1, keepdims=True)
            gg_ref[at] = gg_ref[at] + jnp.where(lane == me, gained, 0.0)
            weighted = (hidden * column).astype(BF16)
            dhidden = pre * column
            dgate = (dhidden * upval * (sigma + silu * (1.0 - sigma))).astype(BF16)
            dup = (dhidden * silu).astype(BF16)
            hg[at], dg[at], du[at] = weighted, dgate, dup
            made[at] += dot(weighted, d_w[...])
            dmoe[at] += dot_nt(dgate, g_w[...]) + dot_nt(dup, u_w[...])
            return carry

        lax.fori_loop(0, tiles, rows_step, 0)
        for copy in late:
            copy.wait()
        late = []
        for copy in stores:
            copy.wait()
        stores = []

        def grads_step(i, carry):
            at = pl.ds(pl.multiple_of(i * TILE, TILE), TILE)
            a = xt[at]
            stage[0, at] = dot(a, dg[...]).astype(BF16)
            stage[1, at] = dot(a, du[...]).astype(BF16)
            stage[2, at] = dot(dyt[at], hg[...]).astype(BF16)
            return carry

        lax.fori_loop(0, x.shape[1] // TILE, grads_step, 0)
        for which in range(3):
            stores.append(load(stage.at[which], grads[index][which], sem_out.at[which]))
    done = [load(made, made_out, sem_acc.at[0]), load(dmoe, dmoe_out, sem_acc.at[1])]
    for copy in stores + done:
        copy.wait()


def moe(slots, me, moe_in, moe_in_t, dy, dy_t, gates, acc, weights):
    rows, width = moe_in.shape
    hidden = weights[0][0][0].shape[1]
    first = acc is None
    flat = [piece for per_slot in weights for pieces in per_slot for piece in pieces]
    chunks = tuple(tuple(len(pieces) for pieces in per_slot) for per_slot in weights)
    accs = [] if first else list(acc)
    grad = jax.ShapeDtypeStruct((width, hidden), BF16)
    outs = pl.pallas_call(
        functools.partial(moe_kernel, tuple(slots), chunks, first, False),
        in_specs=[pl.BlockSpec(memory_space=pltpu.SMEM), ANY, ANY, ANY, ANY, VMEM]
        + ([] if first else [ANY, ANY, VMEM])
        + [ANY] * len(flat),
        out_specs=[ANY, ANY, VMEM] + [ANY] * (3 * len(slots)),
        out_shape=[
            jax.ShapeDtypeStruct((rows, width), F32),
            jax.ShapeDtypeStruct((rows, width), F32),
            jax.ShapeDtypeStruct((rows, LANES), F32),
        ]
        + [grad] * (3 * len(slots)),
        scratch_shapes=[
            pltpu.VMEM((rows, width), BF16),
            pltpu.VMEM((width, rows), BF16),
            pltpu.VMEM((rows, width), BF16),
            pltpu.VMEM((width, rows), BF16),
            pltpu.VMEM((rows, width), F32),
            pltpu.VMEM((rows, width), F32),
            pltpu.VMEM((2, width, hidden), BF16),
            pltpu.VMEM((2, width, hidden), BF16),
            pltpu.VMEM((2, hidden, width), BF16),
            pltpu.VMEM((rows, hidden), BF16),
            pltpu.VMEM((rows, hidden), BF16),
            pltpu.VMEM((rows, hidden), BF16),
            pltpu.VMEM((3, width, hidden), BF16),
            pltpu.SemaphoreType.DMA((4,)),
            pltpu.SemaphoreType.DMA((2, 3, 2)),
            pltpu.SemaphoreType.DMA((3,)),
            pltpu.SemaphoreType.DMA((2,)),
        ],
        compiler_params=params(),
        cost_estimate=cost(18 * rows * width * hidden * len(slots), 20 * rows * width),
        name="experts",
    )(me, moe_in, moe_in_t, dy, dy_t, gates, *accs, *flat)
    return outs[:3], [tuple(outs[3 + 3 * i : 6 + 3 * i]) for i in range(len(slots))]


def turn_kernel(
    resid_ref, made_ref, dmoe_ref, gates_ref, gg_ref, dy_ref, gain_ref, router_ref, mt_ref, w_ref,
    mixed_ref, dresid_ref, dz_ref, da_ref, gain_grad_ref, router_grad_ref,
):
    @pl.when(pl.program_id(0) == 0)
    def _():
        gain_grad_ref[...] = jnp.zeros_like(gain_grad_ref)
        router_grad_ref[...] = jnp.zeros_like(router_grad_ref)

    resid = resid_ref[...]
    mixed_ref[...] = (resid + made_ref[...]).astype(BF16)
    gates, gg = gates_ref[...], gg_ref[...]
    dlogits = (gates * (gg - jnp.sum(gates * gg, axis=1, keepdims=True))).astype(BF16)
    router_grad_ref[...] += dot(mt_ref[...], dlogits)
    dmoe = dmoe_ref[...] + dot_nt(dlogits, router_ref[...])
    inverse = lax.rsqrt(jnp.mean(resid * resid, axis=-1, keepdims=True) + 1e-06)
    gain_grad_ref[...] += jnp.sum(dmoe * resid * inverse, axis=0, keepdims=True)
    scaled = dmoe * gain_ref[...].astype(F32)
    inner = jnp.mean(scaled * resid, axis=-1, keepdims=True)
    dresid = dy_ref[...].astype(F32) + inverse * scaled - resid * (inverse * inverse * inverse * inner)
    dresid_ref[...] = dresid
    dz = dresid.astype(BF16)
    dz_ref[...] = dz
    da_ref[...] = dot_nt(dz, w_ref[...]).astype(BF16)


def turn(resid, made, dmoe, gates, gg, dy, gain, router_w, moe_in_t, out_w):
    rows, width = resid.shape
    return pl.pallas_call(
        turn_kernel,
        grid=(rows // TILE,),
        in_specs=[
            row_block(width), row_block(width), row_block(width), row_block(LANES), row_block(LANES), row_block(width),
            whole_block((1, width)), whole_block(router_w.shape), pl.BlockSpec((width, TILE), lambda i: (0, i)),
            whole_block(out_w.shape),
        ],
        out_specs=[row_block(width)] * 4 + [whole_block((1, width)), whole_block((width, LANES))],
        out_shape=[
            jax.ShapeDtypeStruct((rows, width), BF16),
            jax.ShapeDtypeStruct((rows, width), F32),
            jax.ShapeDtypeStruct((rows, width), BF16),
            jax.ShapeDtypeStruct((rows, width), BF16),
            jax.ShapeDtypeStruct((1, width), F32),
            jax.ShapeDtypeStruct((width, LANES), F32),
        ],
        compiler_params=params(),
        cost_estimate=cost(2 * rows * width * (width + 2 * LANES), 28 * rows * width),
        name="turn",
    )(resid, made, dmoe, gates, gg, dy, gain, router_w, moe_in_t, out_w)


def finish_kernel(dq_ref, dk_ref, dv_ref, w_ref, x_ref, dresid_ref, gain_ref, out_ref, gain_grad_ref):
    @pl.when(pl.program_id(0) == 0)
    def _():
        gain_grad_ref[...] = jnp.zeros_like(gain_grad_ref)

    qw, kw = dq_ref.shape[1], dk_ref.shape[1]
    dn = dot_nt(dq_ref[...], w_ref[:, :qw])
    dn += dot_nt(dk_ref[...], w_ref[:, qw : qw + kw])
    dn += dot_nt(dv_ref[...], w_ref[:, qw + kw :])
    x = x_ref[...].astype(F32)
    inverse = lax.rsqrt(jnp.mean(x * x, axis=-1, keepdims=True) + 1e-06)
    gain_grad_ref[...] += jnp.sum(dn * x * inverse, axis=0, keepdims=True)
    scaled = dn * gain_ref[...].astype(F32)
    inner = jnp.mean(scaled * x, axis=-1, keepdims=True)
    out_ref[...] = dresid_ref[...] + inverse * scaled - x * (inverse * inverse * inverse * inner)


def finish(dq, dk, dv, weights, tokens, dresid, gain):
    rows, width = tokens.shape
    return pl.pallas_call(
        finish_kernel,
        grid=(rows // TILE,),
        in_specs=[
            row_block(dq.shape[1]), row_block(dk.shape[1]), row_block(dv.shape[1]), whole_block(weights.shape),
            row_block(width), row_block(width), whole_block((1, width)),
        ],
        out_specs=[row_block(width), whole_block((1, width))],
        out_shape=[jax.ShapeDtypeStruct((rows, width), F32), jax.ShapeDtypeStruct((1, width), F32)],
        compiler_params=params(),
        cost_estimate=cost(2 * rows * width * weights.shape[1], 20 * rows * width),
        name="finish",
    )(dq, dk, dv, weights, tokens, dresid, gain)


def flip(value, axis, bit):
    size = lax.axis_size(axis)
    return lax.ppermute(value, axis, [(i, i ^ bit) for i in range(size)])


def gather_experts(mats, owners):
    slots = {0: tuple([m] for m in mats)}
    if owners == 8:
        slots[2] = tuple([flip(m, "expert", 2)] for m in mats)
        slots[4] = tuple([flip(m, "expert", 4)] for m in mats)
        third = []
        for (a,), (b,) in zip(slots[2], slots[4]):
            cut = a.shape[0] // 2
            third.append([flip(a[:cut], "expert", 4), flip(b[cut:], "expert", 2)])
        slots[6] = tuple(third)
    else:
        bit = 2
        while bit < owners:
            for j in sorted(slots):
                slots[j | bit] = tuple([flip(p, "expert", bit) for p in m] for m in slots[j])
            bit *= 2
    for j in sorted(slots):
        slots[j | 1] = tuple([flip(p, "expert", 1) for p in m] for m in slots[j])
    return slots


def add(a, b):
    return (a.astype(F32) + b.astype(F32)).astype(BF16)


def reduce_experts(parts, owners):
    pairs = {}
    for j in parts:
        if j & 1:
            pairs[j ^ 1] = tuple(add(m, flip(s, "expert", 1)) for m, s in zip(parts[j ^ 1], parts[j]))
    if owners == 8:
        own = []
        for m0, m2, m4, m6 in zip(pairs[0], pairs[2], pairs[4], pairs[6]):
            cut = m0.shape[0] // 2
            left, right = flip(m6[:cut], "expert", 2), flip(m6[cut:], "expert", 4)
            top = add(m0[:cut], flip(m2[:cut], "expert", 2))
            bottom = add(m0[cut:], flip(m4[cut:], "expert", 4))
            top = add(top, flip(add(m4[:cut], left), "expert", 4))
            bottom = add(bottom, flip(add(m2[cut:], right), "expert", 2))
            own.append(jnp.concatenate([top, bottom], axis=0))
        return tuple(own)
    bit = 2
    while bit < owners:
        for j in sorted(pairs, reverse=True):
            if j & bit:
                gone = pairs.pop(j)
                pairs[j ^ bit] = tuple(add(m, flip(s, "expert", bit)) for m, s in zip(pairs[j ^ bit], gone))
        bit *= 2
    return pairs[0]


def on_device(
    tokens, gain_attn, w_query, key_weight, value_weight, w_out, gain_ffn, w_router, w_gate, w_up, w_down, routes, cotangent
):
    owners = lax.axis_size("expert")
    me = lax.axis_index("expert").astype(jnp.int32)[None]
    rows, width = tokens.shape
    experts = w_router.shape[1] * 1
    slots = gather_experts((w_gate[0], w_up[0], w_down[0]), owners)

    small = jnp.concatenate([gain_attn[:, None], gain_ffn[:, None], w_router], axis=1)
    packed = lax.all_gather(
        jnp.concatenate([w_query, key_weight, value_weight], axis=1), "wshard", axis=0, tiled=True
    )
    small = lax.all_gather(small, "wshard", axis=0, tiled=True)
    out_w = lax.all_gather(w_out, "wshard", axis=0, tiled=True)
    gain_one, gain_two = small[:, 0][None], small[:, 1][None]
    router_w = jnp.pad(small[:, 2:], ((0, 0), (0, LANES - experts)))
    cos, sin = (jnp.asarray(a) for a in rope_tables(rows))

    normed, queries, keys, vals = project(tokens, gain_one, packed, cos, sin)
    attended = attend(queries, keys, vals)
    resid, moe_in, moe_in_t, gates = middle(attended, out_w, tokens, gain_two, router_w, routes)

    order = [2, 3, 4, 5, 6, 7, 0, 1] if owners == 8 else list(range(owners))
    dy_t = cotangent.T
    acc, parts = None, {}
    for at in range(0, len(order), 2):
        pair = order[at : at + 2]
        acc, grads = moe(
            pair, me, moe_in, moe_in_t, cotangent, dy_t, gates, acc, [slots[j] for j in pair]
        )
        parts.update(zip(pair, grads))
    made, dmoe, gate_grads = acc
    mixed, dresid, dz, dattended, gain_two_grad, router_grad = turn(
        resid, made, dmoe, gates, gate_grads, cotangent, gain_two, router_w, moe_in_t, out_w
    )
    own = reduce_experts(parts, owners)
    out_grad = dot_tn(attended, dz)
    dq, dk, dv = attend_back(queries, keys, vals, dattended, cos, sin)
    qkv_grad = dot_tn(normed, jnp.concatenate([dq, dk, dv], axis=1))
    d_tokens, gain_one_grad = finish(dq, dk, dv, packed, tokens, dresid, gain_one)

    small_grad = jnp.concatenate([gain_one_grad.T, gain_two_grad.T, router_grad[:, :experts]], axis=1)

    def total(grad):
        return lax.psum(lax.psum_scatter(grad, "wshard", scatter_dimension=0, tiled=True), "expert")

    small_grad = total(small_grad)
    out_grad = total(out_grad.astype(BF16)).astype(F32)
    qkv_grad = total(qkv_grad.astype(BF16)).astype(F32)
    own = tuple(lax.psum(m, "wshard").astype(F32) for m in own)
    qw, kw = w_query.shape[1], key_weight.shape[1]
    return (
        mixed,
        d_tokens,
        small_grad[:, 0],
        qkv_grad[:, :qw],
        qkv_grad[:, qw : qw + kw],
        qkv_grad[:, qw + kw :],
        out_grad,
        small_grad[:, 1],
        small_grad[:, 2:],
        own[0][None],
        own[1][None],
        own[2].T[None],
    )


def solution(mesh):
    whole, shard, matrix, owned = P(("expert", "wshard"), None), P("wshard"), P("wshard", None), P("expert", None, None)
    return jax.shard_map(
        on_device,
        mesh=mesh,
        in_specs=(whole, shard, matrix, matrix, matrix, matrix, shard, matrix, owned, owned, owned, whole, whole),
        out_specs=(whole, whole, shard, matrix, matrix, matrix, matrix, shard, matrix, owned, owned, owned),
        check_vma=False,
    )
```

time: 1590 us -> 725 us (0.46)
  matrix products: 407 us -> 13.8 us
  waiting for transfers between devices: 603 us -> 278 us
  Pallas kernels: 0 us -> 275 us
  local copies, waits for them, and re-layouts: 255 us -> 26.6 us
  other arithmetic: 178 us -> 22.4 us
  blocking collectives: 74.9 us -> 40.7 us
    all_to_all x8 -> x0, waiting for transfers between devices: 423 us -> none  [the longest x2 133 us: on_device(): lax.all_to_all(grad_send.reshape(owners, local_count, capacity, width), '...]
    dot_general x93 -> x2, matrix products: 407 us -> 13.8 us  [dot_tn(): lax.dot_general(a, b, (((0,), (0,)), ((), ())), preferred_element_type=F32)]
    pallas_call x0 -> x10, Pallas kernels: none -> 275 us  [the longest x4 140 us: moe(): pl.pallas_call(functools.partial(moe_kernel, tuple(slots), chunks, first,...]
    ppermute x0 -> x57, waiting for transfers between devices: none -> 116 us  [flip(): return lax.ppermute(value, axis, [(i, i ^ bit) for i in range(size)])]
    gather x4 -> x0, local copies, waits for them, and re-layouts: 62.4 us -> none  [the longest x2 31.5 us: on_device(): grad_back.reshape(expert_count * capacity, width)[target]]
    reduce_sum x17 -> x0, other arithmetic: 58.8 us -> none  [the longest x1 20.1 us: on_device(): jnp.sum(gathered.astype(jnp.float32) * grad_part[:, None, :], axis=-1)]
    ppermute x0 -> x57, starting transfers between devices: none -> 43 us  [flip(): return lax.ppermute(value, axis, [(i, i ^ bit) for i in range(size)])]
    scatter x2 -> x0, other arithmetic: 42.7 us -> none  [on_device(): jnp.zeros((expert_count * capacity, width), jnp.bfloat16).at[target]]
  transfers between devices with their start and end apart: 14 -> 64, of which waited for: 9 -> 18; matrix products, arithmetic and copies ran while one was open for 50% -> 6% of each run, Pallas kernels for 0% -> 32%
where the time goes in v1:
time: 725 us; the launch traced here: 715 us
  waiting for transfers between devices  278 us (38%)
  Pallas kernels  275 us (38%)
  starting transfers between devices  43.2 us (6%)
  blocking collectives  40.7 us (6%)
  local copies, waits for them, and re-layouts  26.6 us (4%)
  other arithmetic  22.4 us (3%)
  between operations  15.1 us (2%)
  matrix products  13.8 us (2%)
    pallas_call x4, Pallas kernels, moe(): pl.pallas_call(functools.partial(moe_kernel, tuple(slots), chunks, first,...  140 us
    ppermute x57, waiting for transfers between devices, flip(): return lax.ppermute(value, axis, [(i, i ^ bit) for i in range(size)])  116 us
    psum x1, waiting for transfers between devices, on_device(): own = tuple((lax.psum(m, 'wshard').astype(F32) for m in own))  94.7 us
    pallas_call x1, Pallas kernels, attend_back(): pl.pallas_call(attend_back_kernel, grid=(rows // SEQUENCE_LENGTH, steps),...  58 us
    psum x1, waiting for transfers between devices, total(): lax.psum(lax.psum_scatter(grad, 'wshard', scatter_dimension=0, tiled=True...  55.6 us
    ppermute x57, starting transfers between devices, flip(): return lax.ppermute(value, axis, [(i, i ^ bit) for i in range(size)])  43 us
    pallas_call x1, Pallas kernels, attend(): pl.pallas_call(attend_kernel, grid=(rows // SEQUENCE_LENGTH, steps), in_s...  35.3 us
    psum x1, blocking collectives, total(): lax.psum(lax.psum_scatter(grad, 'wshard', scatter_dimension=0, tiled=True...  24.1 us
  transfers between devices with their start and end apart: 64, of which 18 were waited for; matrix products, arithmetic and copies ran while one was open for 6% of the time, Pallas kernels for 32%

profile of v1, /device:TPU:0, one launch (start us, length us, event | category | flops | bytes accessed | tf_op | source)
XLA Modules:
  0.0 714.9 jit_solution(3745565007988569213)
XLA Ops:
  9.6 3.0 collective-permute-start
  16.7 20.3 %collective-permute-done.refs_5_ = bf16[1024,512]{1,0:T(8,128)(2,1)} collective-permute-done((bf16[1024,512]{1,0:T(8,128)(2,1)}, bf16[1024,512]{1,0:T(8,128)(2,1)}, u32[]{:S(2)}, u32[]{:S(2)}) %collective-permute-start) | collective-permute-done | bytes 1048608 | tf_op jit(solution)/shard_map/ppermute | solution.py:475
  39.3 16.6 %all_gather.9 = bf16[1024,10]{1,0:T(8,128)(2,1)S(1)} all-gather(bf16[256,10]{1,0:T(8,128)(2,1)S(1)} %copy.41), channel_id=1, replica_groups=mesh['expert'=8,'wshard'=4] {'wshard'}, dimensions={0}, use_global_device_ids=true | all-gather | bytes 25600 | tf_op jit(solution)/shard_map/all_gather | solution.py:542
  67.4 2.6 copy.43
  71.8 10.1 %collective-permute-done.2.refs_7_ = bf16[512,1024]{1,0:T(8,128)(2,1)} collective-permute-done((bf16[512,1024]{1,0:T(8,128)(2,1)}, bf16[512,1024]{1,0:T(8,128)(2,1)}, u32[]{:S(2)}, u32[]{:S(2)}) %collective-permute-start.2) | collective-permute-done | bytes 1048608 | tf_op jit(solution)/shard_map/ppermute | solution.py:475
  87.7 10.1 %all-gather.3.cloned.1.call-done.w_ref = bf16[1024,2048]{1,0:T(8,128)(2,1)} async-done(((bf16[256,2048]{1,0:T(8,128)(2,1)}), bf16[1024,2048]{1,0:T(8,128)(2,1)}) %all-gather.3.cloned.1.call-update) | async-done | bytes 4194320 | tf_op jit(solution)/shard_map/all_gather | solution.py:539
  97.8 9.0 %project.1 = (bf16[1024,1024]{1,0:T(8,128)(2,1)}, bf16[1024,1024]{1,0:T(8,128)(2,1)}, bf16[1024,512]{1,0:T(8,128)(2,1)}, bf16[1024,512]{1,0:T(8,128)(2,1)}) custom-call(bf16[1024,1024]{1,0:T(8,128)(2,1)} %x_ref.5, bf16[1,1024]{1,0:T(2,128)(2,1)} %broadcast_in_dim_squeeze.6.gain_ref, bf16[1024,2048]{1,0:T(8,128)(2,1)} %all-gather.3.cloned.1.call-done.w_ref, ...), custom_call_target="tpu_custom_call" | custom-call | flops 4294967296 | bytes 12582912 | tf_op jit(solution)/shard_map/project/pallas_call | solution.py:98
  107.5 35.3 %attend.1.a_ref = bf16[1024,1024]{1,0:T(8,128)(2,1)} custom-call(bf16[1024,1024]{1,0:T(8,128)(2,1)} %get-tuple-element.67.q_ref, bf16[1024,512]{1,0:T(8,128)(2,1)} %get-tuple-element.68.k_ref, bf16[1024,512]{1,0:T(8,128)(2,1)} %get-tuple-element.69.v_ref), custom_call_target="tpu_custom_call" | custom-call | flops 34359738368 | bytes 6291456 | tf_op jit(solution)/shard_map/attend/pallas_call | solution.py:134
  143.9 8.8 %middle.1 = (f32[1024,1024]{1,0:T(8,128)}, bf16[1024,1024]{1,0:T(8,128)(2,1)}, bf16[1024,1024]{1,0:T(8,128)(2,1)}, f32[1024,128]{1,0:T(8,128)}) custom-call(bf16[1024,1024]{1,0:T(8,128)(2,1)} %attend.1.a_ref, bf16[1024,1024]{1,0:T(8,128)(2,1)} %all-gather.5.cloned.1.call-done.w_ref, bf16[1024,1024]{1,0:T(8,128)(2,1)} %x_ref.5, ...), custom_call_target="tpu_custom_call" | custom-call | flops 2415919104 | bytes 14680064 | tf_op jit(solution)/shard_map/middle/pallas_call | solution.py:217
  155.3 32.4 %experts.4 = (f32[1024,1024]{1,0:T(8,128)}, f32[1024,1024]{1,0:T(8,128)}, f32[1024,128]{1,0:T(8,128)}, bf16[1024,512]{1,0:T(8,128)(2,1)}, bf16[1024,512]{1,0:T(8...) custom-call(s32[1]{0:T(128)} %bitcast.me_ref, ...), custom_call_target="tpu_custom_call" | custom-call | flops 19327352832 | bytes 20971520 | tf_op jit(solution)/shard_map/experts/pallas_call | solution.py:350
  189.3 35.9 %experts.5 = (f32[1024,1024]{1,0:T(8,128)}, f32[1024,1024]{1,0:T(8,128)}, f32[1024,128]{1,0:T(8,128)}, bf16[1024,512]{1,0:T(8,128)(2,1)}, bf16[1024,512]{1,0:T(8...) custom-call(s32[1]{0:T(128)} %bitcast.me_ref, ...), custom_call_target="tpu_custom_call" | custom-call | flops 19327352832 | bytes 20971520 | tf_op jit(solution)/shard_map/experts/pallas_call | solution.py:350
  226.1 35.6 %experts.6 = (f32[1024,1024]{1,0:T(8,128)}, f32[1024,1024]{1,0:T(8,128)}, f32[1024,128]{1,0:T(8,128)}, bf16[1024,512]{1,0:T(8,128)(2,1)}, bf16[1024,512]{1,0:T(8...) custom-call(s32[1]{0:T(128)} %bitcast.me_ref, ...), custom_call_target="tpu_custom_call" | custom-call | flops 19327352832 | bytes 20971520 | tf_op jit(solution)/shard_map/experts/pallas_call | solution.py:350
  263.4 35.9 %experts.7 = (f32[1024,1024]{1,0:T(8,128)}, f32[1024,1024]{1,0:T(8,128)}, f32[1024,128]{1,0:T(8,128)}, bf16[1024,512]{1,0:T(8,128)(2,1)}, bf16[1024,512]{1,0:T(8...) custom-call(s32[1]{0:T(128)} %bitcast.me_ref, ...), custom_call_target="tpu_custom_call" | custom-call | flops 19327352832 | bytes 20971520 | tf_op jit(solution)/shard_map/experts/pallas_call | solution.py:350
  299.2 12.6 %turn.1 = (bf16[1024,1024]{1,0:T(8,128)(2,1)}, f32[1024,1024]{1,0:T(8,128)}, bf16[1024,1024]{1,0:T(8,128)(2,1)}, bf16[1024,1024]{1,0:T(8,128)(2,1)}, f32[1,1024]{1,0:T(1,128)}, /*index=5*/f32[1024,128]{1,0:T(8,128)}) custom-call(f32[1024,1024]{1,0:T(8,128)} %get-tuple-element.70.resid_ref, f32[1024,1024]{1,0:T(8,128)} %get-tuple-element.83.made_ref, ...), custom_call_target="tpu_custom_call" | custom-call | flops 2684354560 | bytes 29360128 | tf_op jit(solution)/shard_map/turn/pallas_call | solution.py:416
  311.9 5.3 convolution_convert_fusion
  317.2 58.0 %attend_back.1 = (bf16[1024,1024]{1,0:T(8,128)(2,1)}, bf16[1024,512]{1,0:T(8,128)(2,1)}, bf16[1024,512]{1,0:T(8,128)(2,1)}) custom-call(bf16[1024,1024]{1,0:T(8,128)(2,1)} %get-tuple-element.67.q_ref, bf16[1024,512]{1,0:T(8,128)(2,1)} %get-tuple-element.68.k_ref, bf16[1024,512]{1,0:T(8,128)(2,1)} %get-tuple-element.69.v_ref, ...), custom_call_target="tpu_custom_call" | custom-call | flops 85899345920 | bytes 12582912 | tf_op jit(solution)/shard_map/attend_back/pallas_call | solution.py:180
  375.2 8.5 %fusion.6 = bf16[1024,2048]{1,0:T(8,128)(2,1)} fusion(bf16[1024,1024]{1,0:T(8,128)(2,1)S(1)} %copy-done.37, bf16[1024,512]{1,0:T(8,128)(2,1)} %get-tuple-element.90.dv_ref, bf16[1024,512]{1,0:T(8,128)(2,1)} %get-tuple-element.89.dk_ref, bf16[1024,1024]{1,0:T(8,128)(2,1)} %get-tuple-element.88.dq_ref), kind=kOutput, calls=%fused_computation.6 | convolution fusion | flops 4309647360 | bytes 10485760 | tf_op jit(solution)/shard_map/dot_general | solution.py:33
  385.1 11.4 %finish.1 = (f32[1024,1024]{1,0:T(8,128)}, f32[1,1024]{1,0:T(1,128)}) custom-call(bf16[1024,1024]{1,0:T(8,128)(2,1)} %get-tuple-element.88.dq_ref, bf16[1024,512]{1,0:T(8,128)(2,1)} %get-tuple-element.89.dk_ref, bf16[1024,512]{1,0:T(8,128)(2,1)} %get-tuple-element.90.dv_ref, bf16[1024,2048]{1,0:T(8,128)(2,1)} %all-gather.3.cloned.1.call-done.w_ref, ...), custom_call_target="tpu_custom_call" | custom-call | flops 4294967296 | bytes 20971520 | tf_op jit(solution)/shard_map/finish/pallas_call | solution.py:458
  419.4 7.5 %collective-permute-done.45 = bf16[512,512]{1,0:T(8,128)(2,1)S(1)} collective-permute-done((bf16[512,512]{1,0:T(8,128)(2,1)S(1)}, bf16[512,512]{1,0:T(8,128)(2,1)S(1)}, u32[]{:S(2)}, u32[]{:S(2)}) %collective-permute-start.45) | collective-permute-done | bytes 524320 | tf_op jit(solution)/shard_map/ppermute | solution.py:475
  429.5 19.8 %collective-permute-done.35 = bf16[512,512]{1,0:T(8,128)(2,1)S(1)} collective-permute-done((bf16[512,512]{1,0:T(8,128)(2,1)S(1)}, bf16[512,512]{1,0:T(8,128)(2,1)S(1)}, u32[]{:S(2)}, u32[]{:S(2)}) %collective-permute-start.35) | collective-permute-done | bytes 524320 | tf_op jit(solution)/shard_map/ppermute | solution.py:475
  453.6 7.0 collective-permute-done.34
  461.8 10.0 %collective-permute-done.55 = bf16[512,512]{1,0:T(8,128)(2,1)S(1)} collective-permute-done((bf16[512,512]{1,0:T(8,128)(2,1)S(1)}, bf16[512,512]{1,0:T(8,128)(2,1)S(1)}, u32[]{:S(2)}, u32[]{:S(2)}) %collective-permute-start.55) | collective-permute-done | bytes 524320 | tf_op jit(solution)/shard_map/ppermute | solution.py:475
  474.0 2.9 collective-permute-done.29
  477.7 10.4 %collective-permute-done.46 = bf16[512,512]{1,0:T(8,128)(2,1)S(1)} collective-permute-done((bf16[512,512]{1,0:T(8,128)(2,1)S(1)}, bf16[512,512]{1,0:T(8,128)(2,1)S(1)}, u32[]{:S(2)}, u32[]{:S(2)}) %collective-permute-start.46) | collective-permute-done | bytes 524320 | tf_op jit(solution)/shard_map/ppermute | solution.py:475
  490.2 9.2 %collective-permute-done.36 = bf16[512,512]{1,0:T(8,128)(2,1)S(1)} collective-permute-done((bf16[512,512]{1,0:T(8,128)(2,1)S(1)}, bf16[512,512]{1,0:T(8,128)(2,1)S(1)}, u32[]{:S(2)}, u32[]{:S(2)}) %collective-permute-start.36) | collective-permute-done | bytes 524320 | tf_op jit(solution)/shard_map/ppermute | solution.py:475
  502.5 3.1 collective-permute-done.54
  505.5 5.1 collective-permute-done.49
  510.6 8.9 %collective-permute-done.56 = bf16[512,512]{1,0:T(8,128)(2,1)S(1)} collective-permute-done((bf16[512,512]{1,0:T(8,128)(2,1)S(1)}, bf16[512,512]{1,0:T(8,128)(2,1)S(1)}, u32[]{:S(2)}, u32[]{:S(2)}) %collective-permute-start.56) | collective-permute-done | bytes 524320 | tf_op jit(solution)/shard_map/ppermute | solution.py:475
  521.7 24.1 %psum.42 = f32[256,10]{0,1:T(8,128)S(1)} all-reduce(f32[256,10]{0,1:T(8,128)} %reduce-scatter.4.cloned.1.call-done), channel_id=1, replica_groups=mesh['expert'=8,'wshard'=4] {'expert'}, use_global_device_ids=true, to_apply=%region_1.2 | all-reduce | flops 2560 | bytes 20480 | tf_op jit(solution)/shard_map/psum | solution.py:574
  547.0 94.7 %all-reduce.8.cloned.1.call-done = (bf16[1,512,1024]{1,2,0:T(8,128)(2,1)}, bf16[1,1024,512]{2,1,0:T(8,128)(2,1)}, bf16[1,1024,512]{2,1,0:T(8,128)(2,1)}) async-done(((bf16[1,512,1024]{1,2,0:T(8,128)(2,1)}, bf16[1,1024,512]{2,1,0:T(8,128)(2,1)}, bf16[1,1024,512]{2,1,0:T(8,128)(2,1)}), (bf16[1,512,1024]{1,2,0:T(8,128)(2,1)}, bf16[1,1024,512]{2,1,0:T(8,128)(2,1)}, ...) | async-done | bytes 3145744 | tf_op jit(solution)/shard_map/psum | solution.py:579
  641.7 2.9 broadcast_in_dim.31
  647.8 55.6 %all-reduce.6.cloned.1.call-done = (bf16[256,2048]{1,0:T(8,128)(2,1)}, bf16[256,1024]{1,0:T(8,128)(2,1)}) async-done(((bf16[256,2048]{1,0:T(8,128)(2,1)}, bf16[256,1024]{1,0:T(8,128)(2,1)}), (bf16[256,2048]{1,0:T(8,128)(2,1)}, bf16[256,1024]{1,0:T(8,128)(2,1)})) %all-reduce.6.cloned.1.call-update) | async-done | bytes 1572880 | tf_op jit(solution)/shard_map/psum | solution.py:574
  (253 shorter events, 87.5 us)
Async XLA Ops:
  7.2 90.6 %all-gather.3.cloned.1.call-start = ((), (), s32[]{:S(2)}) async-start(), calls=%async_computation.3 | async-start | bytes 5242880 | tf_op jit(solution)/shard_map/all_gather | solution.py:539
  9.6 134.3 %all-gather.5.cloned.1.call-start = ((), (), s32[]{:S(2)}) async-start(), calls=%async_computation.4 | async-start | bytes 2621440 | tf_op jit(solution)/shard_map/all_gather | solution.py:543
  12.6 44.6 %collective-permute-start.6 = (bf16[1024,512]{1,0:T(8,128)(2,1)}, bf16[1024,512]{1,0:T(8,128)(2,1)}, u32[]{:S(2)}, u32[]{:S(2)}) collective-permute-start(bf16[1024,512]{1,0:T(8,128)(2,1)} %bitcast.2.refs_8_), channel_id=1, source_target_pairs={{0,16},{4,20},{8,24},{12,28},{16,0},{20,4},{24,8},{28,12},{1,17},{... | collective-permute-start | bytes 3145736 | tf_op jit(solution)/shard_map/ppermute | solution.py:475
  14.1 45.3 %collective-permute-start.1 = (bf16[1024,512]{1,0:T(8,128)(2,1)}, bf16[1024,512]{1,0:T(8,128)(2,1)}, u32[]{:S(2)}, u32[]{:S(2)}) collective-permute-start(bf16[1024,512]{1,0:T(8,128)(2,1)} %bitcast.3.refs_9_), channel_id=1, source_target_pairs={{0,8},{4,12},{8,0},{12,4},{16,24},{20,28},{24,16},{28,20},{1,9},{5... | collective-permute-start | bytes 3145736 | tf_op jit(solution)/shard_map/ppermute | solution.py:475
  14.7 48.6 %collective-permute-start.7 = (bf16[1024,512]{1,0:T(8,128)(2,1)}, bf16[1024,512]{1,0:T(8,128)(2,1)}, u32[]{:S(2)}, u32[]{:S(2)}) collective-permute-start(bf16[1024,512]{1,0:T(8,128)(2,1)} %bitcast.3.refs_9_), channel_id=1, source_target_pairs={{0,16},{4,20},{8,24},{12,28},{16,0},{20,4},{24,8},{28,12},{1,17},{... | collective-permute-start | bytes 3145736 | tf_op jit(solution)/shard_map/ppermute | solution.py:475
  14.7 67.1 %collective-permute-start.2 = (bf16[512,1024]{1,0:T(8,128)(2,1)}, bf16[512,1024]{1,0:T(8,128)(2,1)}, u32[]{:S(2)}, u32[]{:S(2)}) collective-permute-start(bf16[512,1024]{1,0:T(8,128)(2,1)} %bitcast.4.refs_10_), channel_id=1, source_target_pairs={{0,8},{4,12},{8,0},{12,4},{16,24},{20,28},{24,16},{28,20},{1,9},{5... | collective-permute-start | bytes 3145736 | tf_op jit(solution)/shard_map/ppermute | solution.py:475
  36.9 48.1 %collective-permute-start.8 = (bf16[512,1024]{1,0:T(8,128)(2,1)}, bf16[512,1024]{1,0:T(8,128)(2,1)}, u32[]{:S(2)}, u32[]{:S(2)}) collective-permute-start(bf16[512,1024]{1,0:T(8,128)(2,1)} %bitcast.4.refs_10_), channel_id=1, source_target_pairs={{0,16},{4,20},{8,24},{12,28},{16,0},{20,4},{24,8},{28,12},{1,17},{... | collective-permute-start | bytes 3145736 | tf_op jit(solution)/shard_map/ppermute | solution.py:475
  39.0 482.0 %reduce-scatter.8.cloned.1.call-start = ((), (), s32[]{:S(2)}) async-start(), calls=%async_computation.7 | async-start | bytes 2621440 | tf_op jit(solution)/shard_map/reduce_scatter | solution.py:574
  57.2 49.6 %collective-permute-start.12 = (bf16[512,512]{1,0:T(8,128)(2,1)S(1)}, bf16[512,512]{1,0:T(8,128)(2,1)}, u32[]{:S(2)}, u32[]{:S(2)}) collective-permute-start(bf16[512,512]{1,0:T(8,128)(2,1)S(1)} %slice.163), channel_id=1, source_target_pairs={{0,16},{4,20},{8,24},{12,28},{16,0},{20,4},{24,8},{28,12},{1,17},{... | collective-permute-start | bytes 1572872 | tf_op jit(solution)/shard_map/ppermute | solution.py:475
  59.4 47.5 %collective-permute-start.13 = (bf16[512,512]{1,0:T(8,128)(2,1)S(1)}, bf16[512,512]{1,0:T(8,128)(2,1)}, u32[]{:S(2)}, u32[]{:S(2)}) collective-permute-start(bf16[512,512]{1,0:T(8,128)(2,1)S(1)} %slice.164), channel_id=1, source_target_pairs={{0,8},{4,12},{8,0},{12,4},{16,24},{20,28},{24,16},{28,20},{1,9},{5... | collective-permute-start | bytes 1572872 | tf_op jit(solution)/shard_map/ppermute | solution.py:475
  63.3 44.1 %collective-permute-start.14 = (bf16[512,512]{1,0:T(8,128)(2,1)}, bf16[512,512]{1,0:T(8,128)(2,1)}, u32[]{:S(2)}, u32[]{:S(2)}) collective-permute-start(bf16[512,512]{1,0:T(8,128)(2,1)} %slice.165), channel_id=1, source_target_pairs={{0,16},{4,20},{8,24},{12,28},{16,0},{20,4},{24,8},{28,12},{1,17},{... | collective-permute-start | bytes 1572872 | tf_op jit(solution)/shard_map/ppermute | solution.py:475
  81.9 70.8 %collective-permute-start.15 = (bf16[512,512]{1,0:T(8,128)(2,1)S(1)}, bf16[512,512]{1,0:T(8,128)(2,1)S(1)}, u32[]{:S(2)}, u32[]{:S(2)}) collective-permute-start(bf16[512,512]{1,0:T(8,128)(2,1)S(1)} %slice.166), channel_id=1, source_target_pairs={{0,8},{4,12},{8,0},{12,4},{16,24},{20,28},{24,16},{28,20},{1,9},{5... | collective-permute-start | bytes 1572872 | tf_op jit(solution)/shard_map/ppermute | solution.py:475
  85.0 69.2 %collective-permute-start.16 = (bf16[256,1024]{1,0:T(8,128)(2,1)S(1)}, bf16[256,1024]{1,0:T(8,128)(2,1)}, u32[]{:S(2)}, u32[]{:S(2)}) collective-permute-start(bf16[256,1024]{1,0:T(8,128)(2,1)S(1)} %slice.167), channel_id=1, source_target_pairs={{0,16},{4,20},{8,24},{12,28},{16,0},{20,4},{24,8},{28,12},{1,17},{... | collective-permute-start | bytes 1572872 | tf_op jit(solution)/shard_map/ppermute | solution.py:475
  106.8 47.4 %collective-permute-start.3 = (bf16[1024,512]{1,0:T(8,128)(2,1)}, bf16[1024,512]{1,0:T(8,128)(2,1)}, u32[]{:S(2)}, u32[]{:S(2)}) collective-permute-start(bf16[1024,512]{1,0:T(8,128)(2,1)} %collective-permute-done.refs_5_), channel_id=1, source_target_pairs={{0,4},{4,0},{8,12},{12,8},{16,20},{20,16},{24,28},{28,24},{1,5},{5... | collective-permute-start | bytes 3145736 | tf_op jit(solution)/shard_map/ppermute | solution.py:475
  106.9 47.9 %collective-permute-start.4 = (bf16[1024,512]{1,0:T(8,128)(2,1)}, bf16[1024,512]{1,0:T(8,128)(2,1)}, u32[]{:S(2)}, u32[]{:S(2)}) collective-permute-start(bf16[1024,512]{1,0:T(8,128)(2,1)} %collective-permute-done.1.refs_6_), channel_id=1, source_target_pairs={{0,4},{4,0},{8,12},{12,8},{16,20},{20,16},{24,28},{28,24},{1,5},{5... | collective-permute-start | bytes 3145736 | tf_op jit(solution)/shard_map/ppermute | solution.py:475
  107.4 47.5 %collective-permute-start.5 = (bf16[512,1024]{1,0:T(8,128)(2,1)}, bf16[512,1024]{1,0:T(8,128)(2,1)}, u32[]{:S(2)}, u32[]{:S(2)}) collective-permute-start(bf16[512,1024]{1,0:T(8,128)(2,1)} %collective-permute-done.2.refs_7_), channel_id=1, source_target_pairs={{0,4},{4,0},{8,12},{12,8},{16,20},{20,16},{24,28},{28,24},{1,5},{5... | collective-permute-start | bytes 3145736 | tf_op jit(solution)/shard_map/ppermute | solution.py:475
  152.7 35.0 %collective-permute-start.17 = (bf16[256,1024]{1,0:T(8,128)(2,1)S(1)}, bf16[256,1024]{1,0:T(8,128)(2,1)}, u32[]{:S(2)}, u32[]{:S(2)}) collective-permute-start(bf16[256,1024]{1,0:T(8,128)(2,1)S(1)} %slice.168), channel_id=1, source_target_pairs={{0,8},{4,12},{8,0},{12,4},{16,24},{20,28},{24,16},{28,20},{1,9},{5... | collective-permute-start | bytes 1572872 | tf_op jit(solution)/shard_map/ppermute | solution.py:475
  187.7 37.5 %collective-permute-start.19 = (bf16[512,512]{1,0:T(8,128)(2,1)}, bf16[512,512]{1,0:T(8,128)(2,1)}, u32[]{:S(2)}, u32[]{:S(2)}) collective-permute-start(bf16[512,512]{1,0:T(8,128)(2,1)} %collective-permute-done.13.refs_9_), channel_id=1, source_target_pairs={{0,4},{4,0},{8,12},{12,8},{16,20},{20,16},{24,28},{28,24},{1,5},{5... | collective-permute-start | bytes 1572872 | tf_op jit(solution)/shard_map/ppermute | solution.py:475
  187.8 37.7 %collective-permute-start.20 = (bf16[512,512]{1,0:T(8,128)(2,1)}, bf16[512,512]{1,0:T(8,128)(2,1)}, u32[]{:S(2)}, u32[]{:S(2)}) collective-permute-start(bf16[512,512]{1,0:T(8,128)(2,1)} %collective-permute-done.14.refs_10_), channel_id=1, source_target_pairs={{0,4},{4,0},{8,12},{12,8},{16,20},{20,16},{24,28},{28,24},{1,5},{5... | collective-permute-start | bytes 1572872 | tf_op jit(solution)/shard_map/ppermute | solution.py:475
  188.2 37.5 %collective-permute-start.21 = (bf16[512,512]{1,0:T(8,128)(2,1)S(1)}, bf16[512,512]{1,0:T(8,128)(2,1)}, u32[]{:S(2)}, u32[]{:S(2)}) collective-permute-start(bf16[512,512]{1,0:T(8,128)(2,1)S(1)} %copy-done.32), channel_id=1, source_target_pairs={{0,4},{4,0},{8,12},{12,8},{16,20},{20,16},{24,28},{28,24},{1,5},{5... | collective-permute-start | bytes 1572872 | tf_op jit(solution)/shard_map/ppermute | solution.py:475
  188.4 37.7 %collective-permute-start.22 = (bf16[256,1024]{1,0:T(8,128)(2,1)}, bf16[256,1024]{1,0:T(8,128)(2,1)}, u32[]{:S(2)}, u32[]{:S(2)}) collective-permute-start(bf16[256,1024]{1,0:T(8,128)(2,1)} %collective-permute-done.16.refs_12_), channel_id=1, source_target_pairs={{0,4},{4,0},{8,12},{12,8},{16,20},{20,16},{24,28},{28,24},{1,5},{5... | collective-permute-start | bytes 1572872 | tf_op jit(solution)/shard_map/ppermute | solution.py:475
  188.8 37.3 %collective-permute-start.23 = (bf16[256,1024]{1,0:T(8,128)(2,1)}, bf16[256,1024]{1,0:T(8,128)(2,1)}, u32[]{:S(2)}, u32[]{:S(2)}) collective-permute-start(bf16[256,1024]{1,0:T(8,128)(2,1)} %collective-permute-done.17.refs_13_), channel_id=1, source_target_pairs={{0,4},{4,0},{8,12},{12,8},{16,20},{20,16},{24,28},{28,24},{1,5},{5... | collective-permute-start | bytes 1572872 | tf_op jit(solution)/shard_map/ppermute | solution.py:475
  225.2 36.5 %collective-permute-start.24 = (bf16[1024,512]{1,0:T(8,128)(2,1)}, bf16[1024,512]{1,0:T(8,128)(2,1)S(1)}, u32[]{:S(2)}, u32[]{:S(2)}) collective-permute-start(bf16[1024,512]{1,0:T(8,128)(2,1)} %bitcast.2.refs_8_), channel_id=1, source_target_pairs={{0,4},{4,0},{8,12},{12,8},{16,20},{20,16},{24,28},{28,24},{1,5},{5... | collective-permute-start | bytes 3145736 | tf_op jit(solution)/shard_map/ppermute | solution.py:475
  225.6 36.1 %collective-permute-start.25 = (bf16[1024,512]{1,0:T(8,128)(2,1)}, bf16[1024,512]{1,0:T(8,128)(2,1)S(1)}, u32[]{:S(2)}, u32[]{:S(2)}) collective-permute-start(bf16[1024,512]{1,0:T(8,128)(2,1)} %bitcast.3.refs_9_), channel_id=1, source_target_pairs={{0,4},{4,0},{8,12},{12,8},{16,20},{20,16},{24,28},{28,24},{1,5},{5... | collective-permute-start | bytes 3145736 | tf_op jit(solution)/shard_map/ppermute | solution.py:475
  225.7 36.0 %collective-permute-start.26 = (bf16[512,1024]{1,0:T(8,128)(2,1)}, bf16[512,1024]{1,0:T(8,128)(2,1)S(1)}, u32[]{:S(2)}, u32[]{:S(2)}) collective-permute-start(bf16[512,1024]{1,0:T(8,128)(2,1)} %bitcast.4.refs_10_), channel_id=1, source_target_pairs={{0,4},{4,0},{8,12},{12,8},{16,20},{20,16},{24,28},{28,24},{1,5},{5... | collective-permute-start | bytes 3145736 | tf_op jit(solution)/shard_map/ppermute | solution.py:475
  317.2 203.9 %reduce-scatter.6.cloned.1.call-start = ((), (), s32[]{:S(2)}) async-start(), calls=%async_computation.6 | async-start | bytes 5242880 | tf_op jit(solution)/shard_map/reduce_scatter | solution.py:574
  383.8 137.9 %reduce-scatter.4.cloned.1.call-start = ((), (), s32[]{:S(2)}) async-start(), calls=%async_computation.5 | async-start | bytes 81920 | tf_op jit(solution)/shard_map/reduce_scatter | solution.py:574
  399.1 242.5 %all-reduce.8.cloned.1.call-start = ((), (), s32[]{:S(2)}) async-start(), calls=%async_computation.9 | async-start | bytes 6291456 | tf_op jit(solution)/shard_map/psum | solution.py:579
  414.9 36.6 %collective-permute-start.44 = (bf16[512,512]{1,0:T(8,128)(2,1)S(1)}, bf16[512,512]{1,0:T(8,128)(2,1)S(1)}, u32[]{:S(2)}, u32[]{:S(2)}) collective-permute-start(bf16[512,512]{1,0:T(8,128)(2,1)S(1)} %slice.188), channel_id=1, source_target_pairs={{0,16},{4,20},{8,24},{12,28},{16,0},{20,4},{24,8},{28,12},{1,17},{... | collective-permute-start | bytes 1572872 | tf_op jit(solution)/shard_map/ppermute | solution.py:475
  416.1 37.0 %collective-permute-start.39 = (bf16[512,512]{1,0:T(8,128)(2,1)S(1)}, bf16[512,512]{1,0:T(8,128)(2,1)S(1)}, u32[]{:S(2)}, u32[]{:S(2)}) collective-permute-start(bf16[512,512]{1,0:T(8,128)(2,1)S(1)} %slice.184), channel_id=1, source_target_pairs={{0,8},{4,12},{8,0},{12,4},{16,24},{20,28},{24,16},{28,20},{1,9},{5... | collective-permute-start | bytes 1572872 | tf_op jit(solution)/shard_map/ppermute | solution.py:475
  453.0 35.1 %collective-permute-start.46 = (bf16[512,512]{1,0:T(8,128)(2,1)S(1)}, bf16[512,512]{1,0:T(8,128)(2,1)S(1)}, u32[]{:S(2)}, u32[]{:S(2)}) collective-permute-start(bf16[512,512]{1,0:T(8,128)(2,1)S(1)} %add_convert_fusion.19), channel_id=1, source_target_pairs={{0,8},{4,12},{8,0},{12,4},{16,24},{20,28},{24,16},{28,20},{1,9},{5... | collective-permute-start | bytes 1572872 | tf_op jit(solution)/shard_map/ppermute | solution.py:475
  520.9 182.5 %all-reduce.6.cloned.1.call-start = ((), (), s32[]{:S(2)}) async-start(), calls=%async_computation.8 | async-start | bytes 3145728 | tf_op jit(solution)/shard_map/psum | solution.py:574
  (70 other events, 1021.0 us)
Sparse Core Ops, SparseCore 0:
  10.2 87.5 all-gather.2
  99.4 44.4 all-gather.4
  317.3 42.0 reduce-scatter.7
  383.9 74.9 reduce-scatter.5
  461.6 19.5 reduce-scatter.3
  521.1 120.5 all-reduce.7
  645.3 58.0 all-reduce.5

commit v2 on v1

--- a/solution.py
+++ b/solution.py
@@ -68,6 +68,10 @@
 
 def whole_block(shape):
     return pl.BlockSpec(shape, lambda i: (0,) * len(shape))
+
+
+def tied(kernel, inputs, ties):
+    return lambda *refs: kernel(*refs[:inputs], *refs[inputs + len(ties) :])
 
 
 def project_kernel(x_ref, gain_ref, w_ref, cos_ref, sin_ref, n_ref, q_ref, k_ref, v_ref):
@@ -171,18 +175,22 @@
     dv_ref[...] = dv_acc[...].astype(BF16)
 
 
-def attend_back(queries, keys, vals, grad, cos, sin):
+def attend_back(queries, keys, vals, grad, cos, sin, first=0, steps=KEY_VALUE_HEADS // 2, ties=()):
     rows = queries.shape[0]
-    steps = KEY_VALUE_HEADS // 2
-    flops = 5 * QUERY_HEADS * rows * SEQUENCE_LENGTH * HEAD_WIDTH * 2
+    flops = 5 * QUERY_HEADS * rows * SEQUENCE_LENGTH * HEAD_WIDTH * 2 * steps // (KEY_VALUE_HEADS // 2)
     table = pl.BlockSpec((SEQUENCE_LENGTH, LANES), lambda s, i: (s, 0))
-    two, four = head_block(2 * HEAD_WIDTH), head_block(4 * HEAD_WIDTH)
+
+    def block(width, start):
+        return pl.BlockSpec((SEQUENCE_LENGTH, width), lambda s, i: (s, i + start))
+
+    two, four = block(2 * HEAD_WIDTH, first), block(4 * HEAD_WIDTH, first)
+    out_two, out_four = block(2 * HEAD_WIDTH, 0), block(4 * HEAD_WIDTH, 0)
     return pl.pallas_call(
-        attend_back_kernel,
+        tied(attend_back_kernel, 6, ties),
         grid=(rows // SEQUENCE_LENGTH, steps),
-        in_specs=[four, two, two, four, table, table],
-        out_specs=[four, two, two],
-        out_shape=[jax.ShapeDtypeStruct(a.shape, BF16) for a in (queries, keys, vals)],
+        in_specs=[four, two, two, four, table, table] + [ANY] * len(ties),
+        out_specs=[out_four, out_two, out_two],
+        out_shape=[jax.ShapeDtypeStruct((rows, steps * w), BF16) for w in (4 * HEAD_WIDTH, 2 * HEAD_WIDTH, 2 * HEAD_WIDTH)],
         scratch_shapes=[
             pltpu.VMEM((SEQUENCE_LENGTH, LANES), F32),
             pltpu.VMEM((SEQUENCE_LENGTH, LANES), F32),
@@ -191,7 +199,7 @@
         compiler_params=params(),
         cost_estimate=cost(flops * 8, 12 * rows * 1024, QUERY_HEADS * rows * 640),
         name="attend_back",
-    )(queries, keys, vals, grad, cos, sin)
+    )(queries, keys, vals, grad, cos, sin, *ties)
 
 
 def middle_kernel(a_ref, w_ref, x_ref, gain_ref, router_ref, routes_ref, r_ref, m_ref, mt_ref, gates_ref):
@@ -238,15 +246,16 @@
     )(attended, out_w, tokens, gain, router_w, routes)
 
 
-def moe_kernel(slots, chunks, first, last, me_ref, *refs):
+def moe_kernel(slots, chunks, first, ties, me_ref, *refs):
     refs = list(refs)
     take = lambda count: [refs.pop(0) for _ in range(count)]
     x_hbm, xt_hbm, dy_hbm, dyt_hbm, gates_ref = take(5)
     if not first:
         made_in, dmoe_in, gg_in = take(3)
     weights = [[take(count) for count in per_slot] for per_slot in chunks]
+    take(ties)
     made_out, dmoe_out, gg_ref = take(3)
-    grads = [take(3) for _ in slots]
+    grads = [take(2) for _ in slots]
     x, xt, dy, dyt, made, dmoe, wg, wu, wd, hg, dg, du, stage, sem_in, sem_w, sem_out, sem_acc = take(17)
     rows = x.shape[0]
     tiles = rows // TILE
@@ -332,33 +341,34 @@
             return carry
 
         lax.fori_loop(0, x.shape[1] // TILE, grads_step, 0)
-        for which in range(3):
-            stores.append(load(stage.at[which], grads[index][which], sem_out.at[which]))
+        half = stage.shape[1] // 2
+        for part in range(2):
+            stores.append(load(stage.at[:, part * half : (part + 1) * half], grads[index][part], sem_out.at[part]))
     done = [load(made, made_out, sem_acc.at[0]), load(dmoe, dmoe_out, sem_acc.at[1])]
     for copy in stores + done:
         copy.wait()
 
 
-def moe(slots, me, moe_in, moe_in_t, dy, dy_t, gates, acc, weights):
+def moe(slots, me, moe_in, moe_in_t, dy, dy_t, gates, acc, weights, ties=()):
     rows, width = moe_in.shape
     hidden = weights[0][0][0].shape[1]
     first = acc is None
     flat = [piece for per_slot in weights for pieces in per_slot for piece in pieces]
     chunks = tuple(tuple(len(pieces) for pieces in per_slot) for per_slot in weights)
     accs = [] if first else list(acc)
-    grad = jax.ShapeDtypeStruct((width, hidden), BF16)
+    grad = jax.ShapeDtypeStruct((3, width // 2, hidden), BF16)
     outs = pl.pallas_call(
-        functools.partial(moe_kernel, tuple(slots), chunks, first, False),
+        functools.partial(moe_kernel, tuple(slots), chunks, first, len(ties)),
         in_specs=[pl.BlockSpec(memory_space=pltpu.SMEM), ANY, ANY, ANY, ANY, VMEM]
         + ([] if first else [ANY, ANY, VMEM])
-        + [ANY] * len(flat),
-        out_specs=[ANY, ANY, VMEM] + [ANY] * (3 * len(slots)),
+        + [ANY] * (len(flat) + len(ties)),
+        out_specs=[ANY, ANY, VMEM] + [ANY] * (2 * len(slots)),
         out_shape=[
             jax.ShapeDtypeStruct((rows, width), F32),
             jax.ShapeDtypeStruct((rows, width), F32),
             jax.ShapeDtypeStruct((rows, LANES), F32),
         ]
-        + [grad] * (3 * len(slots)),
+        + [grad] * (2 * len(slots)),
         scratch_shapes=[
             pltpu.VMEM((rows, width), BF16),
             pltpu.VMEM((width, rows), BF16),
@@ -375,14 +385,14 @@
             pltpu.VMEM((3, width, hidden), BF16),
             pltpu.SemaphoreType.DMA((4,)),
             pltpu.SemaphoreType.DMA((2, 3, 2)),
-            pltpu.SemaphoreType.DMA((3,)),
+            pltpu.SemaphoreType.DMA((2,)),
             pltpu.SemaphoreType.DMA((2,)),
         ],
         compiler_params=params(),
         cost_estimate=cost(18 * rows * width * hidden * len(slots), 20 * rows * width),
         name="experts",
-    )(me, moe_in, moe_in_t, dy, dy_t, gates, *accs, *flat)
-    return outs[:3], [tuple(outs[3 + 3 * i : 6 + 3 * i]) for i in range(len(slots))]
+    )(me, moe_in, moe_in_t, dy, dy_t, gates, *accs, *flat, *ties)
+    return outs[:3], [tuple(outs[3 + 2 * i : 5 + 2 * i]) for i in range(len(slots))]
 
 
 def turn_kernel(
@@ -411,16 +421,17 @@
     da_ref[...] = dot_nt(dz, w_ref[...]).astype(BF16)
 
 
-def turn(resid, made, dmoe, gates, gg, dy, gain, router_w, moe_in_t, out_w):
+def turn(resid, made, dmoe, gates, gg, dy, gain, router_w, moe_in_t, out_w, ties=()):
     rows, width = resid.shape
     return pl.pallas_call(
-        turn_kernel,
+        tied(turn_kernel, 10, ties),
         grid=(rows // TILE,),
         in_specs=[
             row_block(width), row_block(width), row_block(width), row_block(LANES), row_block(LANES), row_block(width),
             whole_block((1, width)), whole_block(router_w.shape), pl.BlockSpec((width, TILE), lambda i: (0, i)),
             whole_block(out_w.shape),
-        ],
+        ]
+        + [ANY] * len(ties),
         out_specs=[row_block(width)] * 4 + [whole_block((1, width)), whole_block((width, LANES))],
         out_shape=[
             jax.ShapeDtypeStruct((rows, width), BF16),
@@ -433,18 +444,21 @@
         compiler_params=params(),
         cost_estimate=cost(2 * rows * width * (width + 2 * LANES), 28 * rows * width),
         name="turn",
-    )(resid, made, dmoe, gates, gg, dy, gain, router_w, moe_in_t, out_w)
-
-
-def finish_kernel(dq_ref, dk_ref, dv_ref, w_ref, x_ref, dresid_ref, gain_ref, out_ref, gain_grad_ref):
+    )(resid, made, dmoe, gates, gg, dy, gain, router_w, moe_in_t, out_w, *ties)
+
+
+def finish_kernel(count, *refs):
+    grads = refs[:count]
+    w_ref, x_ref, dresid_ref, gain_ref, out_ref, gain_grad_ref = refs[count:]
+
     @pl.when(pl.program_id(0) == 0)
     def _():
         gain_grad_ref[...] = jnp.zeros_like(gain_grad_ref)
 
-    qw, kw = dq_ref.shape[1], dk_ref.shape[1]
-    dn = dot_nt(dq_ref[...], w_ref[:, :qw])
-    dn += dot_nt(dk_ref[...], w_ref[:, qw : qw + kw])
-    dn += dot_nt(dv_ref[...], w_ref[:, qw + kw :])
+    at, dn = 0, 0.0
+    for ref in grads:
+        dn += dot_nt(ref[...], w_ref[:, at : at + ref.shape[1]])
+        at += ref.shape[1]
     x = x_ref[...].astype(F32)
     inverse = lax.rsqrt(jnp.mean(x * x, axis=-1, keepdims=True) + 1e-06)
     gain_grad_ref[...] += jnp.sum(dn * x * inverse, axis=0, keepdims=True)
@@ -453,21 +467,288 @@
     out_ref[...] = dresid_ref[...] + inverse * scaled - x * (inverse * inverse * inverse * inner)
 
 
-def finish(dq, dk, dv, weights, tokens, dresid, gain):
+def finish(grads, weights, tokens, dresid, gain, ties=()):
     rows, width = tokens.shape
     return pl.pallas_call(
-        finish_kernel,
+        tied(functools.partial(finish_kernel, len(grads)), len(grads) + 4, ties),
         grid=(rows // TILE,),
-        in_specs=[
-            row_block(dq.shape[1]), row_block(dk.shape[1]), row_block(dv.shape[1]), whole_block(weights.shape),
-            row_block(width), row_block(width), whole_block((1, width)),
-        ],
+        in_specs=[row_block(g.shape[1]) for g in grads]
+        + [whole_block(weights.shape), row_block(width), row_block(width), whole_block((1, width))]
+        + [ANY] * len(ties),
         out_specs=[row_block(width), whole_block((1, width))],
         out_shape=[jax.ShapeDtypeStruct((rows, width), F32), jax.ShapeDtypeStruct((1, width), F32)],
         compiler_params=params(),
         cost_estimate=cost(2 * rows * width * weights.shape[1], 20 * rows * width),
         name="finish",
-    )(dq, dk, dv, weights, tokens, dresid, gain)
+    )(*grads, weights, tokens, dresid, gain, *ties)
+
+
+def plus_kernel(*refs):
+    total = refs[0][...].astype(F32)
+    for ref in refs[1:-1]:
+        total += ref[...].astype(F32)
+    refs[-1][...] = total.astype(BF16)
+
+
+def plus(*terms, ties=()):
+    shape = terms[0].shape
+    block = pl.BlockSpec((1,) + shape[1:], lambda i: (i, 0, 0))
+    return pl.pallas_call(
+        tied(plus_kernel, len(terms), ties),
+        grid=(shape[0],),
+        in_specs=[block] * len(terms) + [ANY] * len(ties),
+        out_specs=block,
+        out_shape=jax.ShapeDtypeStruct(shape, BF16),
+        compiler_params=params(),
+        cost_estimate=cost(len(terms) * terms[0].size, 2 * (len(terms) + 1) * terms[0].size),
+        name="plus",
+    )(*terms, *ties)
+
+
+def gather_kernel(size, q_ref, k_ref, v_ref, s_ref, o_ref, packed_ref, small_ref, out_ref, send_sem, recv_sem, pass_sem, take_sem):
+    me, z = lax.axis_index("expert"), lax.axis_index("wshard")
+    core = lax.rem(me, 2)
+    sibling = me + 1 - 2 * core
+    rows = q_ref.shape[0]
+    half = rows // 2
+    there = lambda step: jnp.logical_and(z + step >= 0, z + step < size)
+
+    barrier = pltpu.get_barrier_semaphore()
+    pl.semaphore_signal(barrier, inc=1, device_id=(sibling, z), device_id_type=pl.DeviceIdType.MESH)
+    for step in (1, -1):
+
+        @pl.when(there(step))
+        def _():
+            pl.semaphore_signal(barrier, inc=1, device_id=(me, z + step), device_id_type=pl.DeviceIdType.MESH)
+
+    pl.semaphore_wait(barrier, 1 + jnp.where(z > 0, 1, 0) + jnp.where(z < size - 1, 1, 0))
+
+    own = pl.ds(pl.multiple_of(z * rows, rows), rows)
+    at = 0
+    for ref in (q_ref, k_ref, v_ref):
+        packed_ref[own, at : at + ref.shape[1]] = ref[...]
+        at += ref.shape[1]
+    small_ref[own] = s_ref[...]
+
+    def moves(way, hop, origin, which, device, send, recv):
+        at = pl.ds(pl.multiple_of(origin * rows + which * half, half), half)
+        return [
+            pltpu.make_async_remote_copy(
+                src_ref=ref.at[at], dst_ref=ref.at[at], send_sem=send.at[way, hop, i], recv_sem=recv.at[way, hop, i],
+                device_id=device, device_id_type=pl.DeviceIdType.MESH,
+            )
+            for i, ref in enumerate((packed_ref, small_ref))
+        ]
+
+    def onward(way, step, hop):
+        return moves(way, hop, z - step * (hop - 1), core, (me, z + step), send_sem, recv_sem)
+
+    def across(way, step, hop, which):
+        return moves(way, hop, z - step * hop, which, (sibling, z), pass_sem, take_sem)
+
+    ways = ((0, 1), (1, -1))
+    for way, step in ways:
+
+        @pl.when(there(step))
+        def _():
+            for move in onward(way, step, 1):
+                move.start()
+
+    for hop in range(1, size):
+        for way, step in ways:
+
+            @pl.when(there(-step * hop))
+            def _():
+                for move in moves(way, hop, z - step * hop, core, (me, z), send_sem, recv_sem):
+                    move.wait_recv()
+
+                @pl.when(there(step))
+                def _():
+                    for move in onward(way, step, hop + 1):
+                        move.start()
+
+                for move in across(way, step, hop, core):
+                    move.start()
+
+    for hop in range(1, size):
+        for way, step in ways:
+
+            @pl.when(there(-step * hop))
+            def _():
+                for move in across(way, step, hop, 1 - core):
+                    move.wait_recv()
+                for move in across(way, step, hop, core):
+                    move.wait_send()
+
+            @pl.when(jnp.logical_and(there(step), there(-step * (hop - 1))))
+            def _():
+                for move in onward(way, step, hop):
+                    move.wait_send()
+
+    out_ref[...] = o_ref[...]
+
+
+def gather_weights(query, key, value, small, out):
+    size = lax.axis_size("wshard")
+    rows = query.shape[0]
+    width = query.shape[1] + key.shape[1] + value.shape[1]
+    sems = pltpu.SemaphoreType.DMA((2, size + 1, 2))
+    return pl.pallas_call(
+        functools.partial(gather_kernel, size),
+        in_specs=[VMEM] * 5,
+        out_specs=[VMEM] * 3,
+        out_shape=[
+            jax.ShapeDtypeStruct((size * rows, width), BF16),
+            jax.ShapeDtypeStruct((size * rows, small.shape[1]), BF16),
+            jax.ShapeDtypeStruct(out.shape, BF16),
+        ],
+        scratch_shapes=[sems, sems, sems, sems],
+        compiler_params=pltpu.CompilerParams(collective_id=0, has_side_effects=True, vmem_limit_bytes=VMEM_BYTES),
+        cost_estimate=cost(1e9, 12 * rows * size * width),
+        name="gather_weights",
+    )(query, key, value, small, out)
+
+
+def reduce_kernel(size, columns, *refs):
+    count = len(columns)
+    ins, outs = refs[:count], refs[count : 2 * count]
+    acc, rc, r1, r2, zs, rz, res, send_sem, recv_sem = refs[2 * count :]
+    me, z = lax.axis_index("expert"), lax.axis_index("wshard")
+    core, xb, yb = lax.rem(me, 2), lax.rem(me // 2, 2), me // 4
+    sibling, xp, yp = me + 1 - 2 * core, me + 2 - 4 * xb, me + 4 - 8 * yb
+    half = ins[0].shape[1] // 2
+    n1, n2 = half // 4, half // 8
+
+    barrier = pltpu.get_barrier_semaphore()
+    for peer in (sibling, xp, yp):
+        pl.semaphore_signal(barrier, inc=1, device_id=(peer, z), device_id_type=pl.DeviceIdType.MESH)
+    for d in range(1, size):
+        pl.semaphore_signal(barrier, inc=1, device_id=(me, lax.rem(z + d, size)), device_id_type=pl.DeviceIdType.MESH)
+    pl.semaphore_wait(barrier, 2 + size)
+
+    pieces, at = [], 0
+    for ref, out, width in zip(ins, outs, columns):
+        step = width if width <= 512 else 512
+        for lo in range(0, width, step):
+            pieces.append((ref, out, lo, step, at))
+            at += step
+
+    sent = []
+
+    def move(source, target, piece, kind, device):
+        copy = pltpu.make_async_remote_copy(
+            src_ref=source, dst_ref=target, send_sem=send_sem.at[kind, piece], recv_sem=recv_sem.at[kind, piece],
+            device_id=device, device_id_type=pl.DeviceIdType.MESH,
+        )
+        copy.start()
+        sent.append(copy)
+        return copy
+
+    def rows(start, length):
+        return pl.ds(pl.multiple_of(start, 16), length)
+
+    def sum_of(*terms):
+        total = terms[0].astype(F32)
+        for term in terms[1:]:
+            total += term.astype(F32)
+        return total
+
+    k0, k1 = xb * n1 + yb * n2, half // 2 + yb * n1 + xb * n2
+    base = core * half
+    first = []
+    for p, (ref, _, lo, w, at) in enumerate(pieces):
+        first.append(move(ref.at[:, rows((1 - core) * half, half), lo : lo + w], rc.at[:, :, at : at + w], p, 0, (sibling, z)))
+    second = []
+    for p, (ref, _, lo, w, at) in enumerate(pieces):
+        c = slice(at, at + w)
+        first[p].wait_recv()
+        acc[:, :, c] = sum_of(ref[:, rows(base, half), lo : lo + w], rc[:, :, c]).astype(BF16)
+        second.append((
+            move(acc.at[:, rows((1 - xb) * n1, n1), c], r1.at[0, :, :, c], p, 1, (xp, z)),
+            move(acc.at[:, rows(half // 2 + (1 - yb) * n1, n1), c], r1.at[1, :, :, c], p, 2, (yp, z)),
+        ))
+    third = []
+    for p, (_, _, _, w, at) in enumerate(pieces):
+        c = slice(at, at + w)
+        keep = (rows(xb * n1, n1), rows(half // 2 + yb * n1, n1))
+        for i in range(2):
+            second[p][i].wait_recv()
+            acc[:, keep[i], c] = sum_of(acc[:, keep[i], c], r1[i, :, :, c]).astype(BF16)
+        third.append((
+            move(acc.at[:, rows(xb * n1 + (1 - yb) * n2, n2), c], r2.at[0, :, :, c], p, 3, (yp, z)),
+            move(acc.at[:, rows(half // 2 + yb * n1 + (1 - xb) * n2, n2), c], r2.at[1, :, :, c], p, 4, (xp, z)),
+        ))
+    fourth = []
+    for p, (_, _, _, w, at) in enumerate(pieces):
+        c = slice(at, at + w)
+        for i, k in enumerate((k0, k1)):
+            third[p][i].wait_recv()
+            zs[:, i * n2 : (i + 1) * n2, c] = sum_of(acc[:, rows(k, n2), c], r2[i, :, :, c]).astype(BF16)
+        fourth.append([
+            move(zs.at[lax.rem(z + d, size), :, c], rz.at[d - 1, :, c], p, 8 + d, (me, lax.rem(z + d, size)))
+            for d in range(1, size)
+        ])
+    fifth = []
+    for p, (_, _, _, w, at) in enumerate(pieces):
+        c = slice(at, at + w)
+        for copy in fourth[p]:
+            copy.wait_recv()
+        total = sum_of(zs[z, :, c], *[rz[d, :, c] for d in range(size - 1)]).astype(BF16)
+        for i, k in enumerate((k0, k1)):
+            res[rows(base + k, n2), c] = total[i * n2 : (i + 1) * n2]
+        fifth.append((
+            move(res.at[rows(base + k0, n2), c], res.at[rows(base + k0, n2), c], p, 5, (yp, z)),
+            move(res.at[rows(base + k1, n2), c], res.at[rows(base + k1, n2), c], p, 6, (xp, z)),
+        ))
+    sixth = []
+    for p, (_, _, _, w, at) in enumerate(pieces):
+        c = slice(at, at + w)
+        for copy in fifth[p]:
+            copy.wait_recv()
+        mine = rows(base + xb * n1, n1), rows(base + half // 2 + yb * n1, n1)
+        sixth.append((
+            move(res.at[mine[0], c], res.at[mine[0], c], p, 7, (xp, z)),
+            move(res.at[mine[1], c], res.at[mine[1], c], p, 8, (yp, z)),
+        ))
+    last = []
+    for p, (_, _, _, w, at) in enumerate(pieces):
+        c = slice(at, at + w)
+        for copy in sixth[p]:
+            copy.wait_recv()
+        last.append(move(res.at[rows(base, half), c], res.at[rows(base, half), c], p, 8 + size, (sibling, z)))
+    for p, (_, out, lo, w, at) in enumerate(pieces):
+        last[p].wait_recv()
+        out[:, lo : lo + w] = res[:, at : at + w].astype(F32)
+    for copy in sent:
+        copy.wait_send()
+
+
+def reduce_all(*grads):
+    size = lax.axis_size("wshard")
+    rows = grads[0].shape[0] // size
+    columns = tuple(g.shape[1] for g in grads)
+    count = sum(-(-c // 512) for c in columns)
+    width, half = sum(columns), rows // 2
+    return pl.pallas_call(
+        functools.partial(reduce_kernel, size, columns),
+        in_specs=[VMEM] * len(grads),
+        out_specs=[VMEM] * len(grads),
+        out_shape=[jax.ShapeDtypeStruct((rows, c), F32) for c in columns],
+        scratch_shapes=[
+            pltpu.VMEM((size, half, width), BF16),
+            pltpu.VMEM((size, half, width), BF16),
+            pltpu.VMEM((2, size, half // 4, width), BF16),
+            pltpu.VMEM((2, size, half // 8, width), BF16),
+            pltpu.VMEM((size, half // 4, width), BF16),
+            pltpu.VMEM((size - 1, half // 4, width), BF16),
+            pltpu.VMEM((rows, width), BF16),
+            pltpu.SemaphoreType.DMA((9 + size, count)),
+            pltpu.SemaphoreType.DMA((9 + size, count)),
+        ],
+        compiler_params=pltpu.CompilerParams(collective_id=1, has_side_effects=True, vmem_limit_bytes=VMEM_BYTES),
+        cost_estimate=cost(1e9, 8 * size * rows * width),
+        name="reduce_all",
+    )(*[g.reshape(size, rows, g.shape[1]) for g in grads])
 
 
 def flip(value, axis, bit):
@@ -491,9 +772,11 @@
             for j in sorted(slots):
                 slots[j | bit] = tuple([flip(p, "expert", bit) for p in m] for m in slots[j])
             bit *= 2
-    for j in sorted(slots):
-        slots[j | 1] = tuple([flip(p, "expert", 1) for p in m] for m in slots[j])
     return slots
+
+
+def across_core(slot):
+    return tuple([flip(p, "expert", 1) for p in m] for m in slot)
 
 
 def add(a, b):
@@ -501,29 +784,14 @@
 
 
 def reduce_experts(parts, owners):
-    pairs = {}
-    for j in parts:
-        if j & 1:
-            pairs[j ^ 1] = tuple(add(m, flip(s, "expert", 1)) for m, s in zip(parts[j ^ 1], parts[j]))
-    if owners == 8:
-        own = []
-        for m0, m2, m4, m6 in zip(pairs[0], pairs[2], pairs[4], pairs[6]):
-            cut = m0.shape[0] // 2
-            left, right = flip(m6[:cut], "expert", 2), flip(m6[cut:], "expert", 4)
-            top = add(m0[:cut], flip(m2[:cut], "expert", 2))
-            bottom = add(m0[cut:], flip(m4[cut:], "expert", 4))
-            top = add(top, flip(add(m4[:cut], left), "expert", 4))
-            bottom = add(bottom, flip(add(m2[cut:], right), "expert", 2))
-            own.append(jnp.concatenate([top, bottom], axis=0))
-        return tuple(own)
-    bit = 2
+    bit = 1
     while bit < owners:
-        for j in sorted(pairs, reverse=True):
+        for j in sorted(parts, reverse=True):
             if j & bit:
-                gone = pairs.pop(j)
-                pairs[j ^ bit] = tuple(add(m, flip(s, "expert", bit)) for m, s in zip(pairs[j ^ bit], gone))
+                gone = parts.pop(j)
+                parts[j ^ bit] = tuple(add(m, flip(s, "expert", bit)) for m, s in zip(parts[j ^ bit], gone))
         bit *= 2
-    return pairs[0]
+    return parts[0]
 
 
 def on_device(
@@ -532,51 +800,83 @@
     owners = lax.axis_size("expert")
     me = lax.axis_index("expert").astype(jnp.int32)[None]
     rows, width = tokens.shape
-    experts = w_router.shape[1] * 1
+    experts = w_router.shape[1]
     slots = gather_experts((w_gate[0], w_up[0], w_down[0]), owners)
 
     small = jnp.concatenate([gain_attn[:, None], gain_ffn[:, None], w_router], axis=1)
-    packed = lax.all_gather(
-        jnp.concatenate([w_query, key_weight, value_weight], axis=1), "wshard", axis=0, tiled=True
-    )
-    small = lax.all_gather(small, "wshard", axis=0, tiled=True)
-    out_w = lax.all_gather(w_out, "wshard", axis=0, tiled=True)
+    small = jnp.pad(small, ((0, 0), (0, LANES - small.shape[1])))
+    packed, small, out_shard = gather_weights(w_query, key_weight, value_weight, small, w_out)
+    out_w = lax.all_gather(out_shard, "wshard", axis=0, tiled=True)
     gain_one, gain_two = small[:, 0][None], small[:, 1][None]
-    router_w = jnp.pad(small[:, 2:], ((0, 0), (0, LANES - experts)))
+    router_w = jnp.pad(small[:, 2 : 2 + experts], ((0, 0), (0, LANES - experts)))
     cos, sin = (jnp.asarray(a) for a in rope_tables(rows))
 
     normed, queries, keys, vals = project(tokens, gain_one, packed, cos, sin)
     attended = attend(queries, keys, vals)
     resid, moe_in, moe_in_t, gates = middle(attended, out_w, tokens, gain_two, router_w, routes)
-
-    order = [2, 3, 4, 5, 6, 7, 0, 1] if owners == 8 else list(range(owners))
     dy_t = cotangent.T
-    acc, parts = None, {}
-    for at in range(0, len(order), 2):
-        pair = order[at : at + 2]
-        acc, grads = moe(
-            pair, me, moe_in, moe_in_t, cotangent, dy_t, gates, acc, [slots[j] for j in pair]
+    for j in sorted(slots):
+        here = slots[j] if j == 0 else lax.optimization_barrier((slots[j], attended))[0]
+        slots[j | 1] = across_core(here)
+
+    def some(pair, acc, ties=()):
+        return moe(pair, me, moe_in, moe_in_t, cotangent, dy_t, gates, acc, [slots[j] for j in pair], ties)
+
+    def turned(acc, ties=()):
+        made, dmoe, gate_grads = acc
+        return turn(resid, made, dmoe, gates, gate_grads, cotangent, gain_two, router_w, moe_in_t, out_w, ties)
+
+    if owners == 8:
+        core = lambda halves: [flip(m, "expert", 1) for m in halves]
+        over_x = lambda m: flip(m, "expert", 2)
+        over_y = lambda m: flip(m, "expert", 4)
+        both = lambda a, b: [plus(m, n) for m, n in zip(a, b)]
+        acc, (g2, g3) = some([2, 3], None)
+        c3 = core(g3)
+        acc, (g6, g7) = some([6, 7], acc)
+        s2 = both(g2, c3)
+        c7 = core(g7)
+        x20 = over_x(s2[0])
+        acc, (g4, g5) = some([4, 5], acc, [*s2])
+        s6 = both(g6, c7)
+        c5 = core(g5)
+        x60, y61 = over_x(s6[0]), over_y(s6[1])
+        acc, (g0, g1) = some([0, 1], acc, [*s6, x20])
+        s4 = both(g4, c5)
+        c1 = core(g1)
+        left, right = plus(s4[0], x60), plus(s2[1], y61)
+        y41, x21 = over_y(s4[1]), over_x(right)
+        mixed, dresid, dz, dattended, gain_two_grad, router_grad = turned(acc, [left, right, s4[1]])
+        out_grad = dot_tn(attended, dz)
+        s0 = both(g0, c1)
+        y40 = over_y(left)
+        early = attend_back(queries, keys, vals, dattended, cos, sin, 0, 2, [*s0])
+        own = [plus(s0[0], x20, y40, ties=early[2:]), plus(s0[1], y41, x21, ties=early[2:])]
+        late = attend_back(queries, keys, vals, dattended, cos, sin, 2, 2, own)
+        pieces = [early[0], late[0], early[1], late[1], early[2], late[2]]
+    else:
+        acc, parts = None, {}
+        for at in range(0, owners, 2):
+            acc, grads = some([at, at + 1], acc)
+            parts.update(zip([at, at + 1], grads))
+        mixed, dresid, dz, dattended, gain_two_grad, router_grad = turned(acc)
+        own = reduce_experts(parts, owners)
+        out_grad = dot_tn(attended, dz)
+        pieces = attend_back(queries, keys, vals, dattended, cos, sin)
+    qkv_grad = dot_tn(normed, jnp.concatenate(pieces, axis=1)).astype(BF16)
+    d_tokens, gain_one_grad = finish(pieces, packed, tokens, dresid, gain_one)
+
+    small_grad = jnp.concatenate([gain_one_grad.T, gain_two_grad.T, router_grad[:, :experts]], axis=1)
+
+    small_grad = jnp.pad(small_grad, ((0, 0), (0, LANES - small_grad.shape[1]))).astype(BF16)
+    grads = (out_grad.astype(BF16), qkv_grad, small_grad)
+    if owners == 8:
+        out_grad, qkv_grad, small_grad = reduce_all(*grads)
+    else:
+        out_grad, qkv_grad, small_grad = (
+            lax.psum(lax.psum_scatter(g, "wshard", scatter_dimension=0, tiled=True), "expert").astype(F32) for g in grads
         )
-        parts.update(zip(pair, grads))
-    made, dmoe, gate_grads = acc
-    mixed, dresid, dz, dattended, gain_two_grad, router_grad = turn(
-        resid, made, dmoe, gates, gate_grads, cotangent, gain_two, router_w, moe_in_t, out_w
-    )
-    own = reduce_experts(parts, owners)
-    out_grad = dot_tn(attended, dz)
-    dq, dk, dv = attend_back(queries, keys, vals, dattended, cos, sin)
-    qkv_grad = dot_tn(normed, jnp.concatenate([dq, dk, dv], axis=1))
-    d_tokens, gain_one_grad = finish(dq, dk, dv, packed, tokens, dresid, gain_one)
-
-    small_grad = jnp.concatenate([gain_one_grad.T, gain_two_grad.T, router_grad[:, :experts]], axis=1)
-
-    def total(grad):
-        return lax.psum(lax.psum_scatter(grad, "wshard", scatter_dimension=0, tiled=True), "expert")
-
-    small_grad = total(small_grad)
-    out_grad = total(out_grad.astype(BF16)).astype(F32)
-    qkv_grad = total(qkv_grad.astype(BF16)).astype(F32)
-    own = tuple(lax.psum(m, "wshard").astype(F32) for m in own)
+    own = jnp.concatenate(lax.psum(tuple(own), "wshard"), axis=1).astype(F32)
     qw, kw = w_query.shape[1], key_weight.shape[1]
     return (
         mixed,
@@ -587,10 +887,10 @@
         qkv_grad[:, qw + kw :],
         out_grad,
         small_grad[:, 1],
-        small_grad[:, 2:],
-        own[0][None],
-        own[1][None],
-        own[2].T[None],
+        small_grad[:, 2 : 2 + experts],
+        own[0:1],
+        own[1:2],
+        own[2:3].swapaxes(1, 2),
     )
 
 

time: 725 us -> 589 us (0.81)
  waiting for transfers between devices: 278 us -> 42.5 us
  Pallas kernels: 275 us -> 440 us
  blocking collectives: 40.7 us -> 0 us
  starting transfers between devices: 43.2 us -> 24.8 us
  other arithmetic: 22.4 us -> 4.27 us
  local copies, waits for them, and re-layouts: 26.6 us -> 39.5 us
    pallas_call x3 -> x18, Pallas kernels: 82 us -> 248 us  [the longest x1 67.8 us: reduce_all(): pl.pallas_call(functools.partial(reduce_kernel, size, columns), in_specs=...]
    psum x2 -> x1, waiting for transfers between devices: 150 us -> 25.2 us  [on_device(): own = jnp.concatenate(lax.psum(tuple(own), 'wshard'), axis=1).astype(F32)]
    ppermute x57 -> x41, waiting for transfers between devices: 116 us -> 16.6 us  [flip(): return lax.ppermute(value, axis, [(i, i ^ bit) for i in range(size)])]
    psum x1 -> x0, blocking collectives: 24.1 us -> none  [total(): lax.psum(lax.psum_scatter(grad, 'wshard', scatter_dimension=0, tiled=True...]
    ppermute x57 -> x41, starting transfers between devices: 43 us -> 24.7 us  [flip(): return lax.ppermute(value, axis, [(i, i ^ bit) for i in range(size)])]
    all_gather x1 -> x0, blocking collectives: 16.6 us -> none  [on_device(): small = lax.all_gather(small, 'wshard', axis=0, tiled=True)]
    all_gather x2 -> x1, waiting for transfers between devices: 11.2 us -> 0.01 us  [on_device(): out_w = lax.all_gather(out_shard, 'wshard', axis=0, tiled=True)]
    convert_element_type x22 -> x1, other arithmetic: 11.8 us -> 2.77 us  [on_device(): own = jnp.concatenate(lax.psum(tuple(own), 'wshard'), axis=1).astype(F32)]
  transfers between devices with their start and end apart: 64 -> 43, of which waited for: 18 -> 4; matrix products, arithmetic and copies ran while one was open for 6% -> 6% of each run, Pallas kernels for 32% -> 70%
where the time goes in v2:
time: 589 us; the launch traced here: 578 us
  Pallas kernels  440 us (75%)
  waiting for transfers between devices  42.5 us (7%)
  local copies, waits for them, and re-layouts  39.5 us (7%)
  starting transfers between devices  24.8 us (4%)
  between operations  14.9 us (3%)
  matrix products  11.6 us (2%)
    pallas_call x4, Pallas kernels, moe(): pl.pallas_call(functools.partial(moe_kernel, tuple(slots), chunks, first,...  138 us
    pallas_call x1, Pallas kernels, reduce_all(): pl.pallas_call(functools.partial(reduce_kernel, size, columns), in_specs=...  67.8 us
    pallas_call x2, Pallas kernels, attend_back(): pl.pallas_call(tied(attend_back_kernel, 6, ties), grid=(rows // SEQUENCE_...  60.8 us
    pallas_call x1, Pallas kernels, gather_weights(): pl.pallas_call(functools.partial(gather_kernel, size), in_specs=[VMEM] *...  48.2 us
    pallas_call x12, Pallas kernels, plus(): pl.pallas_call(tied(plus_kernel, len(terms), ties), grid=(shape[0],), in_...  47.7 us
    pallas_call x1, Pallas kernels, attend(): pl.pallas_call(attend_kernel, grid=(rows // SEQUENCE_LENGTH, steps), in_s...  35.4 us
    psum x1, waiting for transfers between devices, on_device(): own = jnp.concatenate(lax.psum(tuple(own), 'wshard'), axis=1).astype(F32)  25.2 us
    ppermute x41, starting transfers between devices, flip(): return lax.ppermute(value, axis, [(i, i ^ bit) for i in range(size)])  24.7 us
  transfers between devices with their start and end apart: 43, of which 4 were waited for; matrix products, arithmetic and copies ran while one was open for 6% of the time, Pallas kernels for 70%

profile of v2, /device:TPU:0, one launch (start us, length us, event | category | flops | bytes accessed | tf_op | source)
XLA Modules:
  0.0 578.1 jit_solution(17589166391134505821)
XLA Ops:
  7.2 3.0 collective-permute-start
  17.1 48.2 %gather_weights.1 = (bf16[1024,2048]{1,0:T(8,128)(2,1)}, bf16[1024,128]{1,0:T(8,128)(2,1)}, bf16[256,1024]{1,0:T(8,128)(2,1)}) custom-call(bf16[256,1024]{1,0:T(8,128)(2,1)} %q_ref.1, bf16[256,512]{1,0:T(8,128)(2,1)} %k_ref.1, bf16[256,512]{1,0:T(8,128)(2,1)} %v_ref.1, bf16[256,128]{1,0:T(8,128)(2,1)} %pad.13.s_ref, bf16[256,1024]{1,0:T(8,128)(2,1)} %o_ref.1), custom_call_target="tpu_custom_call" | custom-call | flops 1000000000 | bytes 25165824 | tf_op jit(solution)/shard_map/gather_weights/pallas_call | solution.py:596
  67.3 9.1 %project.1 = (bf16[1024,1024]{1,0:T(8,128)(2,1)}, bf16[1024,1024]{1,0:T(8,128)(2,1)}, bf16[1024,512]{1,0:T(8,128)(2,1)}, bf16[1024,512]{1,0:T(8,128)(2,1)}) custom-call(bf16[1024,1024]{1,0:T(8,128)(2,1)} %refs_7_.1, bf16[1,1024]{1,0:T(2,128)(2,1)} %broadcast_in_dim_squeeze.6.gain_ref.refs_9_, bf16[1024,2048]{1,0:T(8,128)(2,1)} %get-tuple-element.81.w_ref.refs_6_, ...), custom_call_target="tpu_custom_call" | custom-call | flops 4294967296 | bytes 12582912 | tf_op jit(solution)/shard_map/project/pallas_call | solution.py:102
  86.9 35.4 %attend.1.a_ref = bf16[1024,1024]{1,0:T(8,128)(2,1)} custom-call(bf16[1024,1024]{1,0:T(8,128)(2,1)} %get-tuple-element.82.q_ref.refs_0_, bf16[1024,512]{1,0:T(8,128)(2,1)} %get-tuple-element.83.k_ref.refs_1_, bf16[1024,512]{1,0:T(8,128)(2,1)} %get-tuple-element.84.v_ref.refs_2_), custom_call_target="tpu_custom_call" | custom-call | flops 34359738368 | bytes 6291456 | tf_op jit(solution)/shard_map/attend/pallas_call | solution.py:138
  126.1 13.2 %collective-permute-done.12.refs_12_ = bf16[256,1024]{1,0:T(8,128)(2,1)} collective-permute-done((bf16[256,1024]{1,0:T(8,128)(2,1)S(1)}, bf16[256,1024]{1,0:T(8,128)(2,1)}, u32[]{:S(2)}, u32[]{:S(2)}) %collective-permute-start.12) | collective-permute-done | bytes 524320 | tf_op jit(solution)/shard_map/ppermute | solution.py:756
  145.1 9.1 %middle.1 = (f32[1024,1024]{1,0:T(8,128)}, bf16[1024,1024]{1,0:T(8,128)(2,1)}, bf16[1024,1024]{1,0:T(8,128)(2,1)}, f32[1024,128]{1,0:T(8,128)}) custom-call(bf16[1024,1024]{1,0:T(8,128)(2,1)} %attend.1.a_ref, bf16[1024,1024]{1,0:T(8,128)(2,1)} %all-gather.2.cloned.1.call-done.w_ref.refs_9_, bf16[1024,1024]{1,0:T(8,128)(2,1)} %refs_7_.1, ...), custom_call_target="tpu_custom_call" | custom-call | flops 2415919104 | bytes 14680064 | tf_op jit(solution)/shard_map/middle/pallas_call | solution.py:225
  155.8 32.1 %experts.4 = (f32[1024,1024]{1,0:T(8,128)}, f32[1024,1024]{1,0:T(8,128)}, f32[1024,128]{1,0:T(8,128)}, bf16[3,512,512]{2,1,0:T(8,128)(2,1)}, bf16[3,512,512]{2,1...) custom-call(s32[1]{0:T(128)} %bitcast.me_ref, ...), custom_call_target="tpu_custom_call" | custom-call | flops 19327352832 | bytes 20971520 | tf_op jit(solution)/shard_map/experts/pallas_call | solution.py:360
  189.7 35.4 %experts.5 = (f32[1024,1024]{1,0:T(8,128)}, f32[1024,1024]{1,0:T(8,128)}, f32[1024,128]{1,0:T(8,128)}, bf16[3,512,512]{2,1,0:T(8,128)(2,1)}, bf16[3,512,512]{2,1...) custom-call(s32[1]{0:T(128)} %bitcast.me_ref, ...), custom_call_target="tpu_custom_call" | custom-call | flops 19327352832 | bytes 20971520 | tf_op jit(solution)/shard_map/experts/pallas_call | solution.py:360
  227.2 3.9 plus.12.refs_14_
  232.3 3.9 plus.13.refs_15_.refs_0_
  236.3 4.0 plus.14.refs_14_
  241.1 35.5 %experts.6 = (f32[1024,1024]{1,0:T(8,128)}, f32[1024,1024]{1,0:T(8,128)}, f32[1024,128]{1,0:T(8,128)}, bf16[3,512,512]{2,1,0:T(8,128)(2,1)}, bf16[3,512,512]{2,1...) custom-call(s32[1]{0:T(128)} %bitcast.me_ref, ...), custom_call_target="tpu_custom_call" | custom-call | flops 19327352832 | bytes 20971520 | tf_op jit(solution)/shard_map/experts/pallas_call | solution.py:360
  277.7 4.0 plus.15.refs_15_
  285.1 35.5 %experts.7 = (f32[1024,1024]{1,0:T(8,128)}, f32[1024,1024]{1,0:T(8,128)}, f32[1024,128]{1,0:T(8,128)}, bf16[3,512,512]{2,1,0:T(8,128)(2,1)}, bf16[3,512,512]{2,1...) custom-call(s32[1]{0:T(128)} %bitcast.me_ref, ...), custom_call_target="tpu_custom_call" | custom-call | flops 19327352832 | bytes 20971520 | tf_op jit(solution)/shard_map/experts/pallas_call | solution.py:360
  321.2 3.9 plus.16.refs_0_
  325.0 3.9 plus.17.refs_10_
  329.4 3.9 plus.19.refs_12_
  334.8 3.9 plus.18.refs_11_
  339.2 12.5 %turn.1 = (bf16[1024,1024]{1,0:T(8,128)(2,1)}, f32[1024,1024]{1,0:T(8,128)}, bf16[1024,1024]{1,0:T(8,128)(2,1)}, bf16[1024,1024]{1,0:T(8,128)(2,1)}, f32[1,1024]{1,0:T(1,128)}, /*index=5*/f32[1024,128]{1,0:T(8,128)}) custom-call(f32[1024,1024]{1,0:T(8,128)} %get-tuple-element.86.refs_0_, f32[1024,1024]{1,0:T(8,128)} %get-tuple-element.119.refs_1_, ...), custom_call_target="tpu_custom_call" | custom-call | flops 2684354560 | bytes 29360128 | tf_op jit(solution)/shard_map/turn/pallas_call | solution.py:426
  352.8 3.9 plus.20.refs_6_.refs_0_
  356.7 3.9 plus.21.refs_7_.refs_0_
  360.6 30.5 %attend_back.2 = (bf16[1024,512]{1,0:T(8,128)(2,1)}, bf16[1024,256]{1,0:T(8,128)(2,1)}, bf16[1024,256]{1,0:T(8,128)(2,1)}) custom-call(bf16[1024,1024]{1,0:T(8,128)(2,1)} %get-tuple-element.82.q_ref.refs_0_, bf16[1024,512]{1,0:T(8,128)(2,1)} %get-tuple-element.83.k_ref.refs_1_, bf16[1024,512]{1,0:T(8,128)(2,1)} %get-tuple-element.84.v_ref.refs_2_, ...), custom_call_target="tpu_custom_call" | custom-call | flops 42949672960 | bytes 12582912 | tf_op jit(solution)/shard_map/attend_back/pallas_call | solution.py:188
  392.2 4.4 plus.22.refs_6_
  396.6 3.1 collective-permute-done.39.refs_1_
  399.7 4.3 plus.23.refs_7_
  404.0 30.3 %attend_back.3 = (bf16[1024,512]{1,0:T(8,128)(2,1)}, bf16[1024,256]{1,0:T(8,128)(2,1)}, bf16[1024,256]{1,0:T(8,128)(2,1)}) custom-call(bf16[1024,1024]{1,0:T(8,128)(2,1)} %get-tuple-element.82.q_ref.refs_0_, bf16[1024,512]{1,0:T(8,128)(2,1)} %get-tuple-element.83.k_ref.refs_1_, bf16[1024,512]{1,0:T(8,128)(2,1)} %get-tuple-element.84.v_ref.refs_2_, ...), custom_call_target="tpu_custom_call" | custom-call | flops 42949672960 | bytes 12582912 | tf_op jit(solution)/shard_map/attend_back/pallas_call | solution.py:188
  435.9 5.4 convolution_convert_fusion.1
  441.4 11.2 %finish.1 = (f32[1024,1024]{1,0:T(8,128)}, f32[1,1024]{1,0:T(1,128)}) custom-call(bf16[1024,512]{1,0:T(8,128)(2,1)} %get-tuple-element.132.refs_0_, bf16[1024,512]{1,0:T(8,128)(2,1)} %get-tuple-element.134.refs_1_, bf16[1024,256]{1,0:T(8,128)(2,1)} %get-tuple-element.135.refs_2_, bf16[1024,256]{1,0:T(8,128)(2,1)} %get-tuple-element.136.refs_3_, ...), custom_call_target="tpu_custom_call" | custom-call | flops 4294967296 | bytes 20971520 | tf_op jit(solution)/shard_map/finish/pallas_call | solution.py:472
  457.2 6.3 %convolution_convert_fusion = bf16[1024,2048]{1,0:T(8,128)(2,1)} fusion(bf16[1024,1024]{1,0:T(8,128)(2,1)S(1)} %copy-done.28, bf16[1024,2048]{1,0:T(8,128)(2,1)S(1)} %constant_dynamic-update-slice_fusion), kind=kOutput, calls=%fused_computation | convolution fusion | flops 4297064448 | bytes 10485760 | tf_op jit(solution)/shard_map/dot_general | solution.py:33
  463.5 67.8 %reduce_all.1 = (f32[256,1024]{1,0:T(8,128)}, f32[256,2048]{1,0:T(8,128)}, f32[256,128]{1,0:T(8,128)}) custom-call(bf16[4,256,1024]{2,1,0:T(8,128)(2,1)} %bitcast.19, bf16[4,256,2048]{2,1,0:T(8,128)(2,1)} %bitcast.18, bf16[4,256,128]{2,1,0:T(8,128)(2,1)} %bitcast.24), custom_call_target="tpu_custom_call" | custom-call | flops 1000000000 | bytes 26214400 | tf_op jit(solution)/shard_map/reduce_all/pallas_call | solution.py:732
  537.4 25.2 %all-reduce.6.cloned.1.call-done = (bf16[3,512,512]{2,1,0:T(8,128)(2,1)}, bf16[3,512,512]{2,1,0:T(8,128)(2,1)}) async-done(((bf16[3,512,512]{2,1,0:T(8,128)(2,1)}, bf16[3,512,512]{2,1,0:T(8,128)(2,1)}), (bf16[3,512,512]{2,1,0:T(8,128)(2,1)}, bf16[3,512,512]{2,1,0:T(8,128)(2,1)})) %all-reduce.6.cloned.1.call-update) | async-done | bytes 3145744 | tf_op jit(solution)/shard_map/psum | solution.py:879
  562.6 2.8 maximum_convert_fusion
  (180 shorter events, 63.9 us)
Async XLA Ops:
  7.2 137.9 %all-gather.2.cloned.1.call-start = ((), (), s32[]{:S(2)}) async-start(), calls=%async_computation | async-start | bytes 2621440 | tf_op jit(solution)/shard_map/all_gather | solution.py:809
  7.2 69.2 %collective-permute-start = (bf16[1024,512]{1,0:T(8,128)(2,1)}, bf16[1024,512]{1,0:T(8,128)(2,1)S(1)}, u32[]{:S(2)}, u32[]{:S(2)}) collective-permute-start(bf16[1024,512]{1,0:T(8,128)(2,1)} %bitcast.25), channel_id=1, source_target_pairs={{0,8},{4,12},{8,0},{12,4},{16,24},{20,28},{24,16},{28,20},{1,9},{5... | collective-permute-start | bytes 3145736 | tf_op jit(solution)/shard_map/ppermute | solution.py:756
  10.2 69.7 %collective-permute-start.7 = (bf16[1024,512]{1,0:T(8,128)(2,1)}, bf16[1024,512]{1,0:T(8,128)(2,1)S(1)}, u32[]{:S(2)}, u32[]{:S(2)}) collective-permute-start(bf16[1024,512]{1,0:T(8,128)(2,1)} %bitcast.26), channel_id=1, source_target_pairs={{0,16},{4,20},{8,24},{12,28},{16,0},{20,4},{24,8},{28,12},{1,17},{... | collective-permute-start | bytes 3145736 | tf_op jit(solution)/shard_map/ppermute | solution.py:756
  11.7 68.9 %collective-permute-start.1 = (bf16[1024,512]{1,0:T(8,128)(2,1)}, bf16[1024,512]{1,0:T(8,128)(2,1)}, u32[]{:S(2)}, u32[]{:S(2)}) collective-permute-start(bf16[1024,512]{1,0:T(8,128)(2,1)} %bitcast.3.refs_9_), channel_id=1, source_target_pairs={{0,8},{4,12},{8,0},{12,4},{16,24},{20,28},{24,16},{28,20},{1,9},{5... | collective-permute-start | bytes 3145736 | tf_op jit(solution)/shard_map/ppermute | solution.py:756
  12.3 70.6 %collective-permute-start.10 = (bf16[1024,512]{1,0:T(8,128)(2,1)}, bf16[1024,512]{1,0:T(8,128)(2,1)S(1)}, u32[]{:S(2)}, u32[]{:S(2)}) collective-permute-start(bf16[1024,512]{1,0:T(8,128)(2,1)} %bitcast.3.refs_9_), channel_id=1, source_target_pairs={{0,16},{4,20},{8,24},{12,28},{16,0},{20,4},{24,8},{28,12},{1,17},{... | collective-permute-start | bytes 3145736 | tf_op jit(solution)/shard_map/ppermute | solution.py:756
  12.3 73.0 %collective-permute-start.2 = (bf16[512,1024]{1,0:T(8,128)(2,1)}, bf16[512,1024]{1,0:T(8,128)(2,1)}, u32[]{:S(2)}, u32[]{:S(2)}) collective-permute-start(bf16[512,1024]{1,0:T(8,128)(2,1)} %bitcast.4.refs_10_), channel_id=1, source_target_pairs={{0,8},{4,12},{8,0},{12,4},{16,24},{20,28},{24,16},{28,20},{1,9},{5... | collective-permute-start | bytes 3145736 | tf_op jit(solution)/shard_map/ppermute | solution.py:756
  77.4 46.1 %collective-permute-start.13 = (bf16[512,1024]{1,0:T(8,128)(2,1)}, bf16[512,1024]{1,0:T(8,128)(2,1)}, u32[]{:S(2)}, u32[]{:S(2)}) collective-permute-start(bf16[512,1024]{1,0:T(8,128)(2,1)} %bitcast.4.refs_10_), channel_id=1, source_target_pairs={{0,16},{4,20},{8,24},{12,28},{16,0},{20,4},{24,8},{28,12},{1,17},{... | collective-permute-start | bytes 3145736 | tf_op jit(solution)/shard_map/ppermute | solution.py:756
  80.0 44.7 %collective-permute-start.6 = (bf16[512,512]{1,0:T(8,128)(2,1)S(1)}, bf16[512,512]{1,0:T(8,128)(2,1)}, u32[]{:S(2)}, u32[]{:S(2)}) collective-permute-start(bf16[512,512]{1,0:T(8,128)(2,1)S(1)} %slice.77), channel_id=1, source_target_pairs={{0,16},{4,20},{8,24},{12,28},{16,0},{20,4},{24,8},{28,12},{1,17},{... | collective-permute-start | bytes 1572872 | tf_op jit(solution)/shard_map/ppermute | solution.py:756
  80.6 44.6 %collective-permute-start.8 = (bf16[512,512]{1,0:T(8,128)(2,1)S(1)}, bf16[512,512]{1,0:T(8,128)(2,1)}, u32[]{:S(2)}, u32[]{:S(2)}) collective-permute-start(bf16[512,512]{1,0:T(8,128)(2,1)S(1)} %slice.78), channel_id=1, source_target_pairs={{0,8},{4,12},{8,0},{12,4},{16,24},{20,28},{24,16},{28,20},{1,9},{5... | collective-permute-start | bytes 1572872 | tf_op jit(solution)/shard_map/ppermute | solution.py:756
  82.9 42.9 %collective-permute-start.9 = (bf16[512,512]{1,0:T(8,128)(2,1)}, bf16[512,512]{1,0:T(8,128)(2,1)}, u32[]{:S(2)}, u32[]{:S(2)}) collective-permute-start(bf16[512,512]{1,0:T(8,128)(2,1)} %slice.79), channel_id=1, source_target_pairs={{0,16},{4,20},{8,24},{12,28},{16,0},{20,4},{24,8},{28,12},{1,17},{... | collective-permute-start | bytes 1572872 | tf_op jit(solution)/shard_map/ppermute | solution.py:756
  85.4 40.7 %collective-permute-start.11 = (bf16[512,512]{1,0:T(8,128)(2,1)}, bf16[512,512]{1,0:T(8,128)(2,1)}, u32[]{:S(2)}, u32[]{:S(2)}) collective-permute-start(bf16[512,512]{1,0:T(8,128)(2,1)} %slice.80), channel_id=1, source_target_pairs={{0,8},{4,12},{8,0},{12,4},{16,24},{20,28},{24,16},{28,20},{1,9},{5... | collective-permute-start | bytes 1572872 | tf_op jit(solution)/shard_map/ppermute | solution.py:756
  144.6 43.3 %collective-permute-start.16 = (bf16[512,512]{1,0:T(8,128)(2,1)}, bf16[512,512]{1,0:T(8,128)(2,1)S(1)}, u32[]{:S(2)}, u32[]{:S(2)}) collective-permute-start(bf16[512,512]{1,0:T(8,128)(2,1)} %collective-permute-done.8.refs_9_), channel_id=1, source_target_pairs={{0,4},{4,0},{8,12},{12,8},{16,20},{20,16},{24,28},{28,24},{1,5},{5... | collective-permute-start | bytes 1572872 | tf_op jit(solution)/shard_map/ppermute | solution.py:756
  154.3 33.8 %collective-permute-start.17 = (bf16[512,512]{1,0:T(8,128)(2,1)}, bf16[512,512]{1,0:T(8,128)(2,1)S(1)}, u32[]{:S(2)}, u32[]{:S(2)}) collective-permute-start(bf16[512,512]{1,0:T(8,128)(2,1)} %collective-permute-done.9.refs_10_), channel_id=1, source_target_pairs={{0,4},{4,0},{8,12},{12,8},{16,20},{20,16},{24,28},{28,24},{1,5},{5... | collective-permute-start | bytes 1572872 | tf_op jit(solution)/shard_map/ppermute | solution.py:756
  154.4 35.3 %collective-permute-start.18 = (bf16[512,512]{1,0:T(8,128)(2,1)}, bf16[512,512]{1,0:T(8,128)(2,1)}, u32[]{:S(2)}, u32[]{:S(2)}) collective-permute-start(bf16[512,512]{1,0:T(8,128)(2,1)} %collective-permute-done.11.refs_11_), channel_id=1, source_target_pairs={{0,4},{4,0},{8,12},{12,8},{16,20},{20,16},{24,28},{28,24},{1,5},{5... | collective-permute-start | bytes 1572872 | tf_op jit(solution)/shard_map/ppermute | solution.py:756
  154.9 34.8 %collective-permute-start.19 = (bf16[256,1024]{1,0:T(8,128)(2,1)}, bf16[256,1024]{1,0:T(8,128)(2,1)}, u32[]{:S(2)}, u32[]{:S(2)}) collective-permute-start(bf16[256,1024]{1,0:T(8,128)(2,1)} %collective-permute-done.12.refs_12_), channel_id=1, source_target_pairs={{0,4},{4,0},{8,12},{12,8},{16,20},{20,16},{24,28},{28,24},{1,5},{5... | collective-permute-start | bytes 1572872 | tf_op jit(solution)/shard_map/ppermute | solution.py:756
  155.0 34.7 %collective-permute-start.20 = (bf16[256,1024]{1,0:T(8,128)(2,1)}, bf16[256,1024]{1,0:T(8,128)(2,1)}, u32[]{:S(2)}, u32[]{:S(2)}) collective-permute-start(bf16[256,1024]{1,0:T(8,128)(2,1)} %collective-permute-done.14.refs_13_), channel_id=1, source_target_pairs={{0,4},{4,0},{8,12},{12,8},{16,20},{20,16},{24,28},{28,24},{1,5},{5... | collective-permute-start | bytes 1572872 | tf_op jit(solution)/shard_map/ppermute | solution.py:756
  187.9 38.2 %collective-permute-start.24 = (bf16[3,512,512]{2,1,0:T(8,128)(2,1)}, bf16[3,512,512]{2,1,0:T(8,128)(2,1)S(1)}, u32[]{:S(2)}, u32[]{:S(2)}) collective-permute-start(bf16[3,512,512]{2,1,0:T(8,128)(2,1)} %get-tuple-element.109), channel_id=1, source_target_pairs={{0,4},{4,0},{8,12},{12,8},{16,20},{20,16},{24,28},{28,24},{1,5},{5... | collective-permute-start | bytes 4718600 | tf_op jit(solution)/shard_map/ppermute | solution.py:756
  189.6 41.6 %collective-permute-start.25 = (bf16[3,512,512]{2,1,0:T(8,128)(2,1)}, bf16[3,512,512]{2,1,0:T(8,128)(2,1)S(1)}, u32[]{:S(2)}, u32[]{:S(2)}) collective-permute-start(bf16[3,512,512]{2,1,0:T(8,128)(2,1)} %get-tuple-element.111), channel_id=1, source_target_pairs={{0,4},{4,0},{8,12},{12,8},{16,20},{20,16},{24,28},{28,24},{1,5},{5... | collective-permute-start | bytes 4718600 | tf_op jit(solution)/shard_map/ppermute | solution.py:756
  231.1 50.6 %collective-permute-start.26 = (bf16[1024,512]{1,0:T(8,128)(2,1)}, bf16[1024,512]{1,0:T(8,128)(2,1)}, u32[]{:S(2)}, u32[]{:S(2)}) collective-permute-start(bf16[1024,512]{1,0:T(8,128)(2,1)} %bitcast.27), channel_id=1, source_target_pairs={{0,4},{4,0},{8,12},{12,8},{16,20},{20,16},{24,28},{28,24},{1,5},{5... | collective-permute-start | bytes 3145736 | tf_op jit(solution)/shard_map/ppermute | solution.py:756
  236.2 47.4 %collective-permute-start.27 = (bf16[1024,512]{1,0:T(8,128)(2,1)}, bf16[1024,512]{1,0:T(8,128)(2,1)}, u32[]{:S(2)}, u32[]{:S(2)}) collective-permute-start(bf16[1024,512]{1,0:T(8,128)(2,1)} %bitcast.3.refs_9_), channel_id=1, source_target_pairs={{0,4},{4,0},{8,12},{12,8},{16,20},{20,16},{24,28},{28,24},{1,5},{5... | collective-permute-start | bytes 3145736 | tf_op jit(solution)/shard_map/ppermute | solution.py:756
  240.3 44.8 %collective-permute-start.28 = (bf16[512,1024]{1,0:T(8,128)(2,1)}, bf16[512,1024]{1,0:T(8,128)(2,1)}, u32[]{:S(2)}, u32[]{:S(2)}) collective-permute-start(bf16[512,1024]{1,0:T(8,128)(2,1)} %bitcast.4.refs_10_), channel_id=1, source_target_pairs={{0,4},{4,0},{8,12},{12,8},{16,20},{20,16},{24,28},{28,24},{1,5},{5... | collective-permute-start | bytes 3145736 | tf_op jit(solution)/shard_map/ppermute | solution.py:756
  240.7 35.9 %collective-permute-start.30 = (bf16[3,512,512]{2,1,0:T(8,128)(2,1)}, bf16[3,512,512]{2,1,0:T(8,128)(2,1)S(1)}, u32[]{:S(2)}, u32[]{:S(2)}) collective-permute-start(bf16[3,512,512]{2,1,0:T(8,128)(2,1)} %get-tuple-element.118), channel_id=1, source_target_pairs={{0,4},{4,0},{8,12},{12,8},{16,20},{20,16},{24,28},{28,24},{1,5},{5... | collective-permute-start | bytes 4718600 | tf_op jit(solution)/shard_map/ppermute | solution.py:756
  240.8 44.3 %collective-permute-start.31 = (bf16[3,512,512]{2,1,0:T(8,128)(2,1)S(1)}, bf16[3,512,512]{2,1,0:T(8,128)(2,1)}, u32[]{:S(2)}, u32[]{:S(2)}) collective-permute-start(bf16[3,512,512]{2,1,0:T(8,128)(2,1)S(1)} %copy-done.5), channel_id=1, source_target_pairs={{0,8},{4,12},{8,0},{12,4},{16,24},{20,28},{24,16},{28,20},{1,9},{5... | collective-permute-start | bytes 4718600 | tf_op jit(solution)/shard_map/ppermute | solution.py:756
  276.6 44.5 %collective-permute-start.32 = (bf16[3,512,512]{2,1,0:T(8,128)(2,1)}, bf16[3,512,512]{2,1,0:T(8,128)(2,1)}, u32[]{:S(2)}, u32[]{:S(2)}) collective-permute-start(bf16[3,512,512]{2,1,0:T(8,128)(2,1)} %get-tuple-element.123), channel_id=1, source_target_pairs={{0,4},{4,0},{8,12},{12,8},{16,20},{20,16},{24,28},{28,24},{1,5},{5... | collective-permute-start | bytes 4718600 | tf_op jit(solution)/shard_map/ppermute | solution.py:756
  281.7 43.3 %collective-permute-start.33 = (bf16[3,512,512]{2,1,0:T(8,128)(2,1)S(1)}, bf16[3,512,512]{2,1,0:T(8,128)(2,1)}, u32[]{:S(2)}, u32[]{:S(2)}) collective-permute-start(bf16[3,512,512]{2,1,0:T(8,128)(2,1)S(1)} %copy-done.4), channel_id=1, source_target_pairs={{0,8},{4,12},{8,0},{12,4},{16,24},{20,28},{24,16},{28,20},{1,9},{5... | collective-permute-start | bytes 4718600 | tf_op jit(solution)/shard_map/ppermute | solution.py:756
  283.5 51.3 %collective-permute-start.34 = (bf16[3,512,512]{2,1,0:T(8,128)(2,1)}, bf16[3,512,512]{2,1,0:T(8,128)(2,1)}, u32[]{:S(2)}, u32[]{:S(2)}) collective-permute-start(bf16[3,512,512]{2,1,0:T(8,128)(2,1)} %plus.15.refs_15_), channel_id=1, source_target_pairs={{0,16},{4,20},{8,24},{12,28},{16,0},{20,4},{24,8},{28,12},{1,17},{... | collective-permute-start | bytes 4718600 | tf_op jit(solution)/shard_map/ppermute | solution.py:756
  285.0 44.4 %collective-permute-start.35 = (bf16[3,512,512]{2,1,0:T(8,128)(2,1)}, bf16[3,512,512]{2,1,0:T(8,128)(2,1)}, u32[]{:S(2)}, u32[]{:S(2)}) collective-permute-start(bf16[3,512,512]{2,1,0:T(8,128)(2,1)} %get-tuple-element.125), channel_id=1, source_target_pairs={{0,4},{4,0},{8,12},{12,8},{16,20},{20,16},{24,28},{28,24},{1,5},{5... | collective-permute-start | bytes 4718600 | tf_op jit(solution)/shard_map/ppermute | solution.py:756
  321.1 35.6 %collective-permute-start.37 = (bf16[3,512,512]{2,1,0:T(8,128)(2,1)}, bf16[3,512,512]{2,1,0:T(8,128)(2,1)}, u32[]{:S(2)}, u32[]{:S(2)}) collective-permute-start(bf16[3,512,512]{2,1,0:T(8,128)(2,1)} %get-tuple-element.131), channel_id=1, source_target_pairs={{0,4},{4,0},{8,12},{12,8},{16,20},{20,16},{24,28},{28,24},{1,5},{5... | collective-permute-start | bytes 4718600 | tf_op jit(solution)/shard_map/ppermute | solution.py:756
  328.9 62.2 %collective-permute-start.38 = (bf16[3,512,512]{2,1,0:T(8,128)(2,1)}, bf16[3,512,512]{2,1,0:T(8,128)(2,1)S(1)}, u32[]{:S(2)}, u32[]{:S(2)}) collective-permute-start(bf16[3,512,512]{2,1,0:T(8,128)(2,1)} %plus.17.refs_10_), channel_id=1, source_target_pairs={{0,16},{4,20},{8,24},{12,28},{16,0},{20,4},{24,8},{28,12},{1,17},{... | collective-permute-start | bytes 4718600 | tf_op jit(solution)/shard_map/ppermute | solution.py:756
  333.3 66.3 %collective-permute-start.39 = (bf16[3,512,512]{2,1,0:T(8,128)(2,1)}, bf16[3,512,512]{2,1,0:T(8,128)(2,1)}, u32[]{:S(2)}, u32[]{:S(2)}) collective-permute-start(bf16[3,512,512]{2,1,0:T(8,128)(2,1)} %plus.19.refs_12_), channel_id=1, source_target_pairs={{0,16},{4,20},{8,24},{12,28},{16,0},{20,4},{24,8},{28,12},{1,17},{... | collective-permute-start | bytes 4718600 | tf_op jit(solution)/shard_map/ppermute | solution.py:756
  338.7 61.0 %collective-permute-start.40 = (bf16[3,512,512]{2,1,0:T(8,128)(2,1)}, bf16[3,512,512]{2,1,0:T(8,128)(2,1)}, u32[]{:S(2)}, u32[]{:S(2)}) collective-permute-start(bf16[3,512,512]{2,1,0:T(8,128)(2,1)} %plus.18.refs_11_), channel_id=1, source_target_pairs={{0,8},{4,12},{8,0},{12,4},{16,24},{20,28},{24,16},{28,20},{1,9},{5... | collective-permute-start | bytes 4718600 | tf_op jit(solution)/shard_map/ppermute | solution.py:756
  434.3 128.2 %all-reduce.6.cloned.1.call-start = ((), (), s32[]{:S(2)}) async-start(), calls=%async_computation.1 | async-start | bytes 6291456 | tf_op jit(solution)/shard_map/psum | solution.py:879
  (40 other events, 389.7 us)
Sparse Core Ops, SparseCore 0:
  65.5 43.2 all-gather.1
  437.6 124.9 all-reduce.5

commit v3 on v2

--- a/solution.py
+++ b/solution.py
@@ -19,6 +19,8 @@
 ANY = pl.BlockSpec(memory_space=pl.ANY)
 VMEM = pl.BlockSpec(memory_space=pltpu.VMEM)
 VMEM_BYTES = 60 * 1024 * 1024
+LESS_BYTES = 30 * 1024 * 1024
+EXPERT_BYTES = 26 * 1024 * 1024
 
 
 def dot(a, b):
@@ -33,8 +35,8 @@
     return lax.dot_general(a, b, (((0,), (0,)), ((), ())), preferred_element_type=F32)
 
 
-def params(**kw):
-    return pltpu.CompilerParams(vmem_limit_bytes=VMEM_BYTES, **kw)
+def params(size=VMEM_BYTES):
+    return pltpu.CompilerParams(vmem_limit_bytes=size)
 
 
 def cost(flops, nbytes, transcendentals=0):
@@ -74,11 +76,11 @@
     return lambda *refs: kernel(*refs[:inputs], *refs[inputs + len(ties) :])
 
 
-def project_kernel(x_ref, gain_ref, w_ref, cos_ref, sin_ref, n_ref, q_ref, k_ref, v_ref):
+def project_kernel(lane, x_ref, gain_ref, w_ref, cos_ref, sin_ref, n_ref, q_ref, k_ref, v_ref):
     x = x_ref[...].astype(F32)
     inverse = lax.rsqrt(jnp.mean(x * x, axis=-1, keepdims=True) + 1e-06)
-    normed = (x * inverse * gain_ref[...].astype(F32)).astype(BF16)
-    n_ref[...] = normed
+    normed = (x * inverse * gain_ref[lane : lane + 1].astype(F32)).astype(BF16)
+    n_ref[...] = normed.T
     cos, sin = cos_ref[...], sin_ref[...]
     step = 512
     for at in range(0, w_ref.shape[1], step):
@@ -96,16 +98,16 @@
                 v_ref[:, c : c + LANES] = u.astype(BF16)
 
 
-def project(tokens, gain, weights, cos, sin):
+def project(tokens, gain, lane, weights, cos, sin):
     rows, width = tokens.shape
     qw, kw = QUERY_HEADS * HEAD_WIDTH, KEY_VALUE_HEADS * HEAD_WIDTH
     return pl.pallas_call(
-        project_kernel,
+        functools.partial(project_kernel, lane),
         grid=(rows // TILE,),
-        in_specs=[row_block(width), whole_block((1, width)), whole_block(weights.shape), row_block(LANES), row_block(LANES)],
-        out_specs=[row_block(width), row_block(qw), row_block(kw), row_block(kw)],
-        out_shape=[jax.ShapeDtypeStruct((rows, w), BF16) for w in (width, qw, kw, kw)],
-        compiler_params=params(),
+        in_specs=[row_block(width), whole_block(gain.shape), whole_block(weights.shape), row_block(LANES), row_block(LANES)],
+        out_specs=[pl.BlockSpec((width, TILE), lambda i: (0, i)), row_block(qw), row_block(kw), row_block(kw)],
+        out_shape=[jax.ShapeDtypeStruct(s, BF16) for s in ((width, rows), (rows, qw), (rows, kw), (rows, kw))],
+        compiler_params=params(LESS_BYTES),
         cost_estimate=cost(2 * rows * width * (qw + 2 * kw), 12 * rows * width),
         name="project",
     )(tokens, gain, weights, cos, sin)
@@ -131,20 +133,20 @@
     return pl.BlockSpec((sequence, width), lambda s, i: (s, i))
 
 
-def attend(queries, keys, vals):
+def attend(queries, keys, vals, ties=()):
     rows = queries.shape[0]
     steps = KEY_VALUE_HEADS // 2
     flops = 2 * QUERY_HEADS * rows * SEQUENCE_LENGTH * HEAD_WIDTH * 2
     return pl.pallas_call(
-        attend_kernel,
+        tied(attend_kernel, 3, ties),
         grid=(rows // SEQUENCE_LENGTH, steps),
-        in_specs=[head_block(4 * HEAD_WIDTH), head_block(2 * HEAD_WIDTH), head_block(2 * HEAD_WIDTH)],
+        in_specs=[head_block(4 * HEAD_WIDTH), head_block(2 * HEAD_WIDTH), head_block(2 * HEAD_WIDTH)] + [ANY] * len(ties),
         out_specs=head_block(4 * HEAD_WIDTH),
         out_shape=jax.ShapeDtypeStruct(queries.shape, BF16),
         compiler_params=params(),
         cost_estimate=cost(flops * 8, 6 * rows * 1024, QUERY_HEADS * rows * 640),
         name="attend",
-    )(queries, keys, vals)
+    )(queries, keys, vals, *ties)
 
 
 def attend_back_kernel(q_ref, k_ref, v_ref, g_ref, cos_ref, sin_ref, dq_ref, dk_ref, dv_ref, dk_acc, dv_acc, dq_acc):
@@ -202,11 +204,11 @@
     )(queries, keys, vals, grad, cos, sin, *ties)
 
 
-def middle_kernel(a_ref, w_ref, x_ref, gain_ref, router_ref, routes_ref, r_ref, m_ref, mt_ref, gates_ref):
+def middle_kernel(lane_of, a_ref, w_ref, x_ref, gain_ref, router_ref, routes_ref, r_ref, m_ref, mt_ref, gates_ref):
     resid = x_ref[...].astype(F32) + dot(a_ref[...], w_ref[...])
     r_ref[...] = resid
     inverse = lax.rsqrt(jnp.mean(resid * resid, axis=-1, keepdims=True) + 1e-06)
-    moe_in = (resid * inverse * gain_ref[...].astype(F32)).astype(BF16)
+    moe_in = (resid * inverse * gain_ref[lane_of : lane_of + 1].astype(F32)).astype(BF16)
     m_ref[...] = moe_in
     mt_ref[...] = moe_in.T
     logits = dot(moe_in, router_ref[...])
@@ -220,19 +222,20 @@
     gates_ref[...] = weights / jnp.sum(weights, axis=-1, keepdims=True)
 
 
-def middle(attended, out_w, tokens, gain, router_w, routes):
+def middle(attended, out_w, tokens, gain, lane, router_w, routes, ties=()):
     rows, width = tokens.shape
     return pl.pallas_call(
-        middle_kernel,
+        tied(functools.partial(middle_kernel, lane), 6, ties),
         grid=(rows // TILE,),
         in_specs=[
             row_block(width),
             whole_block(out_w.shape),
             row_block(width),
-            whole_block((1, width)),
+            whole_block(gain.shape),
             whole_block(router_w.shape),
             row_block(routes.shape[1]),
-        ],
+        ]
+        + [ANY] * len(ties),
         out_specs=[row_block(width), row_block(width), pl.BlockSpec((width, TILE), lambda i: (0, i)), row_block(LANES)],
         out_shape=[
             jax.ShapeDtypeStruct((rows, width), F32),
@@ -240,25 +243,25 @@
             jax.ShapeDtypeStruct((width, rows), BF16),
             jax.ShapeDtypeStruct((rows, LANES), F32),
         ],
-        compiler_params=params(),
+        compiler_params=params(LESS_BYTES),
         cost_estimate=cost(2 * rows * width * (width + LANES), 14 * rows * width),
         name="middle",
-    )(attended, out_w, tokens, gain, router_w, routes)
+    )(attended, out_w, tokens, gain, router_w, routes, *ties)
 
 
 def moe_kernel(slots, chunks, first, ties, me_ref, *refs):
     refs = list(refs)
     take = lambda count: [refs.pop(0) for _ in range(count)]
-    x_hbm, xt_hbm, dy_hbm, dyt_hbm, gates_ref = take(5)
+    x, xt, dy, dyt, gates_ref = take(5)
     if not first:
-        made_in, dmoe_in, gg_in = take(3)
+        take(3)
     weights = [[take(count) for count in per_slot] for per_slot in chunks]
     take(ties)
-    made_out, dmoe_out, gg_ref = take(3)
+    made, dmoe, gg_ref = take(3)
     grads = [take(2) for _ in slots]
-    x, xt, dy, dyt, made, dmoe, wg, wu, wd, hg, dg, du, stage, sem_in, sem_w, sem_out, sem_acc = take(17)
-    rows = x.shape[0]
-    tiles = rows // TILE
+    wg, wu, wd, hg, dg, du, stage, sem_w, sem_out = take(9)
+    rows, width = x.shape
+    step = 512
 
     def load(source, target, sem):
         copy = pltpu.make_async_copy(source, target, sem)
@@ -278,37 +281,31 @@
         return out
 
     pending = {0: load_weights(0)}
-    inputs = [load(a, b, sem_in.at[i]) for i, (a, b) in enumerate(((x_hbm, x), (dy_hbm, dy)))]
-    if not first:
-        acc = [load(made_in, made, sem_acc.at[0]), load(dmoe_in, dmoe, sem_acc.at[1])]
-        gg_ref[...] = gg_in[...]
-    else:
-        acc = []
-        made[...] = jnp.zeros_like(made)
-        dmoe[...] = jnp.zeros_like(dmoe)
+    if first:
         gg_ref[...] = jnp.zeros_like(gg_ref)
-    late = [load(a, b, sem_in.at[i]) for i, (a, b) in enumerate(((xt_hbm, xt), (dyt_hbm, dyt)), 2)]
-    for copy in inputs:
-        copy.wait()
     stores = []
-    lane = lax.broadcasted_iota(jnp.int32, (TILE, LANES), 1)
+    lane = lax.broadcasted_iota(jnp.int32, (step, LANES), 1)
     for index, slot in enumerate(slots):
         buffer = index % 2
-        for copies in pending.pop(index):
-            for copy in copies:
-                copy.wait()
+        arriving = pending.pop(index)
         if index + 1 < len(slots):
             pending[index + 1] = load_weights(index + 1)
-        for copy in acc:
-            copy.wait()
-        acc = []
         me = me_ref[0] ^ slot
         g_w, u_w, d_w = wg.at[buffer], wu.at[buffer], wd.at[buffer]
 
-        def rows_step(i, carry):
-            at = pl.ds(pl.multiple_of(i * TILE, TILE), TILE)
-            xi, yi = x[at], dy[at]
-            gate, upval, pre = dot(xi, g_w[...]), dot(xi, u_w[...]), dot_nt(yi, d_w[...])
+        def arrived(which, lo):
+            if lo == 0:
+                for copy in arriving[which]:
+                    copy.wait()
+
+        for lo in range(0, rows, step):
+            at = slice(lo, lo + step)
+            arrived(0, lo)
+            gate = dot(x[at], g_w[...])
+            arrived(1, lo)
+            upval = dot(x[at], u_w[...])
+            arrived(2, lo)
+            pre = dot_nt(dy[at], d_w[...])
             column = jnp.sum(jnp.where(lane == me, gates_ref[at], 0.0), axis=1, keepdims=True)
             sigma = 1.0 / (1.0 + jnp.exp(-gate))
             silu = gate * sigma
@@ -320,32 +317,24 @@
             dgate = (dhidden * upval * (sigma + silu * (1.0 - sigma))).astype(BF16)
             dup = (dhidden * silu).astype(BF16)
             hg[at], dg[at], du[at] = weighted, dgate, dup
-            made[at] += dot(weighted, d_w[...])
-            dmoe[at] += dot_nt(dgate, g_w[...]) + dot_nt(dup, u_w[...])
-            return carry
-
-        lax.fori_loop(0, tiles, rows_step, 0)
-        for copy in late:
-            copy.wait()
-        late = []
+            fresh = dot(weighted, d_w[...])
+            back = dot_nt(dgate, g_w[...]) + dot_nt(dup, u_w[...])
+            if first and index == 0:
+                made[at], dmoe[at] = fresh, back
+            else:
+                made[at] += fresh
+                dmoe[at] += back
         for copy in stores:
             copy.wait()
         stores = []
-
-        def grads_step(i, carry):
-            at = pl.ds(pl.multiple_of(i * TILE, TILE), TILE)
-            a = xt[at]
-            stage[0, at] = dot(a, dg[...]).astype(BF16)
-            stage[1, at] = dot(a, du[...]).astype(BF16)
+        half = width // 2
+        for part in range(2):
+            at = slice(part * half, (part + 1) * half)
+            stage[0, at] = dot(xt[at], dg[...]).astype(BF16)
+            stage[1, at] = dot(xt[at], du[...]).astype(BF16)
             stage[2, at] = dot(dyt[at], hg[...]).astype(BF16)
-            return carry
-
-        lax.fori_loop(0, x.shape[1] // TILE, grads_step, 0)
-        half = stage.shape[1] // 2
-        for part in range(2):
-            stores.append(load(stage.at[:, part * half : (part + 1) * half], grads[index][part], sem_out.at[part]))
-    done = [load(made, made_out, sem_acc.at[0]), load(dmoe, dmoe_out, sem_acc.at[1])]
-    for copy in stores + done:
+            stores.append(load(stage.at[:, at], grads[index][part], sem_out.at[part]))
+    for copy in stores:
         copy.wait()
 
 
@@ -355,27 +344,15 @@
     first = acc is None
     flat = [piece for per_slot in weights for pieces in per_slot for piece in pieces]
     chunks = tuple(tuple(len(pieces) for pieces in per_slot) for per_slot in weights)
-    accs = [] if first else list(acc)
+    held = [pltpu.with_memory_space_constraint(a, pltpu.VMEM) for a in (moe_in, moe_in_t, dy, dy_t, gates, *(acc or ()))]
     grad = jax.ShapeDtypeStruct((3, width // 2, hidden), BF16)
     outs = pl.pallas_call(
         functools.partial(moe_kernel, tuple(slots), chunks, first, len(ties)),
-        in_specs=[pl.BlockSpec(memory_space=pltpu.SMEM), ANY, ANY, ANY, ANY, VMEM]
-        + ([] if first else [ANY, ANY, VMEM])
-        + [ANY] * (len(flat) + len(ties)),
-        out_specs=[ANY, ANY, VMEM] + [ANY] * (2 * len(slots)),
-        out_shape=[
-            jax.ShapeDtypeStruct((rows, width), F32),
-            jax.ShapeDtypeStruct((rows, width), F32),
-            jax.ShapeDtypeStruct((rows, LANES), F32),
-        ]
+        in_specs=[pl.BlockSpec(memory_space=pltpu.SMEM)] + [VMEM] * len(held) + [ANY] * (len(flat) + len(ties)),
+        out_specs=[VMEM, VMEM, VMEM] + [ANY] * (2 * len(slots)),
+        out_shape=[pltpu.VMEM((rows, width), F32), pltpu.VMEM((rows, width), F32), pltpu.VMEM((rows, LANES), F32)]
         + [grad] * (2 * len(slots)),
         scratch_shapes=[
-            pltpu.VMEM((rows, width), BF16),
-            pltpu.VMEM((width, rows), BF16),
-            pltpu.VMEM((rows, width), BF16),
-            pltpu.VMEM((width, rows), BF16),
-            pltpu.VMEM((rows, width), F32),
-            pltpu.VMEM((rows, width), F32),
             pltpu.VMEM((2, width, hidden), BF16),
             pltpu.VMEM((2, width, hidden), BF16),
             pltpu.VMEM((2, hidden, width), BF16),
@@ -383,20 +360,19 @@
             pltpu.VMEM((rows, hidden), BF16),
             pltpu.VMEM((rows, hidden), BF16),
             pltpu.VMEM((3, width, hidden), BF16),
-            pltpu.SemaphoreType.DMA((4,)),
             pltpu.SemaphoreType.DMA((2, 3, 2)),
             pltpu.SemaphoreType.DMA((2,)),
-            pltpu.SemaphoreType.DMA((2,)),
         ],
-        compiler_params=params(),
+        input_output_aliases={} if first else {6: 0, 7: 1, 8: 2},
+        compiler_params=pltpu.CompilerParams(vmem_limit_bytes=EXPERT_BYTES),
         cost_estimate=cost(18 * rows * width * hidden * len(slots), 20 * rows * width),
         name="experts",
-    )(me, moe_in, moe_in_t, dy, dy_t, gates, *accs, *flat, *ties)
+    )(me, *held, *flat, *ties)
     return outs[:3], [tuple(outs[3 + 2 * i : 5 + 2 * i]) for i in range(len(slots))]
 
 
 def turn_kernel(
-    resid_ref, made_ref, dmoe_ref, gates_ref, gg_ref, dy_ref, gain_ref, router_ref, mt_ref, w_ref,
+    lane, resid_ref, made_ref, dmoe_ref, gates_ref, gg_ref, dy_ref, gain_ref, router_ref, mt_ref, w_ref,
     mixed_ref, dresid_ref, dz_ref, da_ref, gain_grad_ref, router_grad_ref,
 ):
     @pl.when(pl.program_id(0) == 0)
@@ -412,7 +388,7 @@
     dmoe = dmoe_ref[...] + dot_nt(dlogits, router_ref[...])
     inverse = lax.rsqrt(jnp.mean(resid * resid, axis=-1, keepdims=True) + 1e-06)
     gain_grad_ref[...] += jnp.sum(dmoe * resid * inverse, axis=0, keepdims=True)
-    scaled = dmoe * gain_ref[...].astype(F32)
+    scaled = dmoe * gain_ref[lane : lane + 1].astype(F32)
     inner = jnp.mean(scaled * resid, axis=-1, keepdims=True)
     dresid = dy_ref[...].astype(F32) + inverse * scaled - resid * (inverse * inverse * inverse * inner)
     dresid_ref[...] = dresid
@@ -421,14 +397,14 @@
     da_ref[...] = dot_nt(dz, w_ref[...]).astype(BF16)
 
 
-def turn(resid, made, dmoe, gates, gg, dy, gain, router_w, moe_in_t, out_w, ties=()):
+def turn(resid, made, dmoe, gates, gg, dy, gain, lane, router_w, moe_in_t, out_w, ties=()):
     rows, width = resid.shape
     return pl.pallas_call(
-        tied(turn_kernel, 10, ties),
+        tied(functools.partial(turn_kernel, lane), 10, ties),
         grid=(rows // TILE,),
         in_specs=[
             row_block(width), row_block(width), row_block(width), row_block(LANES), row_block(LANES), row_block(width),
-            whole_block((1, width)), whole_block(router_w.shape), pl.BlockSpec((width, TILE), lambda i: (0, i)),
+            whole_block(gain.shape), whole_block(router_w.shape), pl.BlockSpec((width, TILE), lambda i: (0, i)),
             whole_block(out_w.shape),
         ]
         + [ANY] * len(ties),
@@ -441,19 +417,19 @@
             jax.ShapeDtypeStruct((1, width), F32),
             jax.ShapeDtypeStruct((width, LANES), F32),
         ],
-        compiler_params=params(),
+        compiler_params=params(LESS_BYTES),
         cost_estimate=cost(2 * rows * width * (width + 2 * LANES), 28 * rows * width),
         name="turn",
     )(resid, made, dmoe, gates, gg, dy, gain, router_w, moe_in_t, out_w, *ties)
 
 
-def finish_kernel(count, *refs):
+def finish_kernel(lane, count, *refs):
     grads = refs[:count]
-    w_ref, x_ref, dresid_ref, gain_ref, out_ref, gain_grad_ref = refs[count:]
+    w_ref, x_ref, dresid_ref, gain_ref, router_ref, second_ref, out_ref, small_ref, first = refs[count:]
 
     @pl.when(pl.program_id(0) == 0)
     def _():
-        gain_grad_ref[...] = jnp.zeros_like(gain_grad_ref)
+        first[...] = jnp.zeros_like(first)
 
     at, dn = 0, 0.0
     for ref in grads:
@@ -461,51 +437,123 @@
         at += ref.shape[1]
     x = x_ref[...].astype(F32)
     inverse = lax.rsqrt(jnp.mean(x * x, axis=-1, keepdims=True) + 1e-06)
-    gain_grad_ref[...] += jnp.sum(dn * x * inverse, axis=0, keepdims=True)
-    scaled = dn * gain_ref[...].astype(F32)
+    first[...] += jnp.sum(dn * x * inverse, axis=0, keepdims=True)
+    scaled = dn * gain_ref[lane : lane + 1].astype(F32)
     inner = jnp.mean(scaled * x, axis=-1, keepdims=True)
     out_ref[...] = dresid_ref[...] + inverse * scaled - x * (inverse * inverse * inverse * inner)
 
-
-def finish(grads, weights, tokens, dresid, gain, ties=()):
+    @pl.when(pl.program_id(0) == pl.num_programs(0) - 1)
+    def _():
+        row = lax.broadcasted_iota(jnp.int32, (LANES, first.shape[1]), 0)
+        gains = jnp.where(row == lane, first[...], 0.0) + jnp.where(row == lane + 1, second_ref[...], 0.0)
+        small_ref[...] = (router_ref[...] + gains.T).astype(BF16)
+
+
+def finish(grads, weights, tokens, dresid, gain, lane, router_grad, second, ties=()):
     rows, width = tokens.shape
     return pl.pallas_call(
-        tied(functools.partial(finish_kernel, len(grads)), len(grads) + 4, ties),
+        tied(functools.partial(finish_kernel, lane, len(grads)), len(grads) + 6, ties),
         grid=(rows // TILE,),
         in_specs=[row_block(g.shape[1]) for g in grads]
-        + [whole_block(weights.shape), row_block(width), row_block(width), whole_block((1, width))]
+        + [whole_block(weights.shape), row_block(width), row_block(width), whole_block(gain.shape)]
+        + [whole_block(router_grad.shape), whole_block(second.shape)]
         + [ANY] * len(ties),
-        out_specs=[row_block(width), whole_block((1, width))],
-        out_shape=[jax.ShapeDtypeStruct((rows, width), F32), jax.ShapeDtypeStruct((1, width), F32)],
+        out_specs=[row_block(width), whole_block((width, LANES))],
+        out_shape=[jax.ShapeDtypeStruct((rows, width), F32), jax.ShapeDtypeStruct((width, LANES), BF16)],
+        scratch_shapes=[pltpu.VMEM((1, width), F32)],
         compiler_params=params(),
-        cost_estimate=cost(2 * rows * width * weights.shape[1], 20 * rows * width),
+        cost_estimate=cost(1, 1),
         name="finish",
-    )(*grads, weights, tokens, dresid, gain, *ties)
-
-
-def plus_kernel(*refs):
-    total = refs[0][...].astype(F32)
-    for ref in refs[1:-1]:
-        total += ref[...].astype(F32)
-    refs[-1][...] = total.astype(BF16)
-
-
-def plus(*terms, ties=()):
-    shape = terms[0].shape
-    block = pl.BlockSpec((1,) + shape[1:], lambda i: (i, 0, 0))
-    return pl.pallas_call(
-        tied(plus_kernel, len(terms), ties),
-        grid=(shape[0],),
-        in_specs=[block] * len(terms) + [ANY] * len(ties),
-        out_specs=block,
-        out_shape=jax.ShapeDtypeStruct(shape, BF16),
+    )(*grads, weights, tokens, dresid, gain, router_grad, second, *ties)
+
+
+def weights_back_kernel(count, *refs):
+    for grad, out in zip(refs[1 : count + 1], refs[count + 1 :]):
+        out[...] = dot(refs[0][...], grad[...]).astype(BF16)
+
+
+def weights_back(turned, grads, ties=()):
+    rows = turned.shape[0]
+    return pl.pallas_call(
+        tied(functools.partial(weights_back_kernel, len(grads)), len(grads) + 1, ties),
+        grid=(rows // TILE,),
+        in_specs=[row_block(turned.shape[1])] + [whole_block(g.shape) for g in grads] + [ANY] * len(ties),
+        out_specs=[row_block(g.shape[1]) for g in grads],
+        out_shape=[jax.ShapeDtypeStruct((rows, g.shape[1]), BF16) for g in grads],
         compiler_params=params(),
-        cost_estimate=cost(len(terms) * terms[0].size, 2 * (len(terms) + 1) * terms[0].size),
+        cost_estimate=cost(1, 1),
+        name="weights_back",
+    )(turned, *grads, *ties)
+
+
+def widen_kernel(top_ref, bottom_ref, gate_ref, up_ref, down_ref):
+    step = pl.program_id(0)
+    for half, ref in enumerate((top_ref, bottom_ref)):
+
+        @pl.when(step // 2 == half)
+        def _():
+            gate_ref[...] = ref[0].astype(F32)
+            up_ref[...] = ref[1].astype(F32)
+            down_ref[...] = ref[2].astype(F32).T
+
+
+def widen(top, bottom):
+    _, rows, columns = top.shape
+    step = rows // 2
+    block = pl.BlockSpec((step, columns), lambda i: (i, 0))
+    return pl.pallas_call(
+        widen_kernel,
+        grid=(4,),
+        in_specs=[
+            pl.BlockSpec((3, step, columns), lambda i: (0, jnp.minimum(i, 1), 0)),
+            pl.BlockSpec((3, step, columns), lambda i: (0, jnp.maximum(i - 2, 0), 0)),
+        ],
+        out_specs=[block, block, pl.BlockSpec((columns, step), lambda i: (0, i))],
+        out_shape=[
+            jax.ShapeDtypeStruct((2 * rows, columns), F32),
+            jax.ShapeDtypeStruct((2 * rows, columns), F32),
+            jax.ShapeDtypeStruct((columns, 2 * rows), F32),
+        ],
+        compiler_params=params(),
+        cost_estimate=cost(1, 1),
+        name="widen",
+    )(top, bottom)
+
+
+def plus_kernel(counts, *refs):
+    refs = list(refs)
+    refs.pop()[...] = jnp.zeros((8, LANES), F32)
+    ins = [[refs.pop(0) for _ in range(count)] for count in counts]
+    for terms, out in zip(ins, refs):
+        total = terms[0][...].astype(F32)
+        for ref in terms[1:]:
+            total += ref[...].astype(F32)
+        out[...] = total.astype(BF16)
+
+
+def plus(*groups, ties=()):
+    shape = groups[0][0].shape
+    block = pl.BlockSpec((1, shape[1] // 2, shape[2]), lambda i, j: (i, j, 0))
+    counts = tuple(len(terms) for terms in groups)
+    flat = [a for terms in groups for a in terms]
+    return pl.pallas_call(
+        tied(functools.partial(plus_kernel, counts), len(flat), ties),
+        grid=(shape[0], 2),
+        in_specs=[block] * len(flat) + [ANY] * len(ties),
+        out_specs=[block] * len(groups) + [pl.BlockSpec((8, LANES), lambda i, j: (0, 0))],
+        out_shape=[jax.ShapeDtypeStruct(shape, BF16)] * len(groups) + [jax.ShapeDtypeStruct((8, LANES), F32)],
+        compiler_params=pltpu.CompilerParams(vmem_limit_bytes=16 * 1024 * 1024),
+        cost_estimate=cost(len(flat) * flat[0].size, 2 * (len(flat) + len(groups)) * flat[0].size),
         name="plus",
-    )(*terms, *ties)
-
-
-def gather_kernel(size, q_ref, k_ref, v_ref, s_ref, o_ref, packed_ref, small_ref, out_ref, send_sem, recv_sem, pass_sem, take_sem):
+    )(*flat, *ties)
+
+
+def gather_kernel(size, count, *refs):
+    q_ref, k_ref, v_ref, s_ref, o_ref = refs[:5]
+    owned, refs = refs[5 : 5 + count], refs[5 + count :]
+    packed_ref, small_ref, out_ref, turned_ref = refs[:4]
+    beside, refs = refs[4 : 4 + 2 * count], refs[4 + 2 * count :]
+    send_sem, recv_sem, pass_sem, take_sem, away_sem, come_sem = refs
     me, z = lax.axis_index("expert"), lax.axis_index("wshard")
     core = lax.rem(me, 2)
     sibling = me + 1 - 2 * core
@@ -521,7 +569,24 @@
         def _():
             pl.semaphore_signal(barrier, inc=1, device_id=(me, z + step), device_id_type=pl.DeviceIdType.MESH)
 
-    pl.semaphore_wait(barrier, 1 + jnp.where(z > 0, 1, 0) + jnp.where(z < size - 1, 1, 0))
+    neighbours = []
+    if count:
+        xb, yb = lax.rem(me // 2, 2), me // 4
+        neighbours = [me + 2 - 4 * xb, me + 4 - 8 * yb]
+    for peer in neighbours:
+        pl.semaphore_signal(barrier, inc=1, device_id=(peer, z), device_id_type=pl.DeviceIdType.MESH)
+    pl.semaphore_wait(barrier, 1 + len(neighbours) + jnp.where(z > 0, 1, 0) + jnp.where(z < size - 1, 1, 0))
+    shipped = []
+    for i, ref in enumerate(owned):
+        for j, peer in enumerate(neighbours):
+            shipped.append(
+                pltpu.make_async_remote_copy(
+                    src_ref=ref, dst_ref=beside[j * count + i], send_sem=away_sem.at[i, j], recv_sem=come_sem.at[i, j],
+                    device_id=(peer, z), device_id_type=pl.DeviceIdType.MESH,
+                )
+            )
+    for copy in shipped:
+        copy.start()
 
     own = pl.ds(pl.multiple_of(z * rows, rows), rows)
     at = 0
@@ -586,33 +651,38 @@
                     move.wait_send()
 
     out_ref[...] = o_ref[...]
-
-
-def gather_weights(query, key, value, small, out):
+    turned_ref[...] = small_ref[...].T
+    for copy in shipped:
+        copy.wait()
+
+
+def gather_weights(query, key, value, small, out, owned=()):
     size = lax.axis_size("wshard")
     rows = query.shape[0]
     width = query.shape[1] + key.shape[1] + value.shape[1]
     sems = pltpu.SemaphoreType.DMA((2, size + 1, 2))
     return pl.pallas_call(
-        functools.partial(gather_kernel, size),
-        in_specs=[VMEM] * 5,
-        out_specs=[VMEM] * 3,
+        functools.partial(gather_kernel, size, len(owned)),
+        in_specs=[VMEM] * 5 + [ANY] * len(owned),
+        out_specs=[VMEM] * 4 + [ANY] * (2 * len(owned)),
         out_shape=[
             jax.ShapeDtypeStruct((size * rows, width), BF16),
             jax.ShapeDtypeStruct((size * rows, small.shape[1]), BF16),
             jax.ShapeDtypeStruct(out.shape, BF16),
-        ],
-        scratch_shapes=[sems, sems, sems, sems],
+            jax.ShapeDtypeStruct((small.shape[1], size * rows), BF16),
+        ]
+        + [jax.ShapeDtypeStruct(a.shape, BF16) for a in owned] * 2,
+        scratch_shapes=[sems, sems, sems, sems] + [pltpu.SemaphoreType.DMA((max(len(owned), 1), 2))] * 2,
         compiler_params=pltpu.CompilerParams(collective_id=0, has_side_effects=True, vmem_limit_bytes=VMEM_BYTES),
         cost_estimate=cost(1e9, 12 * rows * size * width),
         name="gather_weights",
-    )(query, key, value, small, out)
+    )(query, key, value, small, out, *owned)
 
 
 def reduce_kernel(size, columns, *refs):
-    count = len(columns)
-    ins, outs = refs[:count], refs[count : 2 * count]
-    acc, rc, r1, r2, zs, rz, res, send_sem, recv_sem = refs[2 * count :]
+    count = sum(len(widths) for widths in columns)
+    ins, outs = list(refs[:count]), refs[count : count + len(columns)]
+    acc, rc, r1, r2, zs, rz, res, send_sem, recv_sem = refs[count + len(columns) :]
     me, z = lax.axis_index("expert"), lax.axis_index("wshard")
     core, xb, yb = lax.rem(me, 2), lax.rem(me // 2, 2), me // 4
     sibling, xp, yp = me + 1 - 2 * core, me + 2 - 4 * xb, me + 4 - 8 * yb
@@ -627,11 +697,14 @@
     pl.semaphore_wait(barrier, 2 + size)
 
     pieces, at = [], 0
-    for ref, out, width in zip(ins, outs, columns):
-        step = width if width <= 512 else 512
-        for lo in range(0, width, step):
-            pieces.append((ref, out, lo, step, at))
-            at += step
+    for out, widths in zip(outs, columns):
+        start = 0
+        for width in widths:
+            ref, step = ins.pop(0), min(width, 512)
+            for lo in range(0, width, step):
+                pieces.append((ref, out, lo, step, at, start + lo))
+                at += step
+            start += width
 
     sent = []
 
@@ -656,10 +729,10 @@
     k0, k1 = xb * n1 + yb * n2, half // 2 + yb * n1 + xb * n2
     base = core * half
     first = []
-    for p, (ref, _, lo, w, at) in enumerate(pieces):
+    for p, (ref, _, lo, w, at, _) in enumerate(pieces):
         first.append(move(ref.at[:, rows((1 - core) * half, half), lo : lo + w], rc.at[:, :, at : at + w], p, 0, (sibling, z)))
     second = []
-    for p, (ref, _, lo, w, at) in enumerate(pieces):
+    for p, (ref, _, lo, w, at, _) in enumerate(pieces):
         c = slice(at, at + w)
         first[p].wait_recv()
         acc[:, :, c] = sum_of(ref[:, rows(base, half), lo : lo + w], rc[:, :, c]).astype(BF16)
@@ -668,7 +741,7 @@
             move(acc.at[:, rows(half // 2 + (1 - yb) * n1, n1), c], r1.at[1, :, :, c], p, 2, (yp, z)),
         ))
     third = []
-    for p, (_, _, _, w, at) in enumerate(pieces):
+    for p, (_, _, _, w, at, _) in enumerate(pieces):
         c = slice(at, at + w)
         keep = (rows(xb * n1, n1), rows(half // 2 + yb * n1, n1))
         for i in range(2):
@@ -679,7 +752,7 @@
             move(acc.at[:, rows(half // 2 + yb * n1 + (1 - xb) * n2, n2), c], r2.at[1, :, :, c], p, 4, (xp, z)),
         ))
     fourth = []
-    for p, (_, _, _, w, at) in enumerate(pieces):
+    for p, (_, _, _, w, at, _) in enumerate(pieces):
         c = slice(at, at + w)
         for i, k in enumerate((k0, k1)):
             third[p][i].wait_recv()
@@ -689,7 +762,7 @@
             for d in range(1, size)
         ])
     fifth = []
-    for p, (_, _, _, w, at) in enumerate(pieces):
+    for p, (_, _, _, w, at, _) in enumerate(pieces):
         c = slice(at, at + w)
         for copy in fourth[p]:
             copy.wait_recv()
@@ -701,7 +774,7 @@
             move(res.at[rows(base + k1, n2), c], res.at[rows(base + k1, n2), c], p, 6, (xp, z)),
         ))
     sixth = []
-    for p, (_, _, _, w, at) in enumerate(pieces):
+    for p, (_, _, _, w, at, _) in enumerate(pieces):
         c = slice(at, at + w)
         for copy in fifth[p]:
             copy.wait_recv()
@@ -711,29 +784,30 @@
             move(res.at[mine[1], c], res.at[mine[1], c], p, 8, (yp, z)),
         ))
     last = []
-    for p, (_, _, _, w, at) in enumerate(pieces):
+    for p, (_, _, _, w, at, _) in enumerate(pieces):
         c = slice(at, at + w)
         for copy in sixth[p]:
             copy.wait_recv()
         last.append(move(res.at[rows(base, half), c], res.at[rows(base, half), c], p, 8 + size, (sibling, z)))
-    for p, (_, out, lo, w, at) in enumerate(pieces):
+    for p, (_, out, _, w, at, to) in enumerate(pieces):
         last[p].wait_recv()
-        out[:, lo : lo + w] = res[:, at : at + w].astype(F32)
+        out[:, to : to + w] = res[:, at : at + w].astype(F32)
     for copy in sent:
         copy.wait_send()
 
 
-def reduce_all(*grads):
+def reduce_all(*groups):
     size = lax.axis_size("wshard")
-    rows = grads[0].shape[0] // size
-    columns = tuple(g.shape[1] for g in grads)
-    count = sum(-(-c // 512) for c in columns)
-    width, half = sum(columns), rows // 2
+    rows = groups[0][0].shape[0] // size
+    grads = [g for group in groups for g in group]
+    columns = tuple(tuple(g.shape[1] for g in group) for group in groups)
+    count = sum(-(-g.shape[1] // 512) for g in grads)
+    width, half = sum(g.shape[1] for g in grads), rows // 2
     return pl.pallas_call(
         functools.partial(reduce_kernel, size, columns),
         in_specs=[VMEM] * len(grads),
-        out_specs=[VMEM] * len(grads),
-        out_shape=[jax.ShapeDtypeStruct((rows, c), F32) for c in columns],
+        out_specs=[VMEM] * len(groups),
+        out_shape=[jax.ShapeDtypeStruct((rows, sum(widths)), F32) for widths in columns],
         scratch_shapes=[
             pltpu.VMEM((size, half, width), BF16),
             pltpu.VMEM((size, half, width), BF16),
@@ -746,7 +820,7 @@
             pltpu.SemaphoreType.DMA((9 + size, count)),
         ],
         compiler_params=pltpu.CompilerParams(collective_id=1, has_side_effects=True, vmem_limit_bytes=VMEM_BYTES),
-        cost_estimate=cost(1e9, 8 * size * rows * width),
+        cost_estimate=cost(1, 1),
         name="reduce_all",
     )(*[g.reshape(size, rows, g.shape[1]) for g in grads])
 
@@ -757,22 +831,21 @@
 
 
 def gather_experts(mats, owners):
-    slots = {0: tuple([m] for m in mats)}
-    if owners == 8:
-        slots[2] = tuple([flip(m, "expert", 2)] for m in mats)
-        slots[4] = tuple([flip(m, "expert", 4)] for m in mats)
-        third = []
-        for (a,), (b,) in zip(slots[2], slots[4]):
-            cut = a.shape[0] // 2
-            third.append([flip(a[:cut], "expert", 4), flip(b[cut:], "expert", 2)])
-        slots[6] = tuple(third)
-    else:
-        bit = 2
-        while bit < owners:
-            for j in sorted(slots):
-                slots[j | bit] = tuple([flip(p, "expert", bit) for p in m] for m in slots[j])
-            bit *= 2
+    slots, bit = {0: tuple([m] for m in mats)}, 2
+    while bit < owners:
+        for j in sorted(slots):
+            slots[j | bit] = tuple([flip(p, "expert", bit) for p in m] for m in slots[j])
+        bit *= 2
     return slots
+
+
+def third_slot(a, b):
+    cut = a[2][0].shape[0] // 2
+    return (
+        [flip(a[0][0], "expert", 4)],
+        [flip(b[1][0], "expert", 2)],
+        [flip(a[2][0][:cut], "expert", 4), flip(b[2][0][cut:], "expert", 2)],
+    )
 
 
 def across_core(slot):
@@ -801,96 +874,111 @@
     me = lax.axis_index("expert").astype(jnp.int32)[None]
     rows, width = tokens.shape
     experts = w_router.shape[1]
-    slots = gather_experts((w_gate[0], w_up[0], w_down[0]), owners)
-
-    small = jnp.concatenate([gain_attn[:, None], gain_ffn[:, None], w_router], axis=1)
+    mats = (w_gate[0], w_up[0], w_down[0])
+
+    small = jnp.concatenate([w_router, gain_attn[:, None], gain_ffn[:, None]], axis=1)
     small = jnp.pad(small, ((0, 0), (0, LANES - small.shape[1])))
-    packed, small, out_shard = gather_weights(w_query, key_weight, value_weight, small, w_out)
+    packed, small, out_shard, gains, *beside = gather_weights(
+        w_query, key_weight, value_weight, small, w_out, mats[:2] if owners == 8 else ()
+    )
     out_w = lax.all_gather(out_shard, "wshard", axis=0, tiled=True)
-    gain_one, gain_two = small[:, 0][None], small[:, 1][None]
-    router_w = jnp.pad(small[:, 2 : 2 + experts], ((0, 0), (0, LANES - experts)))
     cos, sin = (jnp.asarray(a) for a in rope_tables(rows))
 
-    normed, queries, keys, vals = project(tokens, gain_one, packed, cos, sin)
+    if owners == 8:
+        slots = {0: tuple([m] for m in mats)}
+        slots[2] = ([beside[0]], [beside[1]], [flip(mats[2], "expert", 2)])
+        slots[4] = ([beside[2]], [beside[3]], [flip(mats[2], "expert", 4)])
+        slots[6] = third_slot(slots[2], slots[4])
+    else:
+        slots = gather_experts(mats, owners)
+    normed_t, queries, keys, vals = project(tokens, gains, experts, packed, cos, sin)
+    def pieces_of(*which):
+        return [p for j in which for m in slots[j] for p in m] if owners == 8 else []
+
     attended = attend(queries, keys, vals)
-    resid, moe_in, moe_in_t, gates = middle(attended, out_w, tokens, gain_two, router_w, routes)
+    for j in sorted(slots):
+        slots[j | 1] = across_core(slots[j])
+    resid, moe_in, moe_in_t, gates = middle(
+        attended, out_w, tokens, gains, experts + 1, small, routes, pieces_of(2, 4, 3, 5, 1)
+    )
     dy_t = cotangent.T
-    for j in sorted(slots):
-        here = slots[j] if j == 0 else lax.optimization_barrier((slots[j], attended))[0]
-        slots[j | 1] = across_core(here)
-
-    def some(pair, acc, ties=()):
-        return moe(pair, me, moe_in, moe_in_t, cotangent, dy_t, gates, acc, [slots[j] for j in pair], ties)
+
+    def one(j, acc, ties=()):
+        acc, (halves,) = moe([j], me, moe_in, moe_in_t, cotangent, dy_t, gates, acc, [slots[j]], ties)
+        return acc, halves
 
     def turned(acc, ties=()):
         made, dmoe, gate_grads = acc
-        return turn(resid, made, dmoe, gates, gate_grads, cotangent, gain_two, router_w, moe_in_t, out_w, ties)
+        return turn(
+            resid, made, dmoe, gates, gate_grads, cotangent, gains, experts + 1, small, moe_in_t, out_w, ties
+        )
 
     if owners == 8:
         core = lambda halves: [flip(m, "expert", 1) for m in halves]
         over_x = lambda m: flip(m, "expert", 2)
         over_y = lambda m: flip(m, "expert", 4)
-        both = lambda a, b: [plus(m, n) for m, n in zip(a, b)]
-        acc, (g2, g3) = some([2, 3], None)
+        acc, g3 = one(3, None, pieces_of(6))
         c3 = core(g3)
-        acc, (g6, g7) = some([6, 7], acc)
-        s2 = both(g2, c3)
+        acc, g2 = one(2, acc, pieces_of(7))
+        *s2, t2 = plus((g2[0], c3[0]), (g2[1], c3[1]))
+        x20 = over_x(s2[0])
+        acc, g7 = one(7, acc, [t2])
         c7 = core(g7)
-        x20 = over_x(s2[0])
-        acc, (g4, g5) = some([4, 5], acc, [*s2])
-        s6 = both(g6, c7)
+        acc, g6 = one(6, acc)
+        *s6, t6 = plus((g6[0], c7[0]), (g6[1], c7[1]))
+        x60, y61 = over_x(s6[0]), over_y(s6[1])
+        acc, g5 = one(5, acc, [t6])
         c5 = core(g5)
-        x60, y61 = over_x(s6[0]), over_y(s6[1])
-        acc, (g0, g1) = some([0, 1], acc, [*s6, x20])
-        s4 = both(g4, c5)
+        acc, g4 = one(4, acc, [x20])
+        *s4, t4 = plus((g4[0], c5[0]), (g4[1], c5[1]))
+        y41 = over_y(s4[1])
+        acc, g1 = one(1, acc, [t4])
         c1 = core(g1)
-        left, right = plus(s4[0], x60), plus(s2[1], y61)
-        y41, x21 = over_y(s4[1]), over_x(right)
-        mixed, dresid, dz, dattended, gain_two_grad, router_grad = turned(acc, [left, right, s4[1]])
-        out_grad = dot_tn(attended, dz)
-        s0 = both(g0, c1)
-        y40 = over_y(left)
-        early = attend_back(queries, keys, vals, dattended, cos, sin, 0, 2, [*s0])
-        own = [plus(s0[0], x20, y40, ties=early[2:]), plus(s0[1], y41, x21, ties=early[2:])]
-        late = attend_back(queries, keys, vals, dattended, cos, sin, 2, 2, own)
+        left, right, sides = plus((s4[0], x60), (s2[1], y61))
+        x21, y40 = over_x(right), over_y(left)
+        acc, g0 = one(0, acc, [sides])
+        *s0, t0 = plus((g0[0], c1[0]), (g0[1], c1[1]))
+        mixed, dresid, dz, dattended, gain_two_grad, router_grad = turned(acc, [t0])
+        out_grad = dot_tn(attended, dz).astype(BF16)
+        early = attend_back(queries, keys, vals, dattended, cos, sin, 0, 2, [out_grad])
+        top, bottom, both = plus((s0[0], x20, y40), (s0[1], y41, x21), ties=early[2:])
+        late = attend_back(queries, keys, vals, dattended, cos, sin, 2, 2, [both])
+        top, bottom = lax.psum((top, bottom), "wshard")
         pieces = [early[0], late[0], early[1], late[1], early[2], late[2]]
+        weight_grads = weights_back(normed_t, pieces)
+        own, after = [top, bottom], []
     else:
         acc, parts = None, {}
-        for at in range(0, owners, 2):
-            acc, grads = some([at, at + 1], acc)
-            parts.update(zip([at, at + 1], grads))
+        for j in range(owners):
+            acc, parts[j] = one(j, acc)
         mixed, dresid, dz, dattended, gain_two_grad, router_grad = turned(acc)
-        own = reduce_experts(parts, owners)
-        out_grad = dot_tn(attended, dz)
+        own, after = lax.psum(tuple(reduce_experts(parts, owners)), "wshard"), []
+        out_grad = dot_tn(attended, dz).astype(BF16)
         pieces = attend_back(queries, keys, vals, dattended, cos, sin)
-    qkv_grad = dot_tn(normed, jnp.concatenate(pieces, axis=1)).astype(BF16)
-    d_tokens, gain_one_grad = finish(pieces, packed, tokens, dresid, gain_one)
-
-    small_grad = jnp.concatenate([gain_one_grad.T, gain_two_grad.T, router_grad[:, :experts]], axis=1)
-
-    small_grad = jnp.pad(small_grad, ((0, 0), (0, LANES - small_grad.shape[1]))).astype(BF16)
-    grads = (out_grad.astype(BF16), qkv_grad, small_grad)
+        weight_grads = weights_back(normed_t, pieces)
+    d_tokens, small_grad = finish(pieces, packed, tokens, dresid, gains, experts, router_grad, gain_two_grad, after)
+    third = len(weight_grads) // 3
+    groups = [[out_grad]] + [weight_grads[i : i + third] for i in range(0, 3 * third, third)] + [[small_grad]]
     if owners == 8:
-        out_grad, qkv_grad, small_grad = reduce_all(*grads)
+        sums = reduce_all(*groups)
     else:
-        out_grad, qkv_grad, small_grad = (
-            lax.psum(lax.psum_scatter(g, "wshard", scatter_dimension=0, tiled=True), "expert").astype(F32) for g in grads
-        )
-    own = jnp.concatenate(lax.psum(tuple(own), "wshard"), axis=1).astype(F32)
-    qw, kw = w_query.shape[1], key_weight.shape[1]
+        total = lambda g: lax.psum(lax.psum_scatter(g, "wshard", scatter_dimension=0, tiled=True), "expert")
+        sums = [total(jnp.concatenate(group, axis=1)).astype(F32) for group in groups]
+    out_grad, query_grad, key_grad, value_grad, small_grad = sums
+    gate_grad, up_grad, down_grad = widen(*own)
     return (
         mixed,
         d_tokens,
-        small_grad[:, 0],
-        qkv_grad[:, :qw],
-        qkv_grad[:, qw : qw + kw],
-        qkv_grad[:, qw + kw :],
+        small_grad[:, experts],
+        query_grad,
+        key_grad,
+        value_grad,
         out_grad,
-        small_grad[:, 1],
-        small_grad[:, 2 : 2 + experts],
-        own[0:1],
-        own[1:2],
-        own[2:3].swapaxes(1, 2),
+        small_grad[:, experts + 1],
+        small_grad[:, :experts],
+        gate_grad[None],
+        up_grad[None],
+        down_grad[None],
     )
 
 

time: 589 us -> 536 us (0.910)
  Pallas kernels: 440 us -> 409 us
  waiting for transfers between devices: 42.5 us -> 28.6 us
  local copies, waits for them, and re-layouts: 39.5 us -> 49.3 us
  matrix products: 11.6 us -> 3.71 us
    pallas_call x4 -> x8, Pallas kernels: 138 us -> 102 us  [moe(): pl.pallas_call(functools.partial(moe_kernel, tuple(slots), chunks, first,...]
    unnamed x69 -> x115, local copies, waits for them, and re-layouts: 18.9 us -> 42.7 us
    psum x1, waiting for transfers between devices: 25.2 us -> 5.33 us  [on_device(): top, bottom = lax.psum((top, bottom), 'wshard')]
    pallas_call x1, Pallas kernels: 67.8 us -> 81.4 us  [reduce_all(): pl.pallas_call(functools.partial(reduce_kernel, size, columns), in_specs=...]
    slice x14 -> x3, local copies, waits for them, and re-layouts: 13 us -> 4.54 us  [the longest x1 1.87 us: third_slot(): a[2][0][:cut]]
    pallas_call x18 -> x14, Pallas kernels: 173 us -> 165 us  [the longest x1 69.3 us: gather_weights(): pl.pallas_call(functools.partial(gather_kernel, size, len(owned)), in_spe...]
    dot_general x2 -> x1, matrix products: 11.6 us -> 3.71 us  [dot_tn(): lax.dot_general(a, b, (((0,), (0,)), ((), ())), preferred_element_type=F32)]
    ppermute x41 -> x33, waiting for transfers between devices: 16.6 us -> 23.2 us  [flip(): return lax.ppermute(value, axis, [(i, i ^ bit) for i in range(size)])]
  transfers between devices with their start and end apart: 43 -> 35, of which waited for: 4 -> 7; matrix products, arithmetic and copies ran while one was open for 6% -> 3% of each run, Pallas kernels for 70% -> 73%
where the time goes in v3:
time: 536 us; the launch traced here: 526 us
  Pallas kernels  409 us (76%)
  local copies, waits for them, and re-layouts  49.3 us (9%)
  waiting for transfers between devices  28.6 us (5%)
  starting transfers between devices  19.5 us (4%)
  between operations  14.8 us (3%)
    pallas_call x8, Pallas kernels, moe(): pl.pallas_call(functools.partial(moe_kernel, tuple(slots), chunks, first,...  102 us
    pallas_call x1, Pallas kernels, reduce_all(): pl.pallas_call(functools.partial(reduce_kernel, size, columns), in_specs=...  81.4 us
    pallas_call x1, Pallas kernels, gather_weights(): pl.pallas_call(functools.partial(gather_kernel, size, len(owned)), in_spe...  69.3 us
    pallas_call x2, Pallas kernels, attend_back(): pl.pallas_call(tied(attend_back_kernel, 6, ties), grid=(rows // SEQUENCE_...  61 us
    unnamed x115, local copies, waits for them, and re-layouts  42.7 us
    pallas_call x1, Pallas kernels, attend(): pl.pallas_call(tied(attend_kernel, 3, ties), grid=(rows // SEQUENCE_LENGT...  35.4 us
    ppermute x33, waiting for transfers between devices, flip(): return lax.ppermute(value, axis, [(i, i ^ bit) for i in range(size)])  23.2 us
    ppermute x33, starting transfers between devices, flip(): return lax.ppermute(value, axis, [(i, i ^ bit) for i in range(size)])  19.4 us
  transfers between devices with their start and end apart: 35, of which 7 were waited for; matrix products, arithmetic and copies ran while one was open for 3% of the time, Pallas kernels for 73%

profile of v3, /device:TPU:0, one launch (start us, length us, event | category | flops | bytes accessed | tf_op | source)
XLA Modules:
  0.0 526.1 jit_solution(2597272066806765958)
XLA Ops:
  8.3 2.6 collective-permute-start.1
  15.1 69.3 %gather_weights.1 = (bf16[1024,2048]{1,0:T(8,128)(2,1)}, bf16[1024,128]{1,0:T(8,128)(2,1)}, bf16[256,1024]{1,0:T(8,128)(2,1)}, bf16[128,1024]{1,0:T(8,128)(2,1)}...) custom-call(bf16[256,1024]{1,0:T(8,128)(2,1)} %refs_0_.1, ...), custom_call_target="tpu_custom_call" | custom-call | flops 1000000000 | bytes 25165824 | tf_op jit(solution)/shard_map/gather_weights/pallas_call | solution.py:664
  92.5 5.7 %project.1 = (bf16[1024,1024]{1,0:T(8,128)(2,1)S(1)}, bf16[1024,1024]{1,0:T(8,128)(2,1)S(1)}, bf16[1024,512]{1,0:T(8,128)(2,1)S(1)}, bf16[1024,512]{1,0:T(8,128)(2,1)S(1)}) custom-call(bf16[1024,1024]{1,0:T(8,128)(2,1)S(1)} %copy-done.1, bf16[128,1024]{1,0:T(8,128)(2,1)S(1)} %copy-done.9, bf16[1024,2048]{1,0:T(8,128)(2,1)S(1)} %copy-done.4, ...), custom_call_target="tpu_custom_call" | custom-call | flops 4294967296 | bytes 12582912 | tf_op jit(solution)/shard_map/project/pallas_call | solution.py:104
  104.7 5.8 %collective-permute-done.11.refs_8_ = bf16[1024,512]{1,0:T(8,128)(2,1)} collective-permute-done((bf16[1024,512]{1,0:T(8,128)(2,1)}, bf16[1024,512]{1,0:T(8,128)(2,1)}, u32[]{:S(2)}, u32[]{:S(2)}) %collective-permute-start.11) | collective-permute-done | bytes 1048608 | tf_op jit(solution)/shard_map/ppermute | solution.py:830
  111.7 35.4 %attend.1.refs_0_ = bf16[1024,1024]{1,0:T(8,128)(2,1)} custom-call(bf16[1024,1024]{1,0:T(8,128)(2,1)} %copy-done.46, bf16[1024,512]{1,0:T(8,128)(2,1)} %copy-done.47, bf16[1024,512]{1,0:T(8,128)(2,1)} %copy-done.48), custom_call_target="tpu_custom_call" | custom-call | flops 34359738368 | bytes 6291456 | tf_op jit(solution)/shard_map/attend/pallas_call | solution.py:140
  148.2 2.5 copy.60
  159.0 7.7 %middle.1 = (f32[1024,1024]{1,0:T(8,128)}, bf16[1024,1024]{1,0:T(8,128)(2,1)S(1)}, bf16[1024,1024]{1,0:T(8,128)(2,1)S(1)}, f32[1024,128]{1,0:T(8,128)S(1)}) custom-call(bf16[1024,1024]{1,0:T(8,128)(2,1)S(1)} %copy-done.15, bf16[1024,1024]{1,0:T(8,128)(2,1)} %all-gather.2.cloned.1.call-done.refs_1_.refs_9_, bf16[1024,1024]{1,0:T(8,128)(2,1)} %refs_7_.1, ...), custom_call_target="tpu_custom_call" | custom-call | flops 2415919104 | bytes 14680064 | tf_op jit(solution)/shard_map/middle/pallas_call | solution.py:227
  171.3 12.7 %experts.8 = (f32[1024,1024]{1,0:T(8,128)S(1)}, f32[1024,1024]{1,0:T(8,128)S(1)}, f32[1024,128]{1,0:T(8,128)S(1)}, bf16[3,512,512]{2,1,0:T(8,128)(2,1)}, bf16[3,512,512]{2,1,0:T(8,128)(2,1)S(1)}) custom-call(s32[1]{0:T(128)} %bitcast.3.me_ref, bf16[1024,1024]{1,0:T(8,128)(2,1)S(1)} %get-tuple-element.126.refs_0_, bf16[1024,1024]{1,0:T(8,128)(2,1)S(1)} %copy-done.18, ...), custom_call_target="tpu_custom_call" | custom-call | flops 9663676416 | bytes 20971520 | tf_op jit(solution)/shard_map/experts/pallas_call | solution.py:349
  184.7 6.0 %collective-permute-done.17.refs_13_.refs_10_ = bf16[256,1024]{1,0:T(8,128)(2,1)S(1)} collective-permute-done((bf16[256,1024]{1,0:T(8,128)(2,1)}, bf16[256,1024]{1,0:T(8,128)(2,1)S(1)}, u32[]{:S(2)}, u32[]{:S(2)}) %collective-permute-start.17) | collective-permute-done | bytes 524320 | tf_op jit(solution)/shard_map/ppermute | solution.py:830
  190.7 12.2 %experts.9 = (f32[1024,1024]{1,0:T(8,128)S(1)}, f32[1024,1024]{1,0:T(8,128)S(1)}, f32[1024,128]{1,0:T(8,128)S(1)}, bf16[3,512,512]{2,1,0:T(8,128)(2,1)S(1)}, bf16[3,512,512]{2,1,0:T(8,128)(2,1)S(1)}) custom-call(s32[1]{0:T(128)} %bitcast.3.me_ref, ...), custom_call_target="tpu_custom_call", output_to_operand_aliasing={{0}: (6, {}), {1}: (7, {}), {2}: (8, {})} | custom-call | flops 9663676416 | bytes 20971520 | tf_op jit(solution)/shard_map/experts/pallas_call | solution.py:349
  203.7 13.2 %experts.10 = (f32[1024,1024]{1,0:T(8,128)S(1)}, f32[1024,1024]{1,0:T(8,128)S(1)}, f32[1024,128]{1,0:T(8,128)S(1)}, bf16[3,512,512]{2,1,0:T(8,128)(2,1)}, bf16[3,512,512]{2,1,0:T(8,128)(2,1)S(1)}) custom-call(s32[1]{0:T(128)} %bitcast.3.me_ref, ...), custom_call_target="tpu_custom_call", output_to_operand_aliasing={{0}: (6, {}), {1}: (7, {}), {2}: (8, {})} | custom-call | flops 9663676416 | bytes 20971520 | tf_op jit(solution)/shard_map/experts/pallas_call | solution.py:349
  219.3 13.0 %experts.11 = (f32[1024,1024]{1,0:T(8,128)S(1)}, f32[1024,1024]{1,0:T(8,128)S(1)}, f32[1024,128]{1,0:T(8,128)S(1)}, bf16[3,512,512]{2,1,0:T(8,128)(2,1)S(1)}, bf16[3,512,512]{2,1,0:T(8,128)(2,1)S(1)}) custom-call(s32[1]{0:T(128)} %bitcast.3.me_ref, ...), custom_call_target="tpu_custom_call", output_to_operand_aliasing={{0}: (6, {}), {1}: (7, {}), {2}: (8, {})} | custom-call | flops 9663676416 | bytes 20971520 | tf_op jit(solution)/shard_map/experts/pallas_call | solution.py:349
  232.3 2.6 plus.7
  235.0 12.7 %experts.12 = (f32[1024,1024]{1,0:T(8,128)S(1)}, f32[1024,1024]{1,0:T(8,128)S(1)}, f32[1024,128]{1,0:T(8,128)S(1)}, bf16[3,512,512]{2,1,0:T(8,128)(2,1)}, bf16[3,512,512]{2,1,0:T(8,128)(2,1)S(1)}) custom-call(s32[1]{0:T(128)} %bitcast.3.me_ref, ...), custom_call_target="tpu_custom_call", output_to_operand_aliasing={{0}: (6, {}), {1}: (7, {}), {2}: (8, {})} | custom-call | flops 9663676416 | bytes 20971520 | tf_op jit(solution)/shard_map/experts/pallas_call | solution.py:349
  250.3 4.5 collective-permute-done.23.refs_11_.refs_1_
  254.8 12.9 %experts.13 = (f32[1024,1024]{1,0:T(8,128)S(1)}, f32[1024,1024]{1,0:T(8,128)S(1)}, f32[1024,128]{1,0:T(8,128)S(1)}, bf16[3,512,512]{2,1,0:T(8,128)(2,1)S(1)}, bf16[3,512,512]{2,1,0:T(8,128)(2,1)S(1)}) custom-call(s32[1]{0:T(128)} %bitcast.3.me_ref, ...), custom_call_target="tpu_custom_call", output_to_operand_aliasing={{0}: (6, {}), {1}: (7, {}), {2}: (8, {})} | custom-call | flops 9663676416 | bytes 20971520 | tf_op jit(solution)/shard_map/experts/pallas_call | solution.py:349
  267.7 2.9 plus.8
  270.6 13.0 %experts.14 = (f32[1024,1024]{1,0:T(8,128)S(1)}, f32[1024,1024]{1,0:T(8,128)S(1)}, f32[1024,128]{1,0:T(8,128)S(1)}, bf16[3,512,512]{2,1,0:T(8,128)(2,1)S(1)}, bf16[3,512,512]{2,1,0:T(8,128)(2,1)S(1)}) custom-call(s32[1]{0:T(128)} %bitcast.3.me_ref, ...), custom_call_target="tpu_custom_call", output_to_operand_aliasing={{0}: (6, {}), {1}: (7, {}), {2}: (8, {})} | custom-call | flops 9663676416 | bytes 20971520 | tf_op jit(solution)/shard_map/experts/pallas_call | solution.py:349
  284.2 3.5 collective-permute-done.26.refs_1_
  287.7 2.8 plus.9
  294.3 12.2 %experts.15 = (f32[1024,1024]{1,0:T(8,128)S(1)}, f32[1024,1024]{1,0:T(8,128)S(1)}, f32[1024,128]{1,0:T(8,128)S(1)}, bf16[3,512,512]{2,1,0:T(8,128)(2,1)S(1)}, bf16[3,512,512]{2,1,0:T(8,128)(2,1)S(1)}) custom-call(s32[1]{0:T(128)} %bitcast.3.me_ref, ...), custom_call_target="tpu_custom_call", output_to_operand_aliasing={{0}: (6, {}), {1}: (7, {}), {2}: (8, {})} | custom-call | flops 9663676416 | bytes 20971520 | tf_op jit(solution)/shard_map/experts/pallas_call | solution.py:349
  315.7 7.5 %turn.1 = (bf16[1024,1024]{1,0:T(8,128)(2,1)}, f32[1024,1024]{1,0:T(8,128)S(1)}, bf16[1024,1024]{1,0:T(8,128)(2,1)S(1)}, bf16[1024,1024]{1,0:T(8,128)(2,1)S(1)},...) custom-call(f32[1024,1024]{1,0:T(8,128)S(1)} %copy-done.5, f32[1024,1024]{1,0:T(8,128)} %copy-done.7, ...), custom_call_target="tpu_custom_call" | custom-call | flops 2684354560 | bytes 29360128 | tf_op jit(solution)/shard_map/turn/pallas_call | solution.py:402
  323.3 3.7 convolution_convert_fusion.refs_6_
  327.0 30.7 %attend_back.2 = (bf16[1024,512]{1,0:T(8,128)(2,1)}, bf16[1024,256]{1,0:T(8,128)(2,1)}, bf16[1024,256]{1,0:T(8,128)(2,1)}) custom-call(bf16[1024,1024]{1,0:T(8,128)(2,1)} %copy-done.46, bf16[1024,512]{1,0:T(8,128)(2,1)} %copy-done.47, bf16[1024,512]{1,0:T(8,128)(2,1)} %copy-done.48, bf16[1024,1024]{1,0:T(8,128)(2,1)} %copy-done.41, ...), custom_call_target="tpu_custom_call" | custom-call | flops 42949672960 | bytes 12582912 | tf_op jit(solution)/shard_map/attend_back/pallas_call | solution.py:190
  357.7 2.4 collective-permute-done.31.refs_4_
  362.6 4.3 plus.11
  369.8 30.3 %attend_back.3 = (bf16[1024,512]{1,0:T(8,128)(2,1)}, bf16[1024,256]{1,0:T(8,128)(2,1)}, bf16[1024,256]{1,0:T(8,128)(2,1)}) custom-call(bf16[1024,1024]{1,0:T(8,128)(2,1)} %copy-done.46, bf16[1024,512]{1,0:T(8,128)(2,1)} %copy-done.47, bf16[1024,512]{1,0:T(8,128)(2,1)} %copy-done.48, bf16[1024,1024]{1,0:T(8,128)(2,1)} %copy-done.41, ...), custom_call_target="tpu_custom_call" | custom-call | flops 42949672960 | bytes 12582912 | tf_op jit(solution)/shard_map/attend_back/pallas_call | solution.py:190
  400.1 8.2 %weights_back.1 = (bf16[1024,512]{1,0:T(8,128)(2,1)}, bf16[1024,512]{1,0:T(8,128)(2,1)}, bf16[1024,256]{1,0:T(8,128)(2,1)}, bf16[1024,256]{1,0:T(8,128)(2,1)}, b...) custom-call(bf16[1024,1024]{1,0:T(8,128)(2,1)} %copy-done.11, bf16[1024,512]{1,0:T(8,128)(2,1)} %get-tuple-element.182.refs_0_.refs_1_, ...), custom_call_target="tpu_custom_call" | custom-call | flops 1 | bytes 1 | tf_op jit(solution)/shard_map/weights_back/pallas_call | solution.py:477
  408.3 11.6 %finish.1 = (f32[1024,1024]{1,0:T(8,128)}, bf16[1024,128]{1,0:T(8,128)(2,1)}) custom-call(bf16[1024,512]{1,0:T(8,128)(2,1)} %get-tuple-element.182.refs_0_.refs_1_, bf16[1024,512]{1,0:T(8,128)(2,1)} %get-tuple-element.190.refs_1_.refs_2_, bf16[1024,256]{1,0:T(8,128)(2,1)} %get-tuple-element.191.refs_2_.refs_3_, ...), custom_call_target="tpu_custom_call" | custom-call | flops 1 | bytes 1 | tf_op jit(solution)/shard_map/finish/pallas_call | solution.py:454
  420.0 81.4 %reduce_all.1 = (f32[256,1024]{1,0:T(8,128)}, f32[256,1024]{1,0:T(8,128)}, f32[256,512]{1,0:T(8,128)}, f32[256,512]{1,0:T(8,128)}, f32[256,128]{1,0:T(8,128)}) custom-call(bf16[4,256,1024]{2,1,0:T(8,128)(2,1)} %bitcast.37, bf16[4,256,512]{2,1,0:T(8,128)(2,1)} %bitcast.39, bf16[4,256,512]{2,1,0:T(8,128)(2,1)} %bitcast.40, bf16[4,256,256]{2,1,0:T(8,128)(2,1)} %bitcast.41, ...), custom_call_target="tpu_custom_call" | custom-call | flops 1 | bytes 1 | tf_op jit(solution)/shard_map/reduce_all/pallas_call | solution.py:806
  504.8 5.3 %all-reduce.4.cloned.1.call-done = (bf16[3,512,512]{2,1,0:T(8,128)(2,1)}, bf16[3,512,512]{2,1,0:T(8,128)(2,1)}) async-done(((bf16[3,512,512]{2,1,0:T(8,128)(2,1)}, bf16[3,512,512]{2,1,0:T(8,128)(2,1)}), (bf16[3,512,512]{2,1,0:T(8,128)(2,1)}, bf16[3,512,512]{2,1,0:T(8,128)(2,1)})) %all-reduce.4.cloned.1.call-update) | async-done | bytes 3145744 | tf_op jit(solution)/shard_map/psum | solution.py:946
  510.2 5.3 %widen.1 = (f32[1024,512]{1,0:T(8,128)}, f32[1024,512]{1,0:T(8,128)}, f32[512,1024]{1,0:T(8,128)}) custom-call(bf16[3,512,512]{2,1,0:T(8,128)(2,1)} %get-tuple-element.254.top_ref, bf16[3,512,512]{2,1,0:T(8,128)(2,1)} %get-tuple-element.255.bottom_ref), custom_call_target="tpu_custom_call" | custom-call | flops 1 | bytes 1 | tf_op jit(solution)/shard_map/widen/pallas_call | solution.py:504
  (189 shorter events, 67.0 us)
Async XLA Ops:
  7.2 144.6 %all-gather.2.cloned.1.call-start = ((), (), s32[]{:S(2)}) async-start(), calls=%async_computation | async-start | bytes 2621440 | tf_op jit(solution)/shard_map/all_gather | solution.py:884
  7.2 77.3 %collective-permute-start.8 = (bf16[1024,512]{1,0:T(8,128)(2,1)}, bf16[1024,512]{1,0:T(8,128)(2,1)}, u32[]{:S(2)}, u32[]{:S(2)}) collective-permute-start(bf16[1024,512]{1,0:T(8,128)(2,1)} %bitcast.27), channel_id=1, source_target_pairs={{0,4},{4,0},{8,12},{12,8},{16,20},{20,16},{24,28},{28,24},{1,5},{5... | collective-permute-start | bytes 3145736 | tf_op jit(solution)/shard_map/ppermute | solution.py:830
  7.7 76.8 %collective-permute-start.9 = (bf16[1024,512]{1,0:T(8,128)(2,1)}, bf16[1024,512]{1,0:T(8,128)(2,1)}, u32[]{:S(2)}, u32[]{:S(2)}) collective-permute-start(bf16[1024,512]{1,0:T(8,128)(2,1)} %bitcast.30), channel_id=1, source_target_pairs={{0,4},{4,0},{8,12},{12,8},{16,20},{20,16},{24,28},{28,24},{1,5},{5... | collective-permute-start | bytes 3145736 | tf_op jit(solution)/shard_map/ppermute | solution.py:830
  7.8 77.3 %collective-permute-start.10 = (bf16[512,1024]{1,0:T(8,128)(2,1)}, bf16[512,1024]{1,0:T(8,128)(2,1)}, u32[]{:S(2)}, u32[]{:S(2)}) collective-permute-start(bf16[512,1024]{1,0:T(8,128)(2,1)} %bitcast.33), channel_id=1, source_target_pairs={{0,4},{4,0},{8,12},{12,8},{16,20},{20,16},{24,28},{28,24},{1,5},{5... | collective-permute-start | bytes 3145736 | tf_op jit(solution)/shard_map/ppermute | solution.py:830
  8.3 77.1 %collective-permute-start.1 = (bf16[512,1024]{1,0:T(8,128)(2,1)}, bf16[512,1024]{1,0:T(8,128)(2,1)S(1)}, u32[]{:S(2)}, u32[]{:S(2)}) collective-permute-start(bf16[512,1024]{1,0:T(8,128)(2,1)} %bitcast.34), channel_id=1, source_target_pairs={{0,16},{4,20},{8,24},{12,28},{16,0},{20,4},{24,8},{28,12},{1,17},{... | collective-permute-start | bytes 3145736 | tf_op jit(solution)/shard_map/ppermute | solution.py:830
  10.8 74.5 %collective-permute-start = (bf16[512,1024]{1,0:T(8,128)(2,1)}, bf16[512,1024]{1,0:T(8,128)(2,1)}, u32[]{:S(2)}, u32[]{:S(2)}) collective-permute-start(bf16[512,1024]{1,0:T(8,128)(2,1)} %bitcast.35), channel_id=1, source_target_pairs={{0,8},{4,12},{8,0},{12,4},{16,24},{20,28},{24,16},{28,20},{1,9},{5... | collective-permute-start | bytes 3145736 | tf_op jit(solution)/shard_map/ppermute | solution.py:830
  84.5 19.7 %collective-permute-start.3 = (bf16[1024,512]{1,0:T(8,128)(2,1)}, bf16[1024,512]{1,0:T(8,128)(2,1)}, u32[]{:S(2)}, u32[]{:S(2)}) collective-permute-start(bf16[1024,512]{1,0:T(8,128)(2,1)} %get-tuple-element.122.refs_7_.refs_9_), channel_id=1, source_target_pairs={{0,4},{4,0},{8,12},{12,8},{16,20},{20,16},{24,28},{28,24},{1,5},{5... | collective-permute-start | bytes 3145736 | tf_op jit(solution)/shard_map/ppermute | solution.py:830
  84.6 19.8 %collective-permute-start.5 = (bf16[1024,512]{1,0:T(8,128)(2,1)}, bf16[1024,512]{1,0:T(8,128)(2,1)}, u32[]{:S(2)}, u32[]{:S(2)}) collective-permute-start(bf16[1024,512]{1,0:T(8,128)(2,1)} %get-tuple-element.123.refs_9_.refs_8_), channel_id=1, source_target_pairs={{0,4},{4,0},{8,12},{12,8},{16,20},{20,16},{24,28},{28,24},{1,5},{5... | collective-permute-start | bytes 3145736 | tf_op jit(solution)/shard_map/ppermute | solution.py:830
  85.1 25.5 %collective-permute-start.11 = (bf16[1024,512]{1,0:T(8,128)(2,1)}, bf16[1024,512]{1,0:T(8,128)(2,1)}, u32[]{:S(2)}, u32[]{:S(2)}) collective-permute-start(bf16[1024,512]{1,0:T(8,128)(2,1)} %get-tuple-element.121.refs_6_.refs_8_), channel_id=1, source_target_pairs={{0,16},{4,20},{8,24},{12,28},{16,0},{20,4},{24,8},{28,12},{1,17},{... | collective-permute-start | bytes 3145736 | tf_op jit(solution)/shard_map/ppermute | solution.py:830
  85.4 25.5 %collective-permute-start.2 = (bf16[1024,512]{1,0:T(8,128)(2,1)}, bf16[1024,512]{1,0:T(8,128)(2,1)}, u32[]{:S(2)}, u32[]{:S(2)}) collective-permute-start(bf16[1024,512]{1,0:T(8,128)(2,1)} %get-tuple-element.121.refs_6_.refs_8_), channel_id=1, source_target_pairs={{0,4},{4,0},{8,12},{12,8},{16,20},{20,16},{24,28},{28,24},{1,5},{5... | collective-permute-start | bytes 3145736 | tf_op jit(solution)/shard_map/ppermute | solution.py:830
  85.4 26.3 %collective-permute-start.12 = (bf16[1024,512]{1,0:T(8,128)(2,1)}, bf16[1024,512]{1,0:T(8,128)(2,1)}, u32[]{:S(2)}, u32[]{:S(2)}) collective-permute-start(bf16[1024,512]{1,0:T(8,128)(2,1)} %get-tuple-element.124.refs_10_.refs_9_), channel_id=1, source_target_pairs={{0,8},{4,12},{8,0},{12,4},{16,24},{20,28},{24,16},{28,20},{1,9},{5... | collective-permute-start | bytes 3145736 | tf_op jit(solution)/shard_map/ppermute | solution.py:830
  87.2 423.0 %all-reduce.4.cloned.1.call-start = ((), (), s32[]{:S(2)}) async-start(), calls=%async_computation.1 | async-start | bytes 6291456 | tf_op jit(solution)/shard_map/psum | solution.py:946
  104.2 46.6 %collective-permute-start.6 = (bf16[1024,512]{1,0:T(8,128)(2,1)}, bf16[1024,512]{1,0:T(8,128)(2,1)}, u32[]{:S(2)}, u32[]{:S(2)}) collective-permute-start(bf16[1024,512]{1,0:T(8,128)(2,1)} %get-tuple-element.124.refs_10_.refs_9_), channel_id=1, source_target_pairs={{0,4},{4,0},{8,12},{12,8},{16,20},{20,16},{24,28},{28,24},{1,5},{5... | collective-permute-start | bytes 3145736 | tf_op jit(solution)/shard_map/ppermute | solution.py:830
  104.4 46.9 %collective-permute-start.14 = (bf16[256,1024]{1,0:T(8,128)(2,1)}, bf16[256,1024]{1,0:T(8,128)(2,1)}, u32[]{:S(2)}, u32[]{:S(2)}) collective-permute-start(bf16[256,1024]{1,0:T(8,128)(2,1)} %slice.21), channel_id=1, source_target_pairs={{0,8},{4,12},{8,0},{12,4},{16,24},{20,28},{24,16},{28,20},{1,9},{5... | collective-permute-start | bytes 1572872 | tf_op jit(solution)/shard_map/ppermute | solution.py:830
  110.5 57.5 %collective-permute-start.13 = (bf16[256,1024]{1,0:T(8,128)(2,1)}, bf16[256,1024]{1,0:T(8,128)(2,1)}, u32[]{:S(2)}, u32[]{:S(2)}) collective-permute-start(bf16[256,1024]{1,0:T(8,128)(2,1)} %slice.20), channel_id=1, source_target_pairs={{0,16},{4,20},{8,24},{12,28},{16,0},{20,4},{24,8},{28,12},{1,17},{... | collective-permute-start | bytes 1572872 | tf_op jit(solution)/shard_map/ppermute | solution.py:830
  110.8 40.5 %collective-permute-start.7 = (bf16[512,1024]{1,0:T(8,128)(2,1)S(1)}, bf16[512,1024]{1,0:T(8,128)(2,1)}, u32[]{:S(2)}, u32[]{:S(2)}) collective-permute-start(bf16[512,1024]{1,0:T(8,128)(2,1)S(1)} %collective-permute-done.1.refs_11_.refs_10_), channel_id=1, source_target_pairs={{0,4},{4,0},{8,12},{12,8},{16,20},{20,16},{24,28},{28,24},{1,5},{5... | collective-permute-start | bytes 3145736 | tf_op jit(solution)/shard_map/ppermute | solution.py:830
  111.7 40.0 %collective-permute-start.4 = (bf16[512,1024]{1,0:T(8,128)(2,1)}, bf16[512,1024]{1,0:T(8,128)(2,1)}, u32[]{:S(2)}, u32[]{:S(2)}) collective-permute-start(bf16[512,1024]{1,0:T(8,128)(2,1)} %collective-permute-done.refs_8_.refs_10_), channel_id=1, source_target_pairs={{0,4},{4,0},{8,12},{12,8},{16,20},{20,16},{24,28},{28,24},{1,5},{5... | collective-permute-start | bytes 3145736 | tf_op jit(solution)/shard_map/ppermute | solution.py:830
  150.8 39.9 %collective-permute-start.15 = (bf16[1024,512]{1,0:T(8,128)(2,1)}, bf16[1024,512]{1,0:T(8,128)(2,1)}, u32[]{:S(2)}, u32[]{:S(2)}) collective-permute-start(bf16[1024,512]{1,0:T(8,128)(2,1)} %collective-permute-done.11.refs_8_), channel_id=1, source_target_pairs={{0,4},{4,0},{8,12},{12,8},{16,20},{20,16},{24,28},{28,24},{1,5},{5... | collective-permute-start | bytes 3145736 | tf_op jit(solution)/shard_map/ppermute | solution.py:830
  151.3 39.4 %collective-permute-start.16 = (bf16[1024,512]{1,0:T(8,128)(2,1)}, bf16[1024,512]{1,0:T(8,128)(2,1)}, u32[]{:S(2)}, u32[]{:S(2)}) collective-permute-start(bf16[1024,512]{1,0:T(8,128)(2,1)} %collective-permute-done.12.refs_9_), channel_id=1, source_target_pairs={{0,4},{4,0},{8,12},{12,8},{16,20},{20,16},{24,28},{28,24},{1,5},{5... | collective-permute-start | bytes 3145736 | tf_op jit(solution)/shard_map/ppermute | solution.py:830
  151.3 33.3 %collective-permute-start.18 = (bf16[256,1024]{1,0:T(8,128)(2,1)}, bf16[256,1024]{1,0:T(8,128)(2,1)}, u32[]{:S(2)}, u32[]{:S(2)}) collective-permute-start(bf16[256,1024]{1,0:T(8,128)(2,1)} %collective-permute-done.14.refs_11_), channel_id=1, source_target_pairs={{0,4},{4,0},{8,12},{12,8},{16,20},{20,16},{24,28},{28,24},{1,5},{5... | collective-permute-start | bytes 1572872 | tf_op jit(solution)/shard_map/ppermute | solution.py:830
  184.0 18.9 %collective-permute-start.19 = (bf16[3,512,512]{2,1,0:T(8,128)(2,1)}, bf16[3,512,512]{2,1,0:T(8,128)(2,1)S(1)}, u32[]{:S(2)}, u32[]{:S(2)}) collective-permute-start(bf16[3,512,512]{2,1,0:T(8,128)(2,1)} %get-tuple-element.136), channel_id=1, source_target_pairs={{0,4},{4,0},{8,12},{12,8},{16,20},{20,16},{24,28},{28,24},{1,5},{5... | collective-permute-start | bytes 4718600 | tf_op jit(solution)/shard_map/ppermute | solution.py:830
  184.1 18.7 %collective-permute-start.20 = (bf16[3,512,512]{2,1,0:T(8,128)(2,1)S(1)}, bf16[3,512,512]{2,1,0:T(8,128)(2,1)S(1)}, u32[]{:S(2)}, u32[]{:S(2)}) collective-permute-start(bf16[3,512,512]{2,1,0:T(8,128)(2,1)S(1)} %get-tuple-element.138), channel_id=1, source_target_pairs={{0,4},{4,0},{8,12},{12,8},{16,20},{20,16},{24,28},{28,24},{1,5},{5... | collective-permute-start | bytes 4718600 | tf_op jit(solution)/shard_map/ppermute | solution.py:830
  217.5 37.2 %collective-permute-start.23 = (bf16[3,512,512]{2,1,0:T(8,128)(2,1)S(1)}, bf16[3,512,512]{2,1,0:T(8,128)(2,1)S(1)}, u32[]{:S(2)}, u32[]{:S(2)}) collective-permute-start(bf16[3,512,512]{2,1,0:T(8,128)(2,1)S(1)} %get-tuple-element.154), channel_id=1, source_target_pairs={{0,8},{4,12},{8,0},{12,4},{16,24},{20,28},{24,16},{28,20},{1,9},{5... | collective-permute-start | bytes 4718600 | tf_op jit(solution)/shard_map/ppermute | solution.py:830
  247.7 20.0 %collective-permute-start.24 = (bf16[3,512,512]{2,1,0:T(8,128)(2,1)}, bf16[3,512,512]{2,1,0:T(8,128)(2,1)S(1)}, u32[]{:S(2)}, u32[]{:S(2)}) collective-permute-start(bf16[3,512,512]{2,1,0:T(8,128)(2,1)} %get-tuple-element.159), channel_id=1, source_target_pairs={{0,4},{4,0},{8,12},{12,8},{16,20},{20,16},{24,28},{28,24},{1,5},{5... | collective-permute-start | bytes 4718600 | tf_op jit(solution)/shard_map/ppermute | solution.py:830
  247.7 20.0 %collective-permute-start.25 = (bf16[3,512,512]{2,1,0:T(8,128)(2,1)S(1)}, bf16[3,512,512]{2,1,0:T(8,128)(2,1)S(1)}, u32[]{:S(2)}, u32[]{:S(2)}) collective-permute-start(bf16[3,512,512]{2,1,0:T(8,128)(2,1)S(1)} %get-tuple-element.161), channel_id=1, source_target_pairs={{0,4},{4,0},{8,12},{12,8},{16,20},{20,16},{24,28},{28,24},{1,5},{5... | collective-permute-start | bytes 4718600 | tf_op jit(solution)/shard_map/ppermute | solution.py:830
  248.2 39.5 %collective-permute-start.26 = (bf16[3,512,512]{2,1,0:T(8,128)(2,1)}, bf16[3,512,512]{2,1,0:T(8,128)(2,1)S(1)}, u32[]{:S(2)}, u32[]{:S(2)}) collective-permute-start(bf16[3,512,512]{2,1,0:T(8,128)(2,1)} %get-tuple-element.167), channel_id=1, source_target_pairs={{0,8},{4,12},{8,0},{12,4},{16,24},{20,28},{24,16},{28,20},{1,9},{5... | collective-permute-start | bytes 4718600 | tf_op jit(solution)/shard_map/ppermute | solution.py:830
  248.6 39.1 %collective-permute-start.27 = (bf16[3,512,512]{2,1,0:T(8,128)(2,1)S(1)}, bf16[3,512,512]{2,1,0:T(8,128)(2,1)S(1)}, u32[]{:S(2)}, u32[]{:S(2)}) collective-permute-start(bf16[3,512,512]{2,1,0:T(8,128)(2,1)S(1)} %get-tuple-element.169), channel_id=1, source_target_pairs={{0,16},{4,20},{8,24},{12,28},{16,0},{20,4},{24,8},{28,12},{1,17},{... | collective-permute-start | bytes 4718600 | tf_op jit(solution)/shard_map/ppermute | solution.py:830
  283.6 25.0 %collective-permute-start.28 = (bf16[3,512,512]{2,1,0:T(8,128)(2,1)S(1)}, bf16[3,512,512]{2,1,0:T(8,128)(2,1)S(1)}, u32[]{:S(2)}, u32[]{:S(2)}) collective-permute-start(bf16[3,512,512]{2,1,0:T(8,128)(2,1)S(1)} %get-tuple-element.175), channel_id=1, source_target_pairs={{0,4},{4,0},{8,12},{12,8},{16,20},{20,16},{24,28},{28,24},{1,5},{5... | collective-permute-start | bytes 4718600 | tf_op jit(solution)/shard_map/ppermute | solution.py:830
  283.7 24.9 %collective-permute-start.29 = (bf16[3,512,512]{2,1,0:T(8,128)(2,1)S(1)}, bf16[3,512,512]{2,1,0:T(8,128)(2,1)S(1)}, u32[]{:S(2)}, u32[]{:S(2)}) collective-permute-start(bf16[3,512,512]{2,1,0:T(8,128)(2,1)S(1)} %get-tuple-element.177), channel_id=1, source_target_pairs={{0,4},{4,0},{8,12},{12,8},{16,20},{20,16},{24,28},{28,24},{1,5},{5... | collective-permute-start | bytes 4718600 | tf_op jit(solution)/shard_map/ppermute | solution.py:830
  290.5 67.2 %collective-permute-start.30 = (bf16[3,512,512]{2,1,0:T(8,128)(2,1)}, bf16[3,512,512]{2,1,0:T(8,128)(2,1)}, u32[]{:S(2)}, u32[]{:S(2)}) collective-permute-start(bf16[3,512,512]{2,1,0:T(8,128)(2,1)} %get-tuple-element.184), channel_id=1, source_target_pairs={{0,16},{4,20},{8,24},{12,28},{16,0},{20,4},{24,8},{28,12},{1,17},{... | collective-permute-start | bytes 4718600 | tf_op jit(solution)/shard_map/ppermute | solution.py:830
  292.3 65.5 %collective-permute-start.32 = (bf16[3,512,512]{2,1,0:T(8,128)(2,1)}, bf16[3,512,512]{2,1,0:T(8,128)(2,1)}, u32[]{:S(2)}, u32[]{:S(2)}) collective-permute-start(bf16[3,512,512]{2,1,0:T(8,128)(2,1)} %get-tuple-element.187), channel_id=1, source_target_pairs={{0,8},{4,12},{8,0},{12,4},{16,24},{20,28},{24,16},{28,20},{1,9},{5... | collective-permute-start | bytes 4718600 | tf_op jit(solution)/shard_map/ppermute | solution.py:830
  293.8 66.4 %collective-permute-start.31 = (bf16[3,512,512]{2,1,0:T(8,128)(2,1)}, bf16[3,512,512]{2,1,0:T(8,128)(2,1)}, u32[]{:S(2)}, u32[]{:S(2)}) collective-permute-start(bf16[3,512,512]{2,1,0:T(8,128)(2,1)} %get-tuple-element.186), channel_id=1, source_target_pairs={{0,16},{4,20},{8,24},{12,28},{16,0},{20,4},{24,8},{28,12},{1,17},{... | collective-permute-start | bytes 4718600 | tf_op jit(solution)/shard_map/ppermute | solution.py:830
  (57 other events, 484.0 us)
Sparse Core Ops, SparseCore 0:
  87.3 46.2 all-gather.1
  370.0 140.1 all-reduce.3

commit v4 on v3

--- a/solution.py
+++ b/solution.py
@@ -107,7 +107,7 @@
         in_specs=[row_block(width), whole_block(gain.shape), whole_block(weights.shape), row_block(LANES), row_block(LANES)],
         out_specs=[pl.BlockSpec((width, TILE), lambda i: (0, i)), row_block(qw), row_block(kw), row_block(kw)],
         out_shape=[jax.ShapeDtypeStruct(s, BF16) for s in ((width, rows), (rows, qw), (rows, kw), (rows, kw))],
-        compiler_params=params(LESS_BYTES),
+        compiler_params=params(),
         cost_estimate=cost(2 * rows * width * (qw + 2 * kw), 12 * rows * width),
         name="project",
     )(tokens, gain, weights, cos, sin)
@@ -549,11 +549,13 @@
 
 
 def gather_kernel(size, count, *refs):
-    q_ref, k_ref, v_ref, s_ref, o_ref = refs[:5]
-    owned, refs = refs[5 : 5 + count], refs[5 + count :]
-    packed_ref, small_ref, out_ref, turned_ref = refs[:4]
-    beside, refs = refs[4 : 4 + 2 * count], refs[4 + 2 * count :]
-    send_sem, recv_sem, pass_sem, take_sem, away_sem, come_sem = refs
+    q_ref, k_ref, v_ref, s_ref, o_ref, d_ref = refs[:6]
+    owned, refs = refs[6 : 6 + count], refs[6 + count :]
+    packed_ref, small_ref, out_ref, down_ref, turned_ref = refs[:5]
+    beside, refs = refs[5 : 5 + 2 * count], refs[5 + 2 * count :]
+    beyond, refs = refs[: 2 * count], refs[2 * count :]
+    pair, refs = refs[: count + 1 if count else 0], refs[count + 1 if count else 0 :]
+    send_sem, recv_sem, pass_sem, take_sem, away_sem, come_sem, over_sem, land_sem = refs
     me, z = lax.axis_index("expert"), lax.axis_index("wshard")
     core = lax.rem(me, 2)
     sibling = me + 1 - 2 * core
@@ -588,12 +590,26 @@
     for copy in shipped:
         copy.start()
 
+    def passed(source, target, i, j):
+        return pltpu.make_async_remote_copy(
+            src_ref=source, dst_ref=target, send_sem=over_sem.at[i, j], recv_sem=land_sem.at[i, j],
+            device_id=(sibling, z), device_id_type=pl.DeviceIdType.MESH,
+        )
+
+    swapped = [passed(ref, target, i, 2) for i, (ref, target) in enumerate(zip(owned, pair))]
+
     own = pl.ds(pl.multiple_of(z * rows, rows), rows)
     at = 0
     for ref in (q_ref, k_ref, v_ref):
         packed_ref[own, at : at + ref.shape[1]] = ref[...]
         at += ref.shape[1]
     small_ref[own] = s_ref[...]
+    out_ref[...] = o_ref[...]
+    down_ref[...] = d_ref[...]
+    if count:
+        swapped.append(passed(down_ref, pair[count], count, 2))
+    for copy in swapped:
+        copy.start()
 
     def moves(way, hop, origin, which, device, send, recv):
         at = pl.ds(pl.multiple_of(origin * rows + which * half, half), half)
@@ -650,33 +666,43 @@
                 for move in onward(way, step, hop):
                     move.wait_send()
 
-    out_ref[...] = o_ref[...]
     turned_ref[...] = small_ref[...].T
+    onto = []
+    for n, copy in enumerate(shipped):
+        i, j = n // 2, n % 2
+        copy.wait_recv()
+        onto.append(passed(beside[j * count + i], beyond[j * count + i], i, j))
+        onto[-1].start()
     for copy in shipped:
+        copy.wait_send()
+    for copy in swapped + onto:
         copy.wait()
 
 
-def gather_weights(query, key, value, small, out, owned=()):
+def gather_weights(query, key, value, small, out, down, owned=()):
     size = lax.axis_size("wshard")
     rows = query.shape[0]
     width = query.shape[1] + key.shape[1] + value.shape[1]
     sems = pltpu.SemaphoreType.DMA((2, size + 1, 2))
+    last = [*owned, down] if len(owned) else []
     return pl.pallas_call(
         functools.partial(gather_kernel, size, len(owned)),
-        in_specs=[VMEM] * 5 + [ANY] * len(owned),
-        out_specs=[VMEM] * 4 + [ANY] * (2 * len(owned)),
+        in_specs=[VMEM] * 6 + [ANY] * len(owned),
+        out_specs=[VMEM] * 5 + [ANY] * (4 * len(owned) + len(last)),
         out_shape=[
             jax.ShapeDtypeStruct((size * rows, width), BF16),
             jax.ShapeDtypeStruct((size * rows, small.shape[1]), BF16),
             jax.ShapeDtypeStruct(out.shape, BF16),
+            jax.ShapeDtypeStruct(down.shape, BF16),
             jax.ShapeDtypeStruct((small.shape[1], size * rows), BF16),
         ]
-        + [jax.ShapeDtypeStruct(a.shape, BF16) for a in owned] * 2,
-        scratch_shapes=[sems, sems, sems, sems] + [pltpu.SemaphoreType.DMA((max(len(owned), 1), 2))] * 2,
+        + [jax.ShapeDtypeStruct(a.shape, BF16) for a in owned] * 4
+        + [jax.ShapeDtypeStruct(a.shape, BF16) for a in last],
+        scratch_shapes=[sems, sems, sems, sems] + [pltpu.SemaphoreType.DMA((len(owned) + 1, 3))] * 4,
         compiler_params=pltpu.CompilerParams(collective_id=0, has_side_effects=True, vmem_limit_bytes=VMEM_BYTES),
         cost_estimate=cost(1e9, 12 * rows * size * width),
         name="gather_weights",
-    )(query, key, value, small, out, *owned)
+    )(query, key, value, small, out, down, *owned)
 
 
 def reduce_kernel(size, columns, *refs):
@@ -878,28 +904,35 @@
 
     small = jnp.concatenate([w_router, gain_attn[:, None], gain_ffn[:, None]], axis=1)
     small = jnp.pad(small, ((0, 0), (0, LANES - small.shape[1])))
-    packed, small, out_shard, gains, *beside = gather_weights(
-        w_query, key_weight, value_weight, small, w_out, mats[:2] if owners == 8 else ()
+    packed, small, out_shard, down, gains, *beside = gather_weights(
+        w_query, key_weight, value_weight, small, w_out, mats[2], mats[:2] if owners == 8 else ()
     )
     out_w = lax.all_gather(out_shard, "wshard", axis=0, tiled=True)
     cos, sin = (jnp.asarray(a) for a in rope_tables(rows))
 
     if owners == 8:
         slots = {0: tuple([m] for m in mats)}
-        slots[2] = ([beside[0]], [beside[1]], [flip(mats[2], "expert", 2)])
-        slots[4] = ([beside[2]], [beside[3]], [flip(mats[2], "expert", 4)])
+        slots[2] = ([beside[0]], [beside[1]], [flip(down, "expert", 2)])
+        slots[4] = ([beside[2]], [beside[3]], [flip(down, "expert", 4)])
         slots[6] = third_slot(slots[2], slots[4])
     else:
         slots = gather_experts(mats, owners)
     normed_t, queries, keys, vals = project(tokens, gains, experts, packed, cos, sin)
-    def pieces_of(*which):
-        return [p for j in which for m in slots[j] for p in m] if owners == 8 else []
+    def pieces_of(*which, first=0, last=3):
+        return [p for j in which for m in slots[j][first:last] for p in m] if owners == 8 else []
 
     attended = attend(queries, keys, vals)
-    for j in sorted(slots):
-        slots[j | 1] = across_core(slots[j])
+    if owners == 8:
+        slots[1] = tuple([m] for m in beside[8:])
+        downs = lax.optimization_barrier((slots[2][2][0], slots[4][2][0], attended))
+        slots[3] = ([beside[4]], [beside[5]], [flip(downs[0], "expert", 1)])
+        slots[5] = ([beside[6]], [beside[7]], [flip(downs[1], "expert", 1)])
+        slots[7] = across_core(slots[6])
+    else:
+        for j in sorted(slots):
+            slots[j | 1] = across_core(slots[j])
     resid, moe_in, moe_in_t, gates = middle(
-        attended, out_w, tokens, gains, experts + 1, small, routes, pieces_of(2, 4, 3, 5, 1)
+        attended, out_w, tokens, gains, experts + 1, small, routes, pieces_of(2, 4)
     )
     dy_t = cotangent.T
 
@@ -917,9 +950,9 @@
         core = lambda halves: [flip(m, "expert", 1) for m in halves]
         over_x = lambda m: flip(m, "expert", 2)
         over_y = lambda m: flip(m, "expert", 4)
-        acc, g3 = one(3, None, pieces_of(6))
+        acc, g3 = one(3, None, pieces_of(6, last=2))
         c3 = core(g3)
-        acc, g2 = one(2, acc, pieces_of(7))
+        acc, g2 = one(2, acc, pieces_of(6))
         *s2, t2 = plus((g2[0], c3[0]), (g2[1], c3[1]))
         x20 = over_x(s2[0])
         acc, g7 = one(7, acc, [t2])

time: 536 us -> 523 us (0.976)
  Pallas kernels: 409 us -> 396 us
  local copies, waits for them, and re-layouts: 49.3 us -> 57.3 us
    unnamed x115 -> x147, local copies, waits for them, and re-layouts: 42.7 us -> 52.3 us
    pallas_call x1, Pallas kernels: 69.3 us -> 59.8 us  [gather_weights(): pl.pallas_call(functools.partial(gather_kernel, size, len(owned)), in_spe...]
    ppermute x33 -> x26, starting transfers between devices: 19.4 us -> 14.6 us  [flip(): return lax.ppermute(value, axis, [(i, i ^ bit) for i in range(size)])]
    ppermute x33 -> x26, waiting for transfers between devices: 23.2 us -> 20.9 us  [flip(): return lax.ppermute(value, axis, [(i, i ^ bit) for i in range(size)])]
  transfers between devices with their start and end apart: 35 -> 28, of which waited for: 7 -> 5; matrix products, arithmetic and copies ran while one was open for 3% -> 3% of each run, Pallas kernels for 73% -> 59%
where the time goes in v4:
time: 523 us; the launch traced here: 514 us
  Pallas kernels  396 us (76%)
  local copies, waits for them, and re-layouts  57.3 us (11%)
  waiting for transfers between devices  26.4 us (5%)
  between operations  14.9 us (3%)
  starting transfers between devices  14.6 us (3%)
    pallas_call x8, Pallas kernels, moe(): pl.pallas_call(functools.partial(moe_kernel, tuple(slots), chunks, first,...  99.6 us
    pallas_call x1, Pallas kernels, reduce_all(): pl.pallas_call(functools.partial(reduce_kernel, size, columns), in_specs=...  79 us
    pallas_call x2, Pallas kernels, attend_back(): pl.pallas_call(tied(attend_back_kernel, 6, ties), grid=(rows // SEQUENCE_...  61 us
    pallas_call x1, Pallas kernels, gather_weights(): pl.pallas_call(functools.partial(gather_kernel, size, len(owned)), in_spe...  59.8 us
    unnamed x147, local copies, waits for them, and re-layouts  52.3 us
    pallas_call x1, Pallas kernels, attend(): pl.pallas_call(tied(attend_kernel, 3, ties), grid=(rows // SEQUENCE_LENGT...  35.3 us
    ppermute x26, waiting for transfers between devices, flip(): return lax.ppermute(value, axis, [(i, i ^ bit) for i in range(size)])  20.9 us
    ppermute x26, starting transfers between devices, flip(): return lax.ppermute(value, axis, [(i, i ^ bit) for i in range(size)])  14.6 us
  transfers between devices with their start and end apart: 28, of which 5 were waited for; matrix products, arithmetic and copies ran while one was open for 3% of the time, Pallas kernels for 59%

profile of v4, /device:TPU:0, one launch (start us, length us, event | category | flops | bytes accessed | tf_op | source)
XLA Modules:
  0.0 513.6 jit_solution(7025774633126629528)
XLA Ops:
  10.0 59.8 %gather_weights.1 = (bf16[1024,2048]{1,0:T(8,128)(2,1)}, bf16[1024,128]{1,0:T(8,128)(2,1)}, bf16[256,1024]{1,0:T(8,128)(2,1)}, bf16[512,1024]{1,0:T(8,128)(2,1)}...) custom-call(bf16[256,1024]{1,0:T(8,128)(2,1)} %refs_0_.1, ...), custom_call_target="tpu_custom_call" | custom-call | flops 1000000000 | bytes 25165824 | tf_op jit(solution)/shard_map/gather_weights/pallas_call | solution.py:688
  74.1 9.1 %project.1 = (bf16[1024,1024]{1,0:T(8,128)(2,1)}, bf16[1024,1024]{1,0:T(8,128)(2,1)}, bf16[1024,512]{1,0:T(8,128)(2,1)}, bf16[1024,512]{1,0:T(8,128)(2,1)}) custom-call(bf16[1024,1024]{1,0:T(8,128)(2,1)} %refs_7_.1, bf16[128,1024]{1,0:T(8,128)(2,1)} %get-tuple-element.124.gain_ref.refs_3_.refs_6_.refs_9_, ...), custom_call_target="tpu_custom_call" | custom-call | flops 4294967296 | bytes 12582912 | tf_op jit(solution)/shard_map/project/pallas_call | solution.py:104
  83.2 35.3 %attend.1.refs_0_ = bf16[1024,1024]{1,0:T(8,128)(2,1)} custom-call(bf16[1024,1024]{1,0:T(8,128)(2,1)} %get-tuple-element.126.refs_0_, bf16[1024,512]{1,0:T(8,128)(2,1)} %get-tuple-element.127.refs_1_, bf16[1024,512]{1,0:T(8,128)(2,1)} %get-tuple-element.128.refs_2_), custom_call_target="tpu_custom_call" | custom-call | flops 34359738368 | bytes 6291456 | tf_op jit(solution)/shard_map/attend/pallas_call | solution.py:140
  119.7 4.1 copy.60
  133.8 5.3 %middle.1 = (f32[1024,1024]{1,0:T(8,128)S(1)}, bf16[1024,1024]{1,0:T(8,128)(2,1)S(1)}, bf16[1024,1024]{1,0:T(8,128)(2,1)S(1)}, f32[1024,128]{1,0:T(8,128)S(1)}) custom-call(bf16[1024,1024]{1,0:T(8,128)(2,1)S(1)} %copy-done.10, bf16[1024,1024]{1,0:T(8,128)(2,1)S(1)} %copy-done.2, bf16[1024,1024]{1,0:T(8,128)(2,1)S(1)} %copy-done, ...), custom_call_target="tpu_custom_call" | custom-call | flops 2415919104 | bytes 14680064 | tf_op jit(solution)/shard_map/middle/pallas_call | solution.py:227
  139.2 12.7 %experts.8 = (f32[1024,1024]{1,0:T(8,128)S(1)}, f32[1024,1024]{1,0:T(8,128)S(1)}, f32[1024,128]{1,0:T(8,128)S(1)}, bf16[3,512,512]{2,1,0:T(8,128)(2,1)S(1)}, bf16[3,512,512]{2,1,0:T(8,128)(2,1)S(1)}) custom-call(s32[1]{0:T(128)} %bitcast.3.me_ref, bf16[1024,1024]{1,0:T(8,128)(2,1)S(1)} %get-tuple-element.137.refs_0_, ...), custom_call_target="tpu_custom_call" | custom-call | flops 9663676416 | bytes 20971520 | tf_op jit(solution)/shard_map/experts/pallas_call | solution.py:349
  155.9 12.2 %collective-permute-done.5.refs_13_.refs_10_ = bf16[256,1024]{1,0:T(8,128)(2,1)} collective-permute-done((bf16[256,1024]{1,0:T(8,128)(2,1)S(1)}, bf16[256,1024]{1,0:T(8,128)(2,1)}, u32[]{:S(2)}, u32[]{:S(2)}) %collective-permute-start.5) | collective-permute-done | bytes 524320 | tf_op jit(solution)/shard_map/ppermute | solution.py:856
  171.6 12.1 %experts.9 = (f32[1024,1024]{1,0:T(8,128)S(1)}, f32[1024,1024]{1,0:T(8,128)S(1)}, f32[1024,128]{1,0:T(8,128)S(1)}, bf16[3,512,512]{2,1,0:T(8,128)(2,1)S(1)}, bf16[3,512,512]{2,1,0:T(8,128)(2,1)S(1)}) custom-call(s32[1]{0:T(128)} %bitcast.3.me_ref, bf16[1024,1024]{1,0:T(8,128)(2,1)S(1)} %copy-done.49, ...), custom_call_target="tpu_custom_call", output_to_operand_aliasing={{0}: (6, {}), {1}: (7, {}), {2}: (8, {})} | custom-call | flops 9663676416 | bytes 20971520 | tf_op jit(solution)/shard_map/experts/pallas_call | solution.py:349
  189.0 12.6 %experts.10 = (f32[1024,1024]{1,0:T(8,128)S(1)}, f32[1024,1024]{1,0:T(8,128)S(1)}, f32[1024,128]{1,0:T(8,128)S(1)}, bf16[3,512,512]{2,1,0:T(8,128)(2,1)S(1)}, bf16[3,512,512]{2,1,0:T(8,128)(2,1)S(1)}) custom-call(s32[1]{0:T(128)} %bitcast.3.me_ref, bf16[1024,1024]{1,0:T(8,128)(2,1)S(1)} %copy-done.49, ...), custom_call_target="tpu_custom_call", output_to_operand_aliasing={{0}: (6, {}), {1}: (7, {}), {2}: (8, {})} | custom-call | flops 9663676416 | bytes 20971520 | tf_op jit(solution)/shard_map/experts/pallas_call | solution.py:349
  203.8 13.0 %experts.11 = (f32[1024,1024]{1,0:T(8,128)S(1)}, f32[1024,1024]{1,0:T(8,128)S(1)}, f32[1024,128]{1,0:T(8,128)S(1)}, bf16[3,512,512]{2,1,0:T(8,128)(2,1)S(1)}, bf16[3,512,512]{2,1,0:T(8,128)(2,1)S(1)}) custom-call(s32[1]{0:T(128)} %bitcast.3.me_ref, bf16[1024,1024]{1,0:T(8,128)(2,1)S(1)} %copy-done.49, ...), custom_call_target="tpu_custom_call", output_to_operand_aliasing={{0}: (6, {}), {1}: (7, {}), {2}: (8, {})} | custom-call | flops 9663676416 | bytes 20971520 | tf_op jit(solution)/shard_map/experts/pallas_call | solution.py:349
  217.6 2.8 plus.7
  220.4 12.7 %experts.12 = (f32[1024,1024]{1,0:T(8,128)S(1)}, f32[1024,1024]{1,0:T(8,128)S(1)}, f32[1024,128]{1,0:T(8,128)S(1)}, bf16[3,512,512]{2,1,0:T(8,128)(2,1)}, bf16[3,512,512]{2,1,0:T(8,128)(2,1)}) custom-call(s32[1]{0:T(128)} %bitcast.3.me_ref, bf16[1024,1024]{1,0:T(8,128)(2,1)S(1)} %copy-done.49, ...), custom_call_target="tpu_custom_call", output_to_operand_aliasing={{0}: (6, {}), {1}: (7, {}), {2}: (8, {})} | custom-call | flops 9663676416 | bytes 20971520 | tf_op jit(solution)/shard_map/experts/pallas_call | solution.py:349
  235.8 3.9 collective-permute-done.16.refs_11_.refs_1_
  239.7 1.8 copy-done.33
  242.7 12.1 %experts.13 = (f32[1024,1024]{1,0:T(8,128)S(1)}, f32[1024,1024]{1,0:T(8,128)S(1)}, f32[1024,128]{1,0:T(8,128)S(1)}, bf16[3,512,512]{2,1,0:T(8,128)(2,1)S(1)}, bf16[3,512,512]{2,1,0:T(8,128)(2,1)S(1)}) custom-call(s32[1]{0:T(128)} %bitcast.3.me_ref, bf16[1024,1024]{1,0:T(8,128)(2,1)S(1)} %copy-done.49, ...), custom_call_target="tpu_custom_call", output_to_operand_aliasing={{0}: (6, {}), {1}: (7, {}), {2}: (8, {})} | custom-call | flops 9663676416 | bytes 20971520 | tf_op jit(solution)/shard_map/experts/pallas_call | solution.py:349
  254.9 2.5 plus.8
  262.2 12.3 %experts.14 = (f32[1024,1024]{1,0:T(8,128)S(1)}, f32[1024,1024]{1,0:T(8,128)S(1)}, f32[1024,128]{1,0:T(8,128)S(1)}, bf16[3,512,512]{2,1,0:T(8,128)(2,1)S(1)}, bf16[3,512,512]{2,1,0:T(8,128)(2,1)S(1)}) custom-call(s32[1]{0:T(128)} %bitcast.3.me_ref, bf16[1024,1024]{1,0:T(8,128)(2,1)S(1)} %copy-done.49, ...), custom_call_target="tpu_custom_call", output_to_operand_aliasing={{0}: (6, {}), {1}: (7, {}), {2}: (8, {})} | custom-call | flops 9663676416 | bytes 20971520 | tf_op jit(solution)/shard_map/experts/pallas_call | solution.py:349
  276.6 2.8 plus.9
  283.5 12.1 %experts.15 = (f32[1024,1024]{1,0:T(8,128)S(1)}, f32[1024,1024]{1,0:T(8,128)S(1)}, f32[1024,128]{1,0:T(8,128)S(1)}, bf16[3,512,512]{2,1,0:T(8,128)(2,1)S(1)}, bf16[3,512,512]{2,1,0:T(8,128)(2,1)S(1)}) custom-call(s32[1]{0:T(128)} %bitcast.3.me_ref, bf16[1024,1024]{1,0:T(8,128)(2,1)S(1)} %copy-done.50, ...), custom_call_target="tpu_custom_call", output_to_operand_aliasing={{0}: (6, {}), {1}: (7, {}), {2}: (8, {})} | custom-call | flops 9663676416 | bytes 20971520 | tf_op jit(solution)/shard_map/experts/pallas_call | solution.py:349
  295.7 2.0 copy-done.7
  298.9 2.2 copy-done.24
  304.3 7.6 %turn.1 = (bf16[1024,1024]{1,0:T(8,128)(2,1)}, f32[1024,1024]{1,0:T(8,128)S(1)}, bf16[1024,1024]{1,0:T(8,128)(2,1)S(1)}, bf16[1024,1024]{1,0:T(8,128)(2,1)S(1)},...) custom-call(f32[1024,1024]{1,0:T(8,128)S(1)} %get-tuple-element.136.refs_0_, f32[1024,1024]{1,0:T(8,128)} %copy-done.6, ...), custom_call_target="tpu_custom_call" | custom-call | flops 2684354560 | bytes 29360128 | tf_op jit(solution)/shard_map/turn/pallas_call | solution.py:402
  312.0 3.7 convolution_convert_fusion.refs_6_
  315.7 30.7 %attend_back.2 = (bf16[1024,512]{1,0:T(8,128)(2,1)}, bf16[1024,256]{1,0:T(8,128)(2,1)}, bf16[1024,256]{1,0:T(8,128)(2,1)}) custom-call(bf16[1024,1024]{1,0:T(8,128)(2,1)} %get-tuple-element.126.refs_0_, bf16[1024,512]{1,0:T(8,128)(2,1)} %get-tuple-element.127.refs_1_, bf16[1024,512]{1,0:T(8,128)(2,1)} %get-tuple-element.128.refs_2_, ...), custom_call_target="tpu_custom_call" | custom-call | flops 42949672960 | bytes 12582912 | tf_op jit(solution)/shard_map/attend_back/pallas_call | solution.py:190
  346.5 3.3 collective-permute-done.24.refs_4_
  352.3 4.3 plus.11
  359.5 30.3 %attend_back.3 = (bf16[1024,512]{1,0:T(8,128)(2,1)}, bf16[1024,256]{1,0:T(8,128)(2,1)}, bf16[1024,256]{1,0:T(8,128)(2,1)}) custom-call(bf16[1024,1024]{1,0:T(8,128)(2,1)} %get-tuple-element.126.refs_0_, bf16[1024,512]{1,0:T(8,128)(2,1)} %get-tuple-element.127.refs_1_, bf16[1024,512]{1,0:T(8,128)(2,1)} %get-tuple-element.128.refs_2_, ...), custom_call_target="tpu_custom_call" | custom-call | flops 42949672960 | bytes 12582912 | tf_op jit(solution)/shard_map/attend_back/pallas_call | solution.py:190
  389.8 8.3 %weights_back.1 = (bf16[1024,512]{1,0:T(8,128)(2,1)}, bf16[1024,512]{1,0:T(8,128)(2,1)}, bf16[1024,256]{1,0:T(8,128)(2,1)}, bf16[1024,256]{1,0:T(8,128)(2,1)}, b...) custom-call(bf16[1024,1024]{1,0:T(8,128)(2,1)} %get-tuple-element.218.refs_0_, ...), custom_call_target="tpu_custom_call" | custom-call | flops 1 | bytes 1 | tf_op jit(solution)/shard_map/weights_back/pallas_call | solution.py:477
  398.1 11.6 %finish.1 = (f32[1024,1024]{1,0:T(8,128)}, bf16[1024,128]{1,0:T(8,128)(2,1)}) custom-call(bf16[1024,512]{1,0:T(8,128)(2,1)} %get-tuple-element.202.refs_0_.refs_1_, bf16[1024,512]{1,0:T(8,128)(2,1)} %get-tuple-element.210.refs_1_.refs_2_, bf16[1024,256]{1,0:T(8,128)(2,1)} %get-tuple-element.211.refs_2_.refs_3_, ...), custom_call_target="tpu_custom_call" | custom-call | flops 1 | bytes 1 | tf_op jit(solution)/shard_map/finish/pallas_call | solution.py:454
  409.7 79.0 %reduce_all.1 = (f32[256,1024]{1,0:T(8,128)}, f32[256,1024]{1,0:T(8,128)}, f32[256,512]{1,0:T(8,128)}, f32[256,512]{1,0:T(8,128)}, f32[256,128]{1,0:T(8,128)}) custom-call(bf16[4,256,1024]{2,1,0:T(8,128)(2,1)} %bitcast.33, bf16[4,256,512]{2,1,0:T(8,128)(2,1)} %bitcast.35, bf16[4,256,512]{2,1,0:T(8,128)(2,1)} %bitcast.36, bf16[4,256,256]{2,1,0:T(8,128)(2,1)} %bitcast.37, ...), custom_call_target="tpu_custom_call" | custom-call | flops 1 | bytes 1 | tf_op jit(solution)/shard_map/reduce_all/pallas_call | solution.py:832
  492.2 5.5 %all-reduce.4.cloned.1.call-done = (bf16[3,512,512]{2,1,0:T(8,128)(2,1)}, bf16[3,512,512]{2,1,0:T(8,128)(2,1)}) async-done(((bf16[3,512,512]{2,1,0:T(8,128)(2,1)}, bf16[3,512,512]{2,1,0:T(8,128)(2,1)}), (bf16[3,512,512]{2,1,0:T(8,128)(2,1)}, bf16[3,512,512]{2,1,0:T(8,128)(2,1)})) %all-reduce.4.cloned.1.call-update) | async-done | bytes 3145744 | tf_op jit(solution)/shard_map/psum | solution.py:979
  497.6 5.3 %widen.1 = (f32[1024,512]{1,0:T(8,128)}, f32[1024,512]{1,0:T(8,128)}, f32[512,1024]{1,0:T(8,128)}) custom-call(bf16[3,512,512]{2,1,0:T(8,128)(2,1)} %get-tuple-element.274.top_ref, bf16[3,512,512]{2,1,0:T(8,128)(2,1)} %get-tuple-element.275.bottom_ref), custom_call_target="tpu_custom_call" | custom-call | flops 1 | bytes 1 | tf_op jit(solution)/shard_map/widen/pallas_call | solution.py:504
  (207 shorter events, 65.7 us)
Async XLA Ops:
  7.2 116.6 %all-gather.2.cloned.1.call-start = ((), (), s32[]{:S(2)}) async-start(), calls=%async_computation | async-start | bytes 2621440 | tf_op jit(solution)/shard_map/all_gather | solution.py:910
  69.8 48.7 %collective-permute-start = (bf16[512,1024]{1,0:T(8,128)(2,1)}, bf16[512,1024]{1,0:T(8,128)(2,1)}, u32[]{:S(2)}, u32[]{:S(2)}) collective-permute-start(bf16[512,1024]{1,0:T(8,128)(2,1)} %get-tuple-element.133), channel_id=1, source_target_pairs={{0,8},{4,12},{8,0},{12,4},{16,24},{20,28},{24,16},{28,20},{1,9},{5... | collective-permute-start | bytes 3145736 | tf_op jit(solution)/shard_map/ppermute | solution.py:856
  70.5 48.1 %collective-permute-start.1 = (bf16[512,1024]{1,0:T(8,128)(2,1)}, bf16[512,1024]{1,0:T(8,128)(2,1)S(1)}, u32[]{:S(2)}, u32[]{:S(2)}) collective-permute-start(bf16[512,1024]{1,0:T(8,128)(2,1)} %get-tuple-element.133), channel_id=1, source_target_pairs={{0,16},{4,20},{8,24},{12,28},{16,0},{20,4},{24,8},{28,12},{1,17},{... | collective-permute-start | bytes 3145736 | tf_op jit(solution)/shard_map/ppermute | solution.py:856
  72.0 425.6 %all-reduce.4.cloned.1.call-start = ((), (), s32[]{:S(2)}) async-start(), calls=%async_computation.1 | async-start | bytes 6291456 | tf_op jit(solution)/shard_map/psum | solution.py:979
  72.0 67.1 %collective-permute-start.3 = (bf16[1024,512]{1,0:T(8,128)(2,1)}, bf16[1024,512]{1,0:T(8,128)(2,1)}, u32[]{:S(2)}, u32[]{:S(2)}) collective-permute-start(bf16[1024,512]{1,0:T(8,128)(2,1)} %get-tuple-element.131.refs_6_.refs_8_), channel_id=1, source_target_pairs={{0,16},{4,20},{8,24},{12,28},{16,0},{20,4},{24,8},{28,12},{1,17},{... | collective-permute-start | bytes 3145736 | tf_op jit(solution)/shard_map/ppermute | solution.py:856
  72.6 66.5 %collective-permute-start.4 = (bf16[1024,512]{1,0:T(8,128)(2,1)}, bf16[1024,512]{1,0:T(8,128)(2,1)}, u32[]{:S(2)}, u32[]{:S(2)}) collective-permute-start(bf16[1024,512]{1,0:T(8,128)(2,1)} %get-tuple-element.135.refs_10_.refs_9_), channel_id=1, source_target_pairs={{0,8},{4,12},{8,0},{12,4},{16,24},{20,28},{24,16},{28,20},{1,9},{5... | collective-permute-start | bytes 3145736 | tf_op jit(solution)/shard_map/ppermute | solution.py:856
  83.2 35.4 %copy-start.69 = (s32[1024,4]{0,1:T(4,128)S(1)}, s32[1024,4]{0,1:T(4,128)}, u32[]{:S(2)}) copy-start(s32[1024,4]{0,1:T(4,128)} %param.26) | copy-start | bytes 49156
  118.5 20.6 %collective-permute-start.2 = (bf16[512,1024]{1,0:T(8,128)(2,1)}, bf16[512,1024]{1,0:T(8,128)(2,1)}, u32[]{:S(2)}, u32[]{:S(2)}) collective-permute-start(bf16[512,1024]{1,0:T(8,128)(2,1)} %collective-permute-done.refs_8_.refs_10_), channel_id=1, source_target_pairs={{0,4},{4,0},{8,12},{12,8},{16,20},{20,16},{24,28},{28,24},{1,5},{5... | collective-permute-start | bytes 3145736 | tf_op jit(solution)/shard_map/ppermute | solution.py:856
  139.1 47.4 %copy-start.40 = (f32[1024,128]{1,0:T(8,128)}, f32[1024,128]{1,0:T(8,128)S(1)}, u32[]{:S(2)}) copy-start(f32[1024,128]{1,0:T(8,128)S(1)} %get-tuple-element.139.refs_4_.refs_3_) | copy-start | bytes 1572868
  139.1 142.8 %copy-start.12 = (bf16[1024,1024]{1,0:T(8,128)(2,1)}, bf16[1024,1024]{1,0:T(8,128)(2,1)S(1)}, u32[]{:S(2)}) copy-start(bf16[1024,1024]{1,0:T(8,128)(2,1)S(1)} %get-tuple-element.138.refs_1_.refs_8_) | copy-start | bytes 6291460
  151.9 17.5 %collective-permute-start.11 = (bf16[3,512,512]{2,1,0:T(8,128)(2,1)S(1)}, bf16[3,512,512]{2,1,0:T(8,128)(2,1)S(1)}, u32[]{:S(2)}, u32[]{:S(2)}) collective-permute-start(bf16[3,512,512]{2,1,0:T(8,128)(2,1)S(1)} %get-tuple-element.150), channel_id=1, source_target_pairs={{0,4},{4,0},{8,12},{12,8},{16,20},{20,16},{24,28},{28,24},{1,5},{5... | collective-permute-start | bytes 4718600 | tf_op jit(solution)/shard_map/ppermute | solution.py:856
  152.5 31.2 %collective-permute-start.12 = (bf16[3,512,512]{2,1,0:T(8,128)(2,1)S(1)}, bf16[3,512,512]{2,1,0:T(8,128)(2,1)S(1)}, u32[]{:S(2)}, u32[]{:S(2)}) collective-permute-start(bf16[3,512,512]{2,1,0:T(8,128)(2,1)S(1)} %get-tuple-element.152), channel_id=1, source_target_pairs={{0,4},{4,0},{8,12},{12,8},{16,20},{20,16},{24,28},{28,24},{1,5},{5... | collective-permute-start | bytes 4718600 | tf_op jit(solution)/shard_map/ppermute | solution.py:856
  153.6 14.5 %collective-permute-start.5 = (bf16[256,1024]{1,0:T(8,128)(2,1)S(1)}, bf16[256,1024]{1,0:T(8,128)(2,1)}, u32[]{:S(2)}, u32[]{:S(2)}) collective-permute-start(bf16[256,1024]{1,0:T(8,128)(2,1)S(1)} %slice.20), channel_id=1, source_target_pairs={{0,16},{4,20},{8,24},{12,28},{16,0},{20,4},{24,8},{28,12},{1,17},{... | collective-permute-start | bytes 1572872 | tf_op jit(solution)/shard_map/ppermute | solution.py:856
  155.3 14.2 %collective-permute-start.6 = (bf16[256,1024]{1,0:T(8,128)(2,1)S(1)}, bf16[256,1024]{1,0:T(8,128)(2,1)}, u32[]{:S(2)}, u32[]{:S(2)}) collective-permute-start(bf16[256,1024]{1,0:T(8,128)(2,1)S(1)} %slice.21), channel_id=1, source_target_pairs={{0,8},{4,12},{8,0},{12,4},{16,24},{20,28},{24,16},{28,20},{1,9},{5... | collective-permute-start | bytes 1572872 | tf_op jit(solution)/shard_map/ppermute | solution.py:856
  155.8 28.7 %collective-permute-start.7 = (bf16[1024,512]{1,0:T(8,128)(2,1)}, bf16[1024,512]{1,0:T(8,128)(2,1)S(1)}, u32[]{:S(2)}, u32[]{:S(2)}) collective-permute-start(bf16[1024,512]{1,0:T(8,128)(2,1)} %collective-permute-done.3.refs_8_.refs_11_), channel_id=1, source_target_pairs={{0,4},{4,0},{8,12},{12,8},{16,20},{20,16},{24,28},{28,24},{1,5},{5... | collective-permute-start | bytes 3145736 | tf_op jit(solution)/shard_map/ppermute | solution.py:856
  168.1 17.4 %collective-permute-start.8 = (bf16[1024,512]{1,0:T(8,128)(2,1)}, bf16[1024,512]{1,0:T(8,128)(2,1)S(1)}, u32[]{:S(2)}, u32[]{:S(2)}) collective-permute-start(bf16[1024,512]{1,0:T(8,128)(2,1)} %collective-permute-done.4.refs_9_.refs_12_), channel_id=1, source_target_pairs={{0,4},{4,0},{8,12},{12,8},{16,20},{20,16},{24,28},{28,24},{1,5},{5... | collective-permute-start | bytes 3145736 | tf_op jit(solution)/shard_map/ppermute | solution.py:856
  169.5 17.1 %collective-permute-start.9 = (bf16[256,1024]{1,0:T(8,128)(2,1)}, bf16[256,1024]{1,0:T(8,128)(2,1)}, u32[]{:S(2)}, u32[]{:S(2)}) collective-permute-start(bf16[256,1024]{1,0:T(8,128)(2,1)} %collective-permute-done.5.refs_13_.refs_10_), channel_id=1, source_target_pairs={{0,4},{4,0},{8,12},{12,8},{16,20},{20,16},{24,28},{28,24},{1,5},{5... | collective-permute-start | bytes 1572872 | tf_op jit(solution)/shard_map/ppermute | solution.py:856
  169.5 17.1 %collective-permute-start.10 = (bf16[256,1024]{1,0:T(8,128)(2,1)}, bf16[256,1024]{1,0:T(8,128)(2,1)}, u32[]{:S(2)}, u32[]{:S(2)}) collective-permute-start(bf16[256,1024]{1,0:T(8,128)(2,1)} %collective-permute-done.6.refs_14_.refs_11_), channel_id=1, source_target_pairs={{0,4},{4,0},{8,12},{12,8},{16,20},{20,16},{24,28},{28,24},{1,5},{5... | collective-permute-start | bytes 1572872 | tf_op jit(solution)/shard_map/ppermute | solution.py:856
  201.6 16.0 %collective-permute-start.14 = (bf16[3,512,512]{2,1,0:T(8,128)(2,1)S(1)}, bf16[3,512,512]{2,1,0:T(8,128)(2,1)S(1)}, u32[]{:S(2)}, u32[]{:S(2)}) collective-permute-start(bf16[3,512,512]{2,1,0:T(8,128)(2,1)S(1)} %get-tuple-element.164), channel_id=1, source_target_pairs={{0,4},{4,0},{8,12},{12,8},{16,20},{20,16},{24,28},{28,24},{1,5},{5... | collective-permute-start | bytes 4718600 | tf_op jit(solution)/shard_map/ppermute | solution.py:856
  201.7 15.9 %collective-permute-start.15 = (bf16[3,512,512]{2,1,0:T(8,128)(2,1)S(1)}, bf16[3,512,512]{2,1,0:T(8,128)(2,1)S(1)}, u32[]{:S(2)}, u32[]{:S(2)}) collective-permute-start(bf16[3,512,512]{2,1,0:T(8,128)(2,1)S(1)} %get-tuple-element.166), channel_id=1, source_target_pairs={{0,4},{4,0},{8,12},{12,8},{16,20},{20,16},{24,28},{28,24},{1,5},{5... | collective-permute-start | bytes 4718600 | tf_op jit(solution)/shard_map/ppermute | solution.py:856
  202.2 18.2 %collective-permute-start.13 = (bf16[512,1024]{1,0:T(8,128)(2,1)S(1)}, bf16[512,1024]{1,0:T(8,128)(2,1)}, u32[]{:S(2)}, u32[]{:S(2)}) collective-permute-start(bf16[512,1024]{1,0:T(8,128)(2,1)S(1)} %collective-permute-done.1.refs_11_.refs_10_), channel_id=1, source_target_pairs={{0,4},{4,0},{8,12},{12,8},{16,20},{20,16},{24,28},{28,24},{1,5},{5... | collective-permute-start | bytes 3145736 | tf_op jit(solution)/shard_map/ppermute | solution.py:856
  202.2 37.4 %collective-permute-start.16 = (bf16[3,512,512]{2,1,0:T(8,128)(2,1)}, bf16[3,512,512]{2,1,0:T(8,128)(2,1)S(1)}, u32[]{:S(2)}, u32[]{:S(2)}) collective-permute-start(bf16[3,512,512]{2,1,0:T(8,128)(2,1)} %copy-done.52), channel_id=1, source_target_pairs={{0,8},{4,12},{8,0},{12,4},{16,24},{20,28},{24,16},{28,20},{1,9},{5... | collective-permute-start | bytes 4718600 | tf_op jit(solution)/shard_map/ppermute | solution.py:856
  233.1 21.8 %collective-permute-start.17 = (bf16[3,512,512]{2,1,0:T(8,128)(2,1)}, bf16[3,512,512]{2,1,0:T(8,128)(2,1)S(1)}, u32[]{:S(2)}, u32[]{:S(2)}) collective-permute-start(bf16[3,512,512]{2,1,0:T(8,128)(2,1)} %get-tuple-element.179), channel_id=1, source_target_pairs={{0,4},{4,0},{8,12},{12,8},{16,20},{20,16},{24,28},{28,24},{1,5},{5... | collective-permute-start | bytes 4718600 | tf_op jit(solution)/shard_map/ppermute | solution.py:856
  233.3 21.6 %collective-permute-start.18 = (bf16[3,512,512]{2,1,0:T(8,128)(2,1)}, bf16[3,512,512]{2,1,0:T(8,128)(2,1)S(1)}, u32[]{:S(2)}, u32[]{:S(2)}) collective-permute-start(bf16[3,512,512]{2,1,0:T(8,128)(2,1)} %get-tuple-element.181), channel_id=1, source_target_pairs={{0,4},{4,0},{8,12},{12,8},{16,20},{20,16},{24,28},{28,24},{1,5},{5... | collective-permute-start | bytes 4718600 | tf_op jit(solution)/shard_map/ppermute | solution.py:856
  233.6 41.5 %collective-permute-start.19 = (bf16[3,512,512]{2,1,0:T(8,128)(2,1)}, bf16[3,512,512]{2,1,0:T(8,128)(2,1)S(1)}, u32[]{:S(2)}, u32[]{:S(2)}) collective-permute-start(bf16[3,512,512]{2,1,0:T(8,128)(2,1)} %get-tuple-element.187), channel_id=1, source_target_pairs={{0,8},{4,12},{8,0},{12,4},{16,24},{20,28},{24,16},{28,20},{1,9},{5... | collective-permute-start | bytes 4718600 | tf_op jit(solution)/shard_map/ppermute | solution.py:856
  235.2 40.0 %collective-permute-start.20 = (bf16[3,512,512]{2,1,0:T(8,128)(2,1)}, bf16[3,512,512]{2,1,0:T(8,128)(2,1)S(1)}, u32[]{:S(2)}, u32[]{:S(2)}) collective-permute-start(bf16[3,512,512]{2,1,0:T(8,128)(2,1)} %get-tuple-element.189), channel_id=1, source_target_pairs={{0,16},{4,20},{8,24},{12,28},{16,0},{20,4},{24,8},{28,12},{1,17},{... | collective-permute-start | bytes 4718600 | tf_op jit(solution)/shard_map/ppermute | solution.py:856
  274.6 23.1 %collective-permute-start.21 = (bf16[3,512,512]{2,1,0:T(8,128)(2,1)S(1)}, bf16[3,512,512]{2,1,0:T(8,128)(2,1)S(1)}, u32[]{:S(2)}, u32[]{:S(2)}) collective-permute-start(bf16[3,512,512]{2,1,0:T(8,128)(2,1)S(1)} %get-tuple-element.195), channel_id=1, source_target_pairs={{0,4},{4,0},{8,12},{12,8},{16,20},{20,16},{24,28},{28,24},{1,5},{5... | collective-permute-start | bytes 4718600 | tf_op jit(solution)/shard_map/ppermute | solution.py:856
  274.7 23.0 %collective-permute-start.22 = (bf16[3,512,512]{2,1,0:T(8,128)(2,1)S(1)}, bf16[3,512,512]{2,1,0:T(8,128)(2,1)S(1)}, u32[]{:S(2)}, u32[]{:S(2)}) collective-permute-start(bf16[3,512,512]{2,1,0:T(8,128)(2,1)S(1)} %get-tuple-element.197), channel_id=1, source_target_pairs={{0,4},{4,0},{8,12},{12,8},{16,20},{20,16},{24,28},{28,24},{1,5},{5... | collective-permute-start | bytes 4718600 | tf_op jit(solution)/shard_map/ppermute | solution.py:856
  279.4 67.1 %collective-permute-start.23 = (bf16[3,512,512]{2,1,0:T(8,128)(2,1)}, bf16[3,512,512]{2,1,0:T(8,128)(2,1)}, u32[]{:S(2)}, u32[]{:S(2)}) collective-permute-start(bf16[3,512,512]{2,1,0:T(8,128)(2,1)} %get-tuple-element.204), channel_id=1, source_target_pairs={{0,16},{4,20},{8,24},{12,28},{16,0},{20,4},{24,8},{28,12},{1,17},{... | collective-permute-start | bytes 4718600 | tf_op jit(solution)/shard_map/ppermute | solution.py:856
  280.0 69.8 %collective-permute-start.24 = (bf16[3,512,512]{2,1,0:T(8,128)(2,1)}, bf16[3,512,512]{2,1,0:T(8,128)(2,1)}, u32[]{:S(2)}, u32[]{:S(2)}) collective-permute-start(bf16[3,512,512]{2,1,0:T(8,128)(2,1)} %get-tuple-element.206), channel_id=1, source_target_pairs={{0,16},{4,20},{8,24},{12,28},{16,0},{20,4},{24,8},{28,12},{1,17},{... | collective-permute-start | bytes 4718600 | tf_op jit(solution)/shard_map/ppermute | solution.py:856
  281.4 68.4 %collective-permute-start.25 = (bf16[3,512,512]{2,1,0:T(8,128)(2,1)}, bf16[3,512,512]{2,1,0:T(8,128)(2,1)}, u32[]{:S(2)}, u32[]{:S(2)}) collective-permute-start(bf16[3,512,512]{2,1,0:T(8,128)(2,1)} %get-tuple-element.207), channel_id=1, source_target_pairs={{0,8},{4,12},{8,0},{12,4},{16,24},{20,28},{24,16},{28,20},{1,9},{5... | collective-permute-start | bytes 4718600 | tf_op jit(solution)/shard_map/ppermute | solution.py:856
  315.7 34.1 %copy-start.16 = (bf16[3,512,512]{2,1,0:T(8,128)(2,1)S(1)}, bf16[3,512,512]{2,1,0:T(8,128)(2,1)}, u32[]{:S(2)}) copy-start(bf16[3,512,512]{2,1,0:T(8,128)(2,1)} %copy-done.15) | copy-start | bytes 4718596
  (66 other events, 278.9 us)
Sparse Core Ops, SparseCore 0:
  72.1 46.0 all-gather.1
  359.6 137.9 all-reduce.3

commit v5 on v4

--- a/solution.py
+++ b/solution.py
@@ -950,9 +950,9 @@
         core = lambda halves: [flip(m, "expert", 1) for m in halves]
         over_x = lambda m: flip(m, "expert", 2)
         over_y = lambda m: flip(m, "expert", 4)
-        acc, g3 = one(3, None, pieces_of(6, last=2))
+        acc, g3 = one(3, None, pieces_of(6))
         c3 = core(g3)
-        acc, g2 = one(2, acc, pieces_of(6))
+        acc, g2 = one(2, acc)
         *s2, t2 = plus((g2[0], c3[0]), (g2[1], c3[1]))
         x20 = over_x(s2[0])
         acc, g7 = one(7, acc, [t2])

time: 523 us -> 519 us (level)
  waiting for transfers between devices: 26.4 us -> 11.6 us
    ppermute x26, waiting for transfers between devices: 20.9 us -> 6.26 us  [flip(): return lax.ppermute(value, axis, [(i, i ^ bit) for i in range(size)])]
    unnamed x147 -> x155, local copies, waits for them, and re-layouts: 52.3 us -> 55.5 us
  transfers between devices with their start and end apart: 28 -> 28, of which waited for: 5 -> 6; matrix products, arithmetic and copies ran while one was open for 3% -> 3% of each run, Pallas kernels for 59% -> 60%
where the time goes in v5:
time: 519 us; the launch traced here: 510 us
  Pallas kernels  401 us (77%)
  local copies, waits for them, and re-layouts  62.1 us (12%)
  starting transfers between devices  15.8 us (3%)
  between operations  14.9 us (3%)
  waiting for transfers between devices  11.6 us (2%)
    pallas_call x8, Pallas kernels, moe(): pl.pallas_call(functools.partial(moe_kernel, tuple(slots), chunks, first,...  101 us
    pallas_call x1, Pallas kernels, reduce_all(): pl.pallas_call(functools.partial(reduce_kernel, size, columns), in_specs=...  80.7 us
    pallas_call x2, Pallas kernels, attend_back(): pl.pallas_call(tied(attend_back_kernel, 6, ties), grid=(rows // SEQUENCE_...  61 us
    pallas_call x1, Pallas kernels, gather_weights(): pl.pallas_call(functools.partial(gather_kernel, size, len(owned)), in_spe...  59.7 us
    unnamed x155, local copies, waits for them, and re-layouts  55.5 us
    pallas_call x1, Pallas kernels, attend(): pl.pallas_call(tied(attend_kernel, 3, ties), grid=(rows // SEQUENCE_LENGT...  35.3 us
    ppermute x26, starting transfers between devices, flip(): return lax.ppermute(value, axis, [(i, i ^ bit) for i in range(size)])  15.8 us
    pallas_call x6, Pallas kernels, plus(): pl.pallas_call(tied(functools.partial(plus_kernel, counts), len(flat), ti...  15.5 us
  transfers between devices with their start and end apart: 28, of which 6 were waited for; matrix products, arithmetic and copies ran while one was open for 3% of the time, Pallas kernels for 60%

profile of v5, /device:TPU:0, one launch (start us, length us, event | category | flops | bytes accessed | tf_op | source)
XLA Modules:
  0.0 509.6 jit_solution(13056017195326556635)
XLA Ops:
  10.0 59.7 %gather_weights.1 = (bf16[1024,2048]{1,0:T(8,128)(2,1)}, bf16[1024,128]{1,0:T(8,128)(2,1)}, bf16[256,1024]{1,0:T(8,128)(2,1)}, bf16[512,1024]{1,0:T(8,128)(2,1)}...) custom-call(bf16[256,1024]{1,0:T(8,128)(2,1)} %refs_0_.1, ...), custom_call_target="tpu_custom_call" | custom-call | flops 1000000000 | bytes 25165824 | tf_op jit(solution)/shard_map/gather_weights/pallas_call | solution.py:688
  74.0 9.1 %project.1 = (bf16[1024,1024]{1,0:T(8,128)(2,1)}, bf16[1024,1024]{1,0:T(8,128)(2,1)}, bf16[1024,512]{1,0:T(8,128)(2,1)}, bf16[1024,512]{1,0:T(8,128)(2,1)}) custom-call(bf16[1024,1024]{1,0:T(8,128)(2,1)} %refs_7_.1, bf16[128,1024]{1,0:T(8,128)(2,1)} %get-tuple-element.124.gain_ref.refs_3_.refs_6_.refs_9_, ...), custom_call_target="tpu_custom_call" | custom-call | flops 4294967296 | bytes 12582912 | tf_op jit(solution)/shard_map/project/pallas_call | solution.py:104
  83.1 35.3 %attend.1.refs_0_ = bf16[1024,1024]{1,0:T(8,128)(2,1)} custom-call(bf16[1024,1024]{1,0:T(8,128)(2,1)} %get-tuple-element.126.refs_0_, bf16[1024,512]{1,0:T(8,128)(2,1)} %get-tuple-element.127.refs_1_, bf16[1024,512]{1,0:T(8,128)(2,1)} %get-tuple-element.128.refs_2_), custom_call_target="tpu_custom_call" | custom-call | flops 34359738368 | bytes 6291456 | tf_op jit(solution)/shard_map/attend/pallas_call | solution.py:140
  124.3 4.1 copy.60
  138.5 5.3 %middle.1 = (f32[1024,1024]{1,0:T(8,128)S(1)}, bf16[1024,1024]{1,0:T(8,128)(2,1)S(1)}, bf16[1024,1024]{1,0:T(8,128)(2,1)S(1)}, f32[1024,128]{1,0:T(8,128)S(1)}) custom-call(bf16[1024,1024]{1,0:T(8,128)(2,1)S(1)} %copy-done.10, bf16[1024,1024]{1,0:T(8,128)(2,1)S(1)} %copy-done.2, bf16[1024,1024]{1,0:T(8,128)(2,1)S(1)} %copy-done, ...), custom_call_target="tpu_custom_call" | custom-call | flops 2415919104 | bytes 14680064 | tf_op jit(solution)/shard_map/middle/pallas_call | solution.py:227
  143.9 2.0 copy-done.59
  146.0 12.2 %experts.8 = (f32[1024,1024]{1,0:T(8,128)S(1)}, f32[1024,1024]{1,0:T(8,128)S(1)}, f32[1024,128]{1,0:T(8,128)S(1)}, bf16[3,512,512]{2,1,0:T(8,128)(2,1)S(1)}, bf16[3,512,512]{2,1,0:T(8,128)(2,1)S(1)}) custom-call(s32[1]{0:T(128)} %bitcast.3.me_ref, bf16[1024,1024]{1,0:T(8,128)(2,1)S(1)} %get-tuple-element.137.refs_0_, ...), custom_call_target="tpu_custom_call" | custom-call | flops 9663676416 | bytes 20971520 | tf_op jit(solution)/shard_map/experts/pallas_call | solution.py:349
  159.3 2.3 collective-permute-done.11.refs_1_
  163.4 12.3 %experts.9 = (f32[1024,1024]{1,0:T(8,128)S(1)}, f32[1024,1024]{1,0:T(8,128)S(1)}, f32[1024,128]{1,0:T(8,128)S(1)}, bf16[3,512,512]{2,1,0:T(8,128)(2,1)S(1)}, bf16[3,512,512]{2,1,0:T(8,128)(2,1)S(1)}) custom-call(s32[1]{0:T(128)} %bitcast.3.me_ref, bf16[1024,1024]{1,0:T(8,128)(2,1)S(1)} %copy-done.49, ...), custom_call_target="tpu_custom_call", output_to_operand_aliasing={{0}: (6, {}), {1}: (7, {}), {2}: (8, {})} | custom-call | flops 9663676416 | bytes 20971520 | tf_op jit(solution)/shard_map/experts/pallas_call | solution.py:349
  175.7 2.5 plus.6
  186.3 12.9 %experts.10 = (f32[1024,1024]{1,0:T(8,128)S(1)}, f32[1024,1024]{1,0:T(8,128)S(1)}, f32[1024,128]{1,0:T(8,128)S(1)}, bf16[3,512,512]{2,1,0:T(8,128)(2,1)S(1)}, bf16[3,512,512]{2,1,0:T(8,128)(2,1)S(1)}) custom-call(s32[1]{0:T(128)} %bitcast.3.me_ref, bf16[1024,1024]{1,0:T(8,128)(2,1)S(1)} %copy-done.49, ...), custom_call_target="tpu_custom_call", output_to_operand_aliasing={{0}: (6, {}), {1}: (7, {}), {2}: (8, {})} | custom-call | flops 9663676416 | bytes 20971520 | tf_op jit(solution)/shard_map/experts/pallas_call | solution.py:349
  202.7 13.1 %experts.11 = (f32[1024,1024]{1,0:T(8,128)S(1)}, f32[1024,1024]{1,0:T(8,128)S(1)}, f32[1024,128]{1,0:T(8,128)S(1)}, bf16[3,512,512]{2,1,0:T(8,128)(2,1)S(1)}, bf16[3,512,512]{2,1,0:T(8,128)(2,1)S(1)}) custom-call(s32[1]{0:T(128)} %bitcast.3.me_ref, bf16[1024,1024]{1,0:T(8,128)(2,1)S(1)} %copy-done.49, ...), custom_call_target="tpu_custom_call", output_to_operand_aliasing={{0}: (6, {}), {1}: (7, {}), {2}: (8, {})} | custom-call | flops 9663676416 | bytes 20971520 | tf_op jit(solution)/shard_map/experts/pallas_call | solution.py:349
  216.7 2.5 plus.7
  220.4 12.8 %experts.12 = (f32[1024,1024]{1,0:T(8,128)S(1)}, f32[1024,1024]{1,0:T(8,128)S(1)}, f32[1024,128]{1,0:T(8,128)S(1)}, bf16[3,512,512]{2,1,0:T(8,128)(2,1)}, bf16[3,512,512]{2,1,0:T(8,128)(2,1)}) custom-call(s32[1]{0:T(128)} %bitcast.3.me_ref, bf16[1024,1024]{1,0:T(8,128)(2,1)S(1)} %copy-done.49, ...), custom_call_target="tpu_custom_call", output_to_operand_aliasing={{0}: (6, {}), {1}: (7, {}), {2}: (8, {})} | custom-call | flops 9663676416 | bytes 20971520 | tf_op jit(solution)/shard_map/experts/pallas_call | solution.py:349
  234.8 2.0 collective-permute-done.16.refs_11_.refs_1_
  239.8 12.3 %experts.13 = (f32[1024,1024]{1,0:T(8,128)S(1)}, f32[1024,1024]{1,0:T(8,128)S(1)}, f32[1024,128]{1,0:T(8,128)S(1)}, bf16[3,512,512]{2,1,0:T(8,128)(2,1)S(1)}, bf16[3,512,512]{2,1,0:T(8,128)(2,1)S(1)}) custom-call(s32[1]{0:T(128)} %bitcast.3.me_ref, bf16[1024,1024]{1,0:T(8,128)(2,1)S(1)} %copy-done.49, ...), custom_call_target="tpu_custom_call", output_to_operand_aliasing={{0}: (6, {}), {1}: (7, {}), {2}: (8, {})} | custom-call | flops 9663676416 | bytes 20971520 | tf_op jit(solution)/shard_map/experts/pallas_call | solution.py:349
  252.2 2.5 plus.8
  255.9 13.1 %experts.14 = (f32[1024,1024]{1,0:T(8,128)S(1)}, f32[1024,1024]{1,0:T(8,128)S(1)}, f32[1024,128]{1,0:T(8,128)S(1)}, bf16[3,512,512]{2,1,0:T(8,128)(2,1)}, bf16[3,512,512]{2,1,0:T(8,128)(2,1)}) custom-call(s32[1]{0:T(128)} %bitcast.3.me_ref, bf16[1024,1024]{1,0:T(8,128)(2,1)S(1)} %copy-done.49, ...), custom_call_target="tpu_custom_call", output_to_operand_aliasing={{0}: (6, {}), {1}: (7, {}), {2}: (8, {})} | custom-call | flops 9663676416 | bytes 20971520 | tf_op jit(solution)/shard_map/experts/pallas_call | solution.py:349
  272.0 2.9 plus.9
  280.1 12.3 %experts.15 = (f32[1024,1024]{1,0:T(8,128)S(1)}, f32[1024,1024]{1,0:T(8,128)S(1)}, f32[1024,128]{1,0:T(8,128)S(1)}, bf16[3,512,512]{2,1,0:T(8,128)(2,1)S(1)}, bf16[3,512,512]{2,1,0:T(8,128)(2,1)S(1)}) custom-call(s32[1]{0:T(128)} %bitcast.3.me_ref, bf16[1024,1024]{1,0:T(8,128)(2,1)S(1)} %copy-done.50, ...), custom_call_target="tpu_custom_call", output_to_operand_aliasing={{0}: (6, {}), {1}: (7, {}), {2}: (8, {})} | custom-call | flops 9663676416 | bytes 20971520 | tf_op jit(solution)/shard_map/experts/pallas_call | solution.py:349
  292.4 2.0 copy-done.7
  295.6 2.2 copy-done.24
  301.0 8.1 %turn.1 = (bf16[1024,1024]{1,0:T(8,128)(2,1)}, f32[1024,1024]{1,0:T(8,128)S(1)}, bf16[1024,1024]{1,0:T(8,128)(2,1)S(1)}, bf16[1024,1024]{1,0:T(8,128)(2,1)S(1)},...) custom-call(f32[1024,1024]{1,0:T(8,128)S(1)} %get-tuple-element.136.refs_0_, f32[1024,1024]{1,0:T(8,128)} %copy-done.6, ...), custom_call_target="tpu_custom_call" | custom-call | flops 2684354560 | bytes 29360128 | tf_op jit(solution)/shard_map/turn/pallas_call | solution.py:402
  309.1 3.7 convolution_convert_fusion.refs_6_
  312.9 30.7 %attend_back.2 = (bf16[1024,512]{1,0:T(8,128)(2,1)}, bf16[1024,256]{1,0:T(8,128)(2,1)}, bf16[1024,256]{1,0:T(8,128)(2,1)}) custom-call(bf16[1024,1024]{1,0:T(8,128)(2,1)} %get-tuple-element.126.refs_0_, bf16[1024,512]{1,0:T(8,128)(2,1)} %get-tuple-element.127.refs_1_, bf16[1024,512]{1,0:T(8,128)(2,1)} %get-tuple-element.128.refs_2_, ...), custom_call_target="tpu_custom_call" | custom-call | flops 42949672960 | bytes 12582912 | tf_op jit(solution)/shard_map/attend_back/pallas_call | solution.py:190
  346.9 4.3 plus.11
  354.1 30.3 %attend_back.3 = (bf16[1024,512]{1,0:T(8,128)(2,1)}, bf16[1024,256]{1,0:T(8,128)(2,1)}, bf16[1024,256]{1,0:T(8,128)(2,1)}) custom-call(bf16[1024,1024]{1,0:T(8,128)(2,1)} %get-tuple-element.126.refs_0_, bf16[1024,512]{1,0:T(8,128)(2,1)} %get-tuple-element.127.refs_1_, bf16[1024,512]{1,0:T(8,128)(2,1)} %get-tuple-element.128.refs_2_, ...), custom_call_target="tpu_custom_call" | custom-call | flops 42949672960 | bytes 12582912 | tf_op jit(solution)/shard_map/attend_back/pallas_call | solution.py:190
  384.5 8.2 %weights_back.1 = (bf16[1024,512]{1,0:T(8,128)(2,1)}, bf16[1024,512]{1,0:T(8,128)(2,1)}, bf16[1024,256]{1,0:T(8,128)(2,1)}, bf16[1024,256]{1,0:T(8,128)(2,1)}, b...) custom-call(bf16[1024,1024]{1,0:T(8,128)(2,1)} %get-tuple-element.218.refs_0_, ...), custom_call_target="tpu_custom_call" | custom-call | flops 1 | bytes 1 | tf_op jit(solution)/shard_map/weights_back/pallas_call | solution.py:477
  392.6 11.6 %finish.1 = (f32[1024,1024]{1,0:T(8,128)}, bf16[1024,128]{1,0:T(8,128)(2,1)}) custom-call(bf16[1024,512]{1,0:T(8,128)(2,1)} %get-tuple-element.202.refs_0_.refs_1_, bf16[1024,512]{1,0:T(8,128)(2,1)} %get-tuple-element.210.refs_1_.refs_2_, bf16[1024,256]{1,0:T(8,128)(2,1)} %get-tuple-element.211.refs_2_.refs_3_, ...), custom_call_target="tpu_custom_call" | custom-call | flops 1 | bytes 1 | tf_op jit(solution)/shard_map/finish/pallas_call | solution.py:454
  404.3 80.7 %reduce_all.1 = (f32[256,1024]{1,0:T(8,128)}, f32[256,1024]{1,0:T(8,128)}, f32[256,512]{1,0:T(8,128)}, f32[256,512]{1,0:T(8,128)}, f32[256,128]{1,0:T(8,128)}) custom-call(bf16[4,256,1024]{2,1,0:T(8,128)(2,1)} %bitcast.33, bf16[4,256,512]{2,1,0:T(8,128)(2,1)} %bitcast.35, bf16[4,256,512]{2,1,0:T(8,128)(2,1)} %bitcast.36, bf16[4,256,256]{2,1,0:T(8,128)(2,1)} %bitcast.37, ...), custom_call_target="tpu_custom_call" | custom-call | flops 1 | bytes 1 | tf_op jit(solution)/shard_map/reduce_all/pallas_call | solution.py:832
  488.4 5.3 %all-reduce.4.cloned.1.call-done = (bf16[3,512,512]{2,1,0:T(8,128)(2,1)}, bf16[3,512,512]{2,1,0:T(8,128)(2,1)}) async-done(((bf16[3,512,512]{2,1,0:T(8,128)(2,1)}, bf16[3,512,512]{2,1,0:T(8,128)(2,1)}), (bf16[3,512,512]{2,1,0:T(8,128)(2,1)}, bf16[3,512,512]{2,1,0:T(8,128)(2,1)})) %all-reduce.4.cloned.1.call-update) | async-done | bytes 3145744 | tf_op jit(solution)/shard_map/psum | solution.py:979
  493.7 5.3 %widen.1 = (f32[1024,512]{1,0:T(8,128)}, f32[1024,512]{1,0:T(8,128)}, f32[512,1024]{1,0:T(8,128)}) custom-call(bf16[3,512,512]{2,1,0:T(8,128)(2,1)} %get-tuple-element.274.top_ref, bf16[3,512,512]{2,1,0:T(8,128)(2,1)} %get-tuple-element.275.bottom_ref), custom_call_target="tpu_custom_call" | custom-call | flops 1 | bytes 1 | tf_op jit(solution)/shard_map/widen/pallas_call | solution.py:504
  (215 shorter events, 71.1 us)
Async XLA Ops:
  7.2 121.2 %all-gather.2.cloned.1.call-start = ((), (), s32[]{:S(2)}) async-start(), calls=%async_computation | async-start | bytes 2621440 | tf_op jit(solution)/shard_map/all_gather | solution.py:910
  69.7 48.7 %collective-permute-start = (bf16[512,1024]{1,0:T(8,128)(2,1)}, bf16[512,1024]{1,0:T(8,128)(2,1)}, u32[]{:S(2)}, u32[]{:S(2)}) collective-permute-start(bf16[512,1024]{1,0:T(8,128)(2,1)} %get-tuple-element.133), channel_id=1, source_target_pairs={{0,8},{4,12},{8,0},{12,4},{16,24},{20,28},{24,16},{28,20},{1,9},{5... | collective-permute-start | bytes 3145736 | tf_op jit(solution)/shard_map/ppermute | solution.py:856
  70.4 48.1 %collective-permute-start.1 = (bf16[512,1024]{1,0:T(8,128)(2,1)}, bf16[512,1024]{1,0:T(8,128)(2,1)S(1)}, u32[]{:S(2)}, u32[]{:S(2)}) collective-permute-start(bf16[512,1024]{1,0:T(8,128)(2,1)} %get-tuple-element.133), channel_id=1, source_target_pairs={{0,16},{4,20},{8,24},{12,28},{16,0},{20,4},{24,8},{28,12},{1,17},{... | collective-permute-start | bytes 3145736 | tf_op jit(solution)/shard_map/ppermute | solution.py:856
  71.9 421.8 %all-reduce.4.cloned.1.call-start = ((), (), s32[]{:S(2)}) async-start(), calls=%async_computation.1 | async-start | bytes 6291456 | tf_op jit(solution)/shard_map/psum | solution.py:979
  72.0 71.9 %collective-permute-start.3 = (bf16[1024,512]{1,0:T(8,128)(2,1)}, bf16[1024,512]{1,0:T(8,128)(2,1)}, u32[]{:S(2)}, u32[]{:S(2)}) collective-permute-start(bf16[1024,512]{1,0:T(8,128)(2,1)} %get-tuple-element.131.refs_6_.refs_8_), channel_id=1, source_target_pairs={{0,16},{4,20},{8,24},{12,28},{16,0},{20,4},{24,8},{28,12},{1,17},{... | collective-permute-start | bytes 3145736 | tf_op jit(solution)/shard_map/ppermute | solution.py:856
  72.5 71.3 %collective-permute-start.4 = (bf16[1024,512]{1,0:T(8,128)(2,1)}, bf16[1024,512]{1,0:T(8,128)(2,1)}, u32[]{:S(2)}, u32[]{:S(2)}) collective-permute-start(bf16[1024,512]{1,0:T(8,128)(2,1)} %get-tuple-element.135.refs_10_.refs_9_), channel_id=1, source_target_pairs={{0,8},{4,12},{8,0},{12,4},{16,24},{20,28},{24,16},{28,20},{1,9},{5... | collective-permute-start | bytes 3145736 | tf_op jit(solution)/shard_map/ppermute | solution.py:856
  118.4 25.5 %collective-permute-start.2 = (bf16[512,1024]{1,0:T(8,128)(2,1)}, bf16[512,1024]{1,0:T(8,128)(2,1)}, u32[]{:S(2)}, u32[]{:S(2)}) collective-permute-start(bf16[512,1024]{1,0:T(8,128)(2,1)} %collective-permute-done.refs_8_.refs_10_), channel_id=1, source_target_pairs={{0,4},{4,0},{8,12},{12,8},{16,20},{20,16},{24,28},{28,24},{1,5},{5... | collective-permute-start | bytes 3145736 | tf_op jit(solution)/shard_map/ppermute | solution.py:856
  120.4 23.5 %collective-permute-start.5 = (bf16[256,1024]{1,0:T(8,128)(2,1)}, bf16[256,1024]{1,0:T(8,128)(2,1)}, u32[]{:S(2)}, u32[]{:S(2)}) collective-permute-start(bf16[256,1024]{1,0:T(8,128)(2,1)} %slice.20), channel_id=1, source_target_pairs={{0,16},{4,20},{8,24},{12,28},{16,0},{20,4},{24,8},{28,12},{1,17},{... | collective-permute-start | bytes 1572872 | tf_op jit(solution)/shard_map/ppermute | solution.py:856
  122.7 21.2 %collective-permute-start.6 = (bf16[256,1024]{1,0:T(8,128)(2,1)}, bf16[256,1024]{1,0:T(8,128)(2,1)}, u32[]{:S(2)}, u32[]{:S(2)}) collective-permute-start(bf16[256,1024]{1,0:T(8,128)(2,1)} %slice.21), channel_id=1, source_target_pairs={{0,8},{4,12},{8,0},{12,4},{16,24},{20,28},{24,16},{28,20},{1,9},{5... | collective-permute-start | bytes 1572872 | tf_op jit(solution)/shard_map/ppermute | solution.py:856
  143.8 37.9 %copy-start.40 = (f32[1024,128]{1,0:T(8,128)}, f32[1024,128]{1,0:T(8,128)S(1)}, u32[]{:S(2)}) copy-start(f32[1024,128]{1,0:T(8,128)S(1)} %get-tuple-element.139.refs_4_.refs_3_) | copy-start | bytes 1572868
  143.8 134.6 %copy-start.12 = (bf16[1024,1024]{1,0:T(8,128)(2,1)}, bf16[1024,1024]{1,0:T(8,128)(2,1)S(1)}, u32[]{:S(2)}) copy-start(bf16[1024,1024]{1,0:T(8,128)(2,1)S(1)} %get-tuple-element.138.refs_1_.refs_8_) | copy-start | bytes 6291460
  158.2 3.5 collective-permute-start.11
  158.2 17.4 %collective-permute-start.12 = (bf16[3,512,512]{2,1,0:T(8,128)(2,1)S(1)}, bf16[3,512,512]{2,1,0:T(8,128)(2,1)S(1)}, u32[]{:S(2)}, u32[]{:S(2)}) collective-permute-start(bf16[3,512,512]{2,1,0:T(8,128)(2,1)S(1)} %get-tuple-element.152), channel_id=1, source_target_pairs={{0,4},{4,0},{8,12},{12,8},{16,20},{20,16},{24,28},{28,24},{1,5},{5... | collective-permute-start | bytes 4718600 | tf_op jit(solution)/shard_map/ppermute | solution.py:856
  158.7 19.4 %collective-permute-start.7 = (bf16[1024,512]{1,0:T(8,128)(2,1)}, bf16[1024,512]{1,0:T(8,128)(2,1)S(1)}, u32[]{:S(2)}, u32[]{:S(2)}) collective-permute-start(bf16[1024,512]{1,0:T(8,128)(2,1)} %collective-permute-done.3.refs_8_), channel_id=1, source_target_pairs={{0,4},{4,0},{8,12},{12,8},{16,20},{20,16},{24,28},{28,24},{1,5},{5... | collective-permute-start | bytes 3145736 | tf_op jit(solution)/shard_map/ppermute | solution.py:856
  158.8 20.4 %collective-permute-start.8 = (bf16[1024,512]{1,0:T(8,128)(2,1)}, bf16[1024,512]{1,0:T(8,128)(2,1)S(1)}, u32[]{:S(2)}, u32[]{:S(2)}) collective-permute-start(bf16[1024,512]{1,0:T(8,128)(2,1)} %collective-permute-done.4.refs_9_), channel_id=1, source_target_pairs={{0,4},{4,0},{8,12},{12,8},{16,20},{20,16},{24,28},{28,24},{1,5},{5... | collective-permute-start | bytes 3145736 | tf_op jit(solution)/shard_map/ppermute | solution.py:856
  159.3 20.9 %collective-permute-start.9 = (bf16[256,1024]{1,0:T(8,128)(2,1)}, bf16[256,1024]{1,0:T(8,128)(2,1)S(1)}, u32[]{:S(2)}, u32[]{:S(2)}) collective-permute-start(bf16[256,1024]{1,0:T(8,128)(2,1)} %collective-permute-done.5.refs_10_), channel_id=1, source_target_pairs={{0,4},{4,0},{8,12},{12,8},{16,20},{20,16},{24,28},{28,24},{1,5},{5... | collective-permute-start | bytes 1572872 | tf_op jit(solution)/shard_map/ppermute | solution.py:856
  161.6 19.3 %collective-permute-start.10 = (bf16[256,1024]{1,0:T(8,128)(2,1)}, bf16[256,1024]{1,0:T(8,128)(2,1)S(1)}, u32[]{:S(2)}, u32[]{:S(2)}) collective-permute-start(bf16[256,1024]{1,0:T(8,128)(2,1)} %collective-permute-done.6.refs_11_), channel_id=1, source_target_pairs={{0,4},{4,0},{8,12},{12,8},{16,20},{20,16},{24,28},{28,24},{1,5},{5... | collective-permute-start | bytes 1572872 | tf_op jit(solution)/shard_map/ppermute | solution.py:856
  199.2 17.5 %collective-permute-start.14 = (bf16[3,512,512]{2,1,0:T(8,128)(2,1)S(1)}, bf16[3,512,512]{2,1,0:T(8,128)(2,1)S(1)}, u32[]{:S(2)}, u32[]{:S(2)}) collective-permute-start(bf16[3,512,512]{2,1,0:T(8,128)(2,1)S(1)} %get-tuple-element.164), channel_id=1, source_target_pairs={{0,4},{4,0},{8,12},{12,8},{16,20},{20,16},{24,28},{28,24},{1,5},{5... | collective-permute-start | bytes 4718600 | tf_op jit(solution)/shard_map/ppermute | solution.py:856
  199.6 17.0 %collective-permute-start.15 = (bf16[3,512,512]{2,1,0:T(8,128)(2,1)S(1)}, bf16[3,512,512]{2,1,0:T(8,128)(2,1)S(1)}, u32[]{:S(2)}, u32[]{:S(2)}) collective-permute-start(bf16[3,512,512]{2,1,0:T(8,128)(2,1)S(1)} %get-tuple-element.166), channel_id=1, source_target_pairs={{0,4},{4,0},{8,12},{12,8},{16,20},{20,16},{24,28},{28,24},{1,5},{5... | collective-permute-start | bytes 4718600 | tf_op jit(solution)/shard_map/ppermute | solution.py:856
  199.8 19.4 %collective-permute-start.13 = (bf16[512,1024]{1,0:T(8,128)(2,1)S(1)}, bf16[512,1024]{1,0:T(8,128)(2,1)}, u32[]{:S(2)}, u32[]{:S(2)}) collective-permute-start(bf16[512,1024]{1,0:T(8,128)(2,1)S(1)} %collective-permute-done.1.refs_11_.refs_10_), channel_id=1, source_target_pairs={{0,4},{4,0},{8,12},{12,8},{16,20},{20,16},{24,28},{28,24},{1,5},{5... | collective-permute-start | bytes 3145736 | tf_op jit(solution)/shard_map/ppermute | solution.py:856
  200.1 36.7 %collective-permute-start.16 = (bf16[3,512,512]{2,1,0:T(8,128)(2,1)}, bf16[3,512,512]{2,1,0:T(8,128)(2,1)S(1)}, u32[]{:S(2)}, u32[]{:S(2)}) collective-permute-start(bf16[3,512,512]{2,1,0:T(8,128)(2,1)} %get-tuple-element.171), channel_id=1, source_target_pairs={{0,8},{4,12},{8,0},{12,4},{16,24},{20,28},{24,16},{28,20},{1,9},{5... | collective-permute-start | bytes 4718600 | tf_op jit(solution)/shard_map/ppermute | solution.py:856
  233.2 19.0 %collective-permute-start.17 = (bf16[3,512,512]{2,1,0:T(8,128)(2,1)}, bf16[3,512,512]{2,1,0:T(8,128)(2,1)S(1)}, u32[]{:S(2)}, u32[]{:S(2)}) collective-permute-start(bf16[3,512,512]{2,1,0:T(8,128)(2,1)} %get-tuple-element.179), channel_id=1, source_target_pairs={{0,4},{4,0},{8,12},{12,8},{16,20},{20,16},{24,28},{28,24},{1,5},{5... | collective-permute-start | bytes 4718600 | tf_op jit(solution)/shard_map/ppermute | solution.py:856
  233.3 18.9 %collective-permute-start.18 = (bf16[3,512,512]{2,1,0:T(8,128)(2,1)}, bf16[3,512,512]{2,1,0:T(8,128)(2,1)S(1)}, u32[]{:S(2)}, u32[]{:S(2)}) collective-permute-start(bf16[3,512,512]{2,1,0:T(8,128)(2,1)} %get-tuple-element.181), channel_id=1, source_target_pairs={{0,4},{4,0},{8,12},{12,8},{16,20},{20,16},{24,28},{28,24},{1,5},{5... | collective-permute-start | bytes 4718600 | tf_op jit(solution)/shard_map/ppermute | solution.py:856
  233.8 36.7 %collective-permute-start.19 = (bf16[3,512,512]{2,1,0:T(8,128)(2,1)}, bf16[3,512,512]{2,1,0:T(8,128)(2,1)S(1)}, u32[]{:S(2)}, u32[]{:S(2)}) collective-permute-start(bf16[3,512,512]{2,1,0:T(8,128)(2,1)} %get-tuple-element.187), channel_id=1, source_target_pairs={{0,8},{4,12},{8,0},{12,4},{16,24},{20,28},{24,16},{28,20},{1,9},{5... | collective-permute-start | bytes 4718600 | tf_op jit(solution)/shard_map/ppermute | solution.py:856
  234.3 36.3 %collective-permute-start.20 = (bf16[3,512,512]{2,1,0:T(8,128)(2,1)}, bf16[3,512,512]{2,1,0:T(8,128)(2,1)S(1)}, u32[]{:S(2)}, u32[]{:S(2)}) collective-permute-start(bf16[3,512,512]{2,1,0:T(8,128)(2,1)} %copy-done.52), channel_id=1, source_target_pairs={{0,16},{4,20},{8,24},{12,28},{16,0},{20,4},{24,8},{28,12},{1,17},{... | collective-permute-start | bytes 4718600 | tf_op jit(solution)/shard_map/ppermute | solution.py:856
  269.0 25.4 %collective-permute-start.21 = (bf16[3,512,512]{2,1,0:T(8,128)(2,1)}, bf16[3,512,512]{2,1,0:T(8,128)(2,1)S(1)}, u32[]{:S(2)}, u32[]{:S(2)}) collective-permute-start(bf16[3,512,512]{2,1,0:T(8,128)(2,1)} %get-tuple-element.195), channel_id=1, source_target_pairs={{0,4},{4,0},{8,12},{12,8},{16,20},{20,16},{24,28},{28,24},{1,5},{5... | collective-permute-start | bytes 4718600 | tf_op jit(solution)/shard_map/ppermute | solution.py:856
  269.0 25.4 %collective-permute-start.22 = (bf16[3,512,512]{2,1,0:T(8,128)(2,1)}, bf16[3,512,512]{2,1,0:T(8,128)(2,1)S(1)}, u32[]{:S(2)}, u32[]{:S(2)}) collective-permute-start(bf16[3,512,512]{2,1,0:T(8,128)(2,1)} %get-tuple-element.197), channel_id=1, source_target_pairs={{0,4},{4,0},{8,12},{12,8},{16,20},{20,16},{24,28},{28,24},{1,5},{5... | collective-permute-start | bytes 4718600 | tf_op jit(solution)/shard_map/ppermute | solution.py:856
  274.9 68.7 %collective-permute-start.23 = (bf16[3,512,512]{2,1,0:T(8,128)(2,1)}, bf16[3,512,512]{2,1,0:T(8,128)(2,1)}, u32[]{:S(2)}, u32[]{:S(2)}) collective-permute-start(bf16[3,512,512]{2,1,0:T(8,128)(2,1)} %get-tuple-element.204), channel_id=1, source_target_pairs={{0,16},{4,20},{8,24},{12,28},{16,0},{20,4},{24,8},{28,12},{1,17},{... | collective-permute-start | bytes 4718600 | tf_op jit(solution)/shard_map/ppermute | solution.py:856
  275.4 69.0 %collective-permute-start.24 = (bf16[3,512,512]{2,1,0:T(8,128)(2,1)}, bf16[3,512,512]{2,1,0:T(8,128)(2,1)}, u32[]{:S(2)}, u32[]{:S(2)}) collective-permute-start(bf16[3,512,512]{2,1,0:T(8,128)(2,1)} %get-tuple-element.206), channel_id=1, source_target_pairs={{0,16},{4,20},{8,24},{12,28},{16,0},{20,4},{24,8},{28,12},{1,17},{... | collective-permute-start | bytes 4718600 | tf_op jit(solution)/shard_map/ppermute | solution.py:856
  276.9 67.5 %collective-permute-start.25 = (bf16[3,512,512]{2,1,0:T(8,128)(2,1)}, bf16[3,512,512]{2,1,0:T(8,128)(2,1)}, u32[]{:S(2)}, u32[]{:S(2)}) collective-permute-start(bf16[3,512,512]{2,1,0:T(8,128)(2,1)} %get-tuple-element.207), channel_id=1, source_target_pairs={{0,8},{4,12},{8,0},{12,4},{16,24},{20,28},{24,16},{28,20},{1,9},{5... | collective-permute-start | bytes 4718600 | tf_op jit(solution)/shard_map/ppermute | solution.py:856
  312.9 31.6 %copy-start.16 = (bf16[3,512,512]{2,1,0:T(8,128)(2,1)S(1)}, bf16[3,512,512]{2,1,0:T(8,128)(2,1)}, u32[]{:S(2)}) copy-start(bf16[3,512,512]{2,1,0:T(8,128)(2,1)} %copy-done.15) | copy-start | bytes 4718596
  312.9 31.6 %copy-start.18 = (bf16[3,512,512]{2,1,0:T(8,128)(2,1)S(1)}, bf16[3,512,512]{2,1,0:T(8,128)(2,1)}, u32[]{:S(2)}) copy-start(bf16[3,512,512]{2,1,0:T(8,128)(2,1)} %copy-done.17) | copy-start | bytes 4718596
  (70 other events, 246.0 us)
Sparse Core Ops, SparseCore 0:
  72.0 46.0 all-gather.1
  354.3 139.3 all-reduce.3

commit v6 on v5

--- a/solution.py
+++ b/solution.py
@@ -20,7 +20,7 @@
 VMEM = pl.BlockSpec(memory_space=pltpu.VMEM)
 VMEM_BYTES = 60 * 1024 * 1024
 LESS_BYTES = 30 * 1024 * 1024
-EXPERT_BYTES = 26 * 1024 * 1024
+EXPERT_BYTES = 43 * 1024 * 1024
 
 
 def dot(a, b):

time: 519 us -> 550 us (1.060)
  Pallas kernels: 401 us -> 431 us
    pallas_call x8, Pallas kernels: 101 us -> 121 us  [moe(): pl.pallas_call(functools.partial(moe_kernel, tuple(slots), chunks, first,...]
    pallas_call x6, Pallas kernels: 15.5 us -> 26.8 us  [plus(): pl.pallas_call(tied(functools.partial(plus_kernel, counts), len(flat), ti...]
    unnamed x155 -> x137, local copies, waits for them, and re-layouts: 55.5 us -> 57.5 us
  transfers between devices with their start and end apart: 28 -> 28, of which waited for: 6 -> 2; matrix products, arithmetic and copies ran while one was open for 3% -> 3% of each run, Pallas kernels for 60% -> 62%
where the time goes in v6:
time: 550 us; the launch traced here: 541 us
  Pallas kernels  431 us (78%)
  local copies, waits for them, and re-layouts  64.3 us (12%)
  starting transfers between devices  15.9 us (3%)
  between operations  15.1 us (3%)
  waiting for transfers between devices  9.34 us (2%)
    pallas_call x8, Pallas kernels, moe(): pl.pallas_call(functools.partial(moe_kernel, tuple(slots), chunks, first,...  121 us
    pallas_call x1, Pallas kernels, reduce_all(): pl.pallas_call(functools.partial(reduce_kernel, size, columns), in_specs=...  80 us
    pallas_call x2, Pallas kernels, attend_back(): pl.pallas_call(tied(attend_back_kernel, 6, ties), grid=(rows // SEQUENCE_...  60.7 us
    pallas_call x1, Pallas kernels, gather_weights(): pl.pallas_call(functools.partial(gather_kernel, size, len(owned)), in_spe...  59.8 us
    unnamed x137, local copies, waits for them, and re-layouts  57.5 us
    pallas_call x1, Pallas kernels, attend(): pl.pallas_call(tied(attend_kernel, 3, ties), grid=(rows // SEQUENCE_LENGT...  35.3 us
    pallas_call x6, Pallas kernels, plus(): pl.pallas_call(tied(functools.partial(plus_kernel, counts), len(flat), ti...  26.8 us
    ppermute x26, starting transfers between devices, flip(): return lax.ppermute(value, axis, [(i, i ^ bit) for i in range(size)])  15.8 us
  transfers between devices with their start and end apart: 28, of which 2 were waited for; matrix products, arithmetic and copies ran while one was open for 3% of the time, Pallas kernels for 62%

profile of v6, /device:TPU:0, one launch (start us, length us, event | category | flops | bytes accessed | tf_op | source)
XLA Modules:
  0.0 540.5 jit_solution(4253440531415417711)
XLA Ops:
  10.0 59.8 %gather_weights.1 = (bf16[1024,2048]{1,0:T(8,128)(2,1)}, bf16[1024,128]{1,0:T(8,128)(2,1)}, bf16[256,1024]{1,0:T(8,128)(2,1)}, bf16[512,1024]{1,0:T(8,128)(2,1)}...) custom-call(bf16[256,1024]{1,0:T(8,128)(2,1)} %refs_0_.1, ...), custom_call_target="tpu_custom_call" | custom-call | flops 1000000000 | bytes 25165824 | tf_op jit(solution)/shard_map/gather_weights/pallas_call | solution.py:688
  74.1 9.1 %project.1 = (bf16[1024,1024]{1,0:T(8,128)(2,1)}, bf16[1024,1024]{1,0:T(8,128)(2,1)}, bf16[1024,512]{1,0:T(8,128)(2,1)}, bf16[1024,512]{1,0:T(8,128)(2,1)}) custom-call(bf16[1024,1024]{1,0:T(8,128)(2,1)} %refs_7_.1, bf16[128,1024]{1,0:T(8,128)(2,1)} %get-tuple-element.124.gain_ref.refs_3_.refs_6_.refs_9_, ...), custom_call_target="tpu_custom_call" | custom-call | flops 4294967296 | bytes 12582912 | tf_op jit(solution)/shard_map/project/pallas_call | solution.py:104
  83.2 35.3 %attend.1.refs_0_ = bf16[1024,1024]{1,0:T(8,128)(2,1)} custom-call(bf16[1024,1024]{1,0:T(8,128)(2,1)} %get-tuple-element.126.refs_0_, bf16[1024,512]{1,0:T(8,128)(2,1)} %get-tuple-element.127.refs_1_, bf16[1024,512]{1,0:T(8,128)(2,1)} %get-tuple-element.128.refs_2_), custom_call_target="tpu_custom_call" | custom-call | flops 34359738368 | bytes 6291456 | tf_op jit(solution)/shard_map/attend/pallas_call | solution.py:140
  118.6 2.2 slice.20
  124.7 4.1 copy.60
  138.9 5.5 %middle.1 = (f32[1024,1024]{1,0:T(8,128)S(1)}, bf16[1024,1024]{1,0:T(8,128)(2,1)S(1)}, bf16[1024,1024]{1,0:T(8,128)(2,1)S(1)}, f32[1024,128]{1,0:T(8,128)S(1)}) custom-call(bf16[1024,1024]{1,0:T(8,128)(2,1)S(1)} %copy-done.13, bf16[1024,1024]{1,0:T(8,128)(2,1)S(1)} %copy-done.2, bf16[1024,1024]{1,0:T(8,128)(2,1)S(1)} %copy-done, ...), custom_call_target="tpu_custom_call" | custom-call | flops 2415919104 | bytes 14680064 | tf_op jit(solution)/shard_map/middle/pallas_call | solution.py:227
  146.5 14.4 %experts.8 = (f32[1024,1024]{1,0:T(8,128)S(1)}, f32[1024,1024]{1,0:T(8,128)S(1)}, f32[1024,128]{1,0:T(8,128)S(1)}, bf16[3,512,512]{2,1,0:T(8,128)(2,1)}, bf16[3,512,512]{2,1,0:T(8,128)(2,1)}) custom-call(s32[1]{0:T(128)} %bitcast.3.me_ref, bf16[1024,1024]{1,0:T(8,128)(2,1)S(1)} %get-tuple-element.137.refs_0_, ...), custom_call_target="tpu_custom_call" | custom-call | flops 9663676416 | bytes 20971520 | tf_op jit(solution)/shard_map/experts/pallas_call | solution.py:349
  162.0 4.0 collective-permute-done.11.refs_1_
  167.2 24.9 %experts.9 = (f32[1024,1024]{1,0:T(8,128)S(1)}, f32[1024,1024]{1,0:T(8,128)S(1)}, f32[1024,128]{1,0:T(8,128)S(1)}, bf16[3,512,512]{2,1,0:T(8,128)(2,1)}, bf16[3,512,512]{2,1,0:T(8,128)(2,1)}) custom-call(s32[1]{0:T(128)} %bitcast.3.me_ref, ...), custom_call_target="tpu_custom_call", output_to_operand_aliasing={{0}: (6, {}), {1}: (7, {}), {2}: (8, {})} | custom-call | flops 9663676416 | bytes 20971520 | tf_op jit(solution)/shard_map/experts/pallas_call | solution.py:349
  194.9 3.4 plus.6
  202.6 13.6 %experts.10 = (f32[1024,1024]{1,0:T(8,128)S(1)}, f32[1024,1024]{1,0:T(8,128)S(1)}, f32[1024,128]{1,0:T(8,128)S(1)}, bf16[3,512,512]{2,1,0:T(8,128)(2,1)}, bf16[3,512,512]{2,1,0:T(8,128)(2,1)}) custom-call(s32[1]{0:T(128)} %bitcast.3.me_ref, bf16[1024,1024]{1,0:T(8,128)(2,1)S(1)} %copy-done.47, ...), custom_call_target="tpu_custom_call", output_to_operand_aliasing={{0}: (6, {}), {1}: (7, {}), {2}: (8, {})} | custom-call | flops 9663676416 | bytes 20971520 | tf_op jit(solution)/shard_map/experts/pallas_call | solution.py:349
  218.7 14.0 %experts.11 = (f32[1024,1024]{1,0:T(8,128)S(1)}, f32[1024,1024]{1,0:T(8,128)S(1)}, f32[1024,128]{1,0:T(8,128)S(1)}, bf16[3,512,512]{2,1,0:T(8,128)(2,1)}, bf16[3,512,512]{2,1,0:T(8,128)(2,1)}) custom-call(s32[1]{0:T(128)} %bitcast.3.me_ref, bf16[1024,1024]{1,0:T(8,128)(2,1)S(1)} %copy-done.47, ...), custom_call_target="tpu_custom_call", output_to_operand_aliasing={{0}: (6, {}), {1}: (7, {}), {2}: (8, {})} | custom-call | flops 9663676416 | bytes 20971520 | tf_op jit(solution)/shard_map/experts/pallas_call | solution.py:349
  235.5 3.7 plus.7
  241.0 13.6 %experts.12 = (f32[1024,1024]{1,0:T(8,128)S(1)}, f32[1024,1024]{1,0:T(8,128)S(1)}, f32[1024,128]{1,0:T(8,128)S(1)}, bf16[3,512,512]{2,1,0:T(8,128)(2,1)}, bf16[3,512,512]{2,1,0:T(8,128)(2,1)}) custom-call(s32[1]{0:T(128)} %bitcast.3.me_ref, bf16[1024,1024]{1,0:T(8,128)(2,1)S(1)} %copy-done.47, ...), custom_call_target="tpu_custom_call", output_to_operand_aliasing={{0}: (6, {}), {1}: (7, {}), {2}: (8, {})} | custom-call | flops 9663676416 | bytes 20971520 | tf_op jit(solution)/shard_map/experts/pallas_call | solution.py:349
  257.3 13.7 %experts.13 = (f32[1024,1024]{1,0:T(8,128)S(1)}, f32[1024,1024]{1,0:T(8,128)S(1)}, f32[1024,128]{1,0:T(8,128)S(1)}, bf16[3,512,512]{2,1,0:T(8,128)(2,1)}, bf16[3,512,512]{2,1,0:T(8,128)(2,1)}) custom-call(s32[1]{0:T(128)} %bitcast.3.me_ref, bf16[1024,1024]{1,0:T(8,128)(2,1)S(1)} %copy-done.47, ...), custom_call_target="tpu_custom_call", output_to_operand_aliasing={{0}: (6, {}), {1}: (7, {}), {2}: (8, {})} | custom-call | flops 9663676416 | bytes 20971520 | tf_op jit(solution)/shard_map/experts/pallas_call | solution.py:349
  273.9 4.9 plus.8
  280.6 13.7 %experts.14 = (f32[1024,1024]{1,0:T(8,128)S(1)}, f32[1024,1024]{1,0:T(8,128)S(1)}, f32[1024,128]{1,0:T(8,128)S(1)}, bf16[3,512,512]{2,1,0:T(8,128)(2,1)}, bf16[3,512,512]{2,1,0:T(8,128)(2,1)}) custom-call(s32[1]{0:T(128)} %bitcast.3.me_ref, bf16[1024,1024]{1,0:T(8,128)(2,1)S(1)} %copy-done.47, ...), custom_call_target="tpu_custom_call", output_to_operand_aliasing={{0}: (6, {}), {1}: (7, {}), {2}: (8, {})} | custom-call | flops 9663676416 | bytes 20971520 | tf_op jit(solution)/shard_map/experts/pallas_call | solution.py:349
  296.3 5.8 %plus.9 = (bf16[3,512,512]{2,1,0:T(8,128)(2,1)}, bf16[3,512,512]{2,1,0:T(8,128)(2,1)}, f32[8,128]{1,0:T(8,128)S(1)}) custom-call(bf16[3,512,512]{2,1,0:T(8,128)(2,1)S(1)} %copy-done.27, bf16[3,512,512]{2,1,0:T(8,128)(2,1)} %collective-permute-done.19.refs_1_, bf16[3,512,512]{2,1,0:T(8,128)(2,1)S(1)} %copy-done.25, ...), custom_call_target="tpu_custom_call" | custom-call | flops 3145728 | bytes 9437184 | tf_op jit(solution)/shard_map/plus/pallas_call | solution.py:539
  307.3 13.6 %experts.15 = (f32[1024,1024]{1,0:T(8,128)S(1)}, f32[1024,1024]{1,0:T(8,128)S(1)}, f32[1024,128]{1,0:T(8,128)S(1)}, bf16[3,512,512]{2,1,0:T(8,128)(2,1)}, bf16[3,512,512]{2,1,0:T(8,128)(2,1)}) custom-call(s32[1]{0:T(128)} %bitcast.3.me_ref, bf16[1024,1024]{1,0:T(8,128)(2,1)S(1)} %copy-done.48, ...), custom_call_target="tpu_custom_call", output_to_operand_aliasing={{0}: (6, {}), {1}: (7, {}), {2}: (8, {})} | custom-call | flops 9663676416 | bytes 20971520 | tf_op jit(solution)/shard_map/experts/pallas_call | solution.py:349
  320.9 2.1 copy-done.9
  323.0 2.6 copy-done.30
  327.0 4.6 plus.10
  334.0 7.5 %turn.1 = (bf16[1024,1024]{1,0:T(8,128)(2,1)}, f32[1024,1024]{1,0:T(8,128)S(1)}, bf16[1024,1024]{1,0:T(8,128)(2,1)S(1)}, bf16[1024,1024]{1,0:T(8,128)(2,1)S(1)},...) custom-call(f32[1024,1024]{1,0:T(8,128)S(1)} %copy-done.6, f32[1024,1024]{1,0:T(8,128)} %copy-done.8, ...), custom_call_target="tpu_custom_call" | custom-call | flops 2684354560 | bytes 29360128 | tf_op jit(solution)/shard_map/turn/pallas_call | solution.py:402
  341.6 3.7 convolution_convert_fusion.refs_6_
  345.3 30.4 %attend_back.2 = (bf16[1024,512]{1,0:T(8,128)(2,1)}, bf16[1024,256]{1,0:T(8,128)(2,1)}, bf16[1024,256]{1,0:T(8,128)(2,1)}) custom-call(bf16[1024,1024]{1,0:T(8,128)(2,1)} %get-tuple-element.126.refs_0_, bf16[1024,512]{1,0:T(8,128)(2,1)} %get-tuple-element.127.refs_1_, bf16[1024,512]{1,0:T(8,128)(2,1)} %get-tuple-element.128.refs_2_, ...), custom_call_target="tpu_custom_call" | custom-call | flops 42949672960 | bytes 12582912 | tf_op jit(solution)/shard_map/attend_back/pallas_call | solution.py:190
  378.2 4.3 plus.11
  385.4 30.4 %attend_back.3 = (bf16[1024,512]{1,0:T(8,128)(2,1)}, bf16[1024,256]{1,0:T(8,128)(2,1)}, bf16[1024,256]{1,0:T(8,128)(2,1)}) custom-call(bf16[1024,1024]{1,0:T(8,128)(2,1)} %get-tuple-element.126.refs_0_, bf16[1024,512]{1,0:T(8,128)(2,1)} %get-tuple-element.127.refs_1_, bf16[1024,512]{1,0:T(8,128)(2,1)} %get-tuple-element.128.refs_2_, ...), custom_call_target="tpu_custom_call" | custom-call | flops 42949672960 | bytes 12582912 | tf_op jit(solution)/shard_map/attend_back/pallas_call | solution.py:190
  415.8 8.2 %weights_back.1 = (bf16[1024,512]{1,0:T(8,128)(2,1)}, bf16[1024,512]{1,0:T(8,128)(2,1)}, bf16[1024,256]{1,0:T(8,128)(2,1)}, bf16[1024,256]{1,0:T(8,128)(2,1)}, b...) custom-call(bf16[1024,1024]{1,0:T(8,128)(2,1)} %get-tuple-element.218.refs_0_, ...), custom_call_target="tpu_custom_call" | custom-call | flops 1 | bytes 1 | tf_op jit(solution)/shard_map/weights_back/pallas_call | solution.py:477
  424.0 11.6 %finish.1 = (f32[1024,1024]{1,0:T(8,128)}, bf16[1024,128]{1,0:T(8,128)(2,1)}) custom-call(bf16[1024,512]{1,0:T(8,128)(2,1)} %get-tuple-element.202.refs_0_.refs_1_, bf16[1024,512]{1,0:T(8,128)(2,1)} %get-tuple-element.210.refs_1_.refs_2_, bf16[1024,256]{1,0:T(8,128)(2,1)} %get-tuple-element.211.refs_2_.refs_3_, ...), custom_call_target="tpu_custom_call" | custom-call | flops 1 | bytes 1 | tf_op jit(solution)/shard_map/finish/pallas_call | solution.py:454
  435.7 80.0 %reduce_all.1 = (f32[256,1024]{1,0:T(8,128)}, f32[256,1024]{1,0:T(8,128)}, f32[256,512]{1,0:T(8,128)}, f32[256,512]{1,0:T(8,128)}, f32[256,128]{1,0:T(8,128)}) custom-call(bf16[4,256,1024]{2,1,0:T(8,128)(2,1)} %bitcast.27, bf16[4,256,512]{2,1,0:T(8,128)(2,1)} %bitcast.29, bf16[4,256,512]{2,1,0:T(8,128)(2,1)} %bitcast.30, bf16[4,256,256]{2,1,0:T(8,128)(2,1)} %bitcast.37, ...), custom_call_target="tpu_custom_call" | custom-call | flops 1 | bytes 1 | tf_op jit(solution)/shard_map/reduce_all/pallas_call | solution.py:832
  519.1 5.3 all-reduce.4.cloned.1.call-done
  524.4 5.3 widen.1
  (197 shorter events, 70.1 us)
Async XLA Ops:
  7.2 121.6 %all-gather.2.cloned.1.call-start = ((), (), s32[]{:S(2)}) async-start(), calls=%async_computation | async-start | bytes 2621440 | tf_op jit(solution)/shard_map/all_gather | solution.py:910
  69.8 48.7 %collective-permute-start = (bf16[512,1024]{1,0:T(8,128)(2,1)}, bf16[512,1024]{1,0:T(8,128)(2,1)}, u32[]{:S(2)}, u32[]{:S(2)}) collective-permute-start(bf16[512,1024]{1,0:T(8,128)(2,1)} %get-tuple-element.133), channel_id=1, source_target_pairs={{0,8},{4,12},{8,0},{12,4},{16,24},{20,28},{24,16},{28,20},{1,9},{5... | collective-permute-start | bytes 3145736 | tf_op jit(solution)/shard_map/ppermute | solution.py:856
  70.4 48.1 %collective-permute-start.1 = (bf16[512,1024]{1,0:T(8,128)(2,1)}, bf16[512,1024]{1,0:T(8,128)(2,1)S(1)}, u32[]{:S(2)}, u32[]{:S(2)}) collective-permute-start(bf16[512,1024]{1,0:T(8,128)(2,1)} %get-tuple-element.133), channel_id=1, source_target_pairs={{0,16},{4,20},{8,24},{12,28},{16,0},{20,4},{24,8},{28,12},{1,17},{... | collective-permute-start | bytes 3145736 | tf_op jit(solution)/shard_map/ppermute | solution.py:856
  72.0 452.4 %all-reduce.4.cloned.1.call-start = ((), (), s32[]{:S(2)}) async-start(), calls=%async_computation.1 | async-start | bytes 6291456 | tf_op jit(solution)/shard_map/psum | solution.py:979
  72.0 74.4 %collective-permute-start.3 = (bf16[1024,512]{1,0:T(8,128)(2,1)}, bf16[1024,512]{1,0:T(8,128)(2,1)}, u32[]{:S(2)}, u32[]{:S(2)}) collective-permute-start(bf16[1024,512]{1,0:T(8,128)(2,1)} %get-tuple-element.131.refs_6_.refs_8_), channel_id=1, source_target_pairs={{0,16},{4,20},{8,24},{12,28},{16,0},{20,4},{24,8},{28,12},{1,17},{... | collective-permute-start | bytes 3145736 | tf_op jit(solution)/shard_map/ppermute | solution.py:856
  72.6 73.8 %collective-permute-start.4 = (bf16[1024,512]{1,0:T(8,128)(2,1)}, bf16[1024,512]{1,0:T(8,128)(2,1)}, u32[]{:S(2)}, u32[]{:S(2)}) collective-permute-start(bf16[1024,512]{1,0:T(8,128)(2,1)} %get-tuple-element.135.refs_10_.refs_9_), channel_id=1, source_target_pairs={{0,8},{4,12},{8,0},{12,4},{16,24},{20,28},{24,16},{28,20},{1,9},{5... | collective-permute-start | bytes 3145736 | tf_op jit(solution)/shard_map/ppermute | solution.py:856
  118.5 98.3 %copy-start.11 = (bf16[512,1024]{1,0:T(8,128)(2,1)}, bf16[512,1024]{1,0:T(8,128)(2,1)S(1)}, u32[]{:S(2)}) copy-start(bf16[512,1024]{1,0:T(8,128)(2,1)S(1)} %collective-permute-done.1.refs_11_.refs_10_) | copy-start | bytes 3145732
  118.5 27.9 %collective-permute-start.2 = (bf16[512,1024]{1,0:T(8,128)(2,1)}, bf16[512,1024]{1,0:T(8,128)(2,1)}, u32[]{:S(2)}, u32[]{:S(2)}) collective-permute-start(bf16[512,1024]{1,0:T(8,128)(2,1)} %collective-permute-done.refs_8_.refs_10_), channel_id=1, source_target_pairs={{0,4},{4,0},{8,12},{12,8},{16,20},{20,16},{24,28},{28,24},{1,5},{5... | collective-permute-start | bytes 3145736 | tf_op jit(solution)/shard_map/ppermute | solution.py:856
  120.8 25.6 %collective-permute-start.5 = (bf16[256,1024]{1,0:T(8,128)(2,1)}, bf16[256,1024]{1,0:T(8,128)(2,1)}, u32[]{:S(2)}, u32[]{:S(2)}) collective-permute-start(bf16[256,1024]{1,0:T(8,128)(2,1)} %slice.20), channel_id=1, source_target_pairs={{0,16},{4,20},{8,24},{12,28},{16,0},{20,4},{24,8},{28,12},{1,17},{... | collective-permute-start | bytes 1572872 | tf_op jit(solution)/shard_map/ppermute | solution.py:856
  123.1 23.3 %collective-permute-start.6 = (bf16[256,1024]{1,0:T(8,128)(2,1)}, bf16[256,1024]{1,0:T(8,128)(2,1)}, u32[]{:S(2)}, u32[]{:S(2)}) collective-permute-start(bf16[256,1024]{1,0:T(8,128)(2,1)} %slice.21), channel_id=1, source_target_pairs={{0,8},{4,12},{8,0},{12,4},{16,24},{20,28},{24,16},{28,20},{1,9},{5... | collective-permute-start | bytes 1572872 | tf_op jit(solution)/shard_map/ppermute | solution.py:856
  160.8 5.2 collective-permute-start.11
  160.9 31.2 %collective-permute-start.12 = (bf16[3,512,512]{2,1,0:T(8,128)(2,1)}, bf16[3,512,512]{2,1,0:T(8,128)(2,1)}, u32[]{:S(2)}, u32[]{:S(2)}) collective-permute-start(bf16[3,512,512]{2,1,0:T(8,128)(2,1)} %get-tuple-element.152), channel_id=1, source_target_pairs={{0,4},{4,0},{8,12},{12,8},{16,20},{20,16},{24,28},{28,24},{1,5},{5... | collective-permute-start | bytes 4718600 | tf_op jit(solution)/shard_map/ppermute | solution.py:856
  161.4 38.1 %collective-permute-start.7 = (bf16[1024,512]{1,0:T(8,128)(2,1)}, bf16[1024,512]{1,0:T(8,128)(2,1)}, u32[]{:S(2)}, u32[]{:S(2)}) collective-permute-start(bf16[1024,512]{1,0:T(8,128)(2,1)} %collective-permute-done.3.refs_8_), channel_id=1, source_target_pairs={{0,4},{4,0},{8,12},{12,8},{16,20},{20,16},{24,28},{28,24},{1,5},{5... | collective-permute-start | bytes 3145736 | tf_op jit(solution)/shard_map/ppermute | solution.py:856
  161.5 38.1 %collective-permute-start.8 = (bf16[1024,512]{1,0:T(8,128)(2,1)}, bf16[1024,512]{1,0:T(8,128)(2,1)}, u32[]{:S(2)}, u32[]{:S(2)}) collective-permute-start(bf16[1024,512]{1,0:T(8,128)(2,1)} %collective-permute-done.4.refs_9_), channel_id=1, source_target_pairs={{0,4},{4,0},{8,12},{12,8},{16,20},{20,16},{24,28},{28,24},{1,5},{5... | collective-permute-start | bytes 3145736 | tf_op jit(solution)/shard_map/ppermute | solution.py:856
  161.9 37.6 %collective-permute-start.9 = (bf16[256,1024]{1,0:T(8,128)(2,1)}, bf16[256,1024]{1,0:T(8,128)(2,1)S(1)}, u32[]{:S(2)}, u32[]{:S(2)}) collective-permute-start(bf16[256,1024]{1,0:T(8,128)(2,1)} %collective-permute-done.5.refs_10_), channel_id=1, source_target_pairs={{0,4},{4,0},{8,12},{12,8},{16,20},{20,16},{24,28},{28,24},{1,5},{5... | collective-permute-start | bytes 1572872 | tf_op jit(solution)/shard_map/ppermute | solution.py:856
  166.0 33.6 %collective-permute-start.10 = (bf16[256,1024]{1,0:T(8,128)(2,1)}, bf16[256,1024]{1,0:T(8,128)(2,1)S(1)}, u32[]{:S(2)}, u32[]{:S(2)}) collective-permute-start(bf16[256,1024]{1,0:T(8,128)(2,1)} %collective-permute-done.6.refs_11_), channel_id=1, source_target_pairs={{0,4},{4,0},{8,12},{12,8},{16,20},{20,16},{24,28},{28,24},{1,5},{5... | collective-permute-start | bytes 1572872 | tf_op jit(solution)/shard_map/ppermute | solution.py:856
  216.2 16.5 %collective-permute-start.14 = (bf16[3,512,512]{2,1,0:T(8,128)(2,1)}, bf16[3,512,512]{2,1,0:T(8,128)(2,1)}, u32[]{:S(2)}, u32[]{:S(2)}) collective-permute-start(bf16[3,512,512]{2,1,0:T(8,128)(2,1)} %get-tuple-element.164), channel_id=1, source_target_pairs={{0,4},{4,0},{8,12},{12,8},{16,20},{20,16},{24,28},{28,24},{1,5},{5... | collective-permute-start | bytes 4718600 | tf_op jit(solution)/shard_map/ppermute | solution.py:856
  216.7 16.0 %collective-permute-start.15 = (bf16[3,512,512]{2,1,0:T(8,128)(2,1)}, bf16[3,512,512]{2,1,0:T(8,128)(2,1)}, u32[]{:S(2)}, u32[]{:S(2)}) collective-permute-start(bf16[3,512,512]{2,1,0:T(8,128)(2,1)} %get-tuple-element.166), channel_id=1, source_target_pairs={{0,4},{4,0},{8,12},{12,8},{16,20},{20,16},{24,28},{28,24},{1,5},{5... | collective-permute-start | bytes 4718600 | tf_op jit(solution)/shard_map/ppermute | solution.py:856
  216.8 22.5 %collective-permute-start.13 = (bf16[512,1024]{1,0:T(8,128)(2,1)S(1)}, bf16[512,1024]{1,0:T(8,128)(2,1)}, u32[]{:S(2)}, u32[]{:S(2)}) collective-permute-start(bf16[512,1024]{1,0:T(8,128)(2,1)S(1)} %collective-permute-done.1.refs_11_.refs_10_), channel_id=1, source_target_pairs={{0,4},{4,0},{8,12},{12,8},{16,20},{20,16},{24,28},{28,24},{1,5},{5... | collective-permute-start | bytes 3145736 | tf_op jit(solution)/shard_map/ppermute | solution.py:856
  217.2 39.0 %collective-permute-start.16 = (bf16[3,512,512]{2,1,0:T(8,128)(2,1)}, bf16[3,512,512]{2,1,0:T(8,128)(2,1)S(1)}, u32[]{:S(2)}, u32[]{:S(2)}) collective-permute-start(bf16[3,512,512]{2,1,0:T(8,128)(2,1)} %copy-done.50), channel_id=1, source_target_pairs={{0,8},{4,12},{8,0},{12,4},{16,24},{20,28},{24,16},{28,20},{1,9},{5... | collective-permute-start | bytes 4718600 | tf_op jit(solution)/shard_map/ppermute | solution.py:856
  254.6 16.5 %collective-permute-start.17 = (bf16[3,512,512]{2,1,0:T(8,128)(2,1)}, bf16[3,512,512]{2,1,0:T(8,128)(2,1)}, u32[]{:S(2)}, u32[]{:S(2)}) collective-permute-start(bf16[3,512,512]{2,1,0:T(8,128)(2,1)} %get-tuple-element.179), channel_id=1, source_target_pairs={{0,4},{4,0},{8,12},{12,8},{16,20},{20,16},{24,28},{28,24},{1,5},{5... | collective-permute-start | bytes 4718600 | tf_op jit(solution)/shard_map/ppermute | solution.py:856
  254.7 16.4 %collective-permute-start.18 = (bf16[3,512,512]{2,1,0:T(8,128)(2,1)}, bf16[3,512,512]{2,1,0:T(8,128)(2,1)}, u32[]{:S(2)}, u32[]{:S(2)}) collective-permute-start(bf16[3,512,512]{2,1,0:T(8,128)(2,1)} %get-tuple-element.181), channel_id=1, source_target_pairs={{0,4},{4,0},{8,12},{12,8},{16,20},{20,16},{24,28},{28,24},{1,5},{5... | collective-permute-start | bytes 4718600 | tf_op jit(solution)/shard_map/ppermute | solution.py:856
  255.2 39.7 %collective-permute-start.19 = (bf16[3,512,512]{2,1,0:T(8,128)(2,1)}, bf16[3,512,512]{2,1,0:T(8,128)(2,1)}, u32[]{:S(2)}, u32[]{:S(2)}) collective-permute-start(bf16[3,512,512]{2,1,0:T(8,128)(2,1)} %copy-done.52), channel_id=1, source_target_pairs={{0,8},{4,12},{8,0},{12,4},{16,24},{20,28},{24,16},{28,20},{1,9},{5... | collective-permute-start | bytes 4718600 | tf_op jit(solution)/shard_map/ppermute | solution.py:856
  255.7 39.2 %collective-permute-start.20 = (bf16[3,512,512]{2,1,0:T(8,128)(2,1)}, bf16[3,512,512]{2,1,0:T(8,128)(2,1)}, u32[]{:S(2)}, u32[]{:S(2)}) collective-permute-start(bf16[3,512,512]{2,1,0:T(8,128)(2,1)} %copy-done.51), channel_id=1, source_target_pairs={{0,16},{4,20},{8,24},{12,28},{16,0},{20,4},{24,8},{28,12},{1,17},{... | collective-permute-start | bytes 4718600 | tf_op jit(solution)/shard_map/ppermute | solution.py:856
  294.3 28.7 %collective-permute-start.21 = (bf16[3,512,512]{2,1,0:T(8,128)(2,1)}, bf16[3,512,512]{2,1,0:T(8,128)(2,1)}, u32[]{:S(2)}, u32[]{:S(2)}) collective-permute-start(bf16[3,512,512]{2,1,0:T(8,128)(2,1)} %get-tuple-element.195), channel_id=1, source_target_pairs={{0,4},{4,0},{8,12},{12,8},{16,20},{20,16},{24,28},{28,24},{1,5},{5... | collective-permute-start | bytes 4718600 | tf_op jit(solution)/shard_map/ppermute | solution.py:856
  294.4 28.6 %collective-permute-start.22 = (bf16[3,512,512]{2,1,0:T(8,128)(2,1)}, bf16[3,512,512]{2,1,0:T(8,128)(2,1)}, u32[]{:S(2)}, u32[]{:S(2)}) collective-permute-start(bf16[3,512,512]{2,1,0:T(8,128)(2,1)} %get-tuple-element.197), channel_id=1, source_target_pairs={{0,4},{4,0},{8,12},{12,8},{16,20},{20,16},{24,28},{28,24},{1,5},{5... | collective-permute-start | bytes 4718600 | tf_op jit(solution)/shard_map/ppermute | solution.py:856
  302.1 73.6 %collective-permute-start.23 = (bf16[3,512,512]{2,1,0:T(8,128)(2,1)}, bf16[3,512,512]{2,1,0:T(8,128)(2,1)}, u32[]{:S(2)}, u32[]{:S(2)}) collective-permute-start(bf16[3,512,512]{2,1,0:T(8,128)(2,1)} %get-tuple-element.204), channel_id=1, source_target_pairs={{0,16},{4,20},{8,24},{12,28},{16,0},{20,4},{24,8},{28,12},{1,17},{... | collective-permute-start | bytes 4718600 | tf_op jit(solution)/shard_map/ppermute | solution.py:856
  303.7 72.0 %collective-permute-start.24 = (bf16[3,512,512]{2,1,0:T(8,128)(2,1)}, bf16[3,512,512]{2,1,0:T(8,128)(2,1)}, u32[]{:S(2)}, u32[]{:S(2)}) collective-permute-start(bf16[3,512,512]{2,1,0:T(8,128)(2,1)} %get-tuple-element.206), channel_id=1, source_target_pairs={{0,16},{4,20},{8,24},{12,28},{16,0},{20,4},{24,8},{28,12},{1,17},{... | collective-permute-start | bytes 4718600 | tf_op jit(solution)/shard_map/ppermute | solution.py:856
  304.2 71.5 %collective-permute-start.25 = (bf16[3,512,512]{2,1,0:T(8,128)(2,1)}, bf16[3,512,512]{2,1,0:T(8,128)(2,1)}, u32[]{:S(2)}, u32[]{:S(2)}) collective-permute-start(bf16[3,512,512]{2,1,0:T(8,128)(2,1)} %get-tuple-element.207), channel_id=1, source_target_pairs={{0,8},{4,12},{8,0},{12,4},{16,24},{20,28},{24,16},{28,20},{1,9},{5... | collective-permute-start | bytes 4718600 | tf_op jit(solution)/shard_map/ppermute | solution.py:856
  307.3 26.7 %copy-start.37 = (bf16[1024,128]{1,0:T(8,128)(2,1)S(1)}, bf16[1024,128]{1,0:T(8,128)(2,1)}, u32[]{:S(2)}) copy-start(bf16[1024,128]{1,0:T(8,128)(2,1)} %get-tuple-element.130.refs_4_.refs_7_) | copy-start | bytes 786436
  345.3 30.4 %copy-start.17 = (bf16[3,512,512]{2,1,0:T(8,128)(2,1)S(1)}, bf16[3,512,512]{2,1,0:T(8,128)(2,1)}, u32[]{:S(2)}) copy-start(bf16[3,512,512]{2,1,0:T(8,128)(2,1)} %copy-done.16) | copy-start | bytes 4718596
  345.3 30.4 %copy-start.19 = (bf16[3,512,512]{2,1,0:T(8,128)(2,1)S(1)}, bf16[3,512,512]{2,1,0:T(8,128)(2,1)}, u32[]{:S(2)}) copy-start(bf16[3,512,512]{2,1,0:T(8,128)(2,1)} %copy-done.18) | copy-start | bytes 4718596
  (61 other events, 204.3 us)
Sparse Core Ops, SparseCore 0:
  72.1 46.1 all-gather.1
  385.5 138.8 all-reduce.3

commit v7 on v6

--- a/solution.py
+++ b/solution.py
@@ -20,7 +20,7 @@
 VMEM = pl.BlockSpec(memory_space=pltpu.VMEM)
 VMEM_BYTES = 60 * 1024 * 1024
 LESS_BYTES = 30 * 1024 * 1024
-EXPERT_BYTES = 43 * 1024 * 1024
+EXPERT_BYTES = 22 * 1024 * 1024
 
 
 def dot(a, b):

time: 550 us -> 518 us (0.942)
  Pallas kernels: 431 us -> 404 us
  local copies, waits for them, and re-layouts: 64.3 us -> 57.9 us
    pallas_call x8, Pallas kernels: 121 us -> 101 us  [moe(): pl.pallas_call(functools.partial(moe_kernel, tuple(slots), chunks, first,...]
    pallas_call x6, Pallas kernels: 26.8 us -> 18.5 us  [plus(): pl.pallas_call(tied(functools.partial(plus_kernel, counts), len(flat), ti...]
    unnamed x137 -> x143, local copies, waits for them, and re-layouts: 57.5 us -> 51.3 us
  transfers between devices with their start and end apart: 28 -> 28, of which waited for: 2 -> 4; matrix products, arithmetic and copies ran while one was open for 3% -> 3% of each run, Pallas kernels for 62% -> 61%
where the time goes in v7:
time: 518 us; the launch traced here: 509 us
  Pallas kernels  404 us (78%)
  local copies, waits for them, and re-layouts  57.9 us (11%)
  starting transfers between devices  16.6 us (3%)
  between operations  14.9 us (3%)
  waiting for transfers between devices  11.3 us (2%)
    pallas_call x8, Pallas kernels, moe(): pl.pallas_call(functools.partial(moe_kernel, tuple(slots), chunks, first,...  101 us
    pallas_call x1, Pallas kernels, reduce_all(): pl.pallas_call(functools.partial(reduce_kernel, size, columns), in_specs=...  81 us
    pallas_call x2, Pallas kernels, attend_back(): pl.pallas_call(tied(attend_back_kernel, 6, ties), grid=(rows // SEQUENCE_...  60.9 us
    pallas_call x1, Pallas kernels, gather_weights(): pl.pallas_call(functools.partial(gather_kernel, size, len(owned)), in_spe...  59.7 us
    unnamed x143, local copies, waits for them, and re-layouts  51.3 us
    pallas_call x1, Pallas kernels, attend(): pl.pallas_call(tied(attend_kernel, 3, ties), grid=(rows // SEQUENCE_LENGT...  35.3 us
    pallas_call x6, Pallas kernels, plus(): pl.pallas_call(tied(functools.partial(plus_kernel, counts), len(flat), ti...  18.5 us
    ppermute x26, starting transfers between devices, flip(): return lax.ppermute(value, axis, [(i, i ^ bit) for i in range(size)])  16.5 us
  transfers between devices with their start and end apart: 28, of which 4 were waited for; matrix products, arithmetic and copies ran while one was open for 3% of the time, Pallas kernels for 61%

profile of v7, /device:TPU:0, one launch (start us, length us, event | category | flops | bytes accessed | tf_op | source)
XLA Modules:
  0.0 508.7 jit_solution(2221696962748478455)
XLA Ops:
  10.0 59.7 %gather_weights.1 = (bf16[1024,2048]{1,0:T(8,128)(2,1)}, bf16[1024,128]{1,0:T(8,128)(2,1)}, bf16[256,1024]{1,0:T(8,128)(2,1)}, bf16[512,1024]{1,0:T(8,128)(2,1)}...) custom-call(bf16[256,1024]{1,0:T(8,128)(2,1)} %refs_0_.1, ...), custom_call_target="tpu_custom_call" | custom-call | flops 1000000000 | bytes 25165824 | tf_op jit(solution)/shard_map/gather_weights/pallas_call | solution.py:688
  74.0 9.1 %project.1 = (bf16[1024,1024]{1,0:T(8,128)(2,1)}, bf16[1024,1024]{1,0:T(8,128)(2,1)}, bf16[1024,512]{1,0:T(8,128)(2,1)}, bf16[1024,512]{1,0:T(8,128)(2,1)}) custom-call(bf16[1024,1024]{1,0:T(8,128)(2,1)} %refs_7_.1, bf16[128,1024]{1,0:T(8,128)(2,1)} %get-tuple-element.124.gain_ref.refs_3_.refs_6_.refs_9_, ...), custom_call_target="tpu_custom_call" | custom-call | flops 4294967296 | bytes 12582912 | tf_op jit(solution)/shard_map/project/pallas_call | solution.py:104
  83.1 35.3 %attend.1.refs_0_ = bf16[1024,1024]{1,0:T(8,128)(2,1)} custom-call(bf16[1024,1024]{1,0:T(8,128)(2,1)} %get-tuple-element.126.refs_0_, bf16[1024,512]{1,0:T(8,128)(2,1)} %get-tuple-element.127.refs_1_, bf16[1024,512]{1,0:T(8,128)(2,1)} %get-tuple-element.128.refs_2_), custom_call_target="tpu_custom_call" | custom-call | flops 34359738368 | bytes 6291456 | tf_op jit(solution)/shard_map/attend/pallas_call | solution.py:140
  124.2 4.1 copy.60
  138.4 5.3 %middle.1 = (f32[1024,1024]{1,0:T(8,128)S(1)}, bf16[1024,1024]{1,0:T(8,128)(2,1)S(1)}, bf16[1024,1024]{1,0:T(8,128)(2,1)S(1)}, f32[1024,128]{1,0:T(8,128)S(1)}) custom-call(bf16[1024,1024]{1,0:T(8,128)(2,1)S(1)} %copy-done.17, bf16[1024,1024]{1,0:T(8,128)(2,1)S(1)} %copy-done.2, bf16[1024,1024]{1,0:T(8,128)(2,1)S(1)} %copy-done, ...), custom_call_target="tpu_custom_call" | custom-call | flops 2415919104 | bytes 14680064 | tf_op jit(solution)/shard_map/middle/pallas_call | solution.py:227
  143.8 2.4 copy-done.15
  146.3 12.2 %experts.8 = (f32[1024,1024]{1,0:T(8,128)S(1)}, f32[1024,1024]{1,0:T(8,128)S(1)}, f32[1024,128]{1,0:T(8,128)S(1)}, bf16[3,512,512]{2,1,0:T(8,128)(2,1)S(1)}, bf16[3,512,512]{2,1,0:T(8,128)(2,1)S(1)}) custom-call(s32[1]{0:T(128)} %bitcast.3.me_ref, bf16[1024,1024]{1,0:T(8,128)(2,1)S(1)} %get-tuple-element.137.refs_0_, ...), custom_call_target="tpu_custom_call" | custom-call | flops 9663676416 | bytes 20971520 | tf_op jit(solution)/shard_map/experts/pallas_call | solution.py:349
  159.6 2.3 collective-permute-done.11.refs_1_
  162.1 12.2 %experts.9 = (f32[1024,1024]{1,0:T(8,128)S(1)}, f32[1024,1024]{1,0:T(8,128)S(1)}, f32[1024,128]{1,0:T(8,128)S(1)}, bf16[3,512,512]{2,1,0:T(8,128)(2,1)S(1)}, bf16[3,512,512]{2,1,0:T(8,128)(2,1)S(1)}) custom-call(s32[1]{0:T(128)} %bitcast.3.me_ref, ...), custom_call_target="tpu_custom_call", output_to_operand_aliasing={{0}: (6, {}), {1}: (7, {}), {2}: (8, {})} | custom-call | flops 9663676416 | bytes 20971520 | tf_op jit(solution)/shard_map/experts/pallas_call | solution.py:349
  176.4 2.5 plus.6
  179.8 12.8 %experts.10 = (f32[1024,1024]{1,0:T(8,128)S(1)}, f32[1024,1024]{1,0:T(8,128)S(1)}, f32[1024,128]{1,0:T(8,128)S(1)}, bf16[3,512,512]{2,1,0:T(8,128)(2,1)S(1)}, bf16[3,512,512]{2,1,0:T(8,128)(2,1)S(1)}) custom-call(s32[1]{0:T(128)} %bitcast.3.me_ref, ...), custom_call_target="tpu_custom_call", output_to_operand_aliasing={{0}: (6, {}), {1}: (7, {}), {2}: (8, {})} | custom-call | flops 9663676416 | bytes 20971520 | tf_op jit(solution)/shard_map/experts/pallas_call | solution.py:349
  195.1 13.1 %experts.11 = (f32[1024,1024]{1,0:T(8,128)S(1)}, f32[1024,1024]{1,0:T(8,128)S(1)}, f32[1024,128]{1,0:T(8,128)S(1)}, bf16[3,512,512]{2,1,0:T(8,128)(2,1)S(1)}, bf16[3,512,512]{2,1,0:T(8,128)(2,1)S(1)}) custom-call(s32[1]{0:T(128)} %bitcast.3.me_ref, ...), custom_call_target="tpu_custom_call", output_to_operand_aliasing={{0}: (6, {}), {1}: (7, {}), {2}: (8, {})} | custom-call | flops 9663676416 | bytes 20971520 | tf_op jit(solution)/shard_map/experts/pallas_call | solution.py:349
  208.2 2.9 plus.7
  211.2 12.8 %experts.12 = (f32[1024,1024]{1,0:T(8,128)S(1)}, f32[1024,1024]{1,0:T(8,128)S(1)}, f32[1024,128]{1,0:T(8,128)S(1)}, bf16[3,512,512]{2,1,0:T(8,128)(2,1)}, bf16[3,512,512]{2,1,0:T(8,128)(2,1)}) custom-call(s32[1]{0:T(128)} %bitcast.3.me_ref, ...), custom_call_target="tpu_custom_call", output_to_operand_aliasing={{0}: (6, {}), {1}: (7, {}), {2}: (8, {})} | custom-call | flops 9663676416 | bytes 20971520 | tf_op jit(solution)/shard_map/experts/pallas_call | solution.py:349
  230.2 2.2 copy-done.10
  233.5 12.3 %experts.13 = (f32[1024,1024]{1,0:T(8,128)S(1)}, f32[1024,1024]{1,0:T(8,128)S(1)}, f32[1024,128]{1,0:T(8,128)S(1)}, bf16[3,512,512]{2,1,0:T(8,128)(2,1)S(1)}, bf16[3,512,512]{2,1,0:T(8,128)(2,1)S(1)}) custom-call(s32[1]{0:T(128)} %bitcast.3.me_ref, ...), custom_call_target="tpu_custom_call", output_to_operand_aliasing={{0}: (6, {}), {1}: (7, {}), {2}: (8, {})} | custom-call | flops 9663676416 | bytes 20971520 | tf_op jit(solution)/shard_map/experts/pallas_call | solution.py:349
  255.0 13.0 %experts.14 = (f32[1024,1024]{1,0:T(8,128)S(1)}, f32[1024,1024]{1,0:T(8,128)S(1)}, f32[1024,128]{1,0:T(8,128)S(1)}, bf16[3,512,512]{2,1,0:T(8,128)(2,1)}, bf16[3,512,512]{2,1,0:T(8,128)(2,1)}) custom-call(s32[1]{0:T(128)} %bitcast.3.me_ref, ...), custom_call_target="tpu_custom_call", output_to_operand_aliasing={{0}: (6, {}), {1}: (7, {}), {2}: (8, {})} | custom-call | flops 9663676416 | bytes 20971520 | tf_op jit(solution)/shard_map/experts/pallas_call | solution.py:349
  270.1 2.8 plus.9
  274.9 2.3 collective-permute-start.25
  277.3 12.3 %experts.15 = (f32[1024,1024]{1,0:T(8,128)S(1)}, f32[1024,1024]{1,0:T(8,128)S(1)}, f32[1024,128]{1,0:T(8,128)S(1)}, bf16[3,512,512]{2,1,0:T(8,128)(2,1)S(1)}, bf16[3,512,512]{2,1,0:T(8,128)(2,1)S(1)}) custom-call(s32[1]{0:T(128)} %bitcast.3.me_ref, bf16[1024,1024]{1,0:T(8,128)(2,1)S(1)} %copy-done.52, ...), custom_call_target="tpu_custom_call", output_to_operand_aliasing={{0}: (6, {}), {1}: (7, {}), {2}: (8, {})} | custom-call | flops 9663676416 | bytes 20971520 | tf_op jit(solution)/shard_map/experts/pallas_call | solution.py:349
  289.5 2.0 copy-done.13
  291.6 5.2 %plus.10 = (bf16[3,512,512]{2,1,0:T(8,128)(2,1)S(1)}, bf16[3,512,512]{2,1,0:T(8,128)(2,1)S(1)}, f32[8,128]{1,0:T(8,128)S(1)}) custom-call(bf16[3,512,512]{2,1,0:T(8,128)(2,1)S(1)} %get-tuple-element.194.refs_0_, bf16[3,512,512]{2,1,0:T(8,128)(2,1)} %collective-permute-done.21.refs_1_, bf16[3,512,512]{2,1,0:T(8,128)(2,1)S(1)} %get-tuple-element.196.refs_2_, ...), custom_call_target="tpu_custom_call" | custom-call | flops 3145728 | bytes 9437184 | tf_op jit(solution)/shard_map/plus/pallas_call | solution.py:539
  299.2 8.0 %turn.1 = (bf16[1024,1024]{1,0:T(8,128)(2,1)}, f32[1024,1024]{1,0:T(8,128)S(1)}, bf16[1024,1024]{1,0:T(8,128)(2,1)S(1)}, bf16[1024,1024]{1,0:T(8,128)(2,1)S(1)},...) custom-call(f32[1024,1024]{1,0:T(8,128)S(1)} %get-tuple-element.136.refs_0_, f32[1024,1024]{1,0:T(8,128)} %copy-done.6, ...), custom_call_target="tpu_custom_call" | custom-call | flops 2684354560 | bytes 29360128 | tf_op jit(solution)/shard_map/turn/pallas_call | solution.py:402
  307.2 3.7 convolution_convert_fusion.refs_6_
  311.0 30.6 %attend_back.2 = (bf16[1024,512]{1,0:T(8,128)(2,1)}, bf16[1024,256]{1,0:T(8,128)(2,1)}, bf16[1024,256]{1,0:T(8,128)(2,1)}) custom-call(bf16[1024,1024]{1,0:T(8,128)(2,1)} %get-tuple-element.126.refs_0_, bf16[1024,512]{1,0:T(8,128)(2,1)} %get-tuple-element.127.refs_1_, bf16[1024,512]{1,0:T(8,128)(2,1)} %get-tuple-element.128.refs_2_, ...), custom_call_target="tpu_custom_call" | custom-call | flops 42949672960 | bytes 12582912 | tf_op jit(solution)/shard_map/attend_back/pallas_call | solution.py:190
  345.8 4.3 plus.11
  353.0 30.3 %attend_back.3 = (bf16[1024,512]{1,0:T(8,128)(2,1)}, bf16[1024,256]{1,0:T(8,128)(2,1)}, bf16[1024,256]{1,0:T(8,128)(2,1)}) custom-call(bf16[1024,1024]{1,0:T(8,128)(2,1)} %get-tuple-element.126.refs_0_, bf16[1024,512]{1,0:T(8,128)(2,1)} %get-tuple-element.127.refs_1_, bf16[1024,512]{1,0:T(8,128)(2,1)} %get-tuple-element.128.refs_2_, ...), custom_call_target="tpu_custom_call" | custom-call | flops 42949672960 | bytes 12582912 | tf_op jit(solution)/shard_map/attend_back/pallas_call | solution.py:190
  383.3 8.2 %weights_back.1 = (bf16[1024,512]{1,0:T(8,128)(2,1)}, bf16[1024,512]{1,0:T(8,128)(2,1)}, bf16[1024,256]{1,0:T(8,128)(2,1)}, bf16[1024,256]{1,0:T(8,128)(2,1)}, b...) custom-call(bf16[1024,1024]{1,0:T(8,128)(2,1)} %get-tuple-element.218.refs_0_, ...), custom_call_target="tpu_custom_call" | custom-call | flops 1 | bytes 1 | tf_op jit(solution)/shard_map/weights_back/pallas_call | solution.py:477
  391.5 11.6 %finish.1 = (f32[1024,1024]{1,0:T(8,128)}, bf16[1024,128]{1,0:T(8,128)(2,1)}) custom-call(bf16[1024,512]{1,0:T(8,128)(2,1)} %get-tuple-element.202.refs_0_.refs_1_, bf16[1024,512]{1,0:T(8,128)(2,1)} %get-tuple-element.210.refs_1_.refs_2_, bf16[1024,256]{1,0:T(8,128)(2,1)} %get-tuple-element.211.refs_2_.refs_3_, ...), custom_call_target="tpu_custom_call" | custom-call | flops 1 | bytes 1 | tf_op jit(solution)/shard_map/finish/pallas_call | solution.py:454
  403.1 81.0 %reduce_all.1 = (f32[256,1024]{1,0:T(8,128)}, f32[256,1024]{1,0:T(8,128)}, f32[256,512]{1,0:T(8,128)}, f32[256,512]{1,0:T(8,128)}, f32[256,128]{1,0:T(8,128)}) custom-call(bf16[4,256,1024]{2,1,0:T(8,128)(2,1)} %bitcast.33, bf16[4,256,512]{2,1,0:T(8,128)(2,1)} %bitcast.35, bf16[4,256,512]{2,1,0:T(8,128)(2,1)} %bitcast.36, bf16[4,256,256]{2,1,0:T(8,128)(2,1)} %bitcast.37, ...), custom_call_target="tpu_custom_call" | custom-call | flops 1 | bytes 1 | tf_op jit(solution)/shard_map/reduce_all/pallas_call | solution.py:832
  487.5 5.2 %all-reduce.4.cloned.1.call-done = (bf16[3,512,512]{2,1,0:T(8,128)(2,1)}, bf16[3,512,512]{2,1,0:T(8,128)(2,1)}) async-done(((bf16[3,512,512]{2,1,0:T(8,128)(2,1)}, bf16[3,512,512]{2,1,0:T(8,128)(2,1)}), (bf16[3,512,512]{2,1,0:T(8,128)(2,1)}, bf16[3,512,512]{2,1,0:T(8,128)(2,1)})) %all-reduce.4.cloned.1.call-update) | async-done | bytes 3145744 | tf_op jit(solution)/shard_map/psum | solution.py:979
  492.7 5.3 %widen.1 = (f32[1024,512]{1,0:T(8,128)}, f32[1024,512]{1,0:T(8,128)}, f32[512,1024]{1,0:T(8,128)}) custom-call(bf16[3,512,512]{2,1,0:T(8,128)(2,1)} %get-tuple-element.274.top_ref, bf16[3,512,512]{2,1,0:T(8,128)(2,1)} %get-tuple-element.275.bottom_ref), custom_call_target="tpu_custom_call" | custom-call | flops 1 | bytes 1 | tf_op jit(solution)/shard_map/widen/pallas_call | solution.py:504
  (203 shorter events, 66.7 us)
Async XLA Ops:
  7.2 121.1 %all-gather.2.cloned.1.call-start = ((), (), s32[]{:S(2)}) async-start(), calls=%async_computation | async-start | bytes 2621440 | tf_op jit(solution)/shard_map/all_gather | solution.py:910
  69.7 48.7 %collective-permute-start = (bf16[512,1024]{1,0:T(8,128)(2,1)}, bf16[512,1024]{1,0:T(8,128)(2,1)}, u32[]{:S(2)}, u32[]{:S(2)}) collective-permute-start(bf16[512,1024]{1,0:T(8,128)(2,1)} %get-tuple-element.133), channel_id=1, source_target_pairs={{0,8},{4,12},{8,0},{12,4},{16,24},{20,28},{24,16},{28,20},{1,9},{5... | collective-permute-start | bytes 3145736 | tf_op jit(solution)/shard_map/ppermute | solution.py:856
  70.3 48.1 %collective-permute-start.1 = (bf16[512,1024]{1,0:T(8,128)(2,1)}, bf16[512,1024]{1,0:T(8,128)(2,1)S(1)}, u32[]{:S(2)}, u32[]{:S(2)}) collective-permute-start(bf16[512,1024]{1,0:T(8,128)(2,1)} %get-tuple-element.133), channel_id=1, source_target_pairs={{0,16},{4,20},{8,24},{12,28},{16,0},{20,4},{24,8},{28,12},{1,17},{... | collective-permute-start | bytes 3145736 | tf_op jit(solution)/shard_map/ppermute | solution.py:856
  71.9 420.9 %all-reduce.4.cloned.1.call-start = ((), (), s32[]{:S(2)}) async-start(), calls=%async_computation.1 | async-start | bytes 6291456 | tf_op jit(solution)/shard_map/psum | solution.py:979
  71.9 71.8 %collective-permute-start.3 = (bf16[1024,512]{1,0:T(8,128)(2,1)}, bf16[1024,512]{1,0:T(8,128)(2,1)}, u32[]{:S(2)}, u32[]{:S(2)}) collective-permute-start(bf16[1024,512]{1,0:T(8,128)(2,1)} %get-tuple-element.131.refs_6_.refs_8_), channel_id=1, source_target_pairs={{0,16},{4,20},{8,24},{12,28},{16,0},{20,4},{24,8},{28,12},{1,17},{... | collective-permute-start | bytes 3145736 | tf_op jit(solution)/shard_map/ppermute | solution.py:856
  72.5 71.3 %collective-permute-start.4 = (bf16[1024,512]{1,0:T(8,128)(2,1)}, bf16[1024,512]{1,0:T(8,128)(2,1)}, u32[]{:S(2)}, u32[]{:S(2)}) collective-permute-start(bf16[1024,512]{1,0:T(8,128)(2,1)} %get-tuple-element.135.refs_10_.refs_9_), channel_id=1, source_target_pairs={{0,8},{4,12},{8,0},{12,4},{16,24},{20,28},{24,16},{28,20},{1,9},{5... | collective-permute-start | bytes 3145736 | tf_op jit(solution)/shard_map/ppermute | solution.py:856
  118.4 25.4 %collective-permute-start.2 = (bf16[512,1024]{1,0:T(8,128)(2,1)}, bf16[512,1024]{1,0:T(8,128)(2,1)}, u32[]{:S(2)}, u32[]{:S(2)}) collective-permute-start(bf16[512,1024]{1,0:T(8,128)(2,1)} %collective-permute-done.refs_8_.refs_10_), channel_id=1, source_target_pairs={{0,4},{4,0},{8,12},{12,8},{16,20},{20,16},{24,28},{28,24},{1,5},{5... | collective-permute-start | bytes 3145736 | tf_op jit(solution)/shard_map/ppermute | solution.py:856
  120.4 23.4 %collective-permute-start.5 = (bf16[256,1024]{1,0:T(8,128)(2,1)}, bf16[256,1024]{1,0:T(8,128)(2,1)}, u32[]{:S(2)}, u32[]{:S(2)}) collective-permute-start(bf16[256,1024]{1,0:T(8,128)(2,1)} %slice.20), channel_id=1, source_target_pairs={{0,16},{4,20},{8,24},{12,28},{16,0},{20,4},{24,8},{28,12},{1,17},{... | collective-permute-start | bytes 1572872 | tf_op jit(solution)/shard_map/ppermute | solution.py:856
  122.7 21.1 %collective-permute-start.6 = (bf16[256,1024]{1,0:T(8,128)(2,1)}, bf16[256,1024]{1,0:T(8,128)(2,1)}, u32[]{:S(2)}, u32[]{:S(2)}) collective-permute-start(bf16[256,1024]{1,0:T(8,128)(2,1)} %slice.21), channel_id=1, source_target_pairs={{0,8},{4,12},{8,0},{12,4},{16,24},{20,28},{24,16},{28,20},{1,9},{5... | collective-permute-start | bytes 1572872 | tf_op jit(solution)/shard_map/ppermute | solution.py:856
  143.7 109.6 %copy-start.51 = (bf16[1024,1024]{1,0:T(8,128)(2,1)}, bf16[1024,1024]{1,0:T(8,128)(2,1)S(1)}, u32[]{:S(2)}) copy-start(bf16[1024,1024]{1,0:T(8,128)(2,1)S(1)} %get-tuple-element.137.refs_0_) | copy-start | bytes 6291460
  143.7 133.5 %copy-start.43 = (f32[1024,128]{1,0:T(8,128)}, f32[1024,128]{1,0:T(8,128)S(1)}, u32[]{:S(2)}) copy-start(f32[1024,128]{1,0:T(8,128)S(1)} %get-tuple-element.139.refs_4_.refs_3_) | copy-start | bytes 1572868
  158.5 3.5 collective-permute-start.11
  158.5 17.8 %collective-permute-start.12 = (bf16[3,512,512]{2,1,0:T(8,128)(2,1)S(1)}, bf16[3,512,512]{2,1,0:T(8,128)(2,1)S(1)}, u32[]{:S(2)}, u32[]{:S(2)}) collective-permute-start(bf16[3,512,512]{2,1,0:T(8,128)(2,1)S(1)} %get-tuple-element.152), channel_id=1, source_target_pairs={{0,4},{4,0},{8,12},{12,8},{16,20},{20,16},{24,28},{28,24},{1,5},{5... | collective-permute-start | bytes 4718600 | tf_op jit(solution)/shard_map/ppermute | solution.py:856
  159.0 19.8 %collective-permute-start.7 = (bf16[1024,512]{1,0:T(8,128)(2,1)}, bf16[1024,512]{1,0:T(8,128)(2,1)S(1)}, u32[]{:S(2)}, u32[]{:S(2)}) collective-permute-start(bf16[1024,512]{1,0:T(8,128)(2,1)} %collective-permute-done.3.refs_8_), channel_id=1, source_target_pairs={{0,4},{4,0},{8,12},{12,8},{16,20},{20,16},{24,28},{28,24},{1,5},{5... | collective-permute-start | bytes 3145736 | tf_op jit(solution)/shard_map/ppermute | solution.py:856
  159.1 19.7 %collective-permute-start.8 = (bf16[1024,512]{1,0:T(8,128)(2,1)}, bf16[1024,512]{1,0:T(8,128)(2,1)S(1)}, u32[]{:S(2)}, u32[]{:S(2)}) collective-permute-start(bf16[1024,512]{1,0:T(8,128)(2,1)} %collective-permute-done.4.refs_9_), channel_id=1, source_target_pairs={{0,4},{4,0},{8,12},{12,8},{16,20},{20,16},{24,28},{28,24},{1,5},{5... | collective-permute-start | bytes 3145736 | tf_op jit(solution)/shard_map/ppermute | solution.py:856
  159.6 19.3 %collective-permute-start.9 = (bf16[256,1024]{1,0:T(8,128)(2,1)}, bf16[256,1024]{1,0:T(8,128)(2,1)S(1)}, u32[]{:S(2)}, u32[]{:S(2)}) collective-permute-start(bf16[256,1024]{1,0:T(8,128)(2,1)} %collective-permute-done.5.refs_10_), channel_id=1, source_target_pairs={{0,4},{4,0},{8,12},{12,8},{16,20},{20,16},{24,28},{28,24},{1,5},{5... | collective-permute-start | bytes 1572872 | tf_op jit(solution)/shard_map/ppermute | solution.py:856
  161.9 16.9 %collective-permute-start.10 = (bf16[256,1024]{1,0:T(8,128)(2,1)}, bf16[256,1024]{1,0:T(8,128)(2,1)S(1)}, u32[]{:S(2)}, u32[]{:S(2)}) collective-permute-start(bf16[256,1024]{1,0:T(8,128)(2,1)} %collective-permute-done.6.refs_11_), channel_id=1, source_target_pairs={{0,4},{4,0},{8,12},{12,8},{16,20},{20,16},{24,28},{28,24},{1,5},{5... | collective-permute-start | bytes 1572872 | tf_op jit(solution)/shard_map/ppermute | solution.py:856
  192.6 15.6 %collective-permute-start.14 = (bf16[3,512,512]{2,1,0:T(8,128)(2,1)S(1)}, bf16[3,512,512]{2,1,0:T(8,128)(2,1)S(1)}, u32[]{:S(2)}, u32[]{:S(2)}) collective-permute-start(bf16[3,512,512]{2,1,0:T(8,128)(2,1)S(1)} %get-tuple-element.164), channel_id=1, source_target_pairs={{0,4},{4,0},{8,12},{12,8},{16,20},{20,16},{24,28},{28,24},{1,5},{5... | collective-permute-start | bytes 4718600 | tf_op jit(solution)/shard_map/ppermute | solution.py:856
  193.0 15.2 %collective-permute-start.15 = (bf16[3,512,512]{2,1,0:T(8,128)(2,1)S(1)}, bf16[3,512,512]{2,1,0:T(8,128)(2,1)S(1)}, u32[]{:S(2)}, u32[]{:S(2)}) collective-permute-start(bf16[3,512,512]{2,1,0:T(8,128)(2,1)S(1)} %get-tuple-element.166), channel_id=1, source_target_pairs={{0,4},{4,0},{8,12},{12,8},{16,20},{20,16},{24,28},{28,24},{1,5},{5... | collective-permute-start | bytes 4718600 | tf_op jit(solution)/shard_map/ppermute | solution.py:856
  193.2 17.9 %collective-permute-start.13 = (bf16[512,1024]{1,0:T(8,128)(2,1)S(1)}, bf16[512,1024]{1,0:T(8,128)(2,1)S(1)}, u32[]{:S(2)}, u32[]{:S(2)}) collective-permute-start(bf16[512,1024]{1,0:T(8,128)(2,1)S(1)} %collective-permute-done.1.refs_11_.refs_10_), channel_id=1, source_target_pairs={{0,4},{4,0},{8,12},{12,8},{16,20},{20,16},{24,28},{28,24},{1,5},{5... | collective-permute-start | bytes 3145736 | tf_op jit(solution)/shard_map/ppermute | solution.py:856
  193.6 36.7 %collective-permute-start.16 = (bf16[3,512,512]{2,1,0:T(8,128)(2,1)}, bf16[3,512,512]{2,1,0:T(8,128)(2,1)S(1)}, u32[]{:S(2)}, u32[]{:S(2)}) collective-permute-start(bf16[3,512,512]{2,1,0:T(8,128)(2,1)} %get-tuple-element.171), channel_id=1, source_target_pairs={{0,8},{4,12},{8,0},{12,4},{16,24},{20,28},{24,16},{28,20},{1,9},{5... | collective-permute-start | bytes 4718600 | tf_op jit(solution)/shard_map/ppermute | solution.py:856
  226.8 21.8 %collective-permute-start.17 = (bf16[3,512,512]{2,1,0:T(8,128)(2,1)}, bf16[3,512,512]{2,1,0:T(8,128)(2,1)S(1)}, u32[]{:S(2)}, u32[]{:S(2)}) collective-permute-start(bf16[3,512,512]{2,1,0:T(8,128)(2,1)} %get-tuple-element.179), channel_id=1, source_target_pairs={{0,4},{4,0},{8,12},{12,8},{16,20},{20,16},{24,28},{28,24},{1,5},{5... | collective-permute-start | bytes 4718600 | tf_op jit(solution)/shard_map/ppermute | solution.py:856
  226.8 21.8 %collective-permute-start.18 = (bf16[3,512,512]{2,1,0:T(8,128)(2,1)}, bf16[3,512,512]{2,1,0:T(8,128)(2,1)S(1)}, u32[]{:S(2)}, u32[]{:S(2)}) collective-permute-start(bf16[3,512,512]{2,1,0:T(8,128)(2,1)} %get-tuple-element.181), channel_id=1, source_target_pairs={{0,4},{4,0},{8,12},{12,8},{16,20},{20,16},{24,28},{28,24},{1,5},{5... | collective-permute-start | bytes 4718600 | tf_op jit(solution)/shard_map/ppermute | solution.py:856
  227.3 41.3 %collective-permute-start.19 = (bf16[3,512,512]{2,1,0:T(8,128)(2,1)}, bf16[3,512,512]{2,1,0:T(8,128)(2,1)S(1)}, u32[]{:S(2)}, u32[]{:S(2)}) collective-permute-start(bf16[3,512,512]{2,1,0:T(8,128)(2,1)} %get-tuple-element.187), channel_id=1, source_target_pairs={{0,8},{4,12},{8,0},{12,4},{16,24},{20,28},{24,16},{28,20},{1,9},{5... | collective-permute-start | bytes 4718600 | tf_op jit(solution)/shard_map/ppermute | solution.py:856
  227.8 40.8 %collective-permute-start.20 = (bf16[3,512,512]{2,1,0:T(8,128)(2,1)}, bf16[3,512,512]{2,1,0:T(8,128)(2,1)S(1)}, u32[]{:S(2)}, u32[]{:S(2)}) collective-permute-start(bf16[3,512,512]{2,1,0:T(8,128)(2,1)} %get-tuple-element.189), channel_id=1, source_target_pairs={{0,16},{4,20},{8,24},{12,28},{16,0},{20,4},{24,8},{28,12},{1,17},{... | collective-permute-start | bytes 4718600 | tf_op jit(solution)/shard_map/ppermute | solution.py:856
  233.5 19.8 %copy-start.57 = (bf16[512,1024]{1,0:T(8,128)(2,1)S(1)}, bf16[512,1024]{1,0:T(8,128)(2,1)}, u32[]{:S(2)}) copy-start(bf16[512,1024]{1,0:T(8,128)(2,1)} %get-tuple-element.177.refs_10_) | copy-start | bytes 3145732
  268.1 23.5 %collective-permute-start.21 = (bf16[3,512,512]{2,1,0:T(8,128)(2,1)}, bf16[3,512,512]{2,1,0:T(8,128)(2,1)}, u32[]{:S(2)}, u32[]{:S(2)}) collective-permute-start(bf16[3,512,512]{2,1,0:T(8,128)(2,1)} %get-tuple-element.195), channel_id=1, source_target_pairs={{0,4},{4,0},{8,12},{12,8},{16,20},{20,16},{24,28},{28,24},{1,5},{5... | collective-permute-start | bytes 4718600 | tf_op jit(solution)/shard_map/ppermute | solution.py:856
  268.1 23.4 %collective-permute-start.22 = (bf16[3,512,512]{2,1,0:T(8,128)(2,1)}, bf16[3,512,512]{2,1,0:T(8,128)(2,1)}, u32[]{:S(2)}, u32[]{:S(2)}) collective-permute-start(bf16[3,512,512]{2,1,0:T(8,128)(2,1)} %get-tuple-element.197), channel_id=1, source_target_pairs={{0,4},{4,0},{8,12},{12,8},{16,20},{20,16},{24,28},{28,24},{1,5},{5... | collective-permute-start | bytes 4718600 | tf_op jit(solution)/shard_map/ppermute | solution.py:856
  272.9 68.7 %collective-permute-start.23 = (bf16[3,512,512]{2,1,0:T(8,128)(2,1)}, bf16[3,512,512]{2,1,0:T(8,128)(2,1)}, u32[]{:S(2)}, u32[]{:S(2)}) collective-permute-start(bf16[3,512,512]{2,1,0:T(8,128)(2,1)} %get-tuple-element.204), channel_id=1, source_target_pairs={{0,16},{4,20},{8,24},{12,28},{16,0},{20,4},{24,8},{28,12},{1,17},{... | collective-permute-start | bytes 4718600 | tf_op jit(solution)/shard_map/ppermute | solution.py:856
  273.4 69.9 %collective-permute-start.24 = (bf16[3,512,512]{2,1,0:T(8,128)(2,1)}, bf16[3,512,512]{2,1,0:T(8,128)(2,1)}, u32[]{:S(2)}, u32[]{:S(2)}) collective-permute-start(bf16[3,512,512]{2,1,0:T(8,128)(2,1)} %copy-done.54), channel_id=1, source_target_pairs={{0,16},{4,20},{8,24},{12,28},{16,0},{20,4},{24,8},{28,12},{1,17},{... | collective-permute-start | bytes 4718600 | tf_op jit(solution)/shard_map/ppermute | solution.py:856
  274.9 68.4 %collective-permute-start.25 = (bf16[3,512,512]{2,1,0:T(8,128)(2,1)}, bf16[3,512,512]{2,1,0:T(8,128)(2,1)}, u32[]{:S(2)}, u32[]{:S(2)}) collective-permute-start(bf16[3,512,512]{2,1,0:T(8,128)(2,1)} %get-tuple-element.207), channel_id=1, source_target_pairs={{0,8},{4,12},{8,0},{12,4},{16,24},{20,28},{24,16},{28,20},{1,9},{5... | collective-permute-start | bytes 4718600 | tf_op jit(solution)/shard_map/ppermute | solution.py:856
  311.0 32.3 %copy-start.21 = (bf16[3,512,512]{2,1,0:T(8,128)(2,1)S(1)}, bf16[3,512,512]{2,1,0:T(8,128)(2,1)}, u32[]{:S(2)}) copy-start(bf16[3,512,512]{2,1,0:T(8,128)(2,1)} %copy-done.20) | copy-start | bytes 4718596
  (64 other events, 300.1 us)
Sparse Core Ops, SparseCore 0:
  72.0 46.1 all-gather.1
  353.1 139.5 all-reduce.3
